TPU v7x, 512 devices: a whole 4x4x16 slice. The times are simulated.
512 devices in a mesh: ctx: 64 (over z, x), head: 8 (over y, core).
Axes of the slice: x: 4, y: 4, z: 16, core: 2. Of those that a mesh axis runs over, the one named last changes fastest.
Arguments:
- qk_vectors: bfloat16 [16384, 1024], P('ctx', 'head'), may hold values from -10 to 10
- token_values: bfloat16 [16384, 1024], P('ctx', 'head'), may hold values from -6 to 6
- grad_output: bfloat16 [16384, 1024], P('ctx', 'head'), may hold values from -6 to 6
- out_weight: bfloat16 [1024, 1024], P('head'), may hold values from -0.1875 to 0.1875
- global_ids: int32 [2], replicated, may hold values from 0 to 63
- pair_active: int32 [4, 32], replicated, may hold values 0 or 1
Outputs:
- projected: bfloat16 [16384, 1024], P('ctx', 'head')
- grad_qk: bfloat16 [16384, 1024], P('ctx', 'head')
- grad_val: bfloat16 [16384, 1024], P('ctx', 'head')
- grad_weight: float32 [1024, 1024], P('head')
All inputs are finite; a program needn't handle non-finite values.
Results may differ from a plain program's by a relative error of at most 0.014.
Values may be sent and summed in bfloat16 or wider, within the bound.
No kernel may reach another device: no remote copies, remote signals or barrier semaphores. Data moves between devices by JAX's collectives and lax.ppermute only.
A program may use at most 64 MiB of HBM per device.

v0:
```python
import math

import jax
import jax.numpy as jnp
from jax import lax
from jax.sharding import PartitionSpec as P

HD = 64
NGLOB = 2
ROUNDS = 4


def padded(block, sides, width):
    for axis, dim in sides:
        count = lax.axis_size(axis)
        forward = [(i, i + 1) for i in range(count - 1)]
        backward = [(target, source) for source, target in forward]
        low = lax.ppermute(
            lax.slice_in_dim(block, block.shape[dim] - width, None, axis=dim), axis, forward
        )
        high = lax.ppermute(lax.slice_in_dim(block, 0, width, axis=dim), axis, backward)
        block = jnp.concatenate([low, block, high], axis=dim)
    return block


def swapped(block, axis, stride):
    count = lax.axis_size(axis)
    route = []
    for low in range(count):
        high = low | 1 << stride
        if high != low and high < count:
            route += [(low, high), (high, low)]
    return lax.ppermute(block, axis, route)


def split_heads(matrix):
    return matrix.reshape(matrix.shape[0], -1, HD)


def local_scores(query_heads, key_heads, scaling):
    return (
        jnp.einsum("qhd,khd->hqk", query_heads, key_heads, preferred_element_type=jnp.float32)
        * scaling
    )


def local(qk_vectors, token_values, grad_output, out_weight, global_ids, pair_active):
    length, width = qk_vectors.shape
    scaling = 1.0 / math.sqrt(HD)
    position = lax.axis_index("ctx")
    devices = lax.axis_size("ctx")
    joined = jnp.concatenate([qk_vectors, token_values], axis=1)
    extended = padded(joined, (("ctx", 0),), length)
    blocks = [extended[:length], joined, extended[2 * length :]]
    marks = [
        (position > 0).astype(jnp.float32),
        jnp.float32(1.0),
        (position < devices - 1).astype(jnp.float32),
    ]
    owned = jnp.stack(
        [
            joined.astype(jnp.float32) * (global_ids[g] == position).astype(jnp.float32)
            for g in range(NGLOB)
        ]
    )
    fetched = lax.psum(owned, "ctx").astype(jnp.bfloat16)
    blocks.extend([fetched[g] for g in range(NGLOB)])
    marks.extend([jnp.float32(1.0)] * NGLOB)
    for k in range(ROUNDS):
        stride = 1 << k
        lowest = jnp.bitwise_and(position, devices - 1 - stride)
        pair_slot = jnp.right_shift(lowest, k + 1) * stride + jnp.bitwise_and(lowest, stride - 1)
        marks.append(
            lax.dynamic_index_in_dim(pair_active[k], pair_slot, keepdims=False).astype(jnp.float32)
        )
        blocks.append(swapped(joined, "ctx", k))
    query_heads = split_heads(qk_vectors)
    key_list = [split_heads(member[:, :width]) for member in blocks]
    value_list = [split_heads(member[:, width:]) for member in blocks]
    score_list = [local_scores(query_heads, member, scaling) for member in key_list]
    highest = jnp.full(score_list[0].shape[:2], -1e30, jnp.float32)
    for member, marker in zip(score_list, marks):
        highest = jnp.maximum(highest, jnp.where(marker > 0, jnp.max(member, axis=2), -1e30))
    summed = jnp.zeros(score_list[0].shape[:2], jnp.float32)
    for member, marker in zip(score_list, marks):
        summed = summed + jnp.where(
            marker > 0, jnp.sum(jnp.exp(member - highest[:, :, None]), axis=2), 0.0
        )
    log_total = highest + jnp.log(summed)
    weight_list = [
        jnp.where(marker > 0, jnp.exp(member - log_total[:, :, None]), 0.0)
        for member, marker in zip(score_list, marks)
    ]
    rounded_list = [member.astype(jnp.bfloat16) for member in weight_list]
    attended = jnp.zeros((length, query_heads.shape[1], HD), jnp.float32)
    for rounded, values_here in zip(rounded_list, value_list):
        attended = attended + jnp.einsum(
            "hqk,khd->qhd", rounded, values_here, preferred_element_type=jnp.float32
        )
    attended_b = attended.reshape(length, width).astype(jnp.bfloat16)
    partial_out = jnp.dot(attended_b, out_weight, preferred_element_type=jnp.float32)
    projected = lax.psum_scatter(partial_out, "head", scatter_dimension=1, tiled=True).astype(
        jnp.bfloat16
    )
    portion = lax.all_gather(grad_output, "head", axis=1, tiled=True)
    grad_att = lax.dot_general(
        portion, out_weight, (((1,), (1,)), ((), ())), preferred_element_type=jnp.float32
    )
    update = lax.dot_general(
        attended_b, portion, (((0,), (0,)), ((), ())), preferred_element_type=jnp.float32
    )
    weight_part = update
    grad_att, weight_part = (grad_att, weight_part)
    grad_weight = lax.psum(weight_part, "ctx")
    grad_b = grad_att.astype(jnp.bfloat16)
    grad_heads = split_heads(grad_b)
    row_dot = jnp.sum(grad_heads.astype(jnp.float32) * attended, axis=2).T
    grad_query = jnp.zeros((length, query_heads.shape[1], HD), jnp.float32)
    returns = []
    for weights, rounded, keys_here, values_here in zip(
        weight_list, rounded_list, key_list, value_list
    ):
        grad_weights = jnp.einsum(
            "qhd,khd->hqk", grad_heads, values_here, preferred_element_type=jnp.float32
        )
        grad_scores = (weights * (grad_weights - row_dot[:, :, None])).astype(jnp.bfloat16)
        grad_query = (
            grad_query
            + jnp.einsum("hqk,khd->qhd", grad_scores, keys_here, preferred_element_type=jnp.float32)
            * scaling
        )
        grad_keys = (
            jnp.einsum("hqk,qhd->khd", grad_scores, query_heads, preferred_element_type=jnp.float32)
            * scaling
        )
        grad_values = jnp.einsum(
            "hqk,qhd->khd", rounded, grad_heads, preferred_element_type=jnp.float32
        )
        returns.append(
            jnp.concatenate(
                [grad_keys.reshape(length, width), grad_values.reshape(length, width)], axis=1
            )
        )
    local_sum = returns[1]
    rim_terms = jnp.concatenate([returns[0], returns[2]], axis=0)
    beside_all = padded(rim_terms.astype(jnp.bfloat16), (("ctx", 0),), length).astype(
        rim_terms.dtype
    )
    local_sum = local_sum + beside_all[:length] + beside_all[3 * length :]
    global_terms = jnp.stack([returns[3 + g] for g in range(NGLOB)])
    global_total = lax.psum(global_terms, "ctx")
    for g in range(NGLOB):
        local_sum = local_sum + global_total[g] * (global_ids[g] == position).astype(jnp.float32)
    for k in range(ROUNDS):
        local_sum = local_sum + swapped(
            returns[3 + NGLOB + k].astype(jnp.bfloat16), "ctx", k
        ).astype(jnp.float32)
    grad_qk = (grad_query.reshape(length, width) + local_sum[:, :width]).astype(jnp.bfloat16)
    grad_val = local_sum[:, width:].astype(jnp.bfloat16)
    return (projected, grad_qk, grad_val, grad_weight)


def solution(mesh):
    return jax.shard_map(
        local,
        mesh=mesh,
        in_specs=(P("ctx", "head"), P("ctx", "head"), P("ctx", "head"), P("head", None), P(), P()),
        out_specs=(P("ctx", "head"), P("ctx", "head"), P("ctx", "head"), P("head", None)),
        check_vma=False,
    )
```

profile of v0, /device:TPU:24, one launch (start us, length us, event | category | flops | bytes accessed | tf_op | source)
XLA Modules:
  0.0 715.6 jit_solution(10499972209845318114)
XLA Ops:
  8.1 1.5 constant_dynamic-update-slice_fusion.1
  10.2 5.2 collective-permute-start.5
  15.4 3.8 collective-permute-start.4
  19.2 4.9 collective-permute-start.3
  24.2 2.5 collective-permute-start.2
  26.7 1.3 collective-permute-start.1
  32.8 286.8 %all-reduce.5 = bf16[2,256,256]{2,1,0:T(8,128)(2,1)S(1)} all-reduce(f32[2,256,256]{2,1,0:T(8,128)S(1)} %pad_maximum_fusion), channel_id=1, replica_groups=mesh['ctx'=64,'head'=8] {'ctx'}, use_global_device_ids=true, to_apply=%region_3.4 | all-reduce | flops 131072 | bytes 786432 | tf_op jit(solution)/shard_map/psum | solution.py:66
  324.3 12.1 %all_gather.3 = bf16[256,1024]{1,0:T(8,128)(2,1)S(1)} all-gather(bf16[256,128]{1,0:T(8,128)(2,1)S(1)} %copy-done.52), channel_id=1, replica_groups=mesh['ctx'=64,'head'=8] {'head'}, dimensions={1}, use_global_device_ids=true | all-gather | bytes 589824 | tf_op jit(solution)/shard_map/all_gather | solution.py:105
  337.2 1.9 collective-permute-start
  343.5 1.7 fusion.114
  345.2 1.5 fusion.106
  346.8 1.6 copy.118
  348.3 2.5 fusion.115
  350.8 1.5 fusion.103
  352.3 1.6 copy.115
  353.9 2.5 fusion.118
  356.4 1.5 fusion.102
  357.9 1.6 copy.112
  359.5 2.5 fusion.120
  362.0 1.6 copy.126
  364.6 1.9 exponential_reduce_fusion.8
  370.1 1.6 copy.132
  371.7 1.9 convolution_bitcast_fusion.12
  373.6 1.6 copy.134
  375.2 1.7 convolution_bitcast_fusion.11
  376.9 1.6 copy.136
  378.4 1.7 convolution_bitcast_fusion.10
  380.2 1.6 copy.138
  381.7 1.7 convolution_bitcast_fusion.9
  383.4 1.6 copy.111
  385.0 1.9 convolution_convert_fusion.6
  387.0 2.2 multiply_reduce_fusion
  405.9 1.9 collective-permute-start.6
  409.4 1.3 collective-permute-start.7
  412.4 4.5 collective-permute-start.8
  418.8 1.9 collective-permute-start.9
  420.7 1.7 copy.170
  422.4 1.7 copy.169
  424.1 1.7 copy.174
  425.7 1.7 copy.173
  427.4 1.0 fusion.126
  433.4 1.3 fusion.125
  434.8 2.1 collective-permute-start.10
  439.8 7.0 collective-permute-start.11
  447.4 5.2 collective-permute-done.11
  452.6 250.5 %all-reduce.4.cloned.1.call-done = (f32[2,256,256]{2,1,0:T(8,128)}, f32[128,1024]{1,0:T(8,128)}) async-done(((f32[2,256,256]{2,1,0:T(8,128)}, f32[128,1024]{1,0:T(8,128)}), (f32[2,256,256]{2,1,0:T(8,128)}, f32[128,1024]{1,0:T(8,128)})) %all-reduce.4.cloned.1.call-update) | async-done | bytes 1048592 | tf_op jit(solution)/shard_map/psum | solution.py:151
  703.1 1.4 fusion.63
  705.8 1.5 convert_element_type.162
  (222 shorter events, 47.9 us)
Async XLA Ops:
  8.0 328.4 %copy-start = (bf16[128,1024]{1,0:T(8,128)(2,1)S(1)}, bf16[128,1024]{1,0:T(8,128)(2,1)}, u32[]{:S(2)}) copy-start(bf16[128,1024]{1,0:T(8,128)(2,1)} %param.9) | copy-start | bytes 786436
  8.0 1.6 copy-start.36
  8.0 695.1 %all-reduce.4.cloned.1.call-start = ((), (), s32[]{:S(2)}) async-start(), calls=%async_computation.2 | async-start | bytes 2097152 | tf_op jit(solution)/shard_map/psum | solution.py:151
  9.6 18.4 %copy-start.35 = (bf16[256,128]{1,0:T(8,128)(2,1)S(1)}, bf16[256,128]{1,0:T(8,128)(2,1)}, u32[]{:S(2)}) copy-start(bf16[256,128]{1,0:T(8,128)(2,1)} %param.6) | copy-start | bytes 196612
  10.2 326.9 %collective-permute-start.5 = (bf16[256,256]{1,0:T(8,128)(2,1)}, bf16[256,256]{1,0:T(8,128)(2,1)S(1)}, u32[]{:S(2)}, u32[]{:S(2)}) collective-permute-start(bf16[256,256]{1,0:T(8,128)(2,1)} %constant_dynamic-update-slice_fusion), channel_id=1, source_target_pairs={{0,64},{64,0},{8,72},{72,8},{16,80},{80,16},{24,88},{88,24},{32,96... | collective-permute-start | bytes 393224 | tf_op jit(solution)/shard_map/ppermute | solution.py:33
  15.4 325.1 %collective-permute-start.4 = (bf16[256,256]{1,0:T(8,128)(2,1)}, bf16[256,256]{1,0:T(8,128)(2,1)S(1)}, u32[]{:S(2)}, u32[]{:S(2)}) collective-permute-start(bf16[256,256]{1,0:T(8,128)(2,1)} %constant_dynamic-update-slice_fusion), channel_id=1, source_target_pairs={{0,32},{32,0},{8,40},{40,8},{16,48},{48,16},{24,56},{56,24},{64,96... | collective-permute-start | bytes 393224 | tf_op jit(solution)/shard_map/ppermute | solution.py:33
  19.2 322.9 %collective-permute-start.3 = (bf16[256,256]{1,0:T(8,128)(2,1)}, bf16[256,256]{1,0:T(8,128)(2,1)S(1)}, u32[]{:S(2)}, u32[]{:S(2)}) collective-permute-start(bf16[256,256]{1,0:T(8,128)(2,1)} %constant_dynamic-update-slice_fusion), channel_id=1, source_target_pairs={{0,16},{16,0},{8,24},{24,8},{32,48},{48,32},{40,56},{56,40},{64,80... | collective-permute-start | bytes 393224 | tf_op jit(solution)/shard_map/ppermute | solution.py:33
  24.2 321.0 %collective-permute-start.2 = (bf16[256,256]{1,0:T(8,128)(2,1)}, bf16[256,256]{1,0:T(8,128)(2,1)}, u32[]{:S(2)}, u32[]{:S(2)}) collective-permute-start(bf16[256,256]{1,0:T(8,128)(2,1)} %constant_dynamic-update-slice_fusion), channel_id=1, source_target_pairs={{0,8},{8,0},{16,24},{24,16},{32,40},{40,32},{48,56},{56,48},{64,72... | collective-permute-start | bytes 393224 | tf_op jit(solution)/shard_map/ppermute | solution.py:33
  26.7 324.1 %collective-permute-start.1 = (bf16[256,256]{1,0:T(8,128)(2,1)}, bf16[256,256]{1,0:T(8,128)(2,1)}, u32[]{:S(2)}, u32[]{:S(2)}) collective-permute-start(bf16[256,256]{1,0:T(8,128)(2,1)} %constant_dynamic-update-slice_fusion), channel_id=1, source_target_pairs={{8,0},{16,8},{24,16},{32,24},{40,32},{48,40},{56,48},{64,56},{72,6... | collective-permute-start | bytes 393224 | tf_op jit(solution)/shard_map/ppermute | solution.py:21
  320.8 15.9 %copy-start.21 = (bf16[256,128]{0,1:T(8,128)(2,1)}, bf16[256,128]{0,1:T(8,128)(2,1)S(1)}, u32[]{:S(2)}) copy-start(bf16[256,128]{0,1:T(8,128)(2,1)S(1)} %copy.116) | copy-start | bytes 196612
  337.2 19.2 %collective-permute-start = (bf16[256,256]{1,0:T(8,128)(2,1)}, bf16[256,256]{1,0:T(8,128)(2,1)}, u32[]{:S(2)}, u32[]{:S(2)}) collective-permute-start(bf16[256,256]{1,0:T(8,128)(2,1)} %constant_dynamic-update-slice_fusion), channel_id=1, source_target_pairs={{0,8},{8,16},{16,24},{24,32},{32,40},{40,48},{48,56},{56,64},{64,7... | collective-permute-start | bytes 393224 | tf_op jit(solution)/shard_map/ppermute | solution.py:18
  341.2 0.9 copy-start.15
  363.6 1.1 copy-start.1
  364.6 1.9 copy-start.3
  364.6 1.9 copy-start.30
  366.5 0.9 copy-start.26
  385.0 1.9 copy-start.5
  385.0 1.9 copy-start.37
  387.0 2.2 copy-start.4
  387.0 2.2 copy-start.31
  390.5 1.0 copy-start.2
  390.5 1.0 copy-start.34
  395.7 0.9 copy-start.27
  396.9 0.9 copy-start.25
  404.1 0.9 copy-start.49
  404.9 2.9 copy-start.10
  405.9 34.0 %collective-permute-start.6 = (bf16[256,256]{1,0:T(8,128)(2,1)}, bf16[256,256]{1,0:T(8,128)(2,1)}, u32[]{:S(2)}, u32[]{:S(2)}) collective-permute-start(bf16[256,256]{1,0:T(8,128)(2,1)} %pad_maximum_fusion.7), channel_id=1, source_target_pairs={{0,8},{8,16},{16,24},{24,32},{32,40},{40,48},{48,56},{56,64},{64,7... | collective-permute-start | bytes 393224 | tf_op jit(solution)/shard_map/ppermute | solution.py:18
  408.0 2.7 copy-start.8
  409.4 37.9 %collective-permute-start.7 = (bf16[256,256]{1,0:T(8,128)(2,1)}, bf16[256,256]{1,0:T(8,128)(2,1)}, u32[]{:S(2)}, u32[]{:S(2)}) collective-permute-start(bf16[256,256]{1,0:T(8,128)(2,1)} %pad_maximum_fusion.8), channel_id=1, source_target_pairs={{8,0},{16,8},{24,16},{32,24},{40,32},{48,40},{56,48},{64,56},{72,6... | collective-permute-start | bytes 393224 | tf_op jit(solution)/shard_map/ppermute | solution.py:21
  411.0 6.0 copy-start.9
  412.4 35.0 %collective-permute-start.8 = (bf16[256,256]{1,0:T(8,128)(2,1)}, bf16[256,256]{1,0:T(8,128)(2,1)}, u32[]{:S(2)}, u32[]{:S(2)}) collective-permute-start(bf16[256,256]{1,0:T(8,128)(2,1)} %pad_maximum_fusion.9), channel_id=1, source_target_pairs={{0,8},{8,0},{16,24},{24,16},{32,40},{40,32},{48,56},{56,48},{64,72... | collective-permute-start | bytes 393224 | tf_op jit(solution)/shard_map/ppermute | solution.py:33
  418.8 28.6 %collective-permute-start.9 = (bf16[256,256]{1,0:T(8,128)(2,1)}, bf16[256,256]{1,0:T(8,128)(2,1)}, u32[]{:S(2)}, u32[]{:S(2)}) collective-permute-start(bf16[256,256]{1,0:T(8,128)(2,1)} %pad_maximum_fusion.10), channel_id=1, source_target_pairs={{0,16},{16,0},{8,24},{24,8},{32,48},{48,32},{40,56},{56,40},{64,80... | collective-permute-start | bytes 393224 | tf_op jit(solution)/shard_map/ppermute | solution.py:33
  420.7 6.7 copy-start.7
  425.7 1.7 copy-start.38
  427.4 1.1 copy-start.44
  427.4 1.1 copy-start.45
  428.5 0.9 copy-start.46
  428.5 1.0 copy-start.47
  430.3 275.5 %reduce-scatter.2.cloned.1.call-start = ((), (), s32[]{:S(2)}) async-start(), calls=%async_computation.1 | async-start | bytes 1179648 | tf_op jit(solution)/shard_map/reduce_scatter | solution.py:102
  434.7 2.1 copy-start.28
  434.8 2.4 copy-start.12
  434.8 12.6 %collective-permute-start.10 = (bf16[256,256]{1,0:T(8,128)(2,1)S(1)}, bf16[256,256]{1,0:T(8,128)(2,1)}, u32[]{:S(2)}, u32[]{:S(2)}) collective-permute-start(bf16[256,256]{1,0:T(8,128)(2,1)S(1)} %pad_maximum_fusion.11), channel_id=1, source_target_pairs={{0,32},{32,0},{8,40},{40,8},{16,48},{48,16},{24,56},{56,24},{64,96... | collective-permute-start | bytes 393224 | tf_op jit(solution)/shard_map/ppermute | solution.py:33
  437.3 0.9 copy-start.39
  437.3 1.0 copy-start.40
  437.3 1.0 copy-start.41
  438.8 0.9 copy-start.42
  439.8 12.8 %collective-permute-start.11 = (bf16[256,256]{1,0:T(8,128)(2,1)S(1)}, bf16[256,256]{1,0:T(8,128)(2,1)S(1)}, u32[]{:S(2)}, u32[]{:S(2)}) collective-permute-start(bf16[256,256]{1,0:T(8,128)(2,1)S(1)} %pad_maximum_fusion.12), channel_id=1, source_target_pairs={{0,64},{64,0},{8,72},{72,8},{16,80},{80,16},{24,88},{88,24},{32,96... | collective-permute-start | bytes 393224 | tf_op jit(solution)/shard_map/ppermute | solution.py:33
  704.5 2.8 copy-start.43
  (21 other events, 17.0 us)
Sparse Core Ops, SparseCore 0:
  430.4 272.6 all-reduce.3
Sparse Core Ops, SparseCore 1:
  434.8 36.3 reduce-scatter.1
where the time goes:
time: 718 us; the launch traced here: 716 us
  blocking collectives  299 us (42%)
  waiting for transfers between devices  256 us (36%)
  matrix products  45.6 us (6%)
  local copies, waits for them, and re-layouts  45.3 us (6%)
  starting transfers between devices  38.5 us (5%)
  between operations  20.2 us (3%)
  other arithmetic  11.3 us (2%)
    psum x1, blocking collectives, local(): fetched = lax.psum(owned, 'ctx').astype(jnp.bfloat16)  287 us
    psum x1, waiting for transfers between devices, local(): global_total = lax.psum(global_terms, 'ctx')  250 us
    ppermute x8, starting transfers between devices, swapped(): return lax.ppermute(block, axis, route)  31.9 us
    slice x14, local copies, waits for them, and re-layouts, local(): value_list = [split_heads(member[:, width:]) for member in blocks]  16.8 us
  transfers between devices with their start and end apart: 14, of which 2 were waited for; matrix products, arithmetic and copies ran while one was open for 6% of the time, Pallas kernels for 0%

commit v1 on v0

v1 whole, which is shorter than its diff:
```python
import functools
import math

import jax
import jax.numpy as jnp
from jax import lax
from jax.experimental import pallas as pl
from jax.experimental.pallas import tpu as pltpu
from jax.sharding import Mesh, PartitionSpec as P

HD = 64
NGLOB = 2
ROUNDS = 4
CTX = ("z", "x")
HEAD = ("y", "core")
NT = (((1,), (1,)), ((), ()))
TN = (((0,), (0,)), ((), ()))
NN = (((1,), (0,)), ((), ()))
F32 = jnp.float32
BF16 = jnp.bfloat16
MASKED = -1e30


def dot(a, b, dims):
    return lax.dot_general(a, b, dims, preferred_element_type=F32)


def attention_kernel(
    bias_ref, own_ref, p0, p1, p2, p3, p4, glob_ref, gout_ref, w_ref,
    partial_ref, sums_ref, r0, r1, r2, r3, r4, gquery_ref, gown_ref,
    score_ref, out_ref,
):
    length = own_ref.shape[0] // 2
    width = own_ref.shape[1]
    pieces = gout_ref.shape[0]
    nheads = width // HD
    scaling = 1.0 / math.sqrt(HD)
    base2 = scaling / math.log(2.0)
    keys = [r[:length] for r in (own_ref, p0, p1, p2, p3, p4)]
    vals = [r[length:] for r in (own_ref, p0, p1, p2, p3, p4)]
    for g in range(NGLOB):
        keys.append(glob_ref[g, :length])
        vals.append(glob_ref[g, length:])
    count = len(keys)
    query = own_ref[:length]
    lane = lax.broadcasted_iota(jnp.int32, (1, width), 1) // HD

    gatt = jnp.zeros((length, width), F32)
    for c in range(pieces):
        gatt = gatt + dot(gout_ref[c], w_ref[:, c * 128:(c + 1) * 128], NT)
    gatt_b = gatt.astype(BF16)

    inverse = []
    for h in range(nheads):
        query_h = jnp.where(lane == h, query, jnp.zeros_like(query))
        highest = jnp.full((length, 1), MASKED, F32)
        for b in range(count):
            s = dot(query_h, keys[b], NT) * base2 + bias_ref[b]
            score_ref[h, :, b * length:(b + 1) * length] = s
            highest = jnp.maximum(highest, jnp.max(s, axis=1, keepdims=True))
        total = jnp.zeros((length, 1), F32)
        for b in range(count):
            e = jnp.exp2(score_ref[h, :, b * length:(b + 1) * length] - highest)
            score_ref[h, :, b * length:(b + 1) * length] = e
            total = total + jnp.sum(e, axis=1, keepdims=True)
        inv = 1.0 / total
        inverse.append(inv)
        acc = jnp.zeros((length, width), F32)
        for b in range(count):
            e = score_ref[h, :, b * length:(b + 1) * length]
            acc = acc + dot((e * inv).astype(BF16), vals[b], NN)
        if h == 0:
            out_ref[...] = acc
        else:
            out_ref[...] = jnp.where(lane == h, acc, out_ref[...])

    attended = out_ref[...]
    attended_b = attended.astype(BF16)
    for c in range(pieces):
        partial_ref[c] = dot(attended_b, w_ref[:, c * 128:(c + 1) * 128], NN)
        part = dot(attended_b, gout_ref[c], TN).astype(BF16)
        n = width // 16
        sums_ref[c * n:(c + 1) * n, 0:16, :] = part.reshape(n, 16, 128)

    product = gatt_b.astype(F32) * attended
    query_t = query.astype(F32).T.astype(BF16)
    gatt_t = gatt_b.astype(F32).T.astype(BF16)
    outs = [gown_ref, r0, r1, r2, r3, r4]
    for h in range(nheads):
        gatt_h = jnp.where(lane == h, gatt_b, jnp.zeros_like(gatt_b))
        row_dot = jnp.sum(jnp.where(lane == h, product, 0.0), axis=1, keepdims=True)
        inv = inverse[h]
        qt = query_t[h * HD:(h + 1) * HD]
        gt = gatt_t[h * HD:(h + 1) * HD]
        acc = jnp.zeros((length, width), F32)
        for b in range(count - 1, -1, -1):
            weights = score_ref[h, :, b * length:(b + 1) * length] * inv
            gw = dot(gatt_h, vals[b], NT)
            gs = (weights * (gw - row_dot)).astype(BF16)
            acc = acc + dot(gs, keys[b], NN)
            gk = dot(qt, gs, NN) * scaling
            gv = dot(gt, weights.astype(BF16), NN)
            if b < count - NGLOB:
                o = outs[b]
                o[h * HD:(h + 1) * HD, :] = gk.astype(o.dtype)
                o[width + h * HD:width + (h + 1) * HD, :] = gv.astype(o.dtype)
            else:
                g = b - (count - NGLOB)
                n = HD // 16
                rows = width * 2 // 16
                for a in range(length // 128):
                    at = (g * (length // 128) + a) * rows
                    sub = gk[:, a * 128:(a + 1) * 128].astype(BF16)
                    sums_ref[at + h * n:at + (h + 1) * n, 16:32, :] = sub.reshape(n, 16, 128)
                    sub = gv[:, a * 128:(a + 1) * 128].astype(BF16)
                    at = at + width // 16
                    sums_ref[at + h * n:at + (h + 1) * n, 16:32, :] = sub.reshape(n, 16, 128)
        if h == 0:
            out_ref[...] = acc
        else:
            out_ref[...] = jnp.where(lane == h, acc, out_ref[...])
    gquery_ref[...] = out_ref[...] * scaling


def finish_kernel(
    mark_ref, b0, b1, b2, b3, b4, gown_ref, gquery_ref, total_ref, gqk_ref, gval_ref, gweight_ref
):
    length, width = gquery_ref.shape
    halves = length // 128
    rows = width * 2 // 16
    for a in range(halves):
        cols = slice(a * 128, (a + 1) * 128)
        acc = gown_ref[:, cols]
        for b in (b0, b1, b2, b3, b4):
            acc = acc + b[:, cols].astype(F32)
        for g in range(NGLOB):
            at = (g * halves + a) * rows
            term = total_ref[at:at + rows, 16:32, :].reshape(2 * width, 128).astype(F32)
            acc = acc + term * mark_ref[g]
        tokens = slice(a * 128, (a + 1) * 128)
        gqk_ref[tokens, :] = (gquery_ref[tokens, :] + acc[:width].T).astype(BF16)
        gval_ref[tokens, :] = acc[width:].T.astype(BF16)
    n = width // 16
    for c in range(gweight_ref.shape[1] // 128):
        piece = total_ref[c * n:(c + 1) * n, 0:16, :].reshape(width, 128)
        gweight_ref[:, c * 128:(c + 1) * 128] = piece.astype(F32)


def vmem(count):
    return [pl.BlockSpec(memory_space=pltpu.VMEM)] * count


def smem():
    return pl.BlockSpec(memory_space=pltpu.SMEM)


def local(qk_vectors, token_values, grad_output, out_weight, global_ids, pair_active):
    length, width = qk_vectors.shape
    devices = lax.axis_size(CTX)
    pieces = lax.axis_size(HEAD)
    position = lax.axis_index(CTX)
    joined = jnp.concatenate([qk_vectors, token_values], axis=0)

    step = 2 * length // devices
    slices = lax.all_to_all(joined.reshape(devices, step, width), CTX, 0, 0)
    routes = [[(i, i ^ 1) for i in range(devices)]]
    other = [i + 1 if i % 2 else i - 1 for i in range(devices)]
    routes.append([(i, j) for i, j in enumerate(other) if 0 <= j < devices])
    routes += [[(i, i ^ (1 << k)) for i in range(devices)] for k in range(1, ROUNDS)]
    received = [lax.ppermute(joined, CTX, route) for route in routes]

    picked = jnp.stack(
        [lax.dynamic_index_in_dim(slices, global_ids[g], keepdims=False) for g in range(NGLOB)]
    )
    spread = lax.all_to_all(
        jnp.broadcast_to(picked[None], (devices, NGLOB, step, width)), CTX, 0, 0
    )
    globals_all = jnp.swapaxes(spread, 0, 1).reshape(NGLOB, 2 * length, width)
    portion = lax.all_gather(grad_output, HEAD, axis=0)

    linked = []
    for k in range(ROUNDS):
        stride = 1 << k
        lowest = jnp.bitwise_and(position, devices - 1 - stride)
        slot = jnp.right_shift(lowest, k + 1) * stride + jnp.bitwise_and(lowest, stride - 1)
        linked.append(lax.dynamic_index_in_dim(pair_active[k], slot, keepdims=False) == 1)
    inside = jnp.logical_and(position > 0, position < devices - 1)
    bias = jnp.stack(
        [jnp.float32(0.0), jnp.where(linked[0], 1.0, 0.0)]
        + [jnp.where(m, 0.0, MASKED) for m in [inside] + linked[1:]]
        + [jnp.float32(0.0)] * NGLOB
    ).astype(F32)

    count = ROUNDS + 2 + NGLOB
    block = jax.ShapeDtypeStruct((2 * width, length), BF16)
    outputs = pl.pallas_call(
        attention_kernel,
        out_shape=(
            jax.ShapeDtypeStruct((pieces, length, 128), F32),
            jax.ShapeDtypeStruct((devices, 32, 128), BF16),
            block, block, block, block, block,
            jax.ShapeDtypeStruct((length, width), F32),
            jax.ShapeDtypeStruct((2 * width, length), F32),
        ),
        in_specs=[smem()] + vmem(9),
        out_specs=tuple(vmem(9)),
        scratch_shapes=[
            pltpu.VMEM((width // HD, length, count * length), F32),
            pltpu.VMEM((length, width), F32),
        ],
        compiler_params=pltpu.CompilerParams(vmem_limit_bytes=40 * 1024 * 1024),
        cost_estimate=pl.CostEstimate(
            flops=4_000_000_000, bytes_accessed=4_000_000, transcendentals=1_100_000
        ),
        name="attention",
    )(bias, joined, *received, globals_all, portion, out_weight)
    partial, sums, gquery, gown = outputs[0], outputs[1], outputs[7], outputs[8]
    returned = [
        lax.ppermute(o, CTX, [(j, i) for i, j in route])
        for o, route in zip(outputs[2:7], routes)
    ]
    projected = lax.psum_scatter(partial, HEAD, scatter_dimension=0, tiled=False).astype(BF16)

    shares = lax.all_to_all(sums, CTX, 0, 0)
    share = jnp.sum(shares.astype(F32), axis=0).astype(BF16)
    totals = lax.all_to_all(jnp.broadcast_to(share[None], shares.shape), CTX, 0, 0)

    marks = (global_ids == position).astype(F32)
    gqk, gval, gweight = pl.pallas_call(
        finish_kernel,
        out_shape=(
            jax.ShapeDtypeStruct((length, width), BF16),
            jax.ShapeDtypeStruct((length, width), BF16),
            jax.ShapeDtypeStruct((width, pieces * 128), F32),
        ),
        in_specs=[smem()] + vmem(8),
        out_specs=tuple(vmem(3)),
        compiler_params=pltpu.CompilerParams(vmem_limit_bytes=16 * 1024 * 1024),
        cost_estimate=pl.CostEstimate(
            flops=2_000_000, bytes_accessed=2_500_000, transcendentals=0
        ),
        name="finish",
    )(marks, *returned, gown, gquery, totals)
    return (projected, gqk, gval, gweight)


def solution(mesh):
    ctx, head = mesh.devices.shape
    cores = 2 if head % 2 == 0 else 1
    inner = Mesh(mesh.devices.reshape(ctx // 4, 4, head // cores, cores), CTX + HEAD)
    row = P(CTX, HEAD)
    return jax.shard_map(
        local,
        mesh=inner,
        in_specs=(row, row, row, P(HEAD, None), P(), P()),
        out_specs=(row, row, row, P(HEAD, None)),
        check_vma=False,
    )
```

time: 718 us -> 194 us (0.27)
  the two profiles are of different devices: /device:TPU:24 before, /device:TPU:32 now
where the time goes in v1:
time: 194 us; the launch traced here: 193 us
  starting transfers between devices  79.2 us (41%)
  waiting for transfers between devices  62.1 us (32%)
  between operations  20.8 us (11%)
  blocking collectives  13.6 us (7%)
  Pallas kernels  8.71 us (4%)
  local copies, waits for them, and re-layouts  5.98 us (3%)
  other arithmetic  2.84 us (1%)
    all_to_all x1, waiting for transfers between devices, local(): shares = lax.all_to_all(sums, CTX, 0, 0)  31.4 us
    all_to_all x1, starting transfers between devices, local(): slices = lax.all_to_all(joined.reshape(devices, step, width), CTX, 0, 0)  18.3 us
    ppermute x5, starting transfers between devices, local(): received = [lax.ppermute(joined, CTX, route) for route in routes]  17.7 us
    ppermute x5, starting transfers between devices, local(): lax.ppermute(o, CTX, [(j, i) for i, j in route])  16.6 us
    ppermute x5, waiting for transfers between devices, local(): lax.ppermute(o, CTX, [(j, i) for i, j in route])  14.5 us
    all_to_all x1, starting transfers between devices, local(): shares = lax.all_to_all(sums, CTX, 0, 0)  13.9 us
    all_gather x1, blocking collectives, local(): portion = lax.all_gather(grad_output, HEAD, axis=0)  13.6 us
    all_to_all x1, waiting for transfers between devices, local(): slices = lax.all_to_all(joined.reshape(devices, step, width), CTX, 0, 0)  12.3 us
  transfers between devices with their start and end apart: 15, of which 6 were waited for; matrix products, arithmetic and copies ran while one was open for 2% of the time, Pallas kernels for 0%

profile of v1, /device:TPU:32, one launch (start us, length us, event | category | flops | bytes accessed | tf_op | source)
XLA Modules:
  0.0 193.3 jit_solution(18046802319138438849)
XLA Ops:
  7.2 1.5 constant_dynamic-update-slice_fusion.1
  8.7 0.6 constant_dynamic-update-slice_fusion.own_ref
  9.3 18.3 %all-to-all-start = ((bf16[64,8,128]{2,1,0:T(8,128)(2,1)}), bf16[64,8,128]{2,1,0:T(8,128)(2,1)S(1)}, u32[]{:S(2)}, u32[]{:S(2)}) async-start(bf16[64,8,128]{2,1,0:T(8,128)(2,1)} %bitcast.5), calls=%async_computation | async-start | bytes 262144 | tf_op jit(solution)/shard_map/all_to_all | solution.py:165
  27.7 0.6 fusion.1
  32.1 12.3 %all-to-all-done = bf16[64,8,128]{2,1,0:T(8,128)(2,1)S(1)} async-done(((bf16[64,8,128]{2,1,0:T(8,128)(2,1)}), bf16[64,8,128]{2,1,0:T(8,128)(2,1)S(1)}, u32[]{:S(2)}, u32[]{:S(2)}) %all-to-all-start) | async-done | bytes 131104 | tf_op jit(solution)/shard_map/all_to_all | solution.py:165
  44.4 0.7 broadcast_in_dim.4
  45.1 5.5 %all-to-all-start.1 = ((bf16[64,2,8,128]{3,2,1,0:T(8,128)(2,1)}), bf16[64,2,8,128]{3,2,1,0:T(8,128)(2,1)S(1)}, u32[]{:S(2)}, u32[]{:S(2)}) async-start(bf16[64,2,8,128]{3,2,1,0:T(8,128)(2,1)} %broadcast_in_dim.4), calls=%async_computation.1 | async-start | bytes 524288 | tf_op jit(solution)/shard_map/all_to_all | solution.py:175
  50.6 0.0 copy-start.1
  50.6 4.5 %collective-permute-start.4 = (bf16[512,128]{1,0:T(8,128)(2,1)}, bf16[512,128]{1,0:T(8,128)(2,1)S(1)}, u32[]{:S(2)}, u32[]{:S(2)}) collective-permute-start(bf16[512,128]{1,0:T(8,128)(2,1)} %constant_dynamic-update-slice_fusion.own_ref), channel_id=1, source_target_pairs={{0,64},{8,72},{16,80},{24,88},{32,96},{40,104},{48,112},{56,120},{... | collective-permute-start | bytes 393224 | tf_op jit(solution)/shard_map/ppermute | solution.py:170
  55.1 2.4 %collective-permute-start.3 = (bf16[512,128]{1,0:T(8,128)(2,1)}, bf16[512,128]{1,0:T(8,128)(2,1)S(1)}, u32[]{:S(2)}, u32[]{:S(2)}) collective-permute-start(bf16[512,128]{1,0:T(8,128)(2,1)} %constant_dynamic-update-slice_fusion.own_ref), channel_id=1, source_target_pairs={{0,32},{8,40},{16,48},{24,56},{32,0},{40,8},{48,16},{56,24},{64,96... | collective-permute-start | bytes 393224 | tf_op jit(solution)/shard_map/ppermute | solution.py:170
  57.5 4.9 %collective-permute-start.2 = (bf16[512,128]{1,0:T(8,128)(2,1)}, bf16[512,128]{1,0:T(8,128)(2,1)S(1)}, u32[]{:S(2)}, u32[]{:S(2)}) collective-permute-start(bf16[512,128]{1,0:T(8,128)(2,1)} %constant_dynamic-update-slice_fusion.own_ref), channel_id=1, source_target_pairs={{0,16},{8,24},{16,0},{24,8},{32,48},{40,56},{48,32},{56,40},{64,80... | collective-permute-start | bytes 393224 | tf_op jit(solution)/shard_map/ppermute | solution.py:170
  62.4 4.0 %collective-permute-start.1 = (bf16[512,128]{1,0:T(8,128)(2,1)}, bf16[512,128]{1,0:T(8,128)(2,1)S(1)}, u32[]{:S(2)}, u32[]{:S(2)}) collective-permute-start(bf16[512,128]{1,0:T(8,128)(2,1)} %constant_dynamic-update-slice_fusion.own_ref), channel_id=1, source_target_pairs={{8,16},{16,8},{24,32},{32,24},{40,48},{48,40},{56,64},{64,56},{72,... | collective-permute-start | bytes 393224 | tf_op jit(solution)/shard_map/ppermute | solution.py:170
  66.5 1.9 collective-permute-start
  68.4 0.0 copy-start.3
  68.4 0.7 copy-done.3
  69.1 0.6 fusion.4
  71.0 0.6 fusion.2
  72.9 0.1 stack.28.bias_ref
  73.0 13.6 %all-gather = bf16[2048,128]{1,0:T(8,128)(2,1)S(1)} all-gather(bf16[256,128]{1,0:T(8,128)(2,1)S(1)} %copy-done.1), channel_id=2, replica_groups=mesh['z'=16,'x'=4,'y'=4,'core'=2] {'y','core'}, dimensions={0}, use_global_device_ids=true | all-gather | bytes 589824 | tf_op jit(solution)/shard_map/all_gather | solution.py:179
  86.6 0.0 all-to-all-done.1
  86.6 0.0 collective-permute-done.4.p4
  86.7 0.0 collective-permute-done.3.p3
  86.7 0.0 collective-permute-done.2.p2
  86.7 0.0 collective-permute-done.1.p1
  86.7 0.0 collective-permute-done.p0
  86.7 0.9 copy-done
  87.6 7.1 %attention.1 = (f32[8,256,128]{2,1,0:T(8,128)}, bf16[64,32,128]{2,1,0:T(8,128)(2,1)}, bf16[256,256]{1,0:T(8,128)(2,1)S(1)}, bf16[256,256]{1,0:T(8,128)(2,1)S(1)}...) custom-call(f32[8]{0:T(128)S(1)} %stack.28.bias_ref, ...), custom_call_target="tpu_custom_call" | custom-call | flops 4000000000 | bytes 4000000 | tf_op jit(solution)/shard_map/attention/pallas_call | solution.py:196
  94.7 13.9 %all-to-all-start.2 = ((bf16[64,32,128]{2,1,0:T(8,128)(2,1)}), bf16[64,32,128]{2,1,0:T(8,128)(2,1)S(1)}, u32[]{:S(2)}, u32[]{:S(2)}) async-start(bf16[64,32,128]{2,1,0:T(8,128)(2,1)} %get-tuple-element.24), calls=%async_computation.3 | async-start | bytes 1048576 | tf_op jit(solution)/shard_map/all_to_all | solution.py:224
  108.6 0.0 reduce-scatter.2.cloned.1.call-start
  108.7 0.7 reduce-scatter.2.cloned.1.call-update
  109.4 31.4 %all-to-all-done.2 = bf16[64,32,128]{2,1,0:T(8,128)(2,1)S(1)} async-done(((bf16[64,32,128]{2,1,0:T(8,128)(2,1)}), bf16[64,32,128]{2,1,0:T(8,128)(2,1)S(1)}, u32[]{:S(2)}, u32[]{:S(2)}) %all-to-all-start.2) | async-done | bytes 524320 | tf_op jit(solution)/shard_map/all_to_all | solution.py:224
  140.7 0.1 reduce_sum.12
  140.8 0.9 broadcast_in_dim.5
  141.7 7.1 %all-to-all-start.3 = ((bf16[64,32,128]{2,1,0:T(8,128)(2,1)}), bf16[64,32,128]{2,1,0:T(8,128)(2,1)S(1)}, u32[]{:S(2)}, u32[]{:S(2)}) async-start(bf16[64,32,128]{2,1,0:T(8,128)(2,1)} %broadcast_in_dim.5), calls=%async_computation.4 | async-start | bytes 1048576 | tf_op jit(solution)/shard_map/all_to_all | solution.py:226
  148.8 3.4 %collective-permute-start.5 = (bf16[256,256]{1,0:T(8,128)(2,1)S(1)}, bf16[256,256]{1,0:T(8,128)(2,1)S(1)}, u32[]{:S(2)}, u32[]{:S(2)}) collective-permute-start(bf16[256,256]{1,0:T(8,128)(2,1)S(1)} %get-tuple-element.17), channel_id=1, source_target_pairs={{8,0},{0,8},{24,16},{16,24},{40,32},{32,40},{56,48},{48,56},{72,64... | collective-permute-start | bytes 393224 | tf_op jit(solution)/shard_map/ppermute | solution.py:219
  152.2 4.0 %collective-permute-start.6 = (bf16[256,256]{1,0:T(8,128)(2,1)S(1)}, bf16[256,256]{1,0:T(8,128)(2,1)S(1)}, u32[]{:S(2)}, u32[]{:S(2)}) collective-permute-start(bf16[256,256]{1,0:T(8,128)(2,1)S(1)} %get-tuple-element.18), channel_id=1, source_target_pairs={{16,8},{8,16},{32,24},{24,32},{48,40},{40,48},{64,56},{56,64},{80,... | collective-permute-start | bytes 393224 | tf_op jit(solution)/shard_map/ppermute | solution.py:219
  156.2 2.5 %collective-permute-start.7 = (bf16[256,256]{1,0:T(8,128)(2,1)S(1)}, bf16[256,256]{1,0:T(8,128)(2,1)S(1)}, u32[]{:S(2)}, u32[]{:S(2)}) collective-permute-start(bf16[256,256]{1,0:T(8,128)(2,1)S(1)} %get-tuple-element.19), channel_id=1, source_target_pairs={{16,0},{24,8},{0,16},{8,24},{48,32},{56,40},{32,48},{40,56},{80,64... | collective-permute-start | bytes 393224 | tf_op jit(solution)/shard_map/ppermute | solution.py:219
  158.7 2.5 %collective-permute-start.8 = (bf16[256,256]{1,0:T(8,128)(2,1)S(1)}, bf16[256,256]{1,0:T(8,128)(2,1)S(1)}, u32[]{:S(2)}, u32[]{:S(2)}) collective-permute-start(bf16[256,256]{1,0:T(8,128)(2,1)S(1)} %get-tuple-element.20), channel_id=1, source_target_pairs={{32,0},{40,8},{48,16},{56,24},{0,32},{8,40},{16,48},{24,56},{96,64... | collective-permute-start | bytes 393224 | tf_op jit(solution)/shard_map/ppermute | solution.py:219
  161.2 4.3 %collective-permute-start.9 = (bf16[256,256]{1,0:T(8,128)(2,1)S(1)}, bf16[256,256]{1,0:T(8,128)(2,1)S(1)}, u32[]{:S(2)}, u32[]{:S(2)}) collective-permute-start(bf16[256,256]{1,0:T(8,128)(2,1)S(1)} %get-tuple-element.21), channel_id=1, source_target_pairs={{64,0},{72,8},{80,16},{88,24},{96,32},{104,40},{112,48},{120,56},{... | collective-permute-start | bytes 393224 | tf_op jit(solution)/shard_map/ppermute | solution.py:219
  165.4 0.0 reduce-scatter.2.cloned.1.call-done
  165.5 1.5 convert_bitcast_fusion
  167.0 0.0 collective-permute-done.5.b0
  167.0 10.9 %collective-permute-done.6.b1 = bf16[256,256]{1,0:T(8,128)(2,1)S(1)} collective-permute-done((bf16[256,256]{1,0:T(8,128)(2,1)S(1)}, bf16[256,256]{1,0:T(8,128)(2,1)S(1)}, u32[]{:S(2)}, u32[]{:S(2)}) %collective-permute-start.6) | collective-permute-done | bytes 131104 | tf_op jit(solution)/shard_map/ppermute | solution.py:219
  177.9 0.0 collective-permute-done.7.b2
  177.9 0.8 collective-permute-done.8.b3
  178.8 2.8 %collective-permute-done.9.b4 = bf16[256,256]{1,0:T(8,128)(2,1)S(1)} collective-permute-done((bf16[256,256]{1,0:T(8,128)(2,1)S(1)}, bf16[256,256]{1,0:T(8,128)(2,1)S(1)}, u32[]{:S(2)}, u32[]{:S(2)}) %collective-permute-start.9) | collective-permute-done | bytes 131104 | tf_op jit(solution)/shard_map/ppermute | solution.py:219
  181.5 3.3 %all-to-all-done.3.total_ref = bf16[64,32,128]{2,1,0:T(8,128)(2,1)S(1)} async-done(((bf16[64,32,128]{2,1,0:T(8,128)(2,1)}), bf16[64,32,128]{2,1,0:T(8,128)(2,1)S(1)}, u32[]{:S(2)}, u32[]{:S(2)}) %all-to-all-start.3) | async-done | bytes 524320 | tf_op jit(solution)/shard_map/all_to_all | solution.py:226
  184.8 1.6 finish.1
  (12 shorter events, 0.1 us)
Async XLA Ops:
  7.2 1.5 copy-start.2
  9.3 18.4 %copy-start.4 = (s32[2]{0:T(128)S(1)}, s32[2]{0:T(128)}, u32[]{:S(2)}) copy-start(s32[2]{0:T(128)} %param.10) | copy-start | bytes 28
  9.3 35.1 %all-to-all-start = ((bf16[64,8,128]{2,1,0:T(8,128)(2,1)}), bf16[64,8,128]{2,1,0:T(8,128)(2,1)S(1)}, u32[]{:S(2)}, u32[]{:S(2)}) async-start(bf16[64,8,128]{2,1,0:T(8,128)(2,1)} %bitcast.5), calls=%async_computation | async-start | bytes 262144 | tf_op jit(solution)/shard_map/all_to_all | solution.py:165
  45.1 41.5 %all-to-all-start.1 = ((bf16[64,2,8,128]{3,2,1,0:T(8,128)(2,1)}), bf16[64,2,8,128]{3,2,1,0:T(8,128)(2,1)S(1)}, u32[]{:S(2)}, u32[]{:S(2)}) async-start(bf16[64,2,8,128]{3,2,1,0:T(8,128)(2,1)} %broadcast_in_dim.4), calls=%async_computation.1 | async-start | bytes 524288 | tf_op jit(solution)/shard_map/all_to_all | solution.py:175
  50.6 22.4 %copy-start.1 = (bf16[256,128]{1,0:T(8,128)(2,1)S(1)}, bf16[256,128]{1,0:T(8,128)(2,1)}, u32[]{:S(2)}) copy-start(bf16[256,128]{1,0:T(8,128)(2,1)} %param.8) | copy-start | bytes 196612
  50.6 36.0 %collective-permute-start.4 = (bf16[512,128]{1,0:T(8,128)(2,1)}, bf16[512,128]{1,0:T(8,128)(2,1)S(1)}, u32[]{:S(2)}, u32[]{:S(2)}) collective-permute-start(bf16[512,128]{1,0:T(8,128)(2,1)} %constant_dynamic-update-slice_fusion.own_ref), channel_id=1, source_target_pairs={{0,64},{8,72},{16,80},{24,88},{32,96},{40,104},{48,112},{56,120},{... | collective-permute-start | bytes 393224 | tf_op jit(solution)/shard_map/ppermute | solution.py:170
  55.1 31.6 %collective-permute-start.3 = (bf16[512,128]{1,0:T(8,128)(2,1)}, bf16[512,128]{1,0:T(8,128)(2,1)S(1)}, u32[]{:S(2)}, u32[]{:S(2)}) collective-permute-start(bf16[512,128]{1,0:T(8,128)(2,1)} %constant_dynamic-update-slice_fusion.own_ref), channel_id=1, source_target_pairs={{0,32},{8,40},{16,48},{24,56},{32,0},{40,8},{48,16},{56,24},{64,96... | collective-permute-start | bytes 393224 | tf_op jit(solution)/shard_map/ppermute | solution.py:170
  57.5 29.1 %collective-permute-start.2 = (bf16[512,128]{1,0:T(8,128)(2,1)}, bf16[512,128]{1,0:T(8,128)(2,1)S(1)}, u32[]{:S(2)}, u32[]{:S(2)}) collective-permute-start(bf16[512,128]{1,0:T(8,128)(2,1)} %constant_dynamic-update-slice_fusion.own_ref), channel_id=1, source_target_pairs={{0,16},{8,24},{16,0},{24,8},{32,48},{40,56},{48,32},{56,40},{64,80... | collective-permute-start | bytes 393224 | tf_op jit(solution)/shard_map/ppermute | solution.py:170
  62.4 24.2 %collective-permute-start.1 = (bf16[512,128]{1,0:T(8,128)(2,1)}, bf16[512,128]{1,0:T(8,128)(2,1)S(1)}, u32[]{:S(2)}, u32[]{:S(2)}) collective-permute-start(bf16[512,128]{1,0:T(8,128)(2,1)} %constant_dynamic-update-slice_fusion.own_ref), channel_id=1, source_target_pairs={{8,16},{16,8},{24,32},{32,24},{40,48},{48,40},{56,64},{64,56},{72,... | collective-permute-start | bytes 393224 | tf_op jit(solution)/shard_map/ppermute | solution.py:170
  66.5 20.2 %collective-permute-start = (bf16[512,128]{1,0:T(8,128)(2,1)}, bf16[512,128]{1,0:T(8,128)(2,1)S(1)}, u32[]{:S(2)}, u32[]{:S(2)}) collective-permute-start(bf16[512,128]{1,0:T(8,128)(2,1)} %constant_dynamic-update-slice_fusion.own_ref), channel_id=1, source_target_pairs={{0,8},{8,0},{16,24},{24,16},{32,40},{40,32},{48,56},{56,48},{64,72... | collective-permute-start | bytes 393224 | tf_op jit(solution)/shard_map/ppermute | solution.py:170
  68.4 0.7 copy-start.3
  86.6 0.9 copy-start
  94.7 46.0 %all-to-all-start.2 = ((bf16[64,32,128]{2,1,0:T(8,128)(2,1)}), bf16[64,32,128]{2,1,0:T(8,128)(2,1)S(1)}, u32[]{:S(2)}, u32[]{:S(2)}) async-start(bf16[64,32,128]{2,1,0:T(8,128)(2,1)} %get-tuple-element.24), calls=%async_computation.3 | async-start | bytes 1048576 | tf_op jit(solution)/shard_map/all_to_all | solution.py:224
  108.6 56.8 %reduce-scatter.2.cloned.1.call-start = ((), (), s32[]{:S(2)}) async-start(), calls=%async_computation.5 | async-start | bytes 1179648 | tf_op jit(solution)/shard_map/reduce_scatter | solution.py:222
  141.7 43.1 %all-to-all-start.3 = ((bf16[64,32,128]{2,1,0:T(8,128)(2,1)}), bf16[64,32,128]{2,1,0:T(8,128)(2,1)S(1)}, u32[]{:S(2)}, u32[]{:S(2)}) async-start(bf16[64,32,128]{2,1,0:T(8,128)(2,1)} %broadcast_in_dim.5), calls=%async_computation.4 | async-start | bytes 1048576 | tf_op jit(solution)/shard_map/all_to_all | solution.py:226
  148.8 18.2 %collective-permute-start.5 = (bf16[256,256]{1,0:T(8,128)(2,1)S(1)}, bf16[256,256]{1,0:T(8,128)(2,1)S(1)}, u32[]{:S(2)}, u32[]{:S(2)}) collective-permute-start(bf16[256,256]{1,0:T(8,128)(2,1)S(1)} %get-tuple-element.17), channel_id=1, source_target_pairs={{8,0},{0,8},{24,16},{16,24},{40,32},{32,40},{56,48},{48,56},{72,64... | collective-permute-start | bytes 393224 | tf_op jit(solution)/shard_map/ppermute | solution.py:219
  152.2 25.8 %collective-permute-start.6 = (bf16[256,256]{1,0:T(8,128)(2,1)S(1)}, bf16[256,256]{1,0:T(8,128)(2,1)S(1)}, u32[]{:S(2)}, u32[]{:S(2)}) collective-permute-start(bf16[256,256]{1,0:T(8,128)(2,1)S(1)} %get-tuple-element.18), channel_id=1, source_target_pairs={{16,8},{8,16},{32,24},{24,32},{48,40},{40,48},{64,56},{56,64},{80,... | collective-permute-start | bytes 393224 | tf_op jit(solution)/shard_map/ppermute | solution.py:219
  156.2 21.8 %collective-permute-start.7 = (bf16[256,256]{1,0:T(8,128)(2,1)S(1)}, bf16[256,256]{1,0:T(8,128)(2,1)S(1)}, u32[]{:S(2)}, u32[]{:S(2)}) collective-permute-start(bf16[256,256]{1,0:T(8,128)(2,1)S(1)} %get-tuple-element.19), channel_id=1, source_target_pairs={{16,0},{24,8},{0,16},{8,24},{48,32},{56,40},{32,48},{40,56},{80,64... | collective-permute-start | bytes 393224 | tf_op jit(solution)/shard_map/ppermute | solution.py:219
  158.7 20.1 %collective-permute-start.8 = (bf16[256,256]{1,0:T(8,128)(2,1)S(1)}, bf16[256,256]{1,0:T(8,128)(2,1)S(1)}, u32[]{:S(2)}, u32[]{:S(2)}) collective-permute-start(bf16[256,256]{1,0:T(8,128)(2,1)S(1)} %get-tuple-element.20), channel_id=1, source_target_pairs={{32,0},{40,8},{48,16},{56,24},{0,32},{8,40},{16,48},{24,56},{96,64... | collective-permute-start | bytes 393224 | tf_op jit(solution)/shard_map/ppermute | solution.py:219
  161.2 20.4 %collective-permute-start.9 = (bf16[256,256]{1,0:T(8,128)(2,1)S(1)}, bf16[256,256]{1,0:T(8,128)(2,1)S(1)}, u32[]{:S(2)}, u32[]{:S(2)}) collective-permute-start(bf16[256,256]{1,0:T(8,128)(2,1)S(1)} %get-tuple-element.21), channel_id=1, source_target_pairs={{64,0},{72,8},{80,16},{88,24},{96,32},{104,40},{112,48},{120,56},{... | collective-permute-start | bytes 393224 | tf_op jit(solution)/shard_map/ppermute | solution.py:219
Sparse Core Ops, SparseCore 0:
  112.3 40.0 reduce-scatter.1

commit v2 on v1

v2 whole, which is shorter than its diff:
```python
import functools
import math

import jax
import jax.numpy as jnp
from jax import lax
from jax.experimental import pallas as pl
from jax.experimental.pallas import tpu as pltpu
from jax.sharding import Mesh, PartitionSpec as P

HD = 64
NGLOB = 2
ROUNDS = 4
CTX = ("z", "x")
HEAD = ("y", "core")
NT = (((1,), (1,)), ((), ()))
TN = (((0,), (0,)), ((), ()))
NN = (((1,), (0,)), ((), ()))
F32 = jnp.float32
BF16 = jnp.bfloat16
MASKED = -1e30


def dot(a, b, dims):
    return lax.dot_general(a, b, dims, preferred_element_type=F32)


def block_bias(pos_ref, pair_ref):
    position = pos_ref[0]
    devices = 2 * pair_ref.shape[1]
    linked = []
    for k in range(ROUNDS):
        stride = 1 << k
        lowest = jnp.bitwise_and(position, devices - 1 - stride)
        slot = jnp.right_shift(lowest, k + 1) * stride + jnp.bitwise_and(lowest, stride - 1)
        linked.append(pair_ref[k, slot] == 1)
    inside = jnp.logical_and(position > 0, position < devices - 1)
    zero = jnp.float32(0.0)
    bias = [zero, jnp.where(linked[0], jnp.float32(1.0), zero)]
    bias += [jnp.where(m, zero, jnp.float32(MASKED)) for m in [inside] + linked[1:]]
    return bias + [zero] * NGLOB


def forward_kernel(
    pos_ref, pair_ref, own_ref, p0, p1, p2, p3, p4, glob_ref, gout_ref, w_ref,
    partial_ref, sums_ref, stats_ref, gatt_ref, gquery_ref,
    score_ref, out_ref,
):
    length = own_ref.shape[0] // 2
    width = own_ref.shape[1]
    pieces = gout_ref.shape[0]
    nheads = width // HD
    scaling = 1.0 / math.sqrt(HD)
    base2 = scaling / math.log(2.0)
    bias = block_bias(pos_ref, pair_ref)
    keys = [r[:length] for r in (own_ref, p0, p1, p2, p3, p4)]
    vals = [r[length:] for r in (own_ref, p0, p1, p2, p3, p4)]
    for g in range(NGLOB):
        keys.append(glob_ref[g, :length])
        vals.append(glob_ref[g, length:])
    count = len(keys)
    query = own_ref[:length]
    lane = lax.broadcasted_iota(jnp.int32, (1, width), 1)
    head = lane // HD

    gatt = jnp.zeros((length, width), F32)
    for c in range(pieces):
        gatt = gatt + dot(gout_ref[c], w_ref[:, c * 128:(c + 1) * 128], NT)
    gatt_b = gatt.astype(BF16)
    gatt_ref[...] = gatt_b

    inverse = []
    stats = jnp.zeros((length, width), F32)
    for h in range(nheads):
        query_h = jnp.where(head == h, query, jnp.zeros_like(query))
        highest = jnp.full((length, 1), MASKED, F32)
        for b in range(count):
            s = dot(query_h, keys[b], NT) * base2 + bias[b]
            score_ref[h, :, b * length:(b + 1) * length] = s
            highest = jnp.maximum(highest, jnp.max(s, axis=1, keepdims=True))
        total = jnp.zeros((length, 1), F32)
        for b in range(count):
            e = jnp.exp2(score_ref[h, :, b * length:(b + 1) * length] - highest)
            score_ref[h, :, b * length:(b + 1) * length] = e
            total = total + jnp.sum(e, axis=1, keepdims=True)
        inv = 1.0 / total
        inverse.append(inv)
        stats = jnp.where(lane == h, highest + jnp.log2(total), stats)
        acc = jnp.zeros((length, width), F32)
        for b in range(count):
            e = score_ref[h, :, b * length:(b + 1) * length]
            acc = acc + dot((e * inv).astype(BF16), vals[b], NN)
        if h == 0:
            out_ref[...] = acc
        else:
            out_ref[...] = jnp.where(head == h, acc, out_ref[...])

    attended = out_ref[...]
    attended_b = attended.astype(BF16)
    for c in range(pieces):
        partial_ref[c] = dot(attended_b, w_ref[:, c * 128:(c + 1) * 128], NN)
        part = dot(attended_b, gout_ref[c], TN).astype(BF16)
        n = width // 16
        at = c * n % sums_ref.shape[0]
        sums_ref[at:at + n, c * n // sums_ref.shape[0], 0:16, :] = part.reshape(n, 16, 128)

    product = gatt_b.astype(F32) * attended
    query_t = query.astype(F32).T.astype(BF16)
    gatt_t = gatt_b.astype(F32).T.astype(BF16)
    for h in range(nheads):
        gatt_h = jnp.where(head == h, gatt_b, jnp.zeros_like(gatt_b))
        row_dot = jnp.sum(jnp.where(head == h, product, 0.0), axis=1, keepdims=True)
        stats = jnp.where(lane == nheads + h, row_dot, stats)
        inv = inverse[h]
        qt = query_t[h * HD:(h + 1) * HD]
        gt = gatt_t[h * HD:(h + 1) * HD]
        acc = jnp.zeros((length, width), F32)
        for g in range(NGLOB):
            b = count - NGLOB + g
            weights = score_ref[h, :, b * length:(b + 1) * length] * inv
            gw = dot(gatt_h, vals[b], NT)
            gs = (weights * (gw - row_dot)).astype(BF16)
            acc = acc + dot(gs, keys[b], NN)
            gk = dot(qt, gs, NN) * scaling
            gv = dot(gt, weights.astype(BF16), NN)
            n = HD // 16
            for a in range(length // 128):
                x = g * (length // 128) + a
                for at, term in ((h * n, gk), (width // 16 + h * n, gv)):
                    sub = term[:, a * 128:(a + 1) * 128].astype(BF16)
                    sums_ref[at:at + n, x, 16:32, :] = sub.reshape(n, 16, 128)
        if h == 0:
            out_ref[...] = acc
        else:
            out_ref[...] = jnp.where(head == h, acc, out_ref[...])
    stats_ref[...] = stats
    gquery_ref[...] = out_ref[...]


def backward_kernel(
    pos_ref, pair_ref, own_ref, p0, p1, p2, p3, p4, stats_ref, gatt_ref, gglob_ref,
    r0, r1, r2, r3, r4, gquery_ref, gown_ref,
):
    length = own_ref.shape[0] // 2
    width = own_ref.shape[1]
    nheads = width // HD
    scaling = 1.0 / math.sqrt(HD)
    base2 = scaling / math.log(2.0)
    bias = block_bias(pos_ref, pair_ref)
    query = own_ref[:length]
    gatt_b = gatt_ref[...]
    head = lax.broadcasted_iota(jnp.int32, (1, width), 1) // HD
    query_t = query.astype(F32).T.astype(BF16)
    gatt_t = gatt_b.astype(F32).T.astype(BF16)
    blocks = (own_ref, p0, p1, p2, p3, p4)
    outs = (gown_ref, r0, r1, r2, r3, r4)
    result = gglob_ref[...]
    for h in range(nheads):
        query_h = jnp.where(head == h, query, jnp.zeros_like(query))
        gatt_h = jnp.where(head == h, gatt_b, jnp.zeros_like(gatt_b))
        log_total = stats_ref[:, h:h + 1]
        row_dot = stats_ref[:, nheads + h:nheads + h + 1]
        qt = query_t[h * HD:(h + 1) * HD]
        gt = gatt_t[h * HD:(h + 1) * HD]
        acc = jnp.zeros((length, width), F32)
        for b in (1, 2, 3, 4, 5, 0):
            keys = blocks[b][:length]
            s = dot(query_h, keys, NT) * base2 + (bias[b] - log_total)
            weights = jnp.exp2(s)
            gw = dot(gatt_h, blocks[b][length:], NT)
            gs = (weights * (gw - row_dot)).astype(BF16)
            acc = acc + dot(gs, keys, NN)
            gk = dot(qt, gs, NN) * scaling
            gv = dot(gt, weights.astype(BF16), NN)
            o = outs[b]
            o[h * HD:(h + 1) * HD, :] = gk.astype(o.dtype)
            o[width + h * HD:width + (h + 1) * HD, :] = gv.astype(o.dtype)
        result = result + jnp.where(head == h, acc, 0.0)
    gquery_ref[...] = result * scaling


def finish_kernel(
    pos_ref, ids_ref, b0, b1, b2, b3, b4, gown_ref, gquery_ref, total_ref,
    gqk_ref, gval_ref, gweight_ref,
):
    length, width = gquery_ref.shape
    halves = length // 128
    rows = width * 2 // 16
    for a in range(halves):
        cols = slice(a * 128, (a + 1) * 128)
        acc = gown_ref[:, cols]
        for b in (b0, b1, b2, b3, b4):
            acc = acc + b[:, cols].astype(F32)
        for g in range(NGLOB):
            at = (g * halves + a) * rows
            term = total_ref[at:at + rows, 16:32, :].reshape(2 * width, 128).astype(F32)
            acc = acc + jnp.where(ids_ref[g] == pos_ref[0], term, 0.0)
        tokens = slice(a * 128, (a + 1) * 128)
        gqk_ref[tokens, :] = (gquery_ref[tokens, :] + acc[:width].T).astype(BF16)
        gval_ref[tokens, :] = acc[width:].T.astype(BF16)
    n = width // 16
    for c in range(gweight_ref.shape[1] // 128):
        piece = total_ref[c * n:(c + 1) * n, 0:16, :].reshape(width, 128)
        gweight_ref[:, c * 128:(c + 1) * 128] = piece.astype(F32)


def vmem(count):
    return [pl.BlockSpec(memory_space=pltpu.VMEM)] * count


def smem():
    return pl.BlockSpec(memory_space=pltpu.SMEM)


def local(qk_vectors, token_values, grad_output, out_weight, global_ids, pair_active):
    length, width = qk_vectors.shape
    devices = lax.axis_size(CTX)
    pieces = lax.axis_size(HEAD)
    position = lax.axis_index(CTX)
    joined = jnp.concatenate([qk_vectors, token_values], axis=0)

    step = 2 * length // devices
    slices = lax.all_to_all(joined.reshape(devices, step, width), CTX, 0, 0)
    routes = [[(i, i ^ 1) for i in range(devices)]]
    other = [i + 1 if i % 2 else i - 1 for i in range(devices)]
    routes.append([(i, j) for i, j in enumerate(other) if 0 <= j < devices])
    routes += [[(i, i ^ (1 << k)) for i in range(devices)] for k in range(1, ROUNDS)]
    received = [lax.ppermute(joined, CTX, route) for route in routes]

    slices, *received = lax.optimization_barrier((slices, *received))
    picked = jnp.stack(
        [lax.dynamic_index_in_dim(slices, global_ids[g], keepdims=False) for g in range(NGLOB)]
    )
    spread = lax.all_to_all(
        jnp.broadcast_to(picked[None], (devices, NGLOB, step, width)), CTX, 0, 0
    )
    globals_all = jnp.swapaxes(spread, 0, 1).reshape(NGLOB, 2 * length, width)
    portion = lax.all_gather(grad_output, HEAD, axis=0)

    count = ROUNDS + 2 + NGLOB
    nheads = width // HD
    block = jax.ShapeDtypeStruct((2 * width, length), BF16)
    square = jax.ShapeDtypeStruct((length, width), F32)
    partial, sums, stats, gatt, gglob = pl.pallas_call(
        forward_kernel,
        out_shape=(
            jax.ShapeDtypeStruct((pieces, length, 128), F32),
            jax.ShapeDtypeStruct((lax.axis_size("z"), lax.axis_size("x"), 32, 128), BF16),
            square,
            jax.ShapeDtypeStruct((length, width), BF16),
            square,
        ),
        in_specs=[smem()] * 2 + vmem(9),
        out_specs=tuple(vmem(5)),
        scratch_shapes=[
            pltpu.VMEM((nheads, length, count * length), F32),
            pltpu.VMEM((length, width), F32),
        ],
        compiler_params=pltpu.CompilerParams(vmem_limit_bytes=40 * 1024 * 1024),
        cost_estimate=pl.CostEstimate(
            flops=3_000_000_000, bytes_accessed=4_000_000, transcendentals=1_100_000
        ),
        name="forward",
    )(position[None], pair_active, joined, *received, globals_all, portion, out_weight)

    shares = lax.all_to_all(sums.reshape(devices, 32, 128), CTX, 0, 0)
    projected = lax.psum_scatter(partial, HEAD, scatter_dimension=0, tiled=False).astype(BF16)
    *terms, gquery, gown = pl.pallas_call(
        backward_kernel,
        out_shape=(
            block, block, block, block, block,
            square,
            jax.ShapeDtypeStruct((2 * width, length), F32),
        ),
        in_specs=[smem()] * 2 + vmem(9),
        out_specs=tuple(vmem(7)),
        compiler_params=pltpu.CompilerParams(vmem_limit_bytes=24 * 1024 * 1024),
        cost_estimate=pl.CostEstimate(
            flops=3_000_000_000, bytes_accessed=4_000_000, transcendentals=800_000
        ),
        name="backward",
    )(position[None], pair_active, joined, *received, stats, gatt, gglob)
    returned = [lax.ppermute(t, CTX, route) for t, route in zip(terms, routes)]

    shares, *returned = lax.optimization_barrier((shares, *returned))
    share = jnp.sum(shares.astype(F32), axis=0).astype(BF16)
    column = lax.all_to_all(
        jnp.broadcast_to(share[None], (lax.axis_size("z"),) + share.shape), "z", 0, 0
    )
    totals = lax.all_to_all(
        jnp.broadcast_to(column[None], (lax.axis_size("x"),) + column.shape), "x", 0, 0
    ).reshape(shares.shape)

    gqk, gval, gweight = pl.pallas_call(
        finish_kernel,
        out_shape=(
            jax.ShapeDtypeStruct((length, width), BF16),
            jax.ShapeDtypeStruct((length, width), BF16),
            jax.ShapeDtypeStruct((width, pieces * 128), F32),
        ),
        in_specs=[smem()] * 2 + vmem(8),
        out_specs=tuple(vmem(3)),
        compiler_params=pltpu.CompilerParams(vmem_limit_bytes=16 * 1024 * 1024),
        cost_estimate=pl.CostEstimate(
            flops=2_000_000, bytes_accessed=2_500_000, transcendentals=0
        ),
        name="finish",
    )(position[None], global_ids, *returned, gown, gquery, totals)
    return (projected, gqk, gval, gweight)


def solution(mesh):
    ctx, head = mesh.devices.shape
    cores = 2 if head % 2 == 0 else 1
    inner = Mesh(mesh.devices.reshape(ctx // 4, 4, head // cores, cores), CTX + HEAD)
    row = P(CTX, HEAD)
    return jax.shard_map(
        local,
        mesh=inner,
        in_specs=(row, row, row, P(HEAD, None), P(), P()),
        out_specs=(row, row, row, P(HEAD, None)),
        check_vma=False,
    )
```

time: 194 us -> 180 us (0.928)
  the two profiles are of different devices: /device:TPU:32 before, /device:TPU:24 now
where the time goes in v2:
time: 180 us; the launch traced here: 179 us
  starting transfers between devices  79.7 us (44%)
  blocking collectives  37.8 us (21%)
  waiting for transfers between devices  25.6 us (14%)
  between operations  18.2 us (10%)
  Pallas kernels  11.2 us (6%)
  local copies, waits for them, and re-layouts  5.04 us (3%)
    all_to_all x1, blocking collectives, local(): lax.all_to_all(jnp.broadcast_to(share[None], (lax.axis_size('z'),) + shar...  24.7 us
    all_to_all x1, starting transfers between devices, local(): slices = lax.all_to_all(joined.reshape(devices, step, width), CTX, 0, 0)  18.7 us
    ppermute x5, starting transfers between devices, local(): returned = [lax.ppermute(t, CTX, route) for t, route in zip(terms, routes)]  17.6 us
    ppermute x5, starting transfers between devices, local(): received = [lax.ppermute(joined, CTX, route) for route in routes]  17 us
    all_to_all x1, starting transfers between devices, local(): lax.all_to_all(jnp.broadcast_to(picked[None], (devices, NGLOB, step, widt...  14.5 us
    all_gather x1, blocking collectives, local(): portion = lax.all_gather(grad_output, HEAD, axis=0)  13.1 us
    ppermute x5, waiting for transfers between devices, local(): returned = [lax.ppermute(t, CTX, route) for t, route in zip(terms, routes)]  10.3 us
    all_to_all x1, waiting for transfers between devices, local(): lax.all_to_all(jnp.broadcast_to(picked[None], (devices, NGLOB, step, widt...  7.71 us
  transfers between devices with their start and end apart: 15, of which 4 were waited for; matrix products, arithmetic and copies ran while one was open for 2% of the time, Pallas kernels for 2%

profile of v2, /device:TPU:24, one launch (start us, length us, event | category | flops | bytes accessed | tf_op | source)
XLA Modules:
  0.0 179.2 jit_solution(7412203138702944325)
XLA Ops:
  7.2 0.0 copy-start.4
  7.2 1.5 constant_dynamic-update-slice_fusion.1
  8.7 0.0 copy-done.4
  8.7 0.6 constant_dynamic-update-slice_fusion.own_ref
  9.3 18.7 %all-to-all-start = ((bf16[64,8,128]{2,1,0:T(8,128)(2,1)}), bf16[64,8,128]{2,1,0:T(8,128)(2,1)S(1)}, u32[]{:S(2)}, u32[]{:S(2)}) async-start(bf16[64,8,128]{2,1,0:T(8,128)(2,1)} %bitcast.1), calls=%async_computation | async-start | bytes 262144 | tf_op jit(solution)/shard_map/all_to_all | solution.py:223
  28.0 4.4 %collective-permute-start.4 = (bf16[512,128]{1,0:T(8,128)(2,1)}, bf16[512,128]{1,0:T(8,128)(2,1)S(1)}, u32[]{:S(2)}, u32[]{:S(2)}) collective-permute-start(bf16[512,128]{1,0:T(8,128)(2,1)} %constant_dynamic-update-slice_fusion.own_ref), channel_id=1, source_target_pairs={{0,64},{8,72},{16,80},{24,88},{32,96},{40,104},{48,112},{56,120},{... | collective-permute-start | bytes 393224 | tf_op jit(solution)/shard_map/ppermute | solution.py:228
  32.4 3.4 %collective-permute-start.3 = (bf16[512,128]{1,0:T(8,128)(2,1)}, bf16[512,128]{1,0:T(8,128)(2,1)S(1)}, u32[]{:S(2)}, u32[]{:S(2)}) collective-permute-start(bf16[512,128]{1,0:T(8,128)(2,1)} %constant_dynamic-update-slice_fusion.own_ref), channel_id=1, source_target_pairs={{0,32},{8,40},{16,48},{24,56},{32,0},{40,8},{48,16},{56,24},{64,96... | collective-permute-start | bytes 393224 | tf_op jit(solution)/shard_map/ppermute | solution.py:228
  35.8 4.9 %collective-permute-start.2 = (bf16[512,128]{1,0:T(8,128)(2,1)}, bf16[512,128]{1,0:T(8,128)(2,1)S(1)}, u32[]{:S(2)}, u32[]{:S(2)}) collective-permute-start(bf16[512,128]{1,0:T(8,128)(2,1)} %constant_dynamic-update-slice_fusion.own_ref), channel_id=1, source_target_pairs={{0,16},{8,24},{16,0},{24,8},{32,48},{40,56},{48,32},{56,40},{64,80... | collective-permute-start | bytes 393224 | tf_op jit(solution)/shard_map/ppermute | solution.py:228
  40.6 0.7 collective-permute-start.1
  41.3 3.7 %collective-permute-start = (bf16[512,128]{1,0:T(8,128)(2,1)}, bf16[512,128]{1,0:T(8,128)(2,1)S(1)}, u32[]{:S(2)}, u32[]{:S(2)}) collective-permute-start(bf16[512,128]{1,0:T(8,128)(2,1)} %constant_dynamic-update-slice_fusion.own_ref), channel_id=1, source_target_pairs={{0,8},{8,0},{16,24},{24,16},{32,40},{40,32},{48,56},{56,48},{64,72... | collective-permute-start | bytes 393224 | tf_op jit(solution)/shard_map/ppermute | solution.py:228
  45.1 0.0 copy-done
  45.1 0.6 fusion
  49.5 0.0 collective-permute-done.4.p4
  49.5 0.0 collective-permute-done.3.p3
  49.6 0.0 collective-permute-done.2.p2
  49.6 0.0 collective-permute-done.1.p1
  49.6 0.0 collective-permute-done.p0
  49.6 0.0 all-to-all-done
  49.6 0.7 broadcast_in_dim.9
  50.4 14.5 %all-to-all-start.1 = ((bf16[64,2,8,128]{3,2,1,0:T(8,128)(2,1)}), bf16[64,2,8,128]{3,2,1,0:T(8,128)(2,1)S(1)}, u32[]{:S(2)}, u32[]{:S(2)}) async-start(bf16[64,2,8,128]{3,2,1,0:T(8,128)(2,1)} %broadcast_in_dim.9), calls=%async_computation.1 | async-start | bytes 524288 | tf_op jit(solution)/shard_map/all_to_all | solution.py:234
  64.9 0.0 copy-done.3
  64.9 13.1 %all-gather = bf16[2048,128]{1,0:T(8,128)(2,1)S(1)} all-gather(bf16[256,128]{1,0:T(8,128)(2,1)S(1)} %copy-done.3), channel_id=2, replica_groups=mesh['z'=16,'x'=4,'y'=4,'core'=2] {'y','core'}, dimensions={0}, use_global_device_ids=true | all-gather | bytes 589824 | tf_op jit(solution)/shard_map/all_gather | solution.py:238
  78.0 7.7 %all-to-all-done.1 = bf16[64,2,8,128]{3,2,1,0:T(8,128)(2,1)S(1)} async-done(((bf16[64,2,8,128]{3,2,1,0:T(8,128)(2,1)}), bf16[64,2,8,128]{3,2,1,0:T(8,128)(2,1)S(1)}, u32[]{:S(2)}, u32[]{:S(2)}) %all-to-all-start.1) | async-done | bytes 262176 | tf_op jit(solution)/shard_map/all_to_all | solution.py:234
  85.7 0.0 copy-start.2
  85.8 0.7 copy-done.2
  86.4 5.4 %forward.1 = (f32[8,256,128]{2,1,0:T(8,128)}, bf16[16,4,32,128]{3,2,1,0:T(8,128)(2,1)}, f32[256,128]{1,0:T(8,128)S(1)}, bf16[256,128]{1,0:T(8,128)(2,1)S(1)}, f32[256,128]{1,0:T(8,128)S(1)}) custom-call(s32[1]{0:T(128)} %bitcast.pos_ref, s32[4,32]{1,0:T(4,128)S(1)} %copy-done.2, bf16[512,128]{1,0:T(8,128)(2,1)} %constant_dynamic-update-slice_fusion.own_ref, ...), custom_call_target="tpu_custom_call" | custom-call | flops 3000000000 | bytes 4000000 | tf_op jit(solution)/shard_map/forward/pallas_call | solution.py:244
  91.8 7.6 %all-to-all-start.2 = ((bf16[64,32,128]{2,1,0:T(8,128)(2,1)}), bf16[64,32,128]{2,1,0:T(8,128)(2,1)S(1)}, u32[]{:S(2)}, u32[]{:S(2)}) async-start(bf16[64,32,128]{2,1,0:T(8,128)(2,1)} %bitcast.8), calls=%async_computation.3 | async-start | bytes 1048576 | tf_op jit(solution)/shard_map/all_to_all | solution.py:266
  99.5 0.0 reduce-scatter.2.cloned.1.call-start
  99.5 0.7 reduce-scatter.2.cloned.1.call-update
  100.2 4.3 %backward.1 = (bf16[256,256]{1,0:T(8,128)(2,1)S(1)}, bf16[256,256]{1,0:T(8,128)(2,1)S(1)}, bf16[256,256]{1,0:T(8,128)(2,1)S(1)}, bf16[256,256]{1,0:T(8,128)(2,1)...) custom-call(s32[1]{0:T(128)} %bitcast.pos_ref, s32[4,32]{1,0:T(4,128)S(1)} %copy-done.2, ...), custom_call_target="tpu_custom_call" | custom-call | flops 3000000000 | bytes 4000000 | tf_op jit(solution)/shard_map/backward/pallas_call | solution.py:268
  104.5 3.5 %collective-permute-start.5 = (bf16[256,256]{1,0:T(8,128)(2,1)S(1)}, bf16[256,256]{1,0:T(8,128)(2,1)S(1)}, u32[]{:S(2)}, u32[]{:S(2)}) collective-permute-start(bf16[256,256]{1,0:T(8,128)(2,1)S(1)} %get-tuple-element.42), channel_id=1, source_target_pairs={{0,8},{8,0},{16,24},{24,16},{32,40},{40,32},{48,56},{56,48},{64,72... | collective-permute-start | bytes 393224 | tf_op jit(solution)/shard_map/ppermute | solution.py:283
  108.0 0.7 collective-permute-start.6
  108.6 5.8 %collective-permute-start.7 = (bf16[256,256]{1,0:T(8,128)(2,1)S(1)}, bf16[256,256]{1,0:T(8,128)(2,1)S(1)}, u32[]{:S(2)}, u32[]{:S(2)}) collective-permute-start(bf16[256,256]{1,0:T(8,128)(2,1)S(1)} %get-tuple-element.44), channel_id=1, source_target_pairs={{0,16},{8,24},{16,0},{24,8},{32,48},{40,56},{48,32},{56,40},{64,80... | collective-permute-start | bytes 393224 | tf_op jit(solution)/shard_map/ppermute | solution.py:283
  114.5 3.4 %collective-permute-start.8 = (bf16[256,256]{1,0:T(8,128)(2,1)S(1)}, bf16[256,256]{1,0:T(8,128)(2,1)S(1)}, u32[]{:S(2)}, u32[]{:S(2)}) collective-permute-start(bf16[256,256]{1,0:T(8,128)(2,1)S(1)} %get-tuple-element.45), channel_id=1, source_target_pairs={{0,32},{8,40},{16,48},{24,56},{32,0},{40,8},{48,16},{56,24},{64,96... | collective-permute-start | bytes 393224 | tf_op jit(solution)/shard_map/ppermute | solution.py:283
  117.8 4.3 %collective-permute-start.9 = (bf16[256,256]{1,0:T(8,128)(2,1)S(1)}, bf16[256,256]{1,0:T(8,128)(2,1)S(1)}, u32[]{:S(2)}, u32[]{:S(2)}) collective-permute-start(bf16[256,256]{1,0:T(8,128)(2,1)S(1)} %get-tuple-element.46), channel_id=1, source_target_pairs={{0,64},{8,72},{16,80},{24,88},{32,96},{40,104},{48,112},{56,120},{... | collective-permute-start | bytes 393224 | tf_op jit(solution)/shard_map/ppermute | solution.py:283
  122.1 0.0 collective-permute-done.5.b0
  122.1 0.0 collective-permute-done.6.b1
  122.1 0.0 collective-permute-done.7.b2
  122.2 10.2 %collective-permute-done.8.b3 = bf16[256,256]{1,0:T(8,128)(2,1)S(1)} collective-permute-done((bf16[256,256]{1,0:T(8,128)(2,1)S(1)}, bf16[256,256]{1,0:T(8,128)(2,1)S(1)}, u32[]{:S(2)}, u32[]{:S(2)}) %collective-permute-start.8) | collective-permute-done | bytes 131104 | tf_op jit(solution)/shard_map/ppermute | solution.py:283
  132.4 0.0 collective-permute-done.9.b4
  132.4 0.4 all-to-all-done.2
  132.8 0.1 reduce_sum.12
  132.9 24.7 %all_to_all.25 = bf16[16,32,128]{2,1,0:T(8,128)(2,1)S(1)} all-to-all(bf16[16,32,128]{2,1,0:T(8,128)(2,1)S(1)} %broadcast_in_dim.10), channel_id=1, replica_groups=mesh['z'=16,'x'=4,'y'=4,'core'=2] {'z'}, dimensions={0} | all-to-all | bytes 262144 | tf_op jit(solution)/shard_map/all_to_all | solution.py:287
  157.6 0.9 broadcast_in_dim.11
  158.5 4.2 %all-to-all-start.4 = ((bf16[4,16,32,128]{3,2,1,0:T(8,128)(2,1)}), bf16[4,16,32,128]{3,2,1,0:T(8,128)(2,1)S(1)}, u32[]{:S(2)}, u32[]{:S(2)}) async-start(bf16[4,16,32,128]{3,2,1,0:T(8,128)(2,1)} %broadcast_in_dim.11), calls=%async_computation.5 | async-start | bytes 1048576 | tf_op jit(solution)/shard_map/all_to_all | solution.py:290
  162.7 1.5 convert_bitcast_fusion
  164.2 6.5 %all-to-all-done.4 = bf16[4,16,32,128]{3,2,1,0:T(8,128)(2,1)S(1)} async-done(((bf16[4,16,32,128]{3,2,1,0:T(8,128)(2,1)}), bf16[4,16,32,128]{3,2,1,0:T(8,128)(2,1)S(1)}, u32[]{:S(2)}, u32[]{:S(2)}) %all-to-all-start.4) | async-done | bytes 524320 | tf_op jit(solution)/shard_map/all_to_all | solution.py:290
  170.8 1.6 finish.1
  (9 shorter events, 0.1 us)
Async XLA Ops:
  7.2 1.5 copy-start.4
  9.3 35.8 %copy-start = (s32[2]{0:T(128)S(1)}, s32[2]{0:T(128)}, u32[]{:S(2)}) copy-start(s32[2]{0:T(128)} %ids_ref.1) | copy-start | bytes 28
  9.3 40.3 %all-to-all-start = ((bf16[64,8,128]{2,1,0:T(8,128)(2,1)}), bf16[64,8,128]{2,1,0:T(8,128)(2,1)S(1)}, u32[]{:S(2)}, u32[]{:S(2)}) async-start(bf16[64,8,128]{2,1,0:T(8,128)(2,1)} %bitcast.1), calls=%async_computation | async-start | bytes 262144 | tf_op jit(solution)/shard_map/all_to_all | solution.py:223
  28.0 21.5 %collective-permute-start.4 = (bf16[512,128]{1,0:T(8,128)(2,1)}, bf16[512,128]{1,0:T(8,128)(2,1)S(1)}, u32[]{:S(2)}, u32[]{:S(2)}) collective-permute-start(bf16[512,128]{1,0:T(8,128)(2,1)} %constant_dynamic-update-slice_fusion.own_ref), channel_id=1, source_target_pairs={{0,64},{8,72},{16,80},{24,88},{32,96},{40,104},{48,112},{56,120},{... | collective-permute-start | bytes 393224 | tf_op jit(solution)/shard_map/ppermute | solution.py:228
  32.4 17.2 %collective-permute-start.3 = (bf16[512,128]{1,0:T(8,128)(2,1)}, bf16[512,128]{1,0:T(8,128)(2,1)S(1)}, u32[]{:S(2)}, u32[]{:S(2)}) collective-permute-start(bf16[512,128]{1,0:T(8,128)(2,1)} %constant_dynamic-update-slice_fusion.own_ref), channel_id=1, source_target_pairs={{0,32},{8,40},{16,48},{24,56},{32,0},{40,8},{48,16},{56,24},{64,96... | collective-permute-start | bytes 393224 | tf_op jit(solution)/shard_map/ppermute | solution.py:228
  35.8 13.8 %collective-permute-start.2 = (bf16[512,128]{1,0:T(8,128)(2,1)}, bf16[512,128]{1,0:T(8,128)(2,1)S(1)}, u32[]{:S(2)}, u32[]{:S(2)}) collective-permute-start(bf16[512,128]{1,0:T(8,128)(2,1)} %constant_dynamic-update-slice_fusion.own_ref), channel_id=1, source_target_pairs={{0,16},{8,24},{16,0},{24,8},{32,48},{40,56},{48,32},{56,40},{64,80... | collective-permute-start | bytes 393224 | tf_op jit(solution)/shard_map/ppermute | solution.py:228
  40.6 8.9 %collective-permute-start.1 = (bf16[512,128]{1,0:T(8,128)(2,1)}, bf16[512,128]{1,0:T(8,128)(2,1)S(1)}, u32[]{:S(2)}, u32[]{:S(2)}) collective-permute-start(bf16[512,128]{1,0:T(8,128)(2,1)} %constant_dynamic-update-slice_fusion.own_ref), channel_id=1, source_target_pairs={{8,16},{16,8},{24,32},{32,24},{40,48},{48,40},{56,64},{64,56},{72,... | collective-permute-start | bytes 393224 | tf_op jit(solution)/shard_map/ppermute | solution.py:228
  41.3 8.3 %collective-permute-start = (bf16[512,128]{1,0:T(8,128)(2,1)}, bf16[512,128]{1,0:T(8,128)(2,1)S(1)}, u32[]{:S(2)}, u32[]{:S(2)}) collective-permute-start(bf16[512,128]{1,0:T(8,128)(2,1)} %constant_dynamic-update-slice_fusion.own_ref), channel_id=1, source_target_pairs={{0,8},{8,0},{16,24},{24,16},{32,40},{40,32},{48,56},{56,48},{64,72... | collective-permute-start | bytes 393224 | tf_op jit(solution)/shard_map/ppermute | solution.py:228
  50.4 14.5 %copy-start.3 = (bf16[256,128]{1,0:T(8,128)(2,1)S(1)}, bf16[256,128]{1,0:T(8,128)(2,1)}, u32[]{:S(2)}) copy-start(bf16[256,128]{1,0:T(8,128)(2,1)} %param.8) | copy-start | bytes 196612
  50.4 35.4 %all-to-all-start.1 = ((bf16[64,2,8,128]{3,2,1,0:T(8,128)(2,1)}), bf16[64,2,8,128]{3,2,1,0:T(8,128)(2,1)S(1)}, u32[]{:S(2)}, u32[]{:S(2)}) async-start(bf16[64,2,8,128]{3,2,1,0:T(8,128)(2,1)} %broadcast_in_dim.9), calls=%async_computation.1 | async-start | bytes 524288 | tf_op jit(solution)/shard_map/all_to_all | solution.py:234
  78.0 7.7 %copy-start.1 = (bf16[128,1024]{1,0:T(8,128)(2,1)S(1)}, bf16[128,1024]{1,0:T(8,128)(2,1)}, u32[]{:S(2)}) copy-start(bf16[128,1024]{1,0:T(8,128)(2,1)} %w_ref.1) | copy-start | bytes 786436
  85.7 0.7 copy-start.2
  91.8 41.0 %all-to-all-start.2 = ((bf16[64,32,128]{2,1,0:T(8,128)(2,1)}), bf16[64,32,128]{2,1,0:T(8,128)(2,1)S(1)}, u32[]{:S(2)}, u32[]{:S(2)}) async-start(bf16[64,32,128]{2,1,0:T(8,128)(2,1)} %bitcast.8), calls=%async_computation.3 | async-start | bytes 1048576 | tf_op jit(solution)/shard_map/all_to_all | solution.py:266
  99.5 63.2 %reduce-scatter.2.cloned.1.call-start = ((), (), s32[]{:S(2)}) async-start(), calls=%async_computation.6 | async-start | bytes 1179648 | tf_op jit(solution)/shard_map/reduce_scatter | solution.py:267
  104.5 17.7 %collective-permute-start.5 = (bf16[256,256]{1,0:T(8,128)(2,1)S(1)}, bf16[256,256]{1,0:T(8,128)(2,1)S(1)}, u32[]{:S(2)}, u32[]{:S(2)}) collective-permute-start(bf16[256,256]{1,0:T(8,128)(2,1)S(1)} %get-tuple-element.42), channel_id=1, source_target_pairs={{0,8},{8,0},{16,24},{24,16},{32,40},{40,32},{48,56},{56,48},{64,72... | collective-permute-start | bytes 393224 | tf_op jit(solution)/shard_map/ppermute | solution.py:283
  108.0 14.2 %collective-permute-start.6 = (bf16[256,256]{1,0:T(8,128)(2,1)S(1)}, bf16[256,256]{1,0:T(8,128)(2,1)S(1)}, u32[]{:S(2)}, u32[]{:S(2)}) collective-permute-start(bf16[256,256]{1,0:T(8,128)(2,1)S(1)} %get-tuple-element.43), channel_id=1, source_target_pairs={{8,16},{16,8},{24,32},{32,24},{40,48},{48,40},{56,64},{64,56},{72,... | collective-permute-start | bytes 393224 | tf_op jit(solution)/shard_map/ppermute | solution.py:283
  108.6 13.5 %collective-permute-start.7 = (bf16[256,256]{1,0:T(8,128)(2,1)S(1)}, bf16[256,256]{1,0:T(8,128)(2,1)S(1)}, u32[]{:S(2)}, u32[]{:S(2)}) collective-permute-start(bf16[256,256]{1,0:T(8,128)(2,1)S(1)} %get-tuple-element.44), channel_id=1, source_target_pairs={{0,16},{8,24},{16,0},{24,8},{32,48},{40,56},{48,32},{56,40},{64,80... | collective-permute-start | bytes 393224 | tf_op jit(solution)/shard_map/ppermute | solution.py:283
  114.5 17.9 %collective-permute-start.8 = (bf16[256,256]{1,0:T(8,128)(2,1)S(1)}, bf16[256,256]{1,0:T(8,128)(2,1)S(1)}, u32[]{:S(2)}, u32[]{:S(2)}) collective-permute-start(bf16[256,256]{1,0:T(8,128)(2,1)S(1)} %get-tuple-element.45), channel_id=1, source_target_pairs={{0,32},{8,40},{16,48},{24,56},{32,0},{40,8},{48,16},{56,24},{64,96... | collective-permute-start | bytes 393224 | tf_op jit(solution)/shard_map/ppermute | solution.py:283
  117.8 14.6 %collective-permute-start.9 = (bf16[256,256]{1,0:T(8,128)(2,1)S(1)}, bf16[256,256]{1,0:T(8,128)(2,1)S(1)}, u32[]{:S(2)}, u32[]{:S(2)}) collective-permute-start(bf16[256,256]{1,0:T(8,128)(2,1)S(1)} %get-tuple-element.46), channel_id=1, source_target_pairs={{0,64},{8,72},{16,80},{24,88},{32,96},{40,104},{48,112},{56,120},{... | collective-permute-start | bytes 393224 | tf_op jit(solution)/shard_map/ppermute | solution.py:283
  158.5 12.3 %all-to-all-start.4 = ((bf16[4,16,32,128]{3,2,1,0:T(8,128)(2,1)}), bf16[4,16,32,128]{3,2,1,0:T(8,128)(2,1)S(1)}, u32[]{:S(2)}, u32[]{:S(2)}) async-start(bf16[4,16,32,128]{3,2,1,0:T(8,128)(2,1)} %broadcast_in_dim.11), calls=%async_computation.5 | async-start | bytes 1048576 | tf_op jit(solution)/shard_map/all_to_all | solution.py:290
Sparse Core Ops, SparseCore 0:
  103.1 37.3 reduce-scatter.1

commit v3 on v2

--- a/solution.py
+++ b/solution.py
@@ -101,8 +101,7 @@
         partial_ref[c] = dot(attended_b, w_ref[:, c * 128:(c + 1) * 128], NN)
         part = dot(attended_b, gout_ref[c], TN).astype(BF16)
         n = width // 16
-        at = c * n % sums_ref.shape[0]
-        sums_ref[at:at + n, c * n // sums_ref.shape[0], 0:16, :] = part.reshape(n, 16, 128)
+        sums_ref[c * n:(c + 1) * n, 0:16, :] = part.reshape(n, 16, 128)
 
     product = gatt_b.astype(F32) * attended
     query_t = query.astype(F32).T.astype(BF16)
@@ -125,10 +124,10 @@
             gv = dot(gt, weights.astype(BF16), NN)
             n = HD // 16
             for a in range(length // 128):
-                x = g * (length // 128) + a
-                for at, term in ((h * n, gk), (width // 16 + h * n, gv)):
+                start = (g * (length // 128) + a) * 2 * width // 16
+                for at, term in ((start + h * n, gk), (start + width // 16 + h * n, gv)):
                     sub = term[:, a * 128:(a + 1) * 128].astype(BF16)
-                    sums_ref[at:at + n, x, 16:32, :] = sub.reshape(n, 16, 128)
+                    sums_ref[at:at + n, 16:32, :] = sub.reshape(n, 16, 128)
         if h == 0:
             out_ref[...] = acc
         else:
@@ -204,6 +203,22 @@
         gweight_ref[:, c * 128:(c + 1) * 128] = piece.astype(F32)
 
 
+def pack_kernel(qk_ref, val_ref, joined_ref, chunks_ref):
+    length = qk_ref.shape[0]
+    for n, ref in enumerate((qk_ref, val_ref)):
+        rows = ref[...]
+        joined_ref[n * length:(n + 1) * length, :] = rows
+        pieces = rows.reshape(chunks_ref.shape[0], 16, rows.shape[1])
+        for g in range(NGLOB):
+            chunks_ref[:, g * 2 + n] = pieces
+
+
+def pick_kernel(pos_ref, ids_ref, slices_ref, out_ref):
+    chosen = slices_ref[ids_ref[pos_ref[0] % 4 // 2]]
+    for z in range(out_ref.shape[0]):
+        out_ref[z] = chosen
+
+
 def vmem(count):
     return [pl.BlockSpec(memory_space=pltpu.VMEM)] * count
 
@@ -219,23 +234,42 @@
     position = lax.axis_index(CTX)
     joined = jnp.concatenate([qk_vectors, token_values], axis=0)
 
-    step = 2 * length // devices
-    slices = lax.all_to_all(joined.reshape(devices, step, width), CTX, 0, 0)
+    zs, xs = lax.axis_size("z"), lax.axis_size("x")
+    joined, chunks = pl.pallas_call(
+        pack_kernel,
+        out_shape=(
+            jax.ShapeDtypeStruct((2 * length, width), BF16),
+            jax.ShapeDtypeStruct((zs, xs, 16, width), BF16),
+        ),
+        in_specs=vmem(2),
+        out_specs=tuple(vmem(2)),
+        name="pack",
+    )(qk_vectors, token_values)
+
+    slices = lax.all_to_all(chunks.reshape(devices, 16, width), CTX, 0, 0)
     routes = [[(i, i ^ 1) for i in range(devices)]]
     other = [i + 1 if i % 2 else i - 1 for i in range(devices)]
     routes.append([(i, j) for i, j in enumerate(other) if 0 <= j < devices])
     routes += [[(i, i ^ (1 << k)) for i in range(devices)] for k in range(1, ROUNDS)]
-    received = [lax.ppermute(joined, CTX, route) for route in routes]
-
-    slices, *received = lax.optimization_barrier((slices, *received))
-    picked = jnp.stack(
-        [lax.dynamic_index_in_dim(slices, global_ids[g], keepdims=False) for g in range(NGLOB)]
-    )
-    spread = lax.all_to_all(
-        jnp.broadcast_to(picked[None], (devices, NGLOB, step, width)), CTX, 0, 0
-    )
-    globals_all = jnp.swapaxes(spread, 0, 1).reshape(NGLOB, 2 * length, width)
-    portion = lax.all_gather(grad_output, HEAD, axis=0)
+    received = [None] * len(routes)
+    for n in (4, 3, 2, 1):
+        received[n] = lax.ppermute(joined, CTX, routes[n])
+    slices, *received[1:] = lax.optimization_barrier((slices, *received[1:]))
+    picked = pl.pallas_call(
+        pick_kernel,
+        out_shape=jax.ShapeDtypeStruct((zs, 16, width), BF16),
+        in_specs=[smem()] * 2 + vmem(1),
+        out_specs=vmem(1)[0],
+        name="pick",
+    )(position[None], global_ids, slices)
+    picked, cotangent = lax.optimization_barrier((picked, grad_output))
+    column = lax.all_to_all(picked, "z", 0, 0)
+    portion = lax.all_gather(cotangent, HEAD, axis=0)
+    column, portion, joined_late = lax.optimization_barrier((column, portion, joined))
+    received[0] = lax.ppermute(joined_late, CTX, routes[0])
+    globals_all = lax.all_to_all(
+        jnp.broadcast_to(column[None], (xs,) + column.shape), "x", 0, 0
+    ).reshape(NGLOB, 2 * length, width)
 
     count = ROUNDS + 2 + NGLOB
     nheads = width // HD
@@ -245,7 +279,7 @@
         forward_kernel,
         out_shape=(
             jax.ShapeDtypeStruct((pieces, length, 128), F32),
-            jax.ShapeDtypeStruct((lax.axis_size("z"), lax.axis_size("x"), 32, 128), BF16),
+            jax.ShapeDtypeStruct((devices, 32, 128), BF16),
             square,
             jax.ShapeDtypeStruct((length, width), BF16),
             square,
@@ -263,7 +297,7 @@
         name="forward",
     )(position[None], pair_active, joined, *received, globals_all, portion, out_weight)
 
-    shares = lax.all_to_all(sums.reshape(devices, 32, 128), CTX, 0, 0)
+    row = lax.all_to_all(sums.reshape(xs, zs, 32, 128), "x", 0, 0)
     projected = lax.psum_scatter(partial, HEAD, scatter_dimension=0, tiled=False).astype(BF16)
     *terms, gquery, gown = pl.pallas_call(
         backward_kernel,
@@ -280,16 +314,18 @@
         ),
         name="backward",
     )(position[None], pair_active, joined, *received, stats, gatt, gglob)
+    row, *terms = lax.optimization_barrier((row, *terms))
     returned = [lax.ppermute(t, CTX, route) for t, route in zip(terms, routes)]
 
-    shares, *returned = lax.optimization_barrier((shares, *returned))
+    row = jnp.sum(row.astype(F32), axis=0).astype(BF16)
+    shares = lax.all_to_all(row, "z", 0, 0)
+    shares, returned[0], returned[2] = lax.optimization_barrier((shares, returned[0], returned[2]))
     share = jnp.sum(shares.astype(F32), axis=0).astype(BF16)
-    column = lax.all_to_all(
-        jnp.broadcast_to(share[None], (lax.axis_size("z"),) + share.shape), "z", 0, 0
-    )
+    column = lax.all_to_all(jnp.broadcast_to(share[None], (zs,) + share.shape), "z", 0, 0)
+    column, returned[1], returned[3] = lax.optimization_barrier((column, returned[1], returned[3]))
     totals = lax.all_to_all(
-        jnp.broadcast_to(column[None], (lax.axis_size("x"),) + column.shape), "x", 0, 0
-    ).reshape(shares.shape)
+        jnp.broadcast_to(column[None], (xs,) + column.shape), "x", 0, 0
+    ).reshape(devices, 32, 128)
 
     gqk, gval, gweight = pl.pallas_call(
         finish_kernel,

time: 180 us -> 185 us (1.028)
  blocking collectives: 37.8 us -> 13.1 us
  starting transfers between devices: 79.7 us -> 95.1 us
  waiting for transfers between devices: 25.6 us -> 40.7 us
  between operations: 18.2 us -> 14.2 us
  Pallas kernels: 11.2 us -> 13.8 us
    all_to_all x1 -> x0, blocking collectives: 24.7 us -> none  [local(): lax.all_to_all(jnp.broadcast_to(share[None], (lax.axis_size('z'),) + shar...]
    all_to_all x4 -> x7, starting transfers between devices: 45 us -> 61.7 us  [the longest x1 18.7 us: local(): slices = lax.all_to_all(chunks.reshape(devices, 16, width), CTX, 0, 0)]
    ppermute x5, waiting for transfers between devices: 0.01 us -> 11.7 us  [the longest x4 6.83 us: local(): received[n] = lax.ppermute(joined, CTX, routes[n])]
    ppermute x5, waiting for transfers between devices: 10.3 us -> 14.9 us  [local(): returned = [lax.ppermute(t, CTX, route) for t, route in zip(terms, routes)]]
    pallas_call x0 -> x2, Pallas kernels: none -> 3.28 us  [the longest x1 1.67 us: local(): pl.pallas_call(pack_kernel, out_shape=(jax.ShapeDtypeStruct((2 * length,...]
    all_to_all x4 -> x7, waiting for transfers between devices: 14.6 us -> 14.1 us  [the longest x1 5.38 us: local(): row = lax.all_to_all(sums.reshape(xs, zs, 32, 128), 'x', 0, 0)]
  transfers between devices with their start and end apart: 15 -> 18, of which waited for: 4 -> 10; matrix products, arithmetic and copies ran while one was open for 2% -> 1% of each run, Pallas kernels for 2% -> 3%
where the time goes in v3:
time: 185 us; the launch traced here: 183 us
  starting transfers between devices  95.1 us (51%)
  waiting for transfers between devices  40.7 us (22%)
  between operations  14.2 us (8%)
  Pallas kernels  13.8 us (7%)
  blocking collectives  13.1 us (7%)
  local copies, waits for them, and re-layouts  3.66 us (2%)
  other arithmetic  2.31 us (1%)
    all_to_all x1, starting transfers between devices, local(): slices = lax.all_to_all(chunks.reshape(devices, 16, width), CTX, 0, 0)  18.7 us
    ppermute x5, starting transfers between devices, local(): returned = [lax.ppermute(t, CTX, route) for t, route in zip(terms, routes)]  16.2 us
    ppermute x5, waiting for transfers between devices, local(): returned = [lax.ppermute(t, CTX, route) for t, route in zip(terms, routes)]  14.9 us
    ppermute x4, starting transfers between devices, local(): received[n] = lax.ppermute(joined, CTX, routes[n])  13.3 us
    all_gather x1, blocking collectives, local(): portion = lax.all_gather(cotangent, HEAD, axis=0)  13.1 us
    all_to_all x1, starting transfers between devices, local(): shares = lax.all_to_all(row, 'z', 0, 0)  12 us
    all_to_all x1, starting transfers between devices, local(): column = lax.all_to_all(picked, 'z', 0, 0)  10.6 us
    all_to_all x1, starting transfers between devices, local(): lax.all_to_all(jnp.broadcast_to(share[None], (zs,) + share.shape), 'z', 0...  9.42 us
  transfers between devices with their start and end apart: 18, of which 10 were waited for; matrix products, arithmetic and copies ran while one was open for 1% of the time, Pallas kernels for 3%

profile of v3, /device:TPU:24, one launch (start us, length us, event | category | flops | bytes accessed | tf_op | source)
XLA Modules:
  0.0 182.8 jit_solution(6924400515393813357)
XLA Ops:
  7.2 1.7 pack.1
  8.8 18.7 %all-to-all-start = ((bf16[64,16,128]{2,1,0:T(8,128)(2,1)}), bf16[64,16,128]{2,1,0:T(8,128)(2,1)S(1)}, u32[]{:S(2)}, u32[]{:S(2)}) async-start(bf16[64,16,128]{2,1,0:T(8,128)(2,1)} %bitcast.11), calls=%async_computation | async-start | bytes 524288 | tf_op jit(solution)/shard_map/all_to_all | solution.py:249
  27.5 4.4 %collective-permute-start.3 = (bf16[512,128]{1,0:T(8,128)(2,1)S(1)}, bf16[512,128]{1,0:T(8,128)(2,1)S(1)}, u32[]{:S(2)}, u32[]{:S(2)}) collective-permute-start(bf16[512,128]{1,0:T(8,128)(2,1)S(1)} %copy-done.2), channel_id=1, source_target_pairs={{0,64},{8,72},{16,80},{24,88},{32,96},{40,104},{48,112},{56,120},{... | collective-permute-start | bytes 393224 | tf_op jit(solution)/shard_map/ppermute | solution.py:256
  31.9 3.4 %collective-permute-start.2 = (bf16[512,128]{1,0:T(8,128)(2,1)S(1)}, bf16[512,128]{1,0:T(8,128)(2,1)S(1)}, u32[]{:S(2)}, u32[]{:S(2)}) collective-permute-start(bf16[512,128]{1,0:T(8,128)(2,1)S(1)} %copy-done.2), channel_id=1, source_target_pairs={{0,32},{8,40},{16,48},{24,56},{32,0},{40,8},{48,16},{56,24},{64,96... | collective-permute-start | bytes 393224 | tf_op jit(solution)/shard_map/ppermute | solution.py:256
  35.3 4.9 %collective-permute-start.1 = (bf16[512,128]{1,0:T(8,128)(2,1)S(1)}, bf16[512,128]{1,0:T(8,128)(2,1)S(1)}, u32[]{:S(2)}, u32[]{:S(2)}) collective-permute-start(bf16[512,128]{1,0:T(8,128)(2,1)S(1)} %copy-done.2), channel_id=1, source_target_pairs={{0,16},{8,24},{16,0},{24,8},{32,48},{40,56},{48,32},{56,40},{64,80... | collective-permute-start | bytes 393224 | tf_op jit(solution)/shard_map/ppermute | solution.py:256
  40.2 0.7 collective-permute-start
  40.9 6.8 %collective-permute-done.3.p4 = bf16[512,128]{1,0:T(8,128)(2,1)S(1)} collective-permute-done((bf16[512,128]{1,0:T(8,128)(2,1)S(1)}, bf16[512,128]{1,0:T(8,128)(2,1)S(1)}, u32[]{:S(2)}, u32[]{:S(2)}) %collective-permute-start.3) | collective-permute-done | bytes 131104 | tf_op jit(solution)/shard_map/ppermute | solution.py:256
  47.7 0.0 collective-permute-done.2.p3
  47.7 0.0 collective-permute-done.1.p2
  47.7 0.0 collective-permute-done.p1
  47.7 3.4 %all-to-all-done.slices_ref = bf16[64,16,128]{2,1,0:T(8,128)(2,1)S(1)} async-done(((bf16[64,16,128]{2,1,0:T(8,128)(2,1)}), bf16[64,16,128]{2,1,0:T(8,128)(2,1)S(1)}, u32[]{:S(2)}, u32[]{:S(2)}) %all-to-all-start) | async-done | bytes 262176 | tf_op jit(solution)/shard_map/all_to_all | solution.py:249
  51.1 0.7 copy-done.4
  51.8 1.6 pick.1
  53.4 10.6 %all-to-all-start.1 = ((bf16[16,16,128]{2,1,0:T(8,128)(2,1)}), bf16[16,16,128]{2,1,0:T(8,128)(2,1)S(1)}, u32[]{:S(2)}, u32[]{:S(2)}) async-start(bf16[16,16,128]{2,1,0:T(8,128)(2,1)} %pick.1), calls=%async_computation.1 | async-start | bytes 131072 | tf_op jit(solution)/shard_map/all_to_all | solution.py:266
  64.1 13.1 %all-gather = bf16[2048,128]{1,0:T(8,128)(2,1)S(1)} all-gather(bf16[256,128]{1,0:T(8,128)(2,1)S(1)} %copy-done.5), channel_id=2, replica_groups=mesh['z'=16,'x'=4,'y'=4,'core'=2] {'y','core'}, dimensions={0}, use_global_device_ids=true | all-gather | bytes 589824 | tf_op jit(solution)/shard_map/all_gather | solution.py:267
  77.2 0.0 all-to-all-done.1
  77.2 0.7 broadcast_in_dim.9
  77.9 3.5 %all-to-all-start.2 = ((bf16[4,16,16,128]{3,2,1,0:T(8,128)(2,1)}), bf16[4,16,16,128]{3,2,1,0:T(8,128)(2,1)S(1)}, u32[]{:S(2)}, u32[]{:S(2)}) async-start(bf16[4,16,16,128]{3,2,1,0:T(8,128)(2,1)} %broadcast_in_dim.9), calls=%async_computation.2 | async-start | bytes 524288 | tf_op jit(solution)/shard_map/all_to_all | solution.py:270
  81.5 0.0 reduce-scatter.2.cloned.1.call-start
  81.5 3.8 %collective-permute-start.4 = (bf16[512,128]{1,0:T(8,128)(2,1)S(1)}, bf16[512,128]{1,0:T(8,128)(2,1)S(1)}, u32[]{:S(2)}, u32[]{:S(2)}) collective-permute-start(bf16[512,128]{1,0:T(8,128)(2,1)S(1)} %copy-done.2), channel_id=1, source_target_pairs={{0,8},{8,0},{16,24},{24,16},{32,40},{40,32},{48,56},{56,48},{64,72... | collective-permute-start | bytes 393224 | tf_op jit(solution)/shard_map/ppermute | solution.py:269
  85.4 4.8 %collective-permute-done.4.p0 = bf16[512,128]{1,0:T(8,128)(2,1)S(1)} collective-permute-done((bf16[512,128]{1,0:T(8,128)(2,1)S(1)}, bf16[512,128]{1,0:T(8,128)(2,1)S(1)}, u32[]{:S(2)}, u32[]{:S(2)}) %collective-permute-start.4) | collective-permute-done | bytes 131104 | tf_op jit(solution)/shard_map/ppermute | solution.py:269
  90.2 0.0 all-to-all-done.2
  90.2 5.0 %forward.1 = (f32[8,256,128]{2,1,0:T(8,128)}, bf16[64,32,128]{2,1,0:T(8,128)(2,1)}, f32[256,128]{1,0:T(8,128)S(1)}, bf16[256,128]{1,0:T(8,128)(2,1)S(1)}, f32[256,128]{1,0:T(8,128)S(1)}) custom-call(s32[1]{0:T(128)} %bitcast.pos_ref, s32[4,32]{1,0:T(4,128)S(1)} %copy-done.3, bf16[512,128]{1,0:T(8,128)(2,1)S(1)} %copy-done.2, ...), custom_call_target="tpu_custom_call" | custom-call | flops 3000000000 | bytes 4000000 | tf_op jit(solution)/shard_map/forward/pallas_call | solution.py:278
  95.2 0.0 reduce-scatter.2.cloned.1.call-update
  95.2 4.0 %all-to-all-start.3 = ((bf16[4,16,32,128]{3,2,1,0:T(8,128)(2,1)}), bf16[4,16,32,128]{3,2,1,0:T(8,128)(2,1)S(1)}, u32[]{:S(2)}, u32[]{:S(2)}) async-start(bf16[4,16,32,128]{3,2,1,0:T(8,128)(2,1)} %bitcast.5), calls=%async_computation.4 | async-start | bytes 1048576 | tf_op jit(solution)/shard_map/all_to_all | solution.py:300
  99.2 3.9 %backward.1 = (bf16[256,256]{1,0:T(8,128)(2,1)S(1)}, bf16[256,256]{1,0:T(8,128)(2,1)S(1)}, bf16[256,256]{1,0:T(8,128)(2,1)S(1)}, bf16[256,256]{1,0:T(8,128)(2,1)...) custom-call(s32[1]{0:T(128)} %bitcast.pos_ref, s32[4,32]{1,0:T(4,128)S(1)} %copy-done.3, ...), custom_call_target="tpu_custom_call" | custom-call | flops 3000000000 | bytes 4000000 | tf_op jit(solution)/shard_map/backward/pallas_call | solution.py:302
  103.1 5.4 %all-to-all-done.3 = bf16[4,16,32,128]{3,2,1,0:T(8,128)(2,1)S(1)} async-done(((bf16[4,16,32,128]{3,2,1,0:T(8,128)(2,1)}), bf16[4,16,32,128]{3,2,1,0:T(8,128)(2,1)S(1)}, u32[]{:S(2)}, u32[]{:S(2)}) %all-to-all-start.3) | async-done | bytes 524320 | tf_op jit(solution)/shard_map/all_to_all | solution.py:300
  108.5 0.7 reduce_sum.24
  109.2 12.0 %all-to-all-start.4 = ((bf16[16,32,128]{2,1,0:T(8,128)(2,1)}), bf16[16,32,128]{2,1,0:T(8,128)(2,1)S(1)}, u32[]{:S(2)}, u32[]{:S(2)}) async-start(bf16[16,32,128]{2,1,0:T(8,128)(2,1)} %reduce_sum.24), calls=%async_computation.5 | async-start | bytes 262144 | tf_op jit(solution)/shard_map/all_to_all | solution.py:321
  121.2 2.5 %collective-permute-start.5 = (bf16[256,256]{1,0:T(8,128)(2,1)S(1)}, bf16[256,256]{1,0:T(8,128)(2,1)S(1)}, u32[]{:S(2)}, u32[]{:S(2)}) collective-permute-start(bf16[256,256]{1,0:T(8,128)(2,1)S(1)} %get-tuple-element.66), channel_id=1, source_target_pairs={{0,8},{8,0},{16,24},{24,16},{32,40},{40,32},{48,56},{56,48},{64,72... | collective-permute-start | bytes 393224 | tf_op jit(solution)/shard_map/ppermute | solution.py:318
  123.7 4.0 %collective-permute-start.6 = (bf16[256,256]{1,0:T(8,128)(2,1)S(1)}, bf16[256,256]{1,0:T(8,128)(2,1)S(1)}, u32[]{:S(2)}, u32[]{:S(2)}) collective-permute-start(bf16[256,256]{1,0:T(8,128)(2,1)S(1)} %get-tuple-element.67), channel_id=1, source_target_pairs={{0,16},{8,24},{16,0},{24,8},{32,48},{40,56},{48,32},{56,40},{64,80... | collective-permute-start | bytes 393224 | tf_op jit(solution)/shard_map/ppermute | solution.py:318
  127.7 0.6 collective-permute-done.5.b0
  128.3 3.8 %collective-permute-done.6.b2 = bf16[256,256]{1,0:T(8,128)(2,1)S(1)} collective-permute-done((bf16[256,256]{1,0:T(8,128)(2,1)S(1)}, bf16[256,256]{1,0:T(8,128)(2,1)S(1)}, u32[]{:S(2)}, u32[]{:S(2)}) %collective-permute-start.6) | collective-permute-done | bytes 131104 | tf_op jit(solution)/shard_map/ppermute | solution.py:318
  132.1 2.6 %all-to-all-done.4 = bf16[16,32,128]{2,1,0:T(8,128)(2,1)S(1)} async-done(((bf16[16,32,128]{2,1,0:T(8,128)(2,1)}), bf16[16,32,128]{2,1,0:T(8,128)(2,1)S(1)}, u32[]{:S(2)}, u32[]{:S(2)}) %all-to-all-start.4) | async-done | bytes 131104 | tf_op jit(solution)/shard_map/all_to_all | solution.py:321
  134.7 0.7 broadcast_in_dim.10
  135.4 9.4 %all-to-all-start.5 = ((bf16[16,32,128]{2,1,0:T(8,128)(2,1)}), bf16[16,32,128]{2,1,0:T(8,128)(2,1)S(1)}, u32[]{:S(2)}, u32[]{:S(2)}) async-start(bf16[16,32,128]{2,1,0:T(8,128)(2,1)} %broadcast_in_dim.10), calls=%async_computation.6 | async-start | bytes 262144 | tf_op jit(solution)/shard_map/all_to_all | solution.py:324
  144.8 0.7 collective-permute-start.7
  145.5 5.2 %collective-permute-start.8 = (bf16[256,256]{1,0:T(8,128)(2,1)S(1)}, bf16[256,256]{1,0:T(8,128)(2,1)S(1)}, u32[]{:S(2)}, u32[]{:S(2)}) collective-permute-start(bf16[256,256]{1,0:T(8,128)(2,1)S(1)} %get-tuple-element.71), channel_id=1, source_target_pairs={{0,32},{8,40},{16,48},{24,56},{32,0},{40,8},{48,16},{56,24},{64,96... | collective-permute-start | bytes 393224 | tf_op jit(solution)/shard_map/ppermute | solution.py:318
  150.7 5.3 %collective-permute-done.8.b3 = bf16[256,256]{1,0:T(8,128)(2,1)S(1)} collective-permute-done((bf16[256,256]{1,0:T(8,128)(2,1)S(1)}, bf16[256,256]{1,0:T(8,128)(2,1)S(1)}, u32[]{:S(2)}, u32[]{:S(2)}) %collective-permute-start.8) | collective-permute-done | bytes 131104 | tf_op jit(solution)/shard_map/ppermute | solution.py:318
  156.1 2.8 %all-to-all-done.5 = bf16[16,32,128]{2,1,0:T(8,128)(2,1)S(1)} async-done(((bf16[16,32,128]{2,1,0:T(8,128)(2,1)}), bf16[16,32,128]{2,1,0:T(8,128)(2,1)S(1)}, u32[]{:S(2)}, u32[]{:S(2)}) %all-to-all-start.5) | async-done | bytes 131104 | tf_op jit(solution)/shard_map/all_to_all | solution.py:324
  158.8 0.9 broadcast_in_dim.11
  159.7 3.5 %all-to-all-start.6 = ((bf16[4,16,32,128]{3,2,1,0:T(8,128)(2,1)}), bf16[4,16,32,128]{3,2,1,0:T(8,128)(2,1)S(1)}, u32[]{:S(2)}, u32[]{:S(2)}) async-start(bf16[4,16,32,128]{3,2,1,0:T(8,128)(2,1)} %broadcast_in_dim.11), calls=%async_computation.7 | async-start | bytes 1048576 | tf_op jit(solution)/shard_map/all_to_all | solution.py:326
  163.2 3.8 %collective-permute-start.9 = (bf16[256,256]{1,0:T(8,128)(2,1)S(1)}, bf16[256,256]{1,0:T(8,128)(2,1)S(1)}, u32[]{:S(2)}, u32[]{:S(2)}) collective-permute-start(bf16[256,256]{1,0:T(8,128)(2,1)S(1)} %get-tuple-element.75), channel_id=1, source_target_pairs={{0,64},{8,72},{16,80},{24,88},{32,96},{40,104},{48,112},{56,120},{... | collective-permute-start | bytes 393224 | tf_op jit(solution)/shard_map/ppermute | solution.py:318
  167.0 5.2 %collective-permute-done.9.b4 = bf16[256,256]{1,0:T(8,128)(2,1)S(1)} collective-permute-done((bf16[256,256]{1,0:T(8,128)(2,1)S(1)}, bf16[256,256]{1,0:T(8,128)(2,1)S(1)}, u32[]{:S(2)}, u32[]{:S(2)}) %collective-permute-start.9) | collective-permute-done | bytes 131104 | tf_op jit(solution)/shard_map/ppermute | solution.py:318
  172.2 0.0 all-to-all-done.6
  172.2 0.7 copy-done
  172.8 1.6 finish.1
  174.4 1.5 convert_bitcast_fusion
  (13 shorter events, 0.0 us)
Async XLA Ops:
  8.8 18.7 %copy-start.2 = (bf16[512,128]{1,0:T(8,128)(2,1)S(1)}, bf16[512,128]{1,0:T(8,128)(2,1)}, u32[]{:S(2)}) copy-start(bf16[512,128]{1,0:T(8,128)(2,1)} %get-tuple-element.48.own_ref) | copy-start | bytes 393220
  8.8 42.3 %all-to-all-start = ((bf16[64,16,128]{2,1,0:T(8,128)(2,1)}), bf16[64,16,128]{2,1,0:T(8,128)(2,1)S(1)}, u32[]{:S(2)}, u32[]{:S(2)}) async-start(bf16[64,16,128]{2,1,0:T(8,128)(2,1)} %bitcast.11), calls=%async_computation | async-start | bytes 524288 | tf_op jit(solution)/shard_map/all_to_all | solution.py:249
  27.5 20.2 %collective-permute-start.3 = (bf16[512,128]{1,0:T(8,128)(2,1)S(1)}, bf16[512,128]{1,0:T(8,128)(2,1)S(1)}, u32[]{:S(2)}, u32[]{:S(2)}) collective-permute-start(bf16[512,128]{1,0:T(8,128)(2,1)S(1)} %copy-done.2), channel_id=1, source_target_pairs={{0,64},{8,72},{16,80},{24,88},{32,96},{40,104},{48,112},{56,120},{... | collective-permute-start | bytes 393224 | tf_op jit(solution)/shard_map/ppermute | solution.py:256
  31.9 15.8 %collective-permute-start.2 = (bf16[512,128]{1,0:T(8,128)(2,1)S(1)}, bf16[512,128]{1,0:T(8,128)(2,1)S(1)}, u32[]{:S(2)}, u32[]{:S(2)}) collective-permute-start(bf16[512,128]{1,0:T(8,128)(2,1)S(1)} %copy-done.2), channel_id=1, source_target_pairs={{0,32},{8,40},{16,48},{24,56},{32,0},{40,8},{48,16},{56,24},{64,96... | collective-permute-start | bytes 393224 | tf_op jit(solution)/shard_map/ppermute | solution.py:256
  35.3 12.4 %collective-permute-start.1 = (bf16[512,128]{1,0:T(8,128)(2,1)S(1)}, bf16[512,128]{1,0:T(8,128)(2,1)S(1)}, u32[]{:S(2)}, u32[]{:S(2)}) collective-permute-start(bf16[512,128]{1,0:T(8,128)(2,1)S(1)} %copy-done.2), channel_id=1, source_target_pairs={{0,16},{8,24},{16,0},{24,8},{32,48},{40,56},{48,32},{56,40},{64,80... | collective-permute-start | bytes 393224 | tf_op jit(solution)/shard_map/ppermute | solution.py:256
  40.2 7.5 %collective-permute-start = (bf16[512,128]{1,0:T(8,128)(2,1)S(1)}, bf16[512,128]{1,0:T(8,128)(2,1)S(1)}, u32[]{:S(2)}, u32[]{:S(2)}) collective-permute-start(bf16[512,128]{1,0:T(8,128)(2,1)S(1)} %copy-done.2), channel_id=1, source_target_pairs={{8,16},{16,8},{24,32},{32,24},{40,48},{48,40},{56,64},{64,56},{72,... | collective-permute-start | bytes 393224 | tf_op jit(solution)/shard_map/ppermute | solution.py:256
  51.1 0.7 copy-start.4
  53.4 10.6 %copy-start.5 = (bf16[256,128]{1,0:T(8,128)(2,1)S(1)}, bf16[256,128]{1,0:T(8,128)(2,1)}, u32[]{:S(2)}) copy-start(bf16[256,128]{1,0:T(8,128)(2,1)} %param.8) | copy-start | bytes 196612
  53.4 23.7 %all-to-all-start.1 = ((bf16[16,16,128]{2,1,0:T(8,128)(2,1)}), bf16[16,16,128]{2,1,0:T(8,128)(2,1)S(1)}, u32[]{:S(2)}, u32[]{:S(2)}) async-start(bf16[16,16,128]{2,1,0:T(8,128)(2,1)} %pick.1), calls=%async_computation.1 | async-start | bytes 131072 | tf_op jit(solution)/shard_map/all_to_all | solution.py:266
  77.9 12.3 %copy-start.1 = (bf16[128,1024]{1,0:T(8,128)(2,1)S(1)}, bf16[128,1024]{1,0:T(8,128)(2,1)}, u32[]{:S(2)}) copy-start(bf16[128,1024]{1,0:T(8,128)(2,1)} %w_ref.1) | copy-start | bytes 786436
  77.9 12.3 %copy-start.3 = (s32[4,32]{1,0:T(4,128)S(1)}, s32[4,32]{1,0:T(4,128)}, u32[]{:S(2)}) copy-start(s32[4,32]{1,0:T(4,128)} %pair_ref.3) | copy-start | bytes 1540
  77.9 12.3 %all-to-all-start.2 = ((bf16[4,16,16,128]{3,2,1,0:T(8,128)(2,1)}), bf16[4,16,16,128]{3,2,1,0:T(8,128)(2,1)S(1)}, u32[]{:S(2)}, u32[]{:S(2)}) async-start(bf16[4,16,16,128]{3,2,1,0:T(8,128)(2,1)} %broadcast_in_dim.9), calls=%async_computation.2 | async-start | bytes 524288 | tf_op jit(solution)/shard_map/all_to_all | solution.py:270
  81.5 93.0 %reduce-scatter.2.cloned.1.call-start = ((), (), s32[]{:S(2)}) async-start(), calls=%async_computation.8 | async-start | bytes 1179648 | tf_op jit(solution)/shard_map/reduce_scatter | solution.py:301
  81.5 8.7 %collective-permute-start.4 = (bf16[512,128]{1,0:T(8,128)(2,1)S(1)}, bf16[512,128]{1,0:T(8,128)(2,1)S(1)}, u32[]{:S(2)}, u32[]{:S(2)}) collective-permute-start(bf16[512,128]{1,0:T(8,128)(2,1)S(1)} %copy-done.2), channel_id=1, source_target_pairs={{0,8},{8,0},{16,24},{24,16},{32,40},{40,32},{48,56},{56,48},{64,72... | collective-permute-start | bytes 393224 | tf_op jit(solution)/shard_map/ppermute | solution.py:269
  95.2 13.2 %all-to-all-start.3 = ((bf16[4,16,32,128]{3,2,1,0:T(8,128)(2,1)}), bf16[4,16,32,128]{3,2,1,0:T(8,128)(2,1)S(1)}, u32[]{:S(2)}, u32[]{:S(2)}) async-start(bf16[4,16,32,128]{3,2,1,0:T(8,128)(2,1)} %bitcast.5), calls=%async_computation.4 | async-start | bytes 1048576 | tf_op jit(solution)/shard_map/all_to_all | solution.py:300
  109.2 25.4 %all-to-all-start.4 = ((bf16[16,32,128]{2,1,0:T(8,128)(2,1)}), bf16[16,32,128]{2,1,0:T(8,128)(2,1)S(1)}, u32[]{:S(2)}, u32[]{:S(2)}) async-start(bf16[16,32,128]{2,1,0:T(8,128)(2,1)} %reduce_sum.24), calls=%async_computation.5 | async-start | bytes 262144 | tf_op jit(solution)/shard_map/all_to_all | solution.py:321
  121.2 7.1 %collective-permute-start.5 = (bf16[256,256]{1,0:T(8,128)(2,1)S(1)}, bf16[256,256]{1,0:T(8,128)(2,1)S(1)}, u32[]{:S(2)}, u32[]{:S(2)}) collective-permute-start(bf16[256,256]{1,0:T(8,128)(2,1)S(1)} %get-tuple-element.66), channel_id=1, source_target_pairs={{0,8},{8,0},{16,24},{24,16},{32,40},{40,32},{48,56},{56,48},{64,72... | collective-permute-start | bytes 393224 | tf_op jit(solution)/shard_map/ppermute | solution.py:318
  123.7 8.4 %collective-permute-start.6 = (bf16[256,256]{1,0:T(8,128)(2,1)S(1)}, bf16[256,256]{1,0:T(8,128)(2,1)S(1)}, u32[]{:S(2)}, u32[]{:S(2)}) collective-permute-start(bf16[256,256]{1,0:T(8,128)(2,1)S(1)} %get-tuple-element.67), channel_id=1, source_target_pairs={{0,16},{8,24},{16,0},{24,8},{32,48},{40,56},{48,32},{56,40},{64,80... | collective-permute-start | bytes 393224 | tf_op jit(solution)/shard_map/ppermute | solution.py:318
  135.4 23.4 %all-to-all-start.5 = ((bf16[16,32,128]{2,1,0:T(8,128)(2,1)}), bf16[16,32,128]{2,1,0:T(8,128)(2,1)S(1)}, u32[]{:S(2)}, u32[]{:S(2)}) async-start(bf16[16,32,128]{2,1,0:T(8,128)(2,1)} %broadcast_in_dim.10), calls=%async_computation.6 | async-start | bytes 262144 | tf_op jit(solution)/shard_map/all_to_all | solution.py:324
  144.8 5.9 %collective-permute-start.7 = (bf16[256,256]{1,0:T(8,128)(2,1)S(1)}, bf16[256,256]{1,0:T(8,128)(2,1)S(1)}, u32[]{:S(2)}, u32[]{:S(2)}) collective-permute-start(bf16[256,256]{1,0:T(8,128)(2,1)S(1)} %get-tuple-element.70), channel_id=1, source_target_pairs={{8,16},{16,8},{24,32},{32,24},{40,48},{48,40},{56,64},{64,56},{72,... | collective-permute-start | bytes 393224 | tf_op jit(solution)/shard_map/ppermute | solution.py:318
  145.5 10.6 %collective-permute-start.8 = (bf16[256,256]{1,0:T(8,128)(2,1)S(1)}, bf16[256,256]{1,0:T(8,128)(2,1)S(1)}, u32[]{:S(2)}, u32[]{:S(2)}) collective-permute-start(bf16[256,256]{1,0:T(8,128)(2,1)S(1)} %get-tuple-element.71), channel_id=1, source_target_pairs={{0,32},{8,40},{16,48},{24,56},{32,0},{40,8},{48,16},{56,24},{64,96... | collective-permute-start | bytes 393224 | tf_op jit(solution)/shard_map/ppermute | solution.py:318
  159.7 12.5 %all-to-all-start.6 = ((bf16[4,16,32,128]{3,2,1,0:T(8,128)(2,1)}), bf16[4,16,32,128]{3,2,1,0:T(8,128)(2,1)S(1)}, u32[]{:S(2)}, u32[]{:S(2)}) async-start(bf16[4,16,32,128]{3,2,1,0:T(8,128)(2,1)} %broadcast_in_dim.11), calls=%async_computation.7 | async-start | bytes 1048576 | tf_op jit(solution)/shard_map/all_to_all | solution.py:326
  163.2 9.0 %collective-permute-start.9 = (bf16[256,256]{1,0:T(8,128)(2,1)S(1)}, bf16[256,256]{1,0:T(8,128)(2,1)S(1)}, u32[]{:S(2)}, u32[]{:S(2)}) collective-permute-start(bf16[256,256]{1,0:T(8,128)(2,1)S(1)} %get-tuple-element.75), channel_id=1, source_target_pairs={{0,64},{8,72},{16,80},{24,88},{32,96},{40,104},{48,112},{56,120},{... | collective-permute-start | bytes 393224 | tf_op jit(solution)/shard_map/ppermute | solution.py:318
  172.2 0.7 copy-start
Sparse Core Ops, SparseCore 0:
  95.4 37.1 reduce-scatter.1

commit v4 on v2

--- a/solution.py
+++ b/solution.py
@@ -41,9 +41,19 @@
     return bias + [zero] * NGLOB
 
 
+def cotangent_kernel(gout_ref, w_ref, out_ref, gatt_ref):
+    pieces, length, width = gout_ref.shape
+    gatt = jnp.zeros((length, width), F32)
+    for c in range(pieces):
+        part = gout_ref[c].astype(BF16)
+        out_ref[c] = part
+        gatt = gatt + dot(part, w_ref[:, c * width:(c + 1) * width], NT)
+    gatt_ref[...] = gatt.astype(BF16)
+
+
 def forward_kernel(
-    pos_ref, pair_ref, own_ref, p0, p1, p2, p3, p4, glob_ref, gout_ref, w_ref,
-    partial_ref, sums_ref, stats_ref, gatt_ref, gquery_ref,
+    pos_ref, pair_ref, own_ref, p0, p1, p2, p3, p4, glob_ref, gout_ref, gatt_ref,
+    att_ref, sums_ref, stats_ref, gquery_ref,
     score_ref, out_ref,
 ):
     length = own_ref.shape[0] // 2
@@ -55,19 +65,15 @@
     bias = block_bias(pos_ref, pair_ref)
     keys = [r[:length] for r in (own_ref, p0, p1, p2, p3, p4)]
     vals = [r[length:] for r in (own_ref, p0, p1, p2, p3, p4)]
+    half = glob_ref.shape[0] // 2
     for g in range(NGLOB):
-        keys.append(glob_ref[g, :length])
-        vals.append(glob_ref[g, length:])
+        keys.append(jnp.concatenate([glob_ref[x, g] for x in range(half)], axis=0))
+        vals.append(jnp.concatenate([glob_ref[half + x, g] for x in range(half)], axis=0))
     count = len(keys)
     query = own_ref[:length]
     lane = lax.broadcasted_iota(jnp.int32, (1, width), 1)
     head = lane // HD
-
-    gatt = jnp.zeros((length, width), F32)
-    for c in range(pieces):
-        gatt = gatt + dot(gout_ref[c], w_ref[:, c * 128:(c + 1) * 128], NT)
-    gatt_b = gatt.astype(BF16)
-    gatt_ref[...] = gatt_b
+    gatt_b = gatt_ref[...]
 
     inverse = []
     stats = jnp.zeros((length, width), F32)
@@ -96,9 +102,9 @@
             out_ref[...] = jnp.where(head == h, acc, out_ref[...])
 
     attended = out_ref[...]
+    att_ref[...] = attended
     attended_b = attended.astype(BF16)
     for c in range(pieces):
-        partial_ref[c] = dot(attended_b, w_ref[:, c * 128:(c + 1) * 128], NN)
         part = dot(attended_b, gout_ref[c], TN).astype(BF16)
         n = width // 16
         at = c * n % sums_ref.shape[0]
@@ -179,6 +185,13 @@
     gquery_ref[...] = result * scaling
 
 
+def project_kernel(att_ref, w_ref, projected_ref):
+    projected = jnp.zeros(projected_ref.shape, F32)
+    for c in range(att_ref.shape[0]):
+        projected = projected + dot(att_ref[c].astype(BF16), w_ref[c], NN)
+    projected_ref[...] = projected.astype(BF16)
+
+
 def finish_kernel(
     pos_ref, ids_ref, b0, b1, b2, b3, b4, gown_ref, gquery_ref, total_ref,
     gqk_ref, gval_ref, gweight_ref,
@@ -204,6 +217,27 @@
         gweight_ref[:, c * 128:(c + 1) * 128] = piece.astype(F32)
 
 
+def pack_kernel(qk_ref, val_ref, gout_ref, joined_ref, chunks_ref, wide_ref):
+    length, width = qk_ref.shape
+    zs, xs, step, _ = chunks_ref.shape
+    joined_ref[:length] = qk_ref[...]
+    joined_ref[length:] = val_ref[...]
+    half = xs // 2
+    for x in range(xs):
+        ref = (qk_ref, val_ref)[x // half]
+        rows = ref[x % half * zs * step:(x % half + 1) * zs * step, :]
+        chunks_ref[:, x] = rows.reshape(zs, step, width)
+    wide_ref[...] = gout_ref[...].astype(F32)
+
+
+def pick_kernel(ids_ref, slices_ref, out_ref):
+    step = slices_ref.shape[1]
+    for g in range(NGLOB):
+        chosen = slices_ref[ids_ref[g]]
+        for z in range(out_ref.shape[0]):
+            out_ref[z, g * step:(g + 1) * step] = chosen
+
+
 def vmem(count):
     return [pl.BlockSpec(memory_space=pltpu.VMEM)] * count
 
@@ -219,39 +253,75 @@
     position = lax.axis_index(CTX)
     joined = jnp.concatenate([qk_vectors, token_values], axis=0)
 
+    zs, xs = lax.axis_size("z"), lax.axis_size("x")
     step = 2 * length // devices
-    slices = lax.all_to_all(joined.reshape(devices, step, width), CTX, 0, 0)
+    joined, chunks, wide = pl.pallas_call(
+        pack_kernel,
+        out_shape=(
+            jax.ShapeDtypeStruct((2 * length, width), BF16),
+            jax.ShapeDtypeStruct((zs, xs, step, width), BF16),
+            jax.ShapeDtypeStruct((length, width), F32),
+        ),
+        in_specs=vmem(3),
+        out_specs=tuple(vmem(3)),
+        name="pack",
+    )(qk_vectors, token_values, grad_output)
+
+    slices = lax.all_to_all(chunks.reshape(devices, step, width), CTX, 0, 0)
+    portion = lax.all_gather(wide, HEAD, axis=0)
+    weight_all = lax.all_gather(out_weight, HEAD, axis=0)
     routes = [[(i, i ^ 1) for i in range(devices)]]
     other = [i + 1 if i % 2 else i - 1 for i in range(devices)]
     routes.append([(i, j) for i, j in enumerate(other) if 0 <= j < devices])
     routes += [[(i, i ^ (1 << k)) for i in range(devices)] for k in range(1, ROUNDS)]
-    received = [lax.ppermute(joined, CTX, route) for route in routes]
-
-    slices, *received = lax.optimization_barrier((slices, *received))
-    picked = jnp.stack(
-        [lax.dynamic_index_in_dim(slices, global_ids[g], keepdims=False) for g in range(NGLOB)]
+    received = [None] * len(routes)
+    for n in (4, 3, 2, 1):
+        received[n] = lax.ppermute(joined, CTX, routes[n])
+    slices, *received[1:] = lax.optimization_barrier((slices, *received[1:]))
+    picked = pl.pallas_call(
+        pick_kernel,
+        out_shape=jax.ShapeDtypeStruct((zs, NGLOB * step, width), BF16),
+        in_specs=[smem()] + vmem(1),
+        out_specs=vmem(1)[0],
+        name="pick",
+    )(global_ids, slices)
+    picked, joined_late, portion = lax.optimization_barrier((picked, joined, portion))
+    column = lax.all_to_all(picked, "z", 0, 0)
+    received[0] = lax.ppermute(joined_late, CTX, routes[0])
+    portion_b, gatt = pl.pallas_call(
+        cotangent_kernel,
+        out_shape=(
+            jax.ShapeDtypeStruct((pieces, length, width), BF16),
+            jax.ShapeDtypeStruct((length, width), BF16),
+        ),
+        in_specs=vmem(2),
+        out_specs=tuple(vmem(2)),
+        compiler_params=pltpu.CompilerParams(vmem_limit_bytes=16 * 1024 * 1024),
+        cost_estimate=pl.CostEstimate(
+            flops=600_000_000, bytes_accessed=2_000_000, transcendentals=0
+        ),
+        name="cotangent",
+    )(portion, out_weight)
+    column, portion_b, gatt = lax.optimization_barrier((column, portion_b, gatt))
+    column = jnp.swapaxes(column.reshape(zs, NGLOB, step, width), 0, 1)
+    column = column.reshape(NGLOB, zs * step, width)
+    globals_all = lax.all_to_all(
+        jnp.broadcast_to(column[None], (xs,) + column.shape), "x", 0, 0
     )
-    spread = lax.all_to_all(
-        jnp.broadcast_to(picked[None], (devices, NGLOB, step, width)), CTX, 0, 0
-    )
-    globals_all = jnp.swapaxes(spread, 0, 1).reshape(NGLOB, 2 * length, width)
-    portion = lax.all_gather(grad_output, HEAD, axis=0)
-
     count = ROUNDS + 2 + NGLOB
     nheads = width // HD
     block = jax.ShapeDtypeStruct((2 * width, length), BF16)
     square = jax.ShapeDtypeStruct((length, width), F32)
-    partial, sums, stats, gatt, gglob = pl.pallas_call(
+    attended, sums, stats, gglob = pl.pallas_call(
         forward_kernel,
         out_shape=(
-            jax.ShapeDtypeStruct((pieces, length, 128), F32),
-            jax.ShapeDtypeStruct((lax.axis_size("z"), lax.axis_size("x"), 32, 128), BF16),
             square,
-            jax.ShapeDtypeStruct((length, width), BF16),
+            jax.ShapeDtypeStruct((zs, xs, 32, 128), BF16),
             square,
+            square,
         ),
         in_specs=[smem()] * 2 + vmem(9),
-        out_specs=tuple(vmem(5)),
+        out_specs=tuple(vmem(4)),
         scratch_shapes=[
             pltpu.VMEM((nheads, length, count * length), F32),
             pltpu.VMEM((length, width), F32),
@@ -261,10 +331,10 @@
             flops=3_000_000_000, bytes_accessed=4_000_000, transcendentals=1_100_000
         ),
         name="forward",
-    )(position[None], pair_active, joined, *received, globals_all, portion, out_weight)
+    )(position[None], pair_active, joined, *received, globals_all, portion_b, gatt)
 
     shares = lax.all_to_all(sums.reshape(devices, 32, 128), CTX, 0, 0)
-    projected = lax.psum_scatter(partial, HEAD, scatter_dimension=0, tiled=False).astype(BF16)
+    attended_all = lax.all_gather(attended, HEAD, axis=0)
     *terms, gquery, gown = pl.pallas_call(
         backward_kernel,
         out_shape=(
@@ -281,16 +351,26 @@
         name="backward",
     )(position[None], pair_active, joined, *received, stats, gatt, gglob)
     returned = [lax.ppermute(t, CTX, route) for t, route in zip(terms, routes)]
-
     shares, *returned = lax.optimization_barrier((shares, *returned))
     share = jnp.sum(shares.astype(F32), axis=0).astype(BF16)
-    column = lax.all_to_all(
-        jnp.broadcast_to(share[None], (lax.axis_size("z"),) + share.shape), "z", 0, 0
+    column = lax.all_to_all(jnp.broadcast_to(share[None], (zs,) + share.shape), "z", 0, 0)
+    weight_cols = lax.dynamic_slice_in_dim(
+        weight_all, lax.axis_index(HEAD) * width, width, axis=2
     )
     totals = lax.all_to_all(
-        jnp.broadcast_to(column[None], (lax.axis_size("x"),) + column.shape), "x", 0, 0
-    ).reshape(shares.shape)
-
+        jnp.broadcast_to(column[None], (xs,) + column.shape), "x", 0, 0
+    ).reshape(devices, 32, 128)
+
+    projected = pl.pallas_call(
+        project_kernel,
+        out_shape=jax.ShapeDtypeStruct((length, width), BF16),
+        in_specs=vmem(2),
+        out_specs=vmem(1)[0],
+        cost_estimate=pl.CostEstimate(
+            flops=70_000_000, bytes_accessed=1_500_000, transcendentals=0
+        ),
+        name="project",
+    )(attended_all, weight_cols)
     gqk, gval, gweight = pl.pallas_call(
         finish_kernel,
         out_shape=(

time: 180 us -> 172 us (0.956)
  blocking collectives: 37.8 us -> 22.5 us
  waiting for transfers between devices: 25.6 us -> 31.2 us
  Pallas kernels: 11.2 us -> 15.9 us
  between operations: 18.2 us -> 13.9 us
    all_gather x1 -> x0, blocking collectives: 13.1 us -> none  [local(): portion = lax.all_gather(grad_output, HEAD, axis=0)]
    ppermute x5, waiting for transfers between devices: 0.01 us -> 5.99 us  [the longest x4 3.02 us: local(): received[n] = lax.ppermute(joined, CTX, routes[n])]
    pallas_call x1 -> x5, Pallas kernels: 5.4 us -> 10.4 us  [the longest x1 4.67 us: local(): pl.pallas_call(forward_kernel, out_shape=(square, jax.ShapeDtypeStruct((z...]
    ppermute x5, waiting for transfers between devices: 10.3 us -> 5.4 us  [local(): returned = [lax.ppermute(t, CTX, route) for t, route in zip(terms, routes)]]
    all_to_all x3 -> x4, waiting for transfers between devices: 14.2 us -> 16.7 us  [the longest x1 10.3 us: local(): column = lax.all_to_all(picked, 'z', 0, 0)]
    all_to_all x1, blocking collectives: 24.7 us -> 22.5 us  [local(): lax.all_to_all(jnp.broadcast_to(share[None], (zs,) + share.shape), 'z', 0...]
    all_to_all x3 -> x4, starting transfers between devices: 37.4 us -> 39.5 us  [the longest x1 18.6 us: local(): slices = lax.all_to_all(chunks.reshape(devices, step, width), CTX, 0, 0)]
  transfers between devices with their start and end apart: 15 -> 18, of which waited for: 4 -> 8; matrix products, arithmetic and copies ran while one was open for 2% -> 2% of each run, Pallas kernels for 2% -> 7%
where the time goes in v4:
time: 172 us; the launch traced here: 171 us
  starting transfers between devices  81.1 us (47%)
  waiting for transfers between devices  31.2 us (18%)
  blocking collectives  22.5 us (13%)
  Pallas kernels  15.9 us (9%)
  between operations  13.9 us (8%)
  local copies, waits for them, and re-layouts  6.16 us (4%)
    all_to_all x1, blocking collectives, local(): lax.all_to_all(jnp.broadcast_to(share[None], (zs,) + share.shape), 'z', 0...  22.5 us
    all_to_all x1, starting transfers between devices, local(): slices = lax.all_to_all(chunks.reshape(devices, step, width), CTX, 0, 0)  18.6 us
    ppermute x5, starting transfers between devices, local(): returned = [lax.ppermute(t, CTX, route) for t, route in zip(terms, routes)]  17.6 us
    all_to_all x1, starting transfers between devices, local(): column = lax.all_to_all(picked, 'z', 0, 0)  13.6 us
    ppermute x4, starting transfers between devices, local(): received[n] = lax.ppermute(joined, CTX, routes[n])  13.3 us
    all_to_all x1, waiting for transfers between devices, local(): column = lax.all_to_all(picked, 'z', 0, 0)  10.3 us
    all_to_all x2, starting transfers between devices, local(): lax.all_to_all(jnp.broadcast_to(column[None], (xs,) + column.shape), 'x',...  7.35 us
    all_to_all x1, starting transfers between devices, local(): shares = lax.all_to_all(sums.reshape(devices, 32, 128), CTX, 0, 0)  6.75 us
  transfers between devices with their start and end apart: 18, of which 8 were waited for; matrix products, arithmetic and copies ran while one was open for 2% of the time, Pallas kernels for 7%

profile of v4, /device:TPU:24, one launch (start us, length us, event | category | flops | bytes accessed | tf_op | source)
XLA Modules:
  0.0 171.0 jit_solution(17128932710653464544)
XLA Ops:
  7.2 0.0 all-gather.7.cloned.1.call-start
  7.2 1.7 pack.1
  8.9 0.0 all-gather.7.cloned.1.call-update
  8.9 0.0 all-gather.11.cloned.1.call-start
  9.0 0.7 all-gather.11.cloned.1.call-update
  9.7 18.6 %all-to-all-start = ((bf16[64,8,128]{2,1,0:T(8,128)(2,1)}), bf16[64,8,128]{2,1,0:T(8,128)(2,1)S(1)}, u32[]{:S(2)}, u32[]{:S(2)}) async-start(bf16[64,8,128]{2,1,0:T(8,128)(2,1)} %bitcast.17), calls=%async_computation | async-start | bytes 262144 | tf_op jit(solution)/shard_map/all_to_all | solution.py:270
  28.2 4.4 %collective-permute-start.3 = (bf16[512,128]{1,0:T(8,128)(2,1)}, bf16[512,128]{1,0:T(8,128)(2,1)S(1)}, u32[]{:S(2)}, u32[]{:S(2)}) collective-permute-start(bf16[512,128]{1,0:T(8,128)(2,1)} %get-tuple-element.44.own_ref), channel_id=1, source_target_pairs={{0,64},{8,72},{16,80},{24,88},{32,96},{40,104},{48,112},{56,120},{... | collective-permute-start | bytes 393224 | tf_op jit(solution)/shard_map/ppermute | solution.py:279
  32.6 3.4 %collective-permute-start.2 = (bf16[512,128]{1,0:T(8,128)(2,1)}, bf16[512,128]{1,0:T(8,128)(2,1)S(1)}, u32[]{:S(2)}, u32[]{:S(2)}) collective-permute-start(bf16[512,128]{1,0:T(8,128)(2,1)} %get-tuple-element.44.own_ref), channel_id=1, source_target_pairs={{0,32},{8,40},{16,48},{24,56},{32,0},{40,8},{48,16},{56,24},{64,96... | collective-permute-start | bytes 393224 | tf_op jit(solution)/shard_map/ppermute | solution.py:279
  36.0 4.9 %collective-permute-start.1 = (bf16[512,128]{1,0:T(8,128)(2,1)}, bf16[512,128]{1,0:T(8,128)(2,1)S(1)}, u32[]{:S(2)}, u32[]{:S(2)}) collective-permute-start(bf16[512,128]{1,0:T(8,128)(2,1)} %get-tuple-element.44.own_ref), channel_id=1, source_target_pairs={{0,16},{8,24},{16,0},{24,8},{32,48},{40,56},{48,32},{56,40},{64,80... | collective-permute-start | bytes 393224 | tf_op jit(solution)/shard_map/ppermute | solution.py:279
  40.9 0.7 collective-permute-start
  41.6 0.8 collective-permute-done.3.p4
  42.4 0.0 collective-permute-done.2.p3
  42.4 2.2 %collective-permute-done.1.p2 = bf16[512,128]{1,0:T(8,128)(2,1)S(1)} collective-permute-done((bf16[512,128]{1,0:T(8,128)(2,1)}, bf16[512,128]{1,0:T(8,128)(2,1)S(1)}, u32[]{:S(2)}, u32[]{:S(2)}) %collective-permute-start.1) | collective-permute-done | bytes 131104 | tf_op jit(solution)/shard_map/ppermute | solution.py:279
  44.6 2.2 %all-to-all-done.slices_ref = bf16[64,8,128]{2,1,0:T(8,128)(2,1)S(1)} async-done(((bf16[64,8,128]{2,1,0:T(8,128)(2,1)}), bf16[64,8,128]{2,1,0:T(8,128)(2,1)S(1)}, u32[]{:S(2)}, u32[]{:S(2)}) %all-to-all-start) | async-done | bytes 131104 | tf_op jit(solution)/shard_map/all_to_all | solution.py:270
  46.8 0.7 copy-done.5
  47.4 1.6 pick.1
  49.0 13.6 %all-to-all-start.1 = ((bf16[16,16,128]{2,1,0:T(8,128)(2,1)}), bf16[16,16,128]{2,1,0:T(8,128)(2,1)S(1)}, u32[]{:S(2)}, u32[]{:S(2)}) async-start(bf16[16,16,128]{2,1,0:T(8,128)(2,1)} %pick.1), calls=%async_computation.1 | async-start | bytes 131072 | tf_op jit(solution)/shard_map/all_to_all | solution.py:289
  62.6 0.0 copy-start
  62.6 0.9 copy-done
  63.5 1.3 copy-done.2
  64.8 0.3 cotangent.1
  65.1 10.3 %all-to-all-done.1 = bf16[16,16,128]{2,1,0:T(8,128)(2,1)S(1)} async-done(((bf16[16,16,128]{2,1,0:T(8,128)(2,1)}), bf16[16,16,128]{2,1,0:T(8,128)(2,1)S(1)}, u32[]{:S(2)}, u32[]{:S(2)}) %all-to-all-start.1) | async-done | bytes 65568 | tf_op jit(solution)/shard_map/all_to_all | solution.py:289
  75.4 0.7 broadcast_in_dim.12
  76.1 3.4 %all-to-all-start.2 = ((bf16[4,2,128,128]{3,2,1,0:T(8,128)(2,1)}), bf16[4,2,128,128]{3,2,1,0:T(8,128)(2,1)S(1)}, u32[]{:S(2)}, u32[]{:S(2)}) async-start(bf16[4,2,128,128]{3,2,1,0:T(8,128)(2,1)} %broadcast_in_dim.12), calls=%async_computation.2 | async-start | bytes 524288 | tf_op jit(solution)/shard_map/all_to_all | solution.py:308
  79.5 3.9 %collective-permute-start.4 = (bf16[512,128]{1,0:T(8,128)(2,1)S(1)}, bf16[512,128]{1,0:T(8,128)(2,1)S(1)}, u32[]{:S(2)}, u32[]{:S(2)}) collective-permute-start(bf16[512,128]{1,0:T(8,128)(2,1)S(1)} %copy-done.3), channel_id=1, source_target_pairs={{0,8},{8,0},{16,24},{24,16},{32,40},{40,32},{48,56},{56,48},{64,72... | collective-permute-start | bytes 393224 | tf_op jit(solution)/shard_map/ppermute | solution.py:290
  83.4 3.0 %collective-permute-done.4.p0 = bf16[512,128]{1,0:T(8,128)(2,1)S(1)} collective-permute-done((bf16[512,128]{1,0:T(8,128)(2,1)S(1)}, bf16[512,128]{1,0:T(8,128)(2,1)S(1)}, u32[]{:S(2)}, u32[]{:S(2)}) %collective-permute-start.4) | collective-permute-done | bytes 131104 | tf_op jit(solution)/shard_map/ppermute | solution.py:290
  86.4 0.0 all-to-all-done.2.glob_ref
  86.4 4.7 %forward.1 = (f32[256,128]{1,0:T(8,128)}, bf16[16,4,32,128]{3,2,1,0:T(8,128)(2,1)}, f32[256,128]{1,0:T(8,128)S(1)}, f32[256,128]{1,0:T(8,128)S(1)}) custom-call(s32[1]{0:T(128)} %bitcast.pos_ref, s32[4,32]{1,0:T(4,128)S(1)} %copy-done.4, bf16[512,128]{1,0:T(8,128)(2,1)S(1)} %copy-done.3, bf16[512,128]{1,0:T(8,128)(2,1)S(1)} %collective-permute-done.4.p0, ...), custom_call_target="tpu_custom_call" | custom-call | flops 3000000000 | bytes 4000000 | tf_op jit(solution)/shard_map/forward/pallas_call | solution.py:315
  91.1 6.7 %all-to-all-start.3 = ((bf16[64,32,128]{2,1,0:T(8,128)(2,1)}), bf16[64,32,128]{2,1,0:T(8,128)(2,1)S(1)}, u32[]{:S(2)}, u32[]{:S(2)}) async-start(bf16[64,32,128]{2,1,0:T(8,128)(2,1)} %bitcast.8), calls=%async_computation.3 | async-start | bytes 1048576 | tf_op jit(solution)/shard_map/all_to_all | solution.py:336
  97.8 0.0 all-gather.9.cloned.1.call-start
  97.9 0.7 all-gather.9.cloned.1.call-update
  98.6 3.9 %backward.1 = (bf16[256,256]{1,0:T(8,128)(2,1)S(1)}, bf16[256,256]{1,0:T(8,128)(2,1)S(1)}, bf16[256,256]{1,0:T(8,128)(2,1)S(1)}, bf16[256,256]{1,0:T(8,128)(2,1)...) custom-call(s32[1]{0:T(128)} %bitcast.pos_ref, s32[4,32]{1,0:T(4,128)S(1)} %copy-done.4, ...), custom_call_target="tpu_custom_call" | custom-call | flops 3000000000 | bytes 4000000 | tf_op jit(solution)/shard_map/backward/pallas_call | solution.py:338
  102.5 3.5 %collective-permute-start.5 = (bf16[256,256]{1,0:T(8,128)(2,1)S(1)}, bf16[256,256]{1,0:T(8,128)(2,1)S(1)}, u32[]{:S(2)}, u32[]{:S(2)}) collective-permute-start(bf16[256,256]{1,0:T(8,128)(2,1)S(1)} %get-tuple-element.60), channel_id=1, source_target_pairs={{0,8},{8,0},{16,24},{24,16},{32,40},{40,32},{48,56},{56,48},{64,72... | collective-permute-start | bytes 393224 | tf_op jit(solution)/shard_map/ppermute | solution.py:353
  106.0 0.7 collective-permute-start.6
  106.6 5.8 %collective-permute-start.7 = (bf16[256,256]{1,0:T(8,128)(2,1)S(1)}, bf16[256,256]{1,0:T(8,128)(2,1)S(1)}, u32[]{:S(2)}, u32[]{:S(2)}) collective-permute-start(bf16[256,256]{1,0:T(8,128)(2,1)S(1)} %get-tuple-element.62), channel_id=1, source_target_pairs={{0,16},{8,24},{16,0},{24,8},{32,48},{40,56},{48,32},{56,40},{64,80... | collective-permute-start | bytes 393224 | tf_op jit(solution)/shard_map/ppermute | solution.py:353
  112.5 3.4 %collective-permute-start.8 = (bf16[256,256]{1,0:T(8,128)(2,1)S(1)}, bf16[256,256]{1,0:T(8,128)(2,1)S(1)}, u32[]{:S(2)}, u32[]{:S(2)}) collective-permute-start(bf16[256,256]{1,0:T(8,128)(2,1)S(1)} %get-tuple-element.63), channel_id=1, source_target_pairs={{0,32},{8,40},{16,48},{24,56},{32,0},{40,8},{48,16},{56,24},{64,96... | collective-permute-start | bytes 393224 | tf_op jit(solution)/shard_map/ppermute | solution.py:353
  115.9 4.3 %collective-permute-start.9 = (bf16[256,256]{1,0:T(8,128)(2,1)S(1)}, bf16[256,256]{1,0:T(8,128)(2,1)S(1)}, u32[]{:S(2)}, u32[]{:S(2)}) collective-permute-start(bf16[256,256]{1,0:T(8,128)(2,1)S(1)} %get-tuple-element.64), channel_id=1, source_target_pairs={{0,64},{8,72},{16,80},{24,88},{32,96},{40,104},{48,112},{56,120},{... | collective-permute-start | bytes 393224 | tf_op jit(solution)/shard_map/ppermute | solution.py:353
  120.2 0.0 collective-permute-done.7.b2
  120.2 5.4 %collective-permute-done.8.b3 = bf16[256,256]{1,0:T(8,128)(2,1)S(1)} collective-permute-done((bf16[256,256]{1,0:T(8,128)(2,1)S(1)}, bf16[256,256]{1,0:T(8,128)(2,1)S(1)}, u32[]{:S(2)}, u32[]{:S(2)}) %collective-permute-start.8) | collective-permute-done | bytes 131104 | tf_op jit(solution)/shard_map/ppermute | solution.py:353
  125.6 1.7 %all-to-all-done.3 = bf16[64,32,128]{2,1,0:T(8,128)(2,1)S(1)} async-done(((bf16[64,32,128]{2,1,0:T(8,128)(2,1)}), bf16[64,32,128]{2,1,0:T(8,128)(2,1)S(1)}, u32[]{:S(2)}, u32[]{:S(2)}) %all-to-all-start.3) | async-done | bytes 524320 | tf_op jit(solution)/shard_map/all_to_all | solution.py:336
  127.3 0.1 reduce_sum.12
  127.4 22.5 %all_to_all.30 = bf16[16,32,128]{2,1,0:T(8,128)(2,1)S(1)} all-to-all(bf16[16,32,128]{2,1,0:T(8,128)(2,1)S(1)} %broadcast_in_dim.13), channel_id=1, replica_groups=mesh['z'=16,'x'=4,'y'=4,'core'=2] {'z'}, dimensions={0} | all-to-all | bytes 262144 | tf_op jit(solution)/shard_map/all_to_all | solution.py:356
  149.9 0.9 broadcast_in_dim.28
  150.8 3.9 %all-to-all-start.5 = ((bf16[4,16,32,128]{3,2,1,0:T(8,128)(2,1)}), bf16[4,16,32,128]{3,2,1,0:T(8,128)(2,1)S(1)}, u32[]{:S(2)}, u32[]{:S(2)}) async-start(bf16[4,16,32,128]{3,2,1,0:T(8,128)(2,1)} %broadcast_in_dim.28), calls=%async_computation.5 | async-start | bytes 1048576 | tf_op jit(solution)/shard_map/all_to_all | solution.py:360
  154.8 1.7 constant_dynamic-slice_fusion.w_ref
  156.4 2.2 %project.1 = bf16[256,128]{1,0:T(8,128)(2,1)} custom-call(f32[8,256,128]{2,1,0:T(8,128)} %bitcast.16, bf16[8,128,128]{2,1,0:T(8,128)(2,1)} %constant_dynamic-slice_fusion.w_ref), custom_call_target="tpu_custom_call" | custom-call | flops 70000000 | bytes 1500000 | tf_op jit(solution)/shard_map/project/pallas_call | solution.py:364
  158.6 4.2 %all-to-all-done.5 = bf16[4,16,32,128]{3,2,1,0:T(8,128)(2,1)S(1)} async-done(((bf16[4,16,32,128]{3,2,1,0:T(8,128)(2,1)}), bf16[4,16,32,128]{3,2,1,0:T(8,128)(2,1)S(1)}, u32[]{:S(2)}, u32[]{:S(2)}) %all-to-all-start.5) | async-done | bytes 524320 | tf_op jit(solution)/shard_map/all_to_all | solution.py:360
  162.9 1.6 finish.1
  (17 shorter events, 0.1 us)
Async XLA Ops:
  7.2 41.8 %all-gather.7.cloned.1.call-start = ((), (), s32[]{:S(2)}) async-start(), calls=%async_computation.6 | async-start | bytes 1179648 | tf_op jit(solution)/shard_map/all_gather | solution.py:271
  8.9 70.7 %copy-start.3 = (bf16[512,128]{1,0:T(8,128)(2,1)S(1)}, bf16[512,128]{1,0:T(8,128)(2,1)}, u32[]{:S(2)}) copy-start(bf16[512,128]{1,0:T(8,128)(2,1)} %get-tuple-element.44.own_ref) | copy-start | bytes 393220
  8.9 77.5 %copy-start.4 = (s32[4,32]{1,0:T(4,128)S(1)}, s32[4,32]{1,0:T(4,128)}, u32[]{:S(2)}) copy-start(s32[4,32]{1,0:T(4,128)} %pair_ref.3) | copy-start | bytes 1540
  8.9 145.9 %all-gather.11.cloned.1.call-start = ((), (), s32[]{:S(2)}) async-start(), calls=%async_computation.8 | async-start | bytes 2359296 | tf_op jit(solution)/shard_map/all_gather | solution.py:272
  9.7 37.1 %all-to-all-start = ((bf16[64,8,128]{2,1,0:T(8,128)(2,1)}), bf16[64,8,128]{2,1,0:T(8,128)(2,1)S(1)}, u32[]{:S(2)}, u32[]{:S(2)}) async-start(bf16[64,8,128]{2,1,0:T(8,128)(2,1)} %bitcast.17), calls=%async_computation | async-start | bytes 262144 | tf_op jit(solution)/shard_map/all_to_all | solution.py:270
  28.2 14.2 %collective-permute-start.3 = (bf16[512,128]{1,0:T(8,128)(2,1)}, bf16[512,128]{1,0:T(8,128)(2,1)S(1)}, u32[]{:S(2)}, u32[]{:S(2)}) collective-permute-start(bf16[512,128]{1,0:T(8,128)(2,1)} %get-tuple-element.44.own_ref), channel_id=1, source_target_pairs={{0,64},{8,72},{16,80},{24,88},{32,96},{40,104},{48,112},{56,120},{... | collective-permute-start | bytes 393224 | tf_op jit(solution)/shard_map/ppermute | solution.py:279
  32.6 9.8 %collective-permute-start.2 = (bf16[512,128]{1,0:T(8,128)(2,1)}, bf16[512,128]{1,0:T(8,128)(2,1)S(1)}, u32[]{:S(2)}, u32[]{:S(2)}) collective-permute-start(bf16[512,128]{1,0:T(8,128)(2,1)} %get-tuple-element.44.own_ref), channel_id=1, source_target_pairs={{0,32},{8,40},{16,48},{24,56},{32,0},{40,8},{48,16},{56,24},{64,96... | collective-permute-start | bytes 393224 | tf_op jit(solution)/shard_map/ppermute | solution.py:279
  36.0 8.6 %collective-permute-start.1 = (bf16[512,128]{1,0:T(8,128)(2,1)}, bf16[512,128]{1,0:T(8,128)(2,1)S(1)}, u32[]{:S(2)}, u32[]{:S(2)}) collective-permute-start(bf16[512,128]{1,0:T(8,128)(2,1)} %get-tuple-element.44.own_ref), channel_id=1, source_target_pairs={{0,16},{8,24},{16,0},{24,8},{32,48},{40,56},{48,32},{56,40},{64,80... | collective-permute-start | bytes 393224 | tf_op jit(solution)/shard_map/ppermute | solution.py:279
  40.9 3.7 %collective-permute-start = (bf16[512,128]{1,0:T(8,128)(2,1)}, bf16[512,128]{1,0:T(8,128)(2,1)S(1)}, u32[]{:S(2)}, u32[]{:S(2)}) collective-permute-start(bf16[512,128]{1,0:T(8,128)(2,1)} %get-tuple-element.44.own_ref), channel_id=1, source_target_pairs={{8,16},{16,8},{24,32},{32,24},{40,48},{48,40},{56,64},{64,56},{72,... | collective-permute-start | bytes 393224 | tf_op jit(solution)/shard_map/ppermute | solution.py:279
  46.8 0.7 copy-start.5
  49.0 26.4 %all-to-all-start.1 = ((bf16[16,16,128]{2,1,0:T(8,128)(2,1)}), bf16[16,16,128]{2,1,0:T(8,128)(2,1)S(1)}, u32[]{:S(2)}, u32[]{:S(2)}) async-start(bf16[16,16,128]{2,1,0:T(8,128)(2,1)} %pick.1), calls=%async_computation.1 | async-start | bytes 131072 | tf_op jit(solution)/shard_map/all_to_all | solution.py:289
  62.6 1.0 copy-start
  63.5 1.3 copy-start.2
  76.1 10.3 %all-to-all-start.2 = ((bf16[4,2,128,128]{3,2,1,0:T(8,128)(2,1)}), bf16[4,2,128,128]{3,2,1,0:T(8,128)(2,1)S(1)}, u32[]{:S(2)}, u32[]{:S(2)}) async-start(bf16[4,2,128,128]{3,2,1,0:T(8,128)(2,1)} %broadcast_in_dim.12), calls=%async_computation.2 | async-start | bytes 524288 | tf_op jit(solution)/shard_map/all_to_all | solution.py:308
  79.5 6.9 %collective-permute-start.4 = (bf16[512,128]{1,0:T(8,128)(2,1)S(1)}, bf16[512,128]{1,0:T(8,128)(2,1)S(1)}, u32[]{:S(2)}, u32[]{:S(2)}) collective-permute-start(bf16[512,128]{1,0:T(8,128)(2,1)S(1)} %copy-done.3), channel_id=1, source_target_pairs={{0,8},{8,0},{16,24},{24,16},{32,40},{40,32},{48,56},{56,48},{64,72... | collective-permute-start | bytes 393224 | tf_op jit(solution)/shard_map/ppermute | solution.py:290
  91.1 36.2 %all-to-all-start.3 = ((bf16[64,32,128]{2,1,0:T(8,128)(2,1)}), bf16[64,32,128]{2,1,0:T(8,128)(2,1)S(1)}, u32[]{:S(2)}, u32[]{:S(2)}) async-start(bf16[64,32,128]{2,1,0:T(8,128)(2,1)} %bitcast.8), calls=%async_computation.3 | async-start | bytes 1048576 | tf_op jit(solution)/shard_map/all_to_all | solution.py:336
  97.8 58.6 %all-gather.9.cloned.1.call-start = ((), (), s32[]{:S(2)}) async-start(), calls=%async_computation.7 | async-start | bytes 1179648 | tf_op jit(solution)/shard_map/all_gather | solution.py:337
  102.5 17.7 %collective-permute-start.5 = (bf16[256,256]{1,0:T(8,128)(2,1)S(1)}, bf16[256,256]{1,0:T(8,128)(2,1)S(1)}, u32[]{:S(2)}, u32[]{:S(2)}) collective-permute-start(bf16[256,256]{1,0:T(8,128)(2,1)S(1)} %get-tuple-element.60), channel_id=1, source_target_pairs={{0,8},{8,0},{16,24},{24,16},{32,40},{40,32},{48,56},{56,48},{64,72... | collective-permute-start | bytes 393224 | tf_op jit(solution)/shard_map/ppermute | solution.py:353
  106.0 14.2 %collective-permute-start.6 = (bf16[256,256]{1,0:T(8,128)(2,1)S(1)}, bf16[256,256]{1,0:T(8,128)(2,1)S(1)}, u32[]{:S(2)}, u32[]{:S(2)}) collective-permute-start(bf16[256,256]{1,0:T(8,128)(2,1)S(1)} %get-tuple-element.61), channel_id=1, source_target_pairs={{8,16},{16,8},{24,32},{32,24},{40,48},{48,40},{56,64},{64,56},{72,... | collective-permute-start | bytes 393224 | tf_op jit(solution)/shard_map/ppermute | solution.py:353
  106.6 13.5 %collective-permute-start.7 = (bf16[256,256]{1,0:T(8,128)(2,1)S(1)}, bf16[256,256]{1,0:T(8,128)(2,1)S(1)}, u32[]{:S(2)}, u32[]{:S(2)}) collective-permute-start(bf16[256,256]{1,0:T(8,128)(2,1)S(1)} %get-tuple-element.62), channel_id=1, source_target_pairs={{0,16},{8,24},{16,0},{24,8},{32,48},{40,56},{48,32},{56,40},{64,80... | collective-permute-start | bytes 393224 | tf_op jit(solution)/shard_map/ppermute | solution.py:353
  112.5 13.1 %collective-permute-start.8 = (bf16[256,256]{1,0:T(8,128)(2,1)S(1)}, bf16[256,256]{1,0:T(8,128)(2,1)S(1)}, u32[]{:S(2)}, u32[]{:S(2)}) collective-permute-start(bf16[256,256]{1,0:T(8,128)(2,1)S(1)} %get-tuple-element.63), channel_id=1, source_target_pairs={{0,32},{8,40},{16,48},{24,56},{32,0},{40,8},{48,16},{56,24},{64,96... | collective-permute-start | bytes 393224 | tf_op jit(solution)/shard_map/ppermute | solution.py:353
  115.9 9.7 %collective-permute-start.9 = (bf16[256,256]{1,0:T(8,128)(2,1)S(1)}, bf16[256,256]{1,0:T(8,128)(2,1)S(1)}, u32[]{:S(2)}, u32[]{:S(2)}) collective-permute-start(bf16[256,256]{1,0:T(8,128)(2,1)S(1)} %get-tuple-element.64), channel_id=1, source_target_pairs={{0,64},{8,72},{16,80},{24,88},{32,96},{40,104},{48,112},{56,120},{... | collective-permute-start | bytes 393224 | tf_op jit(solution)/shard_map/ppermute | solution.py:353
  127.4 35.5 %copy-start.1 = (s32[2]{0:T(128)S(1)}, s32[2]{0:T(128)}, u32[]{:S(2)}) copy-start(s32[2]{0:T(128)} %ids_ref.3) | copy-start | bytes 28
  150.8 12.0 %all-to-all-start.5 = ((bf16[4,16,32,128]{3,2,1,0:T(8,128)(2,1)}), bf16[4,16,32,128]{3,2,1,0:T(8,128)(2,1)S(1)}, u32[]{:S(2)}, u32[]{:S(2)}) async-start(bf16[4,16,32,128]{3,2,1,0:T(8,128)(2,1)} %broadcast_in_dim.28), calls=%async_computation.5 | async-start | bytes 1048576 | tf_op jit(solution)/shard_map/all_to_all | solution.py:360
Sparse Core Ops, SparseCore 0:
  10.2 33.9 all-gather.6
  46.3 32.7 all-gather.10
  100.8 30.4 all-gather.8

commit v5 on v4

--- a/solution.py
+++ b/solution.py
@@ -11,8 +11,9 @@
 HD = 64
 NGLOB = 2
 ROUNDS = 4
-CTX = ("z", "x")
-HEAD = ("y", "core")
+CTX = ("hi", "lo")
+HEAD = "head"
+PATCH = 16
 NT = (((1,), (1,)), ((), ()))
 TN = (((0,), (0,)), ((), ()))
 NN = (((1,), (0,)), ((), ()))
@@ -41,13 +42,15 @@
     return bias + [zero] * NGLOB
 
 
-def cotangent_kernel(gout_ref, w_ref, out_ref, gatt_ref):
-    pieces, length, width = gout_ref.shape
+def cotangent_kernel(head_ref, all_ref, w_ref, out_ref, gatt_ref, cols_ref):
+    pieces, length, width = out_ref.shape
+    blocks = length // 128
     gatt = jnp.zeros((length, width), F32)
     for c in range(pieces):
-        part = gout_ref[c].astype(BF16)
+        part = all_ref[c, 0:blocks].reshape(length, width)
         out_ref[c] = part
         gatt = gatt + dot(part, w_ref[:, c * width:(c + 1) * width], NT)
+        cols_ref[c] = all_ref[c, blocks + head_ref[0]]
     gatt_ref[...] = gatt.astype(BF16)
 
 
@@ -67,8 +70,8 @@
     vals = [r[length:] for r in (own_ref, p0, p1, p2, p3, p4)]
     half = glob_ref.shape[0] // 2
     for g in range(NGLOB):
-        keys.append(jnp.concatenate([glob_ref[x, g] for x in range(half)], axis=0))
-        vals.append(jnp.concatenate([glob_ref[half + x, g] for x in range(half)], axis=0))
+        keys.append(jnp.concatenate([glob_ref[p, g] for p in range(half)], axis=0))
+        vals.append(jnp.concatenate([glob_ref[half + p, g] for p in range(half)], axis=0))
     count = len(keys)
     query = own_ref[:length]
     lane = lax.broadcasted_iota(jnp.int32, (1, width), 1)
@@ -106,9 +109,8 @@
     attended_b = attended.astype(BF16)
     for c in range(pieces):
         part = dot(attended_b, gout_ref[c], TN).astype(BF16)
-        n = width // 16
-        at = c * n % sums_ref.shape[0]
-        sums_ref[at:at + n, c * n // sums_ref.shape[0], 0:16, :] = part.reshape(n, 16, 128)
+        n = width // HD
+        sums_ref[c * n:(c + 1) * n, 0:HD, :] = part.reshape(n, HD, 128)
 
     product = gatt_b.astype(F32) * attended
     query_t = query.astype(F32).T.astype(BF16)
@@ -129,12 +131,11 @@
             acc = acc + dot(gs, keys[b], NN)
             gk = dot(qt, gs, NN) * scaling
             gv = dot(gt, weights.astype(BF16), NN)
-            n = HD // 16
             for a in range(length // 128):
-                x = g * (length // 128) + a
-                for at, term in ((h * n, gk), (width // 16 + h * n, gv)):
-                    sub = term[:, a * 128:(a + 1) * 128].astype(BF16)
-                    sums_ref[at:at + n, x, 16:32, :] = sub.reshape(n, 16, 128)
+                at = (g * (length // 128) + a) * 2 * nheads + h
+                cols = slice(a * 128, (a + 1) * 128)
+                sums_ref[at, HD:2 * HD, :] = gk[:, cols].astype(BF16)
+                sums_ref[at + nheads, HD:2 * HD, :] = gv[:, cols].astype(BF16)
         if h == 0:
             out_ref[...] = acc
         else:
@@ -198,7 +199,7 @@
 ):
     length, width = gquery_ref.shape
     halves = length // 128
-    rows = width * 2 // 16
+    rows = width * 2 // HD
     for a in range(halves):
         cols = slice(a * 128, (a + 1) * 128)
         acc = gown_ref[:, cols]
@@ -206,36 +207,39 @@
             acc = acc + b[:, cols].astype(F32)
         for g in range(NGLOB):
             at = (g * halves + a) * rows
-            term = total_ref[at:at + rows, 16:32, :].reshape(2 * width, 128).astype(F32)
+            term = total_ref[at:at + rows, HD:2 * HD, :].reshape(2 * width, 128).astype(F32)
             acc = acc + jnp.where(ids_ref[g] == pos_ref[0], term, 0.0)
         tokens = slice(a * 128, (a + 1) * 128)
         gqk_ref[tokens, :] = (gquery_ref[tokens, :] + acc[:width].T).astype(BF16)
         gval_ref[tokens, :] = acc[width:].T.astype(BF16)
-    n = width // 16
+    n = width // HD
     for c in range(gweight_ref.shape[1] // 128):
-        piece = total_ref[c * n:(c + 1) * n, 0:16, :].reshape(width, 128)
+        piece = total_ref[c * n:(c + 1) * n, 0:HD, :].reshape(width, 128)
         gweight_ref[:, c * 128:(c + 1) * 128] = piece.astype(F32)
 
 
-def pack_kernel(qk_ref, val_ref, gout_ref, joined_ref, chunks_ref, wide_ref):
+def pack_kernel(qk_ref, val_ref, gout_ref, w_ref, joined_ref, share_ref):
     length, width = qk_ref.shape
-    zs, xs, step, _ = chunks_ref.shape
+    blocks = length // 128
     joined_ref[:length] = qk_ref[...]
     joined_ref[length:] = val_ref[...]
-    half = xs // 2
-    for x in range(xs):
-        ref = (qk_ref, val_ref)[x // half]
-        rows = ref[x % half * zs * step:(x % half + 1) * zs * step, :]
-        chunks_ref[:, x] = rows.reshape(zs, step, width)
-    wide_ref[...] = gout_ref[...].astype(F32)
+    share_ref[0:blocks] = gout_ref[...].reshape(blocks, 128, width)
+    for c in range(w_ref.shape[1] // 128):
+        share_ref[blocks + c] = w_ref[:, c * 128:(c + 1) * 128]
 
 
 def pick_kernel(ids_ref, slices_ref, out_ref):
-    step = slices_ref.shape[1]
     for g in range(NGLOB):
-        chosen = slices_ref[ids_ref[g]]
-        for z in range(out_ref.shape[0]):
-            out_ref[z, g * step:(g + 1) * step] = chosen
+        chosen = slices_ref[lax.rem(ids_ref[g], PATCH)]
+        for n in range(out_ref.shape[0]):
+            out_ref[n, g] = chosen
+
+
+def spread_kernel(ids_ref, slices_ref, out_ref):
+    for g in range(NGLOB):
+        chosen = slices_ref[lax.div(ids_ref[g], PATCH), g]
+        for n in range(out_ref.shape[0]):
+            out_ref[n, g] = chosen
 
 
 def vmem(count):
@@ -253,61 +257,67 @@
     position = lax.axis_index(CTX)
     joined = jnp.concatenate([qk_vectors, token_values], axis=0)
 
-    zs, xs = lax.axis_size("z"), lax.axis_size("x")
-    step = 2 * length // devices
-    joined, chunks, wide = pl.pallas_call(
+    his, los = lax.axis_size("hi"), lax.axis_size("lo")
+    step = 2 * length // los
+    joined, share = pl.pallas_call(
         pack_kernel,
         out_shape=(
             jax.ShapeDtypeStruct((2 * length, width), BF16),
-            jax.ShapeDtypeStruct((zs, xs, step, width), BF16),
-            jax.ShapeDtypeStruct((length, width), F32),
-        ),
-        in_specs=vmem(3),
-        out_specs=tuple(vmem(3)),
+            jax.ShapeDtypeStruct((length // 128 + pieces, 128, width), BF16),
+        ),
+        in_specs=vmem(4),
+        out_specs=tuple(vmem(2)),
         name="pack",
-    )(qk_vectors, token_values, grad_output)
-
-    slices = lax.all_to_all(chunks.reshape(devices, step, width), CTX, 0, 0)
-    portion = lax.all_gather(wide, HEAD, axis=0)
-    weight_all = lax.all_gather(out_weight, HEAD, axis=0)
+    )(qk_vectors, token_values, grad_output, out_weight)
+
+    slices = lax.all_to_all(joined.reshape(los, step, width), "lo", 0, 0)
+    portion = lax.all_gather(share, HEAD, axis=0)
     routes = [[(i, i ^ 1) for i in range(devices)]]
     other = [i + 1 if i % 2 else i - 1 for i in range(devices)]
     routes.append([(i, j) for i, j in enumerate(other) if 0 <= j < devices])
     routes += [[(i, i ^ (1 << k)) for i in range(devices)] for k in range(1, ROUNDS)]
     received = [None] * len(routes)
-    for n in (4, 3, 2, 1):
+    for n in (0, 2):
         received[n] = lax.ppermute(joined, CTX, routes[n])
-    slices, *received[1:] = lax.optimization_barrier((slices, *received[1:]))
+    slices, received[0], received[2] = lax.optimization_barrier((slices, received[0], received[2]))
     picked = pl.pallas_call(
         pick_kernel,
-        out_shape=jax.ShapeDtypeStruct((zs, NGLOB * step, width), BF16),
+        out_shape=jax.ShapeDtypeStruct((his, NGLOB, step, width), BF16),
         in_specs=[smem()] + vmem(1),
         out_specs=vmem(1)[0],
         name="pick",
     )(global_ids, slices)
-    picked, joined_late, portion = lax.optimization_barrier((picked, joined, portion))
-    column = lax.all_to_all(picked, "z", 0, 0)
-    received[0] = lax.ppermute(joined_late, CTX, routes[0])
-    portion_b, gatt = pl.pallas_call(
+    picked, joined_late = lax.optimization_barrier((picked, joined))
+    column = lax.all_to_all(picked, "hi", 0, 0)
+    for n in (4, 3):
+        received[n] = lax.ppermute(joined_late, CTX, routes[n])
+    column, received[3], received[4] = lax.optimization_barrier((column, received[3], received[4]))
+    chosen = pl.pallas_call(
+        spread_kernel,
+        out_shape=jax.ShapeDtypeStruct((los, NGLOB, step, width), BF16),
+        in_specs=[smem()] + vmem(1),
+        out_specs=vmem(1)[0],
+        name="spread",
+    )(global_ids, column)
+    chosen, joined_late, portion = lax.optimization_barrier((chosen, joined, portion))
+    globals_all = lax.all_to_all(chosen, "lo", 0, 0)
+    received[1] = lax.ppermute(joined_late, CTX, routes[1])
+    portion_b, gatt, weight_cols = pl.pallas_call(
         cotangent_kernel,
         out_shape=(
             jax.ShapeDtypeStruct((pieces, length, width), BF16),
             jax.ShapeDtypeStruct((length, width), BF16),
-        ),
-        in_specs=vmem(2),
-        out_specs=tuple(vmem(2)),
+            jax.ShapeDtypeStruct((pieces, width, 128), BF16),
+        ),
+        in_specs=[smem()] + vmem(2),
+        out_specs=tuple(vmem(3)),
         compiler_params=pltpu.CompilerParams(vmem_limit_bytes=16 * 1024 * 1024),
         cost_estimate=pl.CostEstimate(
-            flops=600_000_000, bytes_accessed=2_000_000, transcendentals=0
+            flops=600_000_000, bytes_accessed=4_000_000, transcendentals=0
         ),
         name="cotangent",
-    )(portion, out_weight)
-    column, portion_b, gatt = lax.optimization_barrier((column, portion_b, gatt))
-    column = jnp.swapaxes(column.reshape(zs, NGLOB, step, width), 0, 1)
-    column = column.reshape(NGLOB, zs * step, width)
-    globals_all = lax.all_to_all(
-        jnp.broadcast_to(column[None], (xs,) + column.shape), "x", 0, 0
-    )
+    )(lax.axis_index(HEAD)[None], portion, out_weight)
+
     count = ROUNDS + 2 + NGLOB
     nheads = width // HD
     block = jax.ShapeDtypeStruct((2 * width, length), BF16)
@@ -316,7 +326,7 @@
         forward_kernel,
         out_shape=(
             square,
-            jax.ShapeDtypeStruct((zs, xs, 32, 128), BF16),
+            jax.ShapeDtypeStruct((los, 2 * HD, 128), BF16),
             square,
             square,
         ),
@@ -333,7 +343,7 @@
         name="forward",
     )(position[None], pair_active, joined, *received, globals_all, portion_b, gatt)
 
-    shares = lax.all_to_all(sums.reshape(devices, 32, 128), CTX, 0, 0)
+    shares = lax.all_to_all(sums, "lo", 0, 0)
     attended_all = lax.all_gather(attended, HEAD, axis=0)
     *terms, gquery, gown = pl.pallas_call(
         backward_kernel,
@@ -350,16 +360,15 @@
         ),
         name="backward",
     )(position[None], pair_active, joined, *received, stats, gatt, gglob)
+    shares, *terms = lax.optimization_barrier((shares, *terms))
+    share = jnp.sum(shares.astype(F32), axis=0).astype(BF16)
+    column = lax.all_to_all(jnp.broadcast_to(share[None], (his,) + share.shape), "hi", 0, 0)
     returned = [lax.ppermute(t, CTX, route) for t, route in zip(terms, routes)]
-    shares, *returned = lax.optimization_barrier((shares, *returned))
-    share = jnp.sum(shares.astype(F32), axis=0).astype(BF16)
-    column = lax.all_to_all(jnp.broadcast_to(share[None], (zs,) + share.shape), "z", 0, 0)
-    weight_cols = lax.dynamic_slice_in_dim(
-        weight_all, lax.axis_index(HEAD) * width, width, axis=2
+    column, attended_all, *returned[:3] = lax.optimization_barrier(
+        (column, attended_all, *returned[:3])
     )
-    totals = lax.all_to_all(
-        jnp.broadcast_to(column[None], (xs,) + column.shape), "x", 0, 0
-    ).reshape(devices, 32, 128)
+    share = jnp.sum(column.astype(F32), axis=0).astype(BF16)
+    totals = lax.all_to_all(jnp.broadcast_to(share[None], (los,) + share.shape), "lo", 0, 0)
 
     projected = pl.pallas_call(
         project_kernel,
@@ -391,8 +400,7 @@
 
 def solution(mesh):
     ctx, head = mesh.devices.shape
-    cores = 2 if head % 2 == 0 else 1
-    inner = Mesh(mesh.devices.reshape(ctx // 4, 4, head // cores, cores), CTX + HEAD)
+    inner = Mesh(mesh.devices.reshape(ctx // PATCH, PATCH, head), CTX + (HEAD,))
     row = P(CTX, HEAD)
     return jax.shard_map(
         local,

time: 172 us -> 162 us (0.942); the launches traced: 171 us -> 159 us
  blocking collectives: 22.5 us -> 0 us
  starting transfers between devices: 81.1 us -> 88.6 us
  Pallas kernels: 15.9 us -> 17.7 us
    all_to_all x1 -> x0, blocking collectives: 22.5 us -> none  [local(): lax.all_to_all(jnp.broadcast_to(share[None], (zs,) + share.shape), 'z', 0...]
    all_to_all x5 -> x6, starting transfers between devices: 46.2 us -> 54.2 us  [the longest x1 12.4 us: local(): column = lax.all_to_all(picked, 'hi', 0, 0)]
    ppermute x4 -> x2, starting transfers between devices: 13.3 us -> 8.4 us  [local(): received[n] = lax.ppermute(joined, CTX, routes[n])]
    ppermute x1 -> x3, starting transfers between devices: 3.87 us -> 8.06 us  [the longest x2 7.39 us: local(): received[n] = lax.ppermute(joined_late, CTX, routes[n])]
    all_to_all x5 -> x6, waiting for transfers between devices: 18.5 us -> 14.3 us  [the longest x1 7.63 us: local(): shares = lax.all_to_all(sums, 'lo', 0, 0)]
    ppermute x1 -> x3, waiting for transfers between devices: 2.97 us -> 6.26 us  [the longest x2 6.25 us: local(): received[n] = lax.ppermute(joined_late, CTX, routes[n])]
    unnamed x12 -> x16, local copies, waits for them, and re-layouts: 2.87 us -> 4.67 us
    pallas_call x2 -> x3, Pallas kernels: 6.22 us -> 7.81 us  [the longest x1 4.65 us: local(): pl.pallas_call(forward_kernel, out_shape=(square, jax.ShapeDtypeStruct((l...]
  transfers between devices with their start and end apart: 18 -> 18, of which waited for: 8 -> 9; matrix products, arithmetic and copies ran while one was open for 2% -> 0% of each run, Pallas kernels for 7% -> 6%
where the time goes in v5:
time: 162 us; the launch traced here: 159 us
  starting transfers between devices  88.6 us (55%)
  waiting for transfers between devices  32 us (20%)
  Pallas kernels  17.7 us (11%)
  between operations  14.3 us (9%)
  local copies, waits for them, and re-layouts  6.24 us (4%)
    ppermute x5, starting transfers between devices, local(): returned = [lax.ppermute(t, CTX, route) for t, route in zip(terms, routes)]  17.9 us
    all_to_all x1, starting transfers between devices, local(): column = lax.all_to_all(picked, 'hi', 0, 0)  12.4 us
    all_to_all x1, starting transfers between devices, local(): lax.all_to_all(jnp.broadcast_to(share[None], (his,) + share.shape), 'hi',...  10.5 us
    all_to_all x1, starting transfers between devices, local(): lax.all_to_all(jnp.broadcast_to(share[None], (los,) + share.shape), 'lo',...  9.04 us
    all_to_all x1, starting transfers between devices, local(): slices = lax.all_to_all(joined.reshape(los, step, width), 'lo', 0, 0)  8.61 us
    ppermute x2, starting transfers between devices, local(): received[n] = lax.ppermute(joined, CTX, routes[n])  8.4 us
    all_to_all x1, waiting for transfers between devices, local(): shares = lax.all_to_all(sums, 'lo', 0, 0)  7.63 us
    all_to_all x1, starting transfers between devices, local(): shares = lax.all_to_all(sums, 'lo', 0, 0)  7.63 us
  transfers between devices with their start and end apart: 18, of which 9 were waited for; matrix products, arithmetic and copies ran while one was open for 0% of the time, Pallas kernels for 6%

profile of v5, /device:TPU:24, one launch (start us, length us, event | category | flops | bytes accessed | tf_op | source)
XLA Modules:
  0.0 158.9 jit_solution(5487093047606302190)
XLA Ops:
  7.2 0.0 all-gather.5.cloned.1.call-start
  7.2 1.8 %pack.1 = (bf16[512,128]{1,0:T(8,128)(2,1)}, bf16[10,128,128]{2,1,0:T(8,128)(2,1)}) custom-call(bf16[256,128]{1,0:T(8,128)(2,1)} %qk_ref.1, bf16[256,128]{1,0:T(8,128)(2,1)} %val_ref.1, bf16[256,128]{1,0:T(8,128)(2,1)} %gout_ref.1, bf16[128,1024]{1,0:T(8,128)(2,1)} %w_ref.3), custom_call_target="tpu_custom_call" | custom-call | tf_op jit(solution)/shard_map/pack/pallas_call | solution.py:262
  9.1 0.0 all-gather.5.cloned.1.call-update
  9.1 8.6 %all-to-all-start = ((bf16[16,32,128]{2,1,0:T(8,128)(2,1)}), bf16[16,32,128]{2,1,0:T(8,128)(2,1)S(1)}, u32[]{:S(2)}, u32[]{:S(2)}) async-start(bf16[16,32,128]{2,1,0:T(8,128)(2,1)} %bitcast.6), calls=%async_computation | async-start | bytes 262144 | tf_op jit(solution)/shard_map/all_to_all | solution.py:273
  17.7 3.8 %collective-permute-start = (bf16[512,128]{1,0:T(8,128)(2,1)}, bf16[512,128]{1,0:T(8,128)(2,1)S(1)}, u32[]{:S(2)}, u32[]{:S(2)}) collective-permute-start(bf16[512,128]{1,0:T(8,128)(2,1)} %get-tuple-element.52.own_ref), channel_id=1, source_target_pairs={{0,8},{8,0},{16,24},{24,16},{32,40},{40,32},{48,56},{56,48},{64,72... | collective-permute-start | bytes 393224 | tf_op jit(solution)/shard_map/ppermute | solution.py:281
  21.5 4.6 %collective-permute-start.1 = (bf16[512,128]{1,0:T(8,128)(2,1)}, bf16[512,128]{1,0:T(8,128)(2,1)S(1)}, u32[]{:S(2)}, u32[]{:S(2)}) collective-permute-start(bf16[512,128]{1,0:T(8,128)(2,1)} %get-tuple-element.52.own_ref), channel_id=1, source_target_pairs={{0,16},{8,24},{16,0},{24,8},{32,48},{40,56},{48,32},{56,40},{64,80... | collective-permute-start | bytes 393224 | tf_op jit(solution)/shard_map/ppermute | solution.py:281
  26.1 4.2 %collective-permute-done.1.p2 = bf16[512,128]{1,0:T(8,128)(2,1)S(1)} collective-permute-done((bf16[512,128]{1,0:T(8,128)(2,1)}, bf16[512,128]{1,0:T(8,128)(2,1)S(1)}, u32[]{:S(2)}, u32[]{:S(2)}) %collective-permute-start.1) | collective-permute-done | bytes 131104 | tf_op jit(solution)/shard_map/ppermute | solution.py:281
  30.4 0.0 all-to-all-done.slices_ref
  30.4 0.6 copy-done.6
  31.0 1.6 pick.1
  32.6 12.4 %all-to-all-start.1 = ((bf16[4,2,32,128]{3,2,1,0:T(8,128)(2,1)}), bf16[4,2,32,128]{3,2,1,0:T(8,128)(2,1)S(1)}, u32[]{:S(2)}, u32[]{:S(2)}) async-start(bf16[4,2,32,128]{3,2,1,0:T(8,128)(2,1)} %pick.1), calls=%async_computation.1 | async-start | bytes 131072 | tf_op jit(solution)/shard_map/all_to_all | solution.py:291
  45.0 3.2 %collective-permute-start.2 = (bf16[512,128]{1,0:T(8,128)(2,1)}, bf16[512,128]{1,0:T(8,128)(2,1)S(1)}, u32[]{:S(2)}, u32[]{:S(2)}) collective-permute-start(bf16[512,128]{1,0:T(8,128)(2,1)} %get-tuple-element.52.own_ref), channel_id=1, source_target_pairs={{0,32},{8,40},{16,48},{24,56},{32,0},{40,8},{48,16},{56,24},{64,96... | collective-permute-start | bytes 393224 | tf_op jit(solution)/shard_map/ppermute | solution.py:293
  48.2 4.2 %collective-permute-start.3 = (bf16[512,128]{1,0:T(8,128)(2,1)}, bf16[512,128]{1,0:T(8,128)(2,1)S(1)}, u32[]{:S(2)}, u32[]{:S(2)}) collective-permute-start(bf16[512,128]{1,0:T(8,128)(2,1)} %get-tuple-element.52.own_ref), channel_id=1, source_target_pairs={{0,64},{8,72},{16,80},{24,88},{32,96},{40,104},{48,112},{56,120},{... | collective-permute-start | bytes 393224 | tf_op jit(solution)/shard_map/ppermute | solution.py:293
  52.4 0.8 collective-permute-done.2.p3
  53.2 5.5 %collective-permute-done.3.p4 = bf16[512,128]{1,0:T(8,128)(2,1)S(1)} collective-permute-done((bf16[512,128]{1,0:T(8,128)(2,1)}, bf16[512,128]{1,0:T(8,128)(2,1)S(1)}, u32[]{:S(2)}, u32[]{:S(2)}) %collective-permute-start.3) | collective-permute-done | bytes 131104 | tf_op jit(solution)/shard_map/ppermute | solution.py:293
  58.6 0.2 all-to-all-done.1.slices_ref
  58.8 0.6 copy-done.7
  59.5 1.6 %spread.1 = bf16[16,2,32,128]{3,2,1,0:T(8,128)(2,1)} custom-call(s32[2]{0:T(128)} %ids_ref.5, bf16[4,2,32,128]{3,2,1,0:T(8,128)(2,1)} %copy-done.7), custom_call_target="tpu_custom_call" | custom-call | tf_op jit(solution)/shard_map/spread/pallas_call | solution.py:295
  61.1 6.0 %all-to-all-start.2 = ((bf16[16,2,32,128]{3,2,1,0:T(8,128)(2,1)}), bf16[16,2,32,128]{3,2,1,0:T(8,128)(2,1)S(1)}, u32[]{:S(2)}, u32[]{:S(2)}) async-start(bf16[16,2,32,128]{3,2,1,0:T(8,128)(2,1)} %spread.1), calls=%async_computation.2 | async-start | bytes 524288 | tf_op jit(solution)/shard_map/all_to_all | solution.py:303
  67.0 0.7 collective-permute-start.4
  67.7 1.7 %copy-done = bf16[80,128,128]{2,1,0:T(8,128)(2,1)S(1)} copy-done((bf16[80,128,128]{2,1,0:T(8,128)(2,1)S(1)}, bf16[80,128,128]{2,1,0:T(8,128)(2,1)}, u32[]{:S(2)}) %copy-start) | copy-done | bytes 2621464
  69.5 0.9 copy-done.1
  70.4 0.4 cotangent.1
  70.8 0.7 copy-done.2
  71.5 5.5 %all-to-all-done.2.glob_ref = bf16[16,2,32,128]{3,2,1,0:T(8,128)(2,1)S(1)} async-done(((bf16[16,2,32,128]{3,2,1,0:T(8,128)(2,1)}), bf16[16,2,32,128]{3,2,1,0:T(8,128)(2,1)S(1)}, u32[]{:S(2)}, u32[]{:S(2)}) %all-to-all-start.2) | async-done | bytes 262176 | tf_op jit(solution)/shard_map/all_to_all | solution.py:303
  77.0 4.7 %forward.1 = (f32[256,128]{1,0:T(8,128)}, bf16[16,128,128]{2,1,0:T(8,128)(2,1)}, f32[256,128]{1,0:T(8,128)S(1)}, f32[256,128]{1,0:T(8,128)S(1)}) custom-call(s32[1]{0:T(128)} %bitcast.pos_ref, s32[4,32]{1,0:T(4,128)S(1)} %copy-done.5, bf16[512,128]{1,0:T(8,128)(2,1)S(1)} %copy-done.3, bf16[512,128]{1,0:T(8,128)(2,1)S(1)} %collective-permute-done.p0, ...), custom_call_target="tpu_custom_call" | custom-call | flops 3000000000 | bytes 4000000 | tf_op jit(solution)/shard_map/forward/pallas_call | solution.py:325
  81.7 7.6 %all-to-all-start.3 = ((bf16[16,128,128]{2,1,0:T(8,128)(2,1)}), bf16[16,128,128]{2,1,0:T(8,128)(2,1)S(1)}, u32[]{:S(2)}, u32[]{:S(2)}) async-start(bf16[16,128,128]{2,1,0:T(8,128)(2,1)} %get-tuple-element.60), calls=%async_computation.3 | async-start | bytes 1048576 | tf_op jit(solution)/shard_map/all_to_all | solution.py:346
  89.3 0.0 all-gather.7.cloned.1.call-start
  89.4 0.7 all-gather.7.cloned.1.call-update
  90.1 3.9 %backward.1 = (bf16[256,256]{1,0:T(8,128)(2,1)S(1)}, bf16[256,256]{1,0:T(8,128)(2,1)S(1)}, bf16[256,256]{1,0:T(8,128)(2,1)S(1)}, bf16[256,256]{1,0:T(8,128)(2,1)...) custom-call(s32[1]{0:T(128)} %bitcast.pos_ref, s32[4,32]{1,0:T(4,128)S(1)} %copy-done.5, ...), custom_call_target="tpu_custom_call" | custom-call | flops 3000000000 | bytes 4000000 | tf_op jit(solution)/shard_map/backward/pallas_call | solution.py:348
  94.0 0.0 copy-start.4
  94.0 7.6 %all-to-all-done.3 = bf16[16,128,128]{2,1,0:T(8,128)(2,1)S(1)} async-done(((bf16[16,128,128]{2,1,0:T(8,128)(2,1)}), bf16[16,128,128]{2,1,0:T(8,128)(2,1)S(1)}, u32[]{:S(2)}, u32[]{:S(2)}) %all-to-all-start.3) | async-done | bytes 524320 | tf_op jit(solution)/shard_map/all_to_all | solution.py:346
  101.6 0.1 reduce_sum.24
  101.7 0.7 broadcast_in_dim.10
  102.3 10.5 %all-to-all-start.4 = ((bf16[4,128,128]{2,1,0:T(8,128)(2,1)}), bf16[4,128,128]{2,1,0:T(8,128)(2,1)S(1)}, u32[]{:S(2)}, u32[]{:S(2)}) async-start(bf16[4,128,128]{2,1,0:T(8,128)(2,1)} %broadcast_in_dim.10), calls=%async_computation.4 | async-start | bytes 262144 | tf_op jit(solution)/shard_map/all_to_all | solution.py:365
  112.9 2.5 %collective-permute-start.5 = (bf16[256,256]{1,0:T(8,128)(2,1)S(1)}, bf16[256,256]{1,0:T(8,128)(2,1)S(1)}, u32[]{:S(2)}, u32[]{:S(2)}) collective-permute-start(bf16[256,256]{1,0:T(8,128)(2,1)S(1)} %get-tuple-element.70), channel_id=1, source_target_pairs={{0,8},{8,0},{16,24},{24,16},{32,40},{40,32},{48,56},{56,48},{64,72... | collective-permute-start | bytes 393224 | tf_op jit(solution)/shard_map/ppermute | solution.py:366
  115.3 0.7 collective-permute-start.6
  116.0 6.7 %collective-permute-start.7 = (bf16[256,256]{1,0:T(8,128)(2,1)S(1)}, bf16[256,256]{1,0:T(8,128)(2,1)S(1)}, u32[]{:S(2)}, u32[]{:S(2)}) collective-permute-start(bf16[256,256]{1,0:T(8,128)(2,1)S(1)} %get-tuple-element.72), channel_id=1, source_target_pairs={{0,16},{8,24},{16,0},{24,8},{32,48},{40,56},{48,32},{56,40},{64,80... | collective-permute-start | bytes 393224 | tf_op jit(solution)/shard_map/ppermute | solution.py:366
  122.7 0.0 all-gather.7.cloned.1.call-done
  122.7 2.9 %collective-permute-done.7.b2 = bf16[256,256]{1,0:T(8,128)(2,1)S(1)} collective-permute-done((bf16[256,256]{1,0:T(8,128)(2,1)S(1)}, bf16[256,256]{1,0:T(8,128)(2,1)S(1)}, u32[]{:S(2)}, u32[]{:S(2)}) %collective-permute-start.7) | collective-permute-done | bytes 131104 | tf_op jit(solution)/shard_map/ppermute | solution.py:366
  125.6 0.9 all-to-all-done.4
  126.6 0.9 broadcast_in_dim.11
  127.5 9.0 %all-to-all-start.5 = ((bf16[16,128,128]{2,1,0:T(8,128)(2,1)}), bf16[16,128,128]{2,1,0:T(8,128)(2,1)S(1)}, u32[]{:S(2)}, u32[]{:S(2)}) async-start(bf16[16,128,128]{2,1,0:T(8,128)(2,1)} %broadcast_in_dim.11), calls=%async_computation.5 | async-start | bytes 1048576 | tf_op jit(solution)/shard_map/all_to_all | solution.py:371
  136.5 3.8 %collective-permute-start.8 = (bf16[256,256]{1,0:T(8,128)(2,1)S(1)}, bf16[256,256]{1,0:T(8,128)(2,1)S(1)}, u32[]{:S(2)}, u32[]{:S(2)}) collective-permute-start(bf16[256,256]{1,0:T(8,128)(2,1)S(1)} %get-tuple-element.78), channel_id=1, source_target_pairs={{0,32},{8,40},{16,48},{24,56},{32,0},{40,8},{48,16},{56,24},{64,96... | collective-permute-start | bytes 393224 | tf_op jit(solution)/shard_map/ppermute | solution.py:366
  140.4 4.3 %collective-permute-start.9 = (bf16[256,256]{1,0:T(8,128)(2,1)S(1)}, bf16[256,256]{1,0:T(8,128)(2,1)S(1)}, u32[]{:S(2)}, u32[]{:S(2)}) collective-permute-start(bf16[256,256]{1,0:T(8,128)(2,1)S(1)} %get-tuple-element.79), channel_id=1, source_target_pairs={{0,64},{8,72},{16,80},{24,88},{32,96},{40,104},{48,112},{56,120},{... | collective-permute-start | bytes 393224 | tf_op jit(solution)/shard_map/ppermute | solution.py:366
  144.6 2.2 %project.1 = bf16[256,128]{1,0:T(8,128)(2,1)} custom-call(f32[8,256,128]{2,1,0:T(8,128)} %bitcast.7, bf16[8,128,128]{2,1,0:T(8,128)(2,1)} %copy-done.2), custom_call_target="tpu_custom_call" | custom-call | flops 70000000 | bytes 1500000 | tf_op jit(solution)/shard_map/project/pallas_call | solution.py:373
  146.8 3.6 %collective-permute-done.9.b4 = bf16[256,256]{1,0:T(8,128)(2,1)S(1)} collective-permute-done((bf16[256,256]{1,0:T(8,128)(2,1)S(1)}, bf16[256,256]{1,0:T(8,128)(2,1)S(1)}, u32[]{:S(2)}, u32[]{:S(2)}) %collective-permute-start.9) | collective-permute-done | bytes 131104 | tf_op jit(solution)/shard_map/ppermute | solution.py:366
  150.5 1.6 %finish.1 = (bf16[256,128]{1,0:T(8,128)(2,1)}, bf16[256,128]{1,0:T(8,128)(2,1)}, f32[128,1024]{1,0:T(8,128)}) custom-call(s32[1]{0:T(128)} %bitcast.pos_ref, s32[2]{0:T(128)S(1)} %copy-done.4, bf16[256,256]{1,0:T(8,128)(2,1)S(1)} %collective-permute-done.5.b0, bf16[256,256]{1,0:T(8,128)(2,1)S(1)} %collective-permute-done.6.b1, ...), custom_call_target="tpu_custom_call" | custom-call | flops 2000000 | bytes 2500000 | tf_op jit(solution)/shard_map/finish/pallas_call | solution.py:383
  (18 shorter events, 0.1 us)
Async XLA Ops:
  7.2 69.9 %copy-start.5 = (s32[4,32]{1,0:T(4,128)S(1)}, s32[4,32]{1,0:T(4,128)}, u32[]{:S(2)}) copy-start(s32[4,32]{1,0:T(4,128)} %pair_ref.3) | copy-start | bytes 1540
  7.2 53.9 %all-gather.5.cloned.1.call-start = ((), (), s32[]{:S(2)}) async-start(), calls=%async_computation.6 | async-start | bytes 2949120 | tf_op jit(solution)/shard_map/all_gather | solution.py:274
  9.1 68.0 %copy-start.3 = (bf16[512,128]{1,0:T(8,128)(2,1)S(1)}, bf16[512,128]{1,0:T(8,128)(2,1)}, u32[]{:S(2)}) copy-start(bf16[512,128]{1,0:T(8,128)(2,1)} %get-tuple-element.52.own_ref) | copy-start | bytes 393220
  9.1 21.3 %all-to-all-start = ((bf16[16,32,128]{2,1,0:T(8,128)(2,1)}), bf16[16,32,128]{2,1,0:T(8,128)(2,1)S(1)}, u32[]{:S(2)}, u32[]{:S(2)}) async-start(bf16[16,32,128]{2,1,0:T(8,128)(2,1)} %bitcast.6), calls=%async_computation | async-start | bytes 262144 | tf_op jit(solution)/shard_map/all_to_all | solution.py:273
  17.7 8.4 %collective-permute-start = (bf16[512,128]{1,0:T(8,128)(2,1)}, bf16[512,128]{1,0:T(8,128)(2,1)S(1)}, u32[]{:S(2)}, u32[]{:S(2)}) collective-permute-start(bf16[512,128]{1,0:T(8,128)(2,1)} %get-tuple-element.52.own_ref), channel_id=1, source_target_pairs={{0,8},{8,0},{16,24},{24,16},{32,40},{40,32},{48,56},{56,48},{64,72... | collective-permute-start | bytes 393224 | tf_op jit(solution)/shard_map/ppermute | solution.py:281
  21.5 8.8 %collective-permute-start.1 = (bf16[512,128]{1,0:T(8,128)(2,1)}, bf16[512,128]{1,0:T(8,128)(2,1)S(1)}, u32[]{:S(2)}, u32[]{:S(2)}) collective-permute-start(bf16[512,128]{1,0:T(8,128)(2,1)} %get-tuple-element.52.own_ref), channel_id=1, source_target_pairs={{0,16},{8,24},{16,0},{24,8},{32,48},{40,56},{48,32},{56,40},{64,80... | collective-permute-start | bytes 393224 | tf_op jit(solution)/shard_map/ppermute | solution.py:281
  30.4 0.6 copy-start.6
  32.6 26.2 %all-to-all-start.1 = ((bf16[4,2,32,128]{3,2,1,0:T(8,128)(2,1)}), bf16[4,2,32,128]{3,2,1,0:T(8,128)(2,1)S(1)}, u32[]{:S(2)}, u32[]{:S(2)}) async-start(bf16[4,2,32,128]{3,2,1,0:T(8,128)(2,1)} %pick.1), calls=%async_computation.1 | async-start | bytes 131072 | tf_op jit(solution)/shard_map/all_to_all | solution.py:291
  45.0 8.2 %collective-permute-start.2 = (bf16[512,128]{1,0:T(8,128)(2,1)}, bf16[512,128]{1,0:T(8,128)(2,1)S(1)}, u32[]{:S(2)}, u32[]{:S(2)}) collective-permute-start(bf16[512,128]{1,0:T(8,128)(2,1)} %get-tuple-element.52.own_ref), channel_id=1, source_target_pairs={{0,32},{8,40},{16,48},{24,56},{32,0},{40,8},{48,16},{56,24},{64,96... | collective-permute-start | bytes 393224 | tf_op jit(solution)/shard_map/ppermute | solution.py:293
  48.2 10.5 %collective-permute-start.3 = (bf16[512,128]{1,0:T(8,128)(2,1)}, bf16[512,128]{1,0:T(8,128)(2,1)S(1)}, u32[]{:S(2)}, u32[]{:S(2)}) collective-permute-start(bf16[512,128]{1,0:T(8,128)(2,1)} %get-tuple-element.52.own_ref), channel_id=1, source_target_pairs={{0,64},{8,72},{16,80},{24,88},{32,96},{40,104},{48,112},{56,120},{... | collective-permute-start | bytes 393224 | tf_op jit(solution)/shard_map/ppermute | solution.py:293
  58.8 0.6 copy-start.7
  61.1 16.0 %all-to-all-start.2 = ((bf16[16,2,32,128]{3,2,1,0:T(8,128)(2,1)}), bf16[16,2,32,128]{3,2,1,0:T(8,128)(2,1)S(1)}, u32[]{:S(2)}, u32[]{:S(2)}) async-start(bf16[16,2,32,128]{3,2,1,0:T(8,128)(2,1)} %spread.1), calls=%async_computation.2 | async-start | bytes 524288 | tf_op jit(solution)/shard_map/all_to_all | solution.py:303
  67.0 4.4 %collective-permute-start.4 = (bf16[512,128]{1,0:T(8,128)(2,1)}, bf16[512,128]{1,0:T(8,128)(2,1)S(1)}, u32[]{:S(2)}, u32[]{:S(2)}) collective-permute-start(bf16[512,128]{1,0:T(8,128)(2,1)} %get-tuple-element.52.own_ref), channel_id=1, source_target_pairs={{8,16},{16,8},{24,32},{32,24},{40,48},{48,40},{56,64},{64,56},{72,... | collective-permute-start | bytes 393224 | tf_op jit(solution)/shard_map/ppermute | solution.py:304
  67.7 1.7 %copy-start = (bf16[80,128,128]{2,1,0:T(8,128)(2,1)S(1)}, bf16[80,128,128]{2,1,0:T(8,128)(2,1)}, u32[]{:S(2)}) copy-start(bf16[80,128,128]{2,1,0:T(8,128)(2,1)} %all-gather.5.cloned.1.call-done) | copy-start | bytes 7864324
  69.5 0.9 copy-start.1
  70.8 0.7 copy-start.2
  81.7 19.9 %all-to-all-start.3 = ((bf16[16,128,128]{2,1,0:T(8,128)(2,1)}), bf16[16,128,128]{2,1,0:T(8,128)(2,1)S(1)}, u32[]{:S(2)}, u32[]{:S(2)}) async-start(bf16[16,128,128]{2,1,0:T(8,128)(2,1)} %get-tuple-element.60), calls=%async_computation.3 | async-start | bytes 1048576 | tf_op jit(solution)/shard_map/all_to_all | solution.py:346
  89.3 33.4 %all-gather.7.cloned.1.call-start = ((), (), s32[]{:S(2)}) async-start(), calls=%async_computation.7 | async-start | bytes 1179648 | tf_op jit(solution)/shard_map/all_gather | solution.py:347
  94.0 56.5 %copy-start.4 = (s32[2]{0:T(128)S(1)}, s32[2]{0:T(128)}, u32[]{:S(2)}) copy-start(s32[2]{0:T(128)} %ids_ref.5) | copy-start | bytes 28
  102.3 24.2 %all-to-all-start.4 = ((bf16[4,128,128]{2,1,0:T(8,128)(2,1)}), bf16[4,128,128]{2,1,0:T(8,128)(2,1)S(1)}, u32[]{:S(2)}, u32[]{:S(2)}) async-start(bf16[4,128,128]{2,1,0:T(8,128)(2,1)} %broadcast_in_dim.10), calls=%async_computation.4 | async-start | bytes 262144 | tf_op jit(solution)/shard_map/all_to_all | solution.py:365
  112.9 9.9 %collective-permute-start.5 = (bf16[256,256]{1,0:T(8,128)(2,1)S(1)}, bf16[256,256]{1,0:T(8,128)(2,1)S(1)}, u32[]{:S(2)}, u32[]{:S(2)}) collective-permute-start(bf16[256,256]{1,0:T(8,128)(2,1)S(1)} %get-tuple-element.70), channel_id=1, source_target_pairs={{0,8},{8,0},{16,24},{24,16},{32,40},{40,32},{48,56},{56,48},{64,72... | collective-permute-start | bytes 393224 | tf_op jit(solution)/shard_map/ppermute | solution.py:366
  115.3 7.4 %collective-permute-start.6 = (bf16[256,256]{1,0:T(8,128)(2,1)S(1)}, bf16[256,256]{1,0:T(8,128)(2,1)S(1)}, u32[]{:S(2)}, u32[]{:S(2)}) collective-permute-start(bf16[256,256]{1,0:T(8,128)(2,1)S(1)} %get-tuple-element.71), channel_id=1, source_target_pairs={{8,16},{16,8},{24,32},{32,24},{40,48},{48,40},{56,64},{64,56},{72,... | collective-permute-start | bytes 393224 | tf_op jit(solution)/shard_map/ppermute | solution.py:366
  116.0 9.6 %collective-permute-start.7 = (bf16[256,256]{1,0:T(8,128)(2,1)S(1)}, bf16[256,256]{1,0:T(8,128)(2,1)S(1)}, u32[]{:S(2)}, u32[]{:S(2)}) collective-permute-start(bf16[256,256]{1,0:T(8,128)(2,1)S(1)} %get-tuple-element.72), channel_id=1, source_target_pairs={{0,16},{8,24},{16,0},{24,8},{32,48},{40,56},{48,32},{56,40},{64,80... | collective-permute-start | bytes 393224 | tf_op jit(solution)/shard_map/ppermute | solution.py:366
  127.5 23.0 %all-to-all-start.5 = ((bf16[16,128,128]{2,1,0:T(8,128)(2,1)}), bf16[16,128,128]{2,1,0:T(8,128)(2,1)S(1)}, u32[]{:S(2)}, u32[]{:S(2)}) async-start(bf16[16,128,128]{2,1,0:T(8,128)(2,1)} %broadcast_in_dim.11), calls=%async_computation.5 | async-start | bytes 1048576 | tf_op jit(solution)/shard_map/all_to_all | solution.py:371
  136.5 10.3 %collective-permute-start.8 = (bf16[256,256]{1,0:T(8,128)(2,1)S(1)}, bf16[256,256]{1,0:T(8,128)(2,1)S(1)}, u32[]{:S(2)}, u32[]{:S(2)}) collective-permute-start(bf16[256,256]{1,0:T(8,128)(2,1)S(1)} %get-tuple-element.78), channel_id=1, source_target_pairs={{0,32},{8,40},{16,48},{24,56},{32,0},{40,8},{48,16},{56,24},{64,96... | collective-permute-start | bytes 393224 | tf_op jit(solution)/shard_map/ppermute | solution.py:366
  140.4 10.1 %collective-permute-start.9 = (bf16[256,256]{1,0:T(8,128)(2,1)S(1)}, bf16[256,256]{1,0:T(8,128)(2,1)S(1)}, u32[]{:S(2)}, u32[]{:S(2)}) collective-permute-start(bf16[256,256]{1,0:T(8,128)(2,1)S(1)} %get-tuple-element.79), channel_id=1, source_target_pairs={{0,64},{8,72},{16,80},{24,88},{32,96},{40,104},{48,112},{56,120},{... | collective-permute-start | bytes 393224 | tf_op jit(solution)/shard_map/ppermute | solution.py:366
Sparse Core Ops, SparseCore 0:
  10.7 37.0 all-gather.4
  92.3 29.7 all-gather.6

commit v6 on v5

--- a/solution.py
+++ b/solution.py
@@ -228,18 +228,41 @@
         share_ref[blocks + c] = w_ref[:, c * 128:(c + 1) * 128]
 
 
-def pick_kernel(ids_ref, slices_ref, out_ref):
+def copy_all(copies):
+    for copy in copies:
+        copy.start()
+    for copy in copies:
+        copy.wait()
+
+
+def pick_kernel(ids_ref, slices_ref, out_ref, sems):
+    count = out_ref.shape[0]
+    copies = []
     for g in range(NGLOB):
-        chosen = slices_ref[lax.rem(ids_ref[g], PATCH)]
-        for n in range(out_ref.shape[0]):
-            out_ref[n, g] = chosen
-
-
-def spread_kernel(ids_ref, slices_ref, out_ref):
+        chosen = slices_ref.at[lax.rem(ids_ref[g], PATCH)]
+        for n in range(count):
+            sem = sems.at[g * count + n]
+            copies.append(pltpu.make_async_copy(chosen, out_ref.at[n, g], sem))
+    copy_all(copies)
+
+
+def spread_kernel(ids_ref, slices_ref, out_ref, sems):
+    count = out_ref.shape[0]
+    copies = []
     for g in range(NGLOB):
-        chosen = slices_ref[lax.div(ids_ref[g], PATCH), g]
-        for n in range(out_ref.shape[0]):
-            out_ref[n, g] = chosen
+        chosen = slices_ref.at[lax.div(ids_ref[g], PATCH), g]
+        for n in range(count):
+            sem = sems.at[g * count + n]
+            copies.append(pltpu.make_async_copy(chosen, out_ref.at[n, g], sem))
+    copy_all(copies)
+
+
+def anywhere():
+    return pl.BlockSpec(memory_space=pl.ANY)
+
+
+def limit(mebibytes):
+    return pltpu.CompilerParams(vmem_limit_bytes=mebibytes * 1024 * 1024)
 
 
 def vmem(count):
@@ -279,29 +302,20 @@
     received = [None] * len(routes)
     for n in (0, 2):
         received[n] = lax.ppermute(joined, CTX, routes[n])
-    slices, received[0], received[2] = lax.optimization_barrier((slices, received[0], received[2]))
+    slices, received[0] = lax.optimization_barrier((slices, received[0]))
     picked = pl.pallas_call(
         pick_kernel,
         out_shape=jax.ShapeDtypeStruct((his, NGLOB, step, width), BF16),
-        in_specs=[smem()] + vmem(1),
-        out_specs=vmem(1)[0],
+        in_specs=[smem(), anywhere()],
+        out_specs=anywhere(),
+        scratch_shapes=[pltpu.SemaphoreType.DMA((NGLOB * his,))],
+        compiler_params=limit(1),
         name="pick",
     )(global_ids, slices)
-    picked, joined_late = lax.optimization_barrier((picked, joined))
+    picked, joined_late, received[2] = lax.optimization_barrier((picked, joined, received[2]))
     column = lax.all_to_all(picked, "hi", 0, 0)
     for n in (4, 3):
         received[n] = lax.ppermute(joined_late, CTX, routes[n])
-    column, received[3], received[4] = lax.optimization_barrier((column, received[3], received[4]))
-    chosen = pl.pallas_call(
-        spread_kernel,
-        out_shape=jax.ShapeDtypeStruct((los, NGLOB, step, width), BF16),
-        in_specs=[smem()] + vmem(1),
-        out_specs=vmem(1)[0],
-        name="spread",
-    )(global_ids, column)
-    chosen, joined_late, portion = lax.optimization_barrier((chosen, joined, portion))
-    globals_all = lax.all_to_all(chosen, "lo", 0, 0)
-    received[1] = lax.ppermute(joined_late, CTX, routes[1])
     portion_b, gatt, weight_cols = pl.pallas_call(
         cotangent_kernel,
         out_shape=(
@@ -311,13 +325,27 @@
         ),
         in_specs=[smem()] + vmem(2),
         out_specs=tuple(vmem(3)),
-        compiler_params=pltpu.CompilerParams(vmem_limit_bytes=16 * 1024 * 1024),
+        compiler_params=limit(8),
         cost_estimate=pl.CostEstimate(
             flops=600_000_000, bytes_accessed=4_000_000, transcendentals=0
         ),
         name="cotangent",
     )(lax.axis_index(HEAD)[None], portion, out_weight)
-
+    column, received[4], portion_b, gatt, weight_cols = lax.optimization_barrier(
+        (column, received[4], portion_b, gatt, weight_cols)
+    )
+    chosen = pl.pallas_call(
+        spread_kernel,
+        out_shape=jax.ShapeDtypeStruct((los, NGLOB, step, width), BF16),
+        in_specs=[smem(), anywhere()],
+        out_specs=anywhere(),
+        scratch_shapes=[pltpu.SemaphoreType.DMA((NGLOB * los,))],
+        compiler_params=limit(1),
+        name="spread",
+    )(global_ids, column)
+    chosen, joined_late, received[3] = lax.optimization_barrier((chosen, joined, received[3]))
+    globals_all = lax.all_to_all(chosen, "lo", 0, 0)
+    received[1] = lax.ppermute(joined_late, CTX, routes[1])
     count = ROUNDS + 2 + NGLOB
     nheads = width // HD
     block = jax.ShapeDtypeStruct((2 * width, length), BF16)
@@ -336,7 +364,7 @@
             pltpu.VMEM((nheads, length, count * length), F32),
             pltpu.VMEM((length, width), F32),
         ],
-        compiler_params=pltpu.CompilerParams(vmem_limit_bytes=40 * 1024 * 1024),
+        compiler_params=limit(20),
         cost_estimate=pl.CostEstimate(
             flops=3_000_000_000, bytes_accessed=4_000_000, transcendentals=1_100_000
         ),
@@ -354,20 +382,23 @@
         ),
         in_specs=[smem()] * 2 + vmem(9),
         out_specs=tuple(vmem(7)),
-        compiler_params=pltpu.CompilerParams(vmem_limit_bytes=24 * 1024 * 1024),
+        compiler_params=limit(10),
         cost_estimate=pl.CostEstimate(
             flops=3_000_000_000, bytes_accessed=4_000_000, transcendentals=800_000
         ),
         name="backward",
     )(position[None], pair_active, joined, *received, stats, gatt, gglob)
+    returned = [None] * len(routes)
+    returned[0] = lax.ppermute(terms[0], CTX, routes[0])
     shares, *terms = lax.optimization_barrier((shares, *terms))
     share = jnp.sum(shares.astype(F32), axis=0).astype(BF16)
+    share, returned[0] = lax.optimization_barrier((share, returned[0]))
     column = lax.all_to_all(jnp.broadcast_to(share[None], (his,) + share.shape), "hi", 0, 0)
-    returned = [lax.ppermute(t, CTX, route) for t, route in zip(terms, routes)]
-    column, attended_all, *returned[:3] = lax.optimization_barrier(
-        (column, attended_all, *returned[:3])
-    )
+    for n in (4, 2, 3, 1):
+        returned[n] = lax.ppermute(terms[n], CTX, routes[n])
+    column, returned[2], returned[4] = lax.optimization_barrier((column, returned[2], returned[4]))
     share = jnp.sum(column.astype(F32), axis=0).astype(BF16)
+    share, attended_all = lax.optimization_barrier((share, attended_all))
     totals = lax.all_to_all(jnp.broadcast_to(share[None], (los,) + share.shape), "lo", 0, 0)
 
     projected = pl.pallas_call(
@@ -375,6 +406,7 @@
         out_shape=jax.ShapeDtypeStruct((length, width), BF16),
         in_specs=vmem(2),
         out_specs=vmem(1)[0],
+        compiler_params=limit(4),
         cost_estimate=pl.CostEstimate(
             flops=70_000_000, bytes_accessed=1_500_000, transcendentals=0
         ),
@@ -389,7 +421,7 @@
         ),
         in_specs=[smem()] * 2 + vmem(8),
         out_specs=tuple(vmem(3)),
-        compiler_params=pltpu.CompilerParams(vmem_limit_bytes=16 * 1024 * 1024),
+        compiler_params=limit(6),
         cost_estimate=pl.CostEstimate(
             flops=2_000_000, bytes_accessed=2_500_000, transcendentals=0
         ),

time: 162 us -> 153 us (0.944)
  waiting for transfers between devices: 32 us -> 26.8 us
  Pallas kernels: 17.7 us -> 16 us
    ppermute x2, waiting for transfers between devices: 6.25 us -> 1.33 us  [local(): received[n] = lax.ppermute(joined_late, CTX, routes[n])]
    all_to_all x1, waiting for transfers between devices: 7.63 us -> 3.79 us  [local(): shares = lax.all_to_all(sums, 'lo', 0, 0)]
    all_to_all x1, waiting for transfers between devices: 5.54 us -> 9.28 us  [local(): globals_all = lax.all_to_all(chosen, 'lo', 0, 0)]
    ppermute x5, starting transfers between devices: 17.9 us -> 21 us  [the longest x4 17.1 us: local(): returned[n] = lax.ppermute(terms[n], CTX, routes[n])]
    ppermute x2, waiting for transfers between devices: 4.25 us -> 1.84 us  [local(): received[n] = lax.ppermute(joined, CTX, routes[n])]
    all_to_all x1, starting transfers between devices: 10.5 us -> 8.11 us  [local(): lax.all_to_all(jnp.broadcast_to(share[None], (his,) + share.shape), 'hi',...]
    all_to_all x1, starting transfers between devices: 9.04 us -> 7.14 us  [local(): lax.all_to_all(jnp.broadcast_to(share[None], (los,) + share.shape), 'lo',...]
    all_to_all x1, waiting for transfers between devices: 0.18 us -> 2.05 us  [local(): column = lax.all_to_all(picked, 'hi', 0, 0)]
  transfers between devices with their start and end apart: 18 -> 18, of which waited for: 9 -> 8; matrix products, arithmetic and copies ran while one was open for 0% -> 1% of each run, Pallas kernels for 6% -> 5%
where the time goes in v6:
time: 153 us; the launch traced here: 151 us
  starting transfers between devices  87.2 us (57%)
  waiting for transfers between devices  26.8 us (18%)
  Pallas kernels  16 us (10%)
  between operations  14.3 us (9%)
  local copies, waits for them, and re-layouts  6.14 us (4%)
    ppermute x4, starting transfers between devices, local(): returned[n] = lax.ppermute(terms[n], CTX, routes[n])  17.1 us
    all_to_all x1, starting transfers between devices, local(): column = lax.all_to_all(picked, 'hi', 0, 0)  12.4 us
    all_to_all x1, waiting for transfers between devices, local(): globals_all = lax.all_to_all(chosen, 'lo', 0, 0)  9.28 us
    all_to_all x1, starting transfers between devices, local(): slices = lax.all_to_all(joined.reshape(los, step, width), 'lo', 0, 0)  8.61 us
    ppermute x2, starting transfers between devices, local(): received[n] = lax.ppermute(joined, CTX, routes[n])  8.4 us
    all_to_all x1, starting transfers between devices, local(): lax.all_to_all(jnp.broadcast_to(share[None], (his,) + share.shape), 'hi',...  8.11 us
    all_to_all x1, starting transfers between devices, local(): shares = lax.all_to_all(sums, 'lo', 0, 0)  7.44 us
    ppermute x2, starting transfers between devices, local(): received[n] = lax.ppermute(joined_late, CTX, routes[n])  7.4 us
  transfers between devices with their start and end apart: 18, of which 8 were waited for; matrix products, arithmetic and copies ran while one was open for 1% of the time, Pallas kernels for 5%

profile of v6, /device:TPU:24, one launch (start us, length us, event | category | flops | bytes accessed | tf_op | source)
XLA Modules:
  0.0 150.6 jit_solution(3395510051295871176)
XLA Ops:
  7.2 0.0 copy-start.5
  7.2 0.0 all-gather.5.cloned.1.call-start
  7.2 1.8 %pack.1 = (bf16[512,128]{1,0:T(8,128)(2,1)}, bf16[10,128,128]{2,1,0:T(8,128)(2,1)}) custom-call(bf16[256,128]{1,0:T(8,128)(2,1)} %qk_ref.1, bf16[256,128]{1,0:T(8,128)(2,1)} %val_ref.1, bf16[256,128]{1,0:T(8,128)(2,1)} %gout_ref.1, bf16[128,1024]{1,0:T(8,128)(2,1)} %w_ref.3), custom_call_target="tpu_custom_call" | custom-call | tf_op jit(solution)/shard_map/pack/pallas_call | solution.py:285
  9.1 0.0 all-gather.5.cloned.1.call-update
  9.1 8.6 %all-to-all-start = ((bf16[16,32,128]{2,1,0:T(8,128)(2,1)}), bf16[16,32,128]{2,1,0:T(8,128)(2,1)S(1)}, u32[]{:S(2)}, u32[]{:S(2)}) async-start(bf16[16,32,128]{2,1,0:T(8,128)(2,1)} %bitcast.7), calls=%async_computation | async-start | bytes 262144 | tf_op jit(solution)/shard_map/all_to_all | solution.py:296
  17.7 3.8 %collective-permute-start = (bf16[512,128]{1,0:T(8,128)(2,1)}, bf16[512,128]{1,0:T(8,128)(2,1)S(1)}, u32[]{:S(2)}, u32[]{:S(2)}) collective-permute-start(bf16[512,128]{1,0:T(8,128)(2,1)} %get-tuple-element.58.own_ref), channel_id=1, source_target_pairs={{0,8},{8,0},{16,24},{24,16},{32,40},{40,32},{48,56},{56,48},{64,72... | collective-permute-start | bytes 393224 | tf_op jit(solution)/shard_map/ppermute | solution.py:304
  21.6 4.6 %collective-permute-start.1 = (bf16[512,128]{1,0:T(8,128)(2,1)}, bf16[512,128]{1,0:T(8,128)(2,1)S(1)}, u32[]{:S(2)}, u32[]{:S(2)}) collective-permute-start(bf16[512,128]{1,0:T(8,128)(2,1)} %get-tuple-element.58.own_ref), channel_id=1, source_target_pairs={{0,16},{8,24},{16,0},{24,8},{32,48},{40,56},{48,32},{56,40},{64,80... | collective-permute-start | bytes 393224 | tf_op jit(solution)/shard_map/ppermute | solution.py:304
  26.1 0.0 collective-permute-done.p0
  26.2 0.5 all-to-all-done.slices_ref
  26.7 0.7 copy-done.4
  27.3 1.2 pick.1
  28.6 1.8 %collective-permute-done.1.p2 = bf16[512,128]{1,0:T(8,128)(2,1)S(1)} collective-permute-done((bf16[512,128]{1,0:T(8,128)(2,1)}, bf16[512,128]{1,0:T(8,128)(2,1)S(1)}, u32[]{:S(2)}, u32[]{:S(2)}) %collective-permute-start.1) | collective-permute-done | bytes 131104 | tf_op jit(solution)/shard_map/ppermute | solution.py:304
  30.4 12.4 %all-to-all-start.1 = ((bf16[4,2,32,128]{3,2,1,0:T(8,128)(2,1)}), bf16[4,2,32,128]{3,2,1,0:T(8,128)(2,1)S(1)}, u32[]{:S(2)}, u32[]{:S(2)}) async-start(bf16[4,2,32,128]{3,2,1,0:T(8,128)(2,1)} %pick.1), calls=%async_computation.1 | async-start | bytes 131072 | tf_op jit(solution)/shard_map/all_to_all | solution.py:316
  42.8 4.0 %collective-permute-start.2 = (bf16[512,128]{1,0:T(8,128)(2,1)}, bf16[512,128]{1,0:T(8,128)(2,1)S(1)}, u32[]{:S(2)}, u32[]{:S(2)}) collective-permute-start(bf16[512,128]{1,0:T(8,128)(2,1)} %get-tuple-element.58.own_ref), channel_id=1, source_target_pairs={{0,64},{8,72},{16,80},{24,88},{32,96},{40,104},{48,112},{56,120},{... | collective-permute-start | bytes 393224 | tf_op jit(solution)/shard_map/ppermute | solution.py:318
  46.8 3.4 %collective-permute-start.3 = (bf16[512,128]{1,0:T(8,128)(2,1)}, bf16[512,128]{1,0:T(8,128)(2,1)S(1)}, u32[]{:S(2)}, u32[]{:S(2)}) collective-permute-start(bf16[512,128]{1,0:T(8,128)(2,1)} %get-tuple-element.58.own_ref), channel_id=1, source_target_pairs={{0,32},{8,40},{16,48},{24,56},{32,0},{40,8},{48,16},{56,24},{64,96... | collective-permute-start | bytes 393224 | tf_op jit(solution)/shard_map/ppermute | solution.py:318
  50.2 0.0 all-gather.5.cloned.1.call-done
  50.2 1.7 %copy-done = bf16[80,128,128]{2,1,0:T(8,128)(2,1)S(1)} copy-done((bf16[80,128,128]{2,1,0:T(8,128)(2,1)S(1)}, bf16[80,128,128]{2,1,0:T(8,128)(2,1)}, u32[]{:S(2)}) %copy-start) | copy-done | bytes 2621464
  52.0 0.9 copy-done.1
  52.9 0.3 cotangent.1
  53.3 1.3 collective-permute-done.2.p4
  54.6 2.0 %all-to-all-done.1.slices_ref = bf16[4,2,32,128]{3,2,1,0:T(8,128)(2,1)S(1)} async-done(((bf16[4,2,32,128]{3,2,1,0:T(8,128)(2,1)}), bf16[4,2,32,128]{3,2,1,0:T(8,128)(2,1)S(1)}, u32[]{:S(2)}, u32[]{:S(2)}) %all-to-all-start.1) | async-done | bytes 65568 | tf_op jit(solution)/shard_map/all_to_all | solution.py:316
  56.7 1.5 %spread.1 = bf16[16,2,32,128]{3,2,1,0:T(8,128)(2,1)} custom-call(s32[2]{0:T(128)S(1)} %copy-done.5, bf16[4,2,32,128]{3,2,1,0:T(8,128)(2,1)S(1)} %all-to-all-done.1.slices_ref), custom_call_target="tpu_custom_call" | custom-call | tf_op jit(solution)/shard_map/spread/pallas_call | solution.py:337
  58.2 6.0 %all-to-all-start.2 = ((bf16[16,2,32,128]{3,2,1,0:T(8,128)(2,1)}), bf16[16,2,32,128]{3,2,1,0:T(8,128)(2,1)S(1)}, u32[]{:S(2)}, u32[]{:S(2)}) async-start(bf16[16,2,32,128]{3,2,1,0:T(8,128)(2,1)} %spread.1), calls=%async_computation.2 | async-start | bytes 524288 | tf_op jit(solution)/shard_map/all_to_all | solution.py:347
  64.2 0.7 collective-permute-start.4
  64.9 0.0 collective-permute-done.4.p1
  64.9 9.3 %all-to-all-done.2.glob_ref = bf16[16,2,32,128]{3,2,1,0:T(8,128)(2,1)S(1)} async-done(((bf16[16,2,32,128]{3,2,1,0:T(8,128)(2,1)}), bf16[16,2,32,128]{3,2,1,0:T(8,128)(2,1)S(1)}, u32[]{:S(2)}, u32[]{:S(2)}) %all-to-all-start.2) | async-done | bytes 262176 | tf_op jit(solution)/shard_map/all_to_all | solution.py:347
  74.2 4.6 %forward.1 = (f32[256,128]{1,0:T(8,128)}, bf16[16,128,128]{2,1,0:T(8,128)(2,1)}, f32[256,128]{1,0:T(8,128)S(1)}, f32[256,128]{1,0:T(8,128)S(1)}) custom-call(s32[1]{0:T(128)} %bitcast.pos_ref, s32[4,32]{1,0:T(4,128)S(1)} %copy-done.6, bf16[512,128]{1,0:T(8,128)(2,1)S(1)} %copy-done.3, bf16[512,128]{1,0:T(8,128)(2,1)S(1)} %collective-permute-done.p0, ...), custom_call_target="tpu_custom_call" | custom-call | flops 3000000000 | bytes 4000000 | tf_op jit(solution)/shard_map/forward/pallas_call | solution.py:353
  78.8 7.4 %all-to-all-start.3 = ((bf16[16,128,128]{2,1,0:T(8,128)(2,1)}), bf16[16,128,128]{2,1,0:T(8,128)(2,1)S(1)}, u32[]{:S(2)}, u32[]{:S(2)}) async-start(bf16[16,128,128]{2,1,0:T(8,128)(2,1)} %get-tuple-element.65), calls=%async_computation.3 | async-start | bytes 1048576 | tf_op jit(solution)/shard_map/all_to_all | solution.py:374
  86.3 0.0 all-gather.7.cloned.1.call-start
  86.3 0.7 all-gather.7.cloned.1.call-update
  87.0 3.9 %backward.1 = (bf16[256,256]{1,0:T(8,128)(2,1)S(1)}, bf16[256,256]{1,0:T(8,128)(2,1)S(1)}, bf16[256,256]{1,0:T(8,128)(2,1)S(1)}, bf16[256,256]{1,0:T(8,128)(2,1)...) custom-call(s32[1]{0:T(128)} %bitcast.pos_ref, s32[4,32]{1,0:T(4,128)S(1)} %copy-done.6, ...), custom_call_target="tpu_custom_call" | custom-call | flops 3000000000 | bytes 4000000 | tf_op jit(solution)/shard_map/backward/pallas_call | solution.py:376
  90.9 3.8 %collective-permute-start.5 = (bf16[256,256]{1,0:T(8,128)(2,1)S(1)}, bf16[256,256]{1,0:T(8,128)(2,1)S(1)}, u32[]{:S(2)}, u32[]{:S(2)}) collective-permute-start(bf16[256,256]{1,0:T(8,128)(2,1)S(1)} %get-tuple-element.68), channel_id=1, source_target_pairs={{0,8},{8,0},{16,24},{24,16},{32,40},{40,32},{48,56},{56,48},{64,72... | collective-permute-start | bytes 393224 | tf_op jit(solution)/shard_map/ppermute | solution.py:392
  94.8 3.8 %all-to-all-done.3 = bf16[16,128,128]{2,1,0:T(8,128)(2,1)S(1)} async-done(((bf16[16,128,128]{2,1,0:T(8,128)(2,1)}), bf16[16,128,128]{2,1,0:T(8,128)(2,1)S(1)}, u32[]{:S(2)}, u32[]{:S(2)}) %all-to-all-start.3) | async-done | bytes 524320 | tf_op jit(solution)/shard_map/all_to_all | solution.py:374
  98.6 0.1 reduce_sum.24
  98.6 0.7 broadcast_in_dim.10
  99.3 8.1 %all-to-all-start.4 = ((bf16[4,128,128]{2,1,0:T(8,128)(2,1)}), bf16[4,128,128]{2,1,0:T(8,128)(2,1)S(1)}, u32[]{:S(2)}, u32[]{:S(2)}) async-start(bf16[4,128,128]{2,1,0:T(8,128)(2,1)} %broadcast_in_dim.10), calls=%async_computation.4 | async-start | bytes 262144 | tf_op jit(solution)/shard_map/all_to_all | solution.py:396
  107.4 4.5 %collective-permute-start.6 = (bf16[256,256]{1,0:T(8,128)(2,1)S(1)}, bf16[256,256]{1,0:T(8,128)(2,1)S(1)}, u32[]{:S(2)}, u32[]{:S(2)}) collective-permute-start(bf16[256,256]{1,0:T(8,128)(2,1)S(1)} %get-tuple-element.75), channel_id=1, source_target_pairs={{0,16},{8,24},{16,0},{24,8},{32,48},{40,56},{48,32},{56,40},{64,80... | collective-permute-start | bytes 393224 | tf_op jit(solution)/shard_map/ppermute | solution.py:398
  111.9 4.3 %collective-permute-start.7 = (bf16[256,256]{1,0:T(8,128)(2,1)S(1)}, bf16[256,256]{1,0:T(8,128)(2,1)S(1)}, u32[]{:S(2)}, u32[]{:S(2)}) collective-permute-start(bf16[256,256]{1,0:T(8,128)(2,1)S(1)} %get-tuple-element.76), channel_id=1, source_target_pairs={{0,64},{8,72},{16,80},{24,88},{32,96},{40,104},{48,112},{56,120},{... | collective-permute-start | bytes 393224 | tf_op jit(solution)/shard_map/ppermute | solution.py:398
  116.2 5.3 %collective-permute-done.7.b4 = bf16[256,256]{1,0:T(8,128)(2,1)S(1)} collective-permute-done((bf16[256,256]{1,0:T(8,128)(2,1)S(1)}, bf16[256,256]{1,0:T(8,128)(2,1)S(1)}, u32[]{:S(2)}, u32[]{:S(2)}) %collective-permute-start.7) | collective-permute-done | bytes 131104 | tf_op jit(solution)/shard_map/ppermute | solution.py:398
  121.6 0.0 all-gather.7.cloned.1.call-done
  121.6 0.9 broadcast_in_dim.11
  122.5 7.1 %all-to-all-start.5 = ((bf16[16,128,128]{2,1,0:T(8,128)(2,1)}), bf16[16,128,128]{2,1,0:T(8,128)(2,1)S(1)}, u32[]{:S(2)}, u32[]{:S(2)}) async-start(bf16[16,128,128]{2,1,0:T(8,128)(2,1)} %broadcast_in_dim.11), calls=%async_computation.5 | async-start | bytes 1048576 | tf_op jit(solution)/shard_map/all_to_all | solution.py:402
  129.6 0.7 collective-permute-start.8
  130.3 7.7 %collective-permute-start.9 = (bf16[256,256]{1,0:T(8,128)(2,1)S(1)}, bf16[256,256]{1,0:T(8,128)(2,1)S(1)}, u32[]{:S(2)}, u32[]{:S(2)}) collective-permute-start(bf16[256,256]{1,0:T(8,128)(2,1)S(1)} %get-tuple-element.84), channel_id=1, source_target_pairs={{0,32},{8,40},{16,48},{24,56},{32,0},{40,8},{48,16},{56,24},{64,96... | collective-permute-start | bytes 393224 | tf_op jit(solution)/shard_map/ppermute | solution.py:398
  138.1 1.2 copy-done.2
  139.3 0.9 project.1
  140.2 1.9 %collective-permute-done.9.b3 = bf16[256,256]{1,0:T(8,128)(2,1)S(1)} collective-permute-done((bf16[256,256]{1,0:T(8,128)(2,1)S(1)}, bf16[256,256]{1,0:T(8,128)(2,1)S(1)}, u32[]{:S(2)}, u32[]{:S(2)}) %collective-permute-start.9) | collective-permute-done | bytes 131104 | tf_op jit(solution)/shard_map/ppermute | solution.py:398
  142.1 1.6 %finish.1 = (bf16[256,128]{1,0:T(8,128)(2,1)}, bf16[256,128]{1,0:T(8,128)(2,1)}, f32[128,1024]{1,0:T(8,128)}) custom-call(s32[1]{0:T(128)} %bitcast.pos_ref, s32[2]{0:T(128)S(1)} %copy-done.5, bf16[256,256]{1,0:T(8,128)(2,1)S(1)} %collective-permute-done.5.b0, bf16[256,256]{1,0:T(8,128)(2,1)S(1)} %collective-permute-done.8.b1, ...), custom_call_target="tpu_custom_call" | custom-call | flops 2000000 | bytes 2500000 | tf_op jit(solution)/shard_map/finish/pallas_call | solution.py:415
  (16 shorter events, 0.1 us)
Async XLA Ops:
  7.2 49.5 %copy-start.5 = (s32[2]{0:T(128)S(1)}, s32[2]{0:T(128)}, u32[]{:S(2)}) copy-start(s32[2]{0:T(128)} %ids_ref.5) | copy-start | bytes 28
  7.2 67.0 %copy-start.6 = (s32[4,32]{1,0:T(4,128)S(1)}, s32[4,32]{1,0:T(4,128)}, u32[]{:S(2)}) copy-start(s32[4,32]{1,0:T(4,128)} %pair_ref.3) | copy-start | bytes 1540
  7.2 43.0 %all-gather.5.cloned.1.call-start = ((), (), s32[]{:S(2)}) async-start(), calls=%async_computation.6 | async-start | bytes 2949120 | tf_op jit(solution)/shard_map/all_gather | solution.py:297
  9.1 55.1 %copy-start.3 = (bf16[512,128]{1,0:T(8,128)(2,1)S(1)}, bf16[512,128]{1,0:T(8,128)(2,1)}, u32[]{:S(2)}) copy-start(bf16[512,128]{1,0:T(8,128)(2,1)} %get-tuple-element.58.own_ref) | copy-start | bytes 393220
  9.1 17.6 %all-to-all-start = ((bf16[16,32,128]{2,1,0:T(8,128)(2,1)}), bf16[16,32,128]{2,1,0:T(8,128)(2,1)S(1)}, u32[]{:S(2)}, u32[]{:S(2)}) async-start(bf16[16,32,128]{2,1,0:T(8,128)(2,1)} %bitcast.7), calls=%async_computation | async-start | bytes 262144 | tf_op jit(solution)/shard_map/all_to_all | solution.py:296
  17.7 8.4 %collective-permute-start = (bf16[512,128]{1,0:T(8,128)(2,1)}, bf16[512,128]{1,0:T(8,128)(2,1)S(1)}, u32[]{:S(2)}, u32[]{:S(2)}) collective-permute-start(bf16[512,128]{1,0:T(8,128)(2,1)} %get-tuple-element.58.own_ref), channel_id=1, source_target_pairs={{0,8},{8,0},{16,24},{24,16},{32,40},{40,32},{48,56},{56,48},{64,72... | collective-permute-start | bytes 393224 | tf_op jit(solution)/shard_map/ppermute | solution.py:304
  21.6 8.8 %collective-permute-start.1 = (bf16[512,128]{1,0:T(8,128)(2,1)}, bf16[512,128]{1,0:T(8,128)(2,1)S(1)}, u32[]{:S(2)}, u32[]{:S(2)}) collective-permute-start(bf16[512,128]{1,0:T(8,128)(2,1)} %get-tuple-element.58.own_ref), channel_id=1, source_target_pairs={{0,16},{8,24},{16,0},{24,8},{32,48},{40,56},{48,32},{56,40},{64,80... | collective-permute-start | bytes 393224 | tf_op jit(solution)/shard_map/ppermute | solution.py:304
  26.7 0.7 copy-start.4
  30.4 26.3 %all-to-all-start.1 = ((bf16[4,2,32,128]{3,2,1,0:T(8,128)(2,1)}), bf16[4,2,32,128]{3,2,1,0:T(8,128)(2,1)S(1)}, u32[]{:S(2)}, u32[]{:S(2)}) async-start(bf16[4,2,32,128]{3,2,1,0:T(8,128)(2,1)} %pick.1), calls=%async_computation.1 | async-start | bytes 131072 | tf_op jit(solution)/shard_map/all_to_all | solution.py:316
  42.8 11.8 %collective-permute-start.2 = (bf16[512,128]{1,0:T(8,128)(2,1)}, bf16[512,128]{1,0:T(8,128)(2,1)S(1)}, u32[]{:S(2)}, u32[]{:S(2)}) collective-permute-start(bf16[512,128]{1,0:T(8,128)(2,1)} %get-tuple-element.58.own_ref), channel_id=1, source_target_pairs={{0,64},{8,72},{16,80},{24,88},{32,96},{40,104},{48,112},{56,120},{... | collective-permute-start | bytes 393224 | tf_op jit(solution)/shard_map/ppermute | solution.py:318
  46.8 11.4 %collective-permute-start.3 = (bf16[512,128]{1,0:T(8,128)(2,1)}, bf16[512,128]{1,0:T(8,128)(2,1)S(1)}, u32[]{:S(2)}, u32[]{:S(2)}) collective-permute-start(bf16[512,128]{1,0:T(8,128)(2,1)} %get-tuple-element.58.own_ref), channel_id=1, source_target_pairs={{0,32},{8,40},{16,48},{24,56},{32,0},{40,8},{48,16},{56,24},{64,96... | collective-permute-start | bytes 393224 | tf_op jit(solution)/shard_map/ppermute | solution.py:318
  50.2 1.7 %copy-start = (bf16[80,128,128]{2,1,0:T(8,128)(2,1)S(1)}, bf16[80,128,128]{2,1,0:T(8,128)(2,1)}, u32[]{:S(2)}) copy-start(bf16[80,128,128]{2,1,0:T(8,128)(2,1)} %all-gather.5.cloned.1.call-done) | copy-start | bytes 7864324
  52.0 0.9 copy-start.1
  58.2 16.0 %all-to-all-start.2 = ((bf16[16,2,32,128]{3,2,1,0:T(8,128)(2,1)}), bf16[16,2,32,128]{3,2,1,0:T(8,128)(2,1)S(1)}, u32[]{:S(2)}, u32[]{:S(2)}) async-start(bf16[16,2,32,128]{3,2,1,0:T(8,128)(2,1)} %spread.1), calls=%async_computation.2 | async-start | bytes 524288 | tf_op jit(solution)/shard_map/all_to_all | solution.py:347
  64.2 0.7 collective-permute-start.4
  78.8 19.7 %all-to-all-start.3 = ((bf16[16,128,128]{2,1,0:T(8,128)(2,1)}), bf16[16,128,128]{2,1,0:T(8,128)(2,1)S(1)}, u32[]{:S(2)}, u32[]{:S(2)}) async-start(bf16[16,128,128]{2,1,0:T(8,128)(2,1)} %get-tuple-element.65), calls=%async_computation.3 | async-start | bytes 1048576 | tf_op jit(solution)/shard_map/all_to_all | solution.py:374
  86.3 35.3 %all-gather.7.cloned.1.call-start = ((), (), s32[]{:S(2)}) async-start(), calls=%async_computation.7 | async-start | bytes 1179648 | tf_op jit(solution)/shard_map/all_gather | solution.py:375
  90.9 7.7 %collective-permute-start.5 = (bf16[256,256]{1,0:T(8,128)(2,1)S(1)}, bf16[256,256]{1,0:T(8,128)(2,1)S(1)}, u32[]{:S(2)}, u32[]{:S(2)}) collective-permute-start(bf16[256,256]{1,0:T(8,128)(2,1)S(1)} %get-tuple-element.68), channel_id=1, source_target_pairs={{0,8},{8,0},{16,24},{24,16},{32,40},{40,32},{48,56},{56,48},{64,72... | collective-permute-start | bytes 393224 | tf_op jit(solution)/shard_map/ppermute | solution.py:392
  99.3 22.2 %all-to-all-start.4 = ((bf16[4,128,128]{2,1,0:T(8,128)(2,1)}), bf16[4,128,128]{2,1,0:T(8,128)(2,1)S(1)}, u32[]{:S(2)}, u32[]{:S(2)}) async-start(bf16[4,128,128]{2,1,0:T(8,128)(2,1)} %broadcast_in_dim.10), calls=%async_computation.4 | async-start | bytes 262144 | tf_op jit(solution)/shard_map/all_to_all | solution.py:396
  107.4 8.8 %collective-permute-start.6 = (bf16[256,256]{1,0:T(8,128)(2,1)S(1)}, bf16[256,256]{1,0:T(8,128)(2,1)S(1)}, u32[]{:S(2)}, u32[]{:S(2)}) collective-permute-start(bf16[256,256]{1,0:T(8,128)(2,1)S(1)} %get-tuple-element.75), channel_id=1, source_target_pairs={{0,16},{8,24},{16,0},{24,8},{32,48},{40,56},{48,32},{56,40},{64,80... | collective-permute-start | bytes 393224 | tf_op jit(solution)/shard_map/ppermute | solution.py:398
  111.9 9.6 %collective-permute-start.7 = (bf16[256,256]{1,0:T(8,128)(2,1)S(1)}, bf16[256,256]{1,0:T(8,128)(2,1)S(1)}, u32[]{:S(2)}, u32[]{:S(2)}) collective-permute-start(bf16[256,256]{1,0:T(8,128)(2,1)S(1)} %get-tuple-element.76), channel_id=1, source_target_pairs={{0,64},{8,72},{16,80},{24,88},{32,96},{40,104},{48,112},{56,120},{... | collective-permute-start | bytes 393224 | tf_op jit(solution)/shard_map/ppermute | solution.py:398
  122.5 19.6 %all-to-all-start.5 = ((bf16[16,128,128]{2,1,0:T(8,128)(2,1)}), bf16[16,128,128]{2,1,0:T(8,128)(2,1)S(1)}, u32[]{:S(2)}, u32[]{:S(2)}) async-start(bf16[16,128,128]{2,1,0:T(8,128)(2,1)} %broadcast_in_dim.11), calls=%async_computation.5 | async-start | bytes 1048576 | tf_op jit(solution)/shard_map/all_to_all | solution.py:402
  129.6 10.6 %collective-permute-start.8 = (bf16[256,256]{1,0:T(8,128)(2,1)S(1)}, bf16[256,256]{1,0:T(8,128)(2,1)S(1)}, u32[]{:S(2)}, u32[]{:S(2)}) collective-permute-start(bf16[256,256]{1,0:T(8,128)(2,1)S(1)} %get-tuple-element.82), channel_id=1, source_target_pairs={{8,16},{16,8},{24,32},{32,24},{40,48},{48,40},{56,64},{64,56},{72,... | collective-permute-start | bytes 393224 | tf_op jit(solution)/shard_map/ppermute | solution.py:398
  130.3 11.8 %collective-permute-start.9 = (bf16[256,256]{1,0:T(8,128)(2,1)S(1)}, bf16[256,256]{1,0:T(8,128)(2,1)S(1)}, u32[]{:S(2)}, u32[]{:S(2)}) collective-permute-start(bf16[256,256]{1,0:T(8,128)(2,1)S(1)} %get-tuple-element.84), channel_id=1, source_target_pairs={{0,32},{8,40},{16,48},{24,56},{32,0},{40,8},{48,16},{56,24},{64,96... | collective-permute-start | bytes 393224 | tf_op jit(solution)/shard_map/ppermute | solution.py:398
  138.1 1.2 copy-start.2
Sparse Core Ops, SparseCore 0:
  10.7 37.0 all-gather.4
  89.3 27.3 all-gather.6

commit v7 on v6

--- a/solution.py
+++ b/solution.py
@@ -54,8 +54,43 @@
     gatt_ref[...] = gatt.astype(BF16)
 
 
+def near_kernel(
+    pos_ref, pair_ref, own_ref, p0, p2, p3, p4, stats_ref, sum_ref, score_ref,
+):
+    length = own_ref.shape[0] // 2
+    width = own_ref.shape[1]
+    nheads = width // HD
+    base2 = 1.0 / math.sqrt(HD) / math.log(2.0)
+    bias = block_bias(pos_ref, pair_ref)
+    blocks = ((own_ref, bias[0]), (p0, bias[1]), (p2, bias[3]), (p3, bias[4]), (p4, bias[5]))
+    query = own_ref[:length]
+    lane = lax.broadcasted_iota(jnp.int32, (1, width), 1)
+    head = lane // HD
+    stats = jnp.zeros((length, width), F32)
+    for h in range(nheads):
+        query_h = jnp.where(head == h, query, jnp.zeros_like(query))
+        highest = jnp.full((length, 1), MASKED, F32)
+        for b, (ref, shift) in enumerate(blocks):
+            s = dot(query_h, ref[:length], NT) * base2 + shift
+            score_ref[:, b * length:(b + 1) * length] = s
+            highest = jnp.maximum(highest, jnp.max(s, axis=1, keepdims=True))
+        total = jnp.zeros((length, 1), F32)
+        acc = jnp.zeros((length, width), F32)
+        for b, (ref, _) in enumerate(blocks):
+            e = jnp.exp2(score_ref[:, b * length:(b + 1) * length] - highest)
+            total = total + jnp.sum(e, axis=1, keepdims=True)
+            acc = acc + dot(e.astype(BF16), ref[length:], NN)
+        stats = jnp.where(lane == h, highest, stats)
+        stats = jnp.where(lane == nheads + h, total, stats)
+        if h == 0:
+            sum_ref[...] = acc
+        else:
+            sum_ref[...] = jnp.where(head == h, acc, sum_ref[...])
+    stats_ref[...] = stats
+
+
 def forward_kernel(
-    pos_ref, pair_ref, own_ref, p0, p1, p2, p3, p4, glob_ref, gout_ref, gatt_ref,
+    pos_ref, pair_ref, own_ref, p1, near_ref, sum_ref, glob_ref, gout_ref, gatt_ref,
     att_ref, sums_ref, stats_ref, gquery_ref,
     score_ref, out_ref,
 ):
@@ -66,8 +101,9 @@
     scaling = 1.0 / math.sqrt(HD)
     base2 = scaling / math.log(2.0)
     bias = block_bias(pos_ref, pair_ref)
-    keys = [r[:length] for r in (own_ref, p0, p1, p2, p3, p4)]
-    vals = [r[length:] for r in (own_ref, p0, p1, p2, p3, p4)]
+    bias = [bias[2]] + bias[-NGLOB:]
+    keys = [p1[:length]]
+    vals = [p1[length:]]
     half = glob_ref.shape[0] // 2
     for g in range(NGLOB):
         keys.append(jnp.concatenate([glob_ref[p, g] for p in range(half)], axis=0))
@@ -82,27 +118,27 @@
     stats = jnp.zeros((length, width), F32)
     for h in range(nheads):
         query_h = jnp.where(head == h, query, jnp.zeros_like(query))
-        highest = jnp.full((length, 1), MASKED, F32)
+        near = near_ref[:, h:h + 1]
+        highest = near
         for b in range(count):
             s = dot(query_h, keys[b], NT) * base2 + bias[b]
             score_ref[h, :, b * length:(b + 1) * length] = s
             highest = jnp.maximum(highest, jnp.max(s, axis=1, keepdims=True))
-        total = jnp.zeros((length, 1), F32)
+        factor = jnp.exp2(near - highest)
+        total = near_ref[:, nheads + h:nheads + h + 1] * factor
+        acc = sum_ref[...] * factor
         for b in range(count):
             e = jnp.exp2(score_ref[h, :, b * length:(b + 1) * length] - highest)
             score_ref[h, :, b * length:(b + 1) * length] = e
             total = total + jnp.sum(e, axis=1, keepdims=True)
+            acc = acc + dot(e.astype(BF16), vals[b], NN)
         inv = 1.0 / total
         inverse.append(inv)
         stats = jnp.where(lane == h, highest + jnp.log2(total), stats)
-        acc = jnp.zeros((length, width), F32)
-        for b in range(count):
-            e = score_ref[h, :, b * length:(b + 1) * length]
-            acc = acc + dot((e * inv).astype(BF16), vals[b], NN)
         if h == 0:
-            out_ref[...] = acc
+            out_ref[...] = acc * inv
         else:
-            out_ref[...] = jnp.where(head == h, acc, out_ref[...])
+            out_ref[...] = jnp.where(head == h, acc * inv, out_ref[...])
 
     attended = out_ref[...]
     att_ref[...] = attended
@@ -218,21 +254,25 @@
         gweight_ref[:, c * 128:(c + 1) * 128] = piece.astype(F32)
 
 
-def pack_kernel(qk_ref, val_ref, gout_ref, w_ref, joined_ref, share_ref):
-    length, width = qk_ref.shape
-    blocks = length // 128
-    joined_ref[:length] = qk_ref[...]
-    joined_ref[length:] = val_ref[...]
-    share_ref[0:blocks] = gout_ref[...].reshape(blocks, 128, width)
-    for c in range(w_ref.shape[1] // 128):
-        share_ref[blocks + c] = w_ref[:, c * 128:(c + 1) * 128]
-
-
 def copy_all(copies):
     for copy in copies:
         copy.start()
     for copy in copies:
         copy.wait()
+
+
+def pack_kernel(qk_ref, val_ref, gout_ref, w_ref, joined_ref, share_ref, sems):
+    length = qk_ref.shape[0]
+    blocks = length // 128
+    pairs = [
+        (qk_ref, joined_ref.at[pl.ds(0, length)]),
+        (val_ref, joined_ref.at[pl.ds(length, length)]),
+    ]
+    for b in range(blocks):
+        pairs.append((gout_ref.at[pl.ds(b * 128, 128)], share_ref.at[b]))
+    for c in range(w_ref.shape[1] // 128):
+        pairs.append((w_ref.at[:, pl.ds(c * 128, 128)], share_ref.at[blocks + c]))
+    copy_all([pltpu.make_async_copy(a, b, sems.at[n]) for n, (a, b) in enumerate(pairs)])
 
 
 def pick_kernel(ids_ref, slices_ref, out_ref, sems):
@@ -288,8 +328,9 @@
             jax.ShapeDtypeStruct((2 * length, width), BF16),
             jax.ShapeDtypeStruct((length // 128 + pieces, 128, width), BF16),
         ),
-        in_specs=vmem(4),
-        out_specs=tuple(vmem(2)),
+        in_specs=[anywhere()] * 4,
+        out_specs=(anywhere(), anywhere()),
+        scratch_shapes=[pltpu.SemaphoreType.DMA((2 + length // 128 + pieces,))],
         name="pack",
     )(qk_vectors, token_values, grad_output, out_weight)
 
@@ -346,10 +387,24 @@
     chosen, joined_late, received[3] = lax.optimization_barrier((chosen, joined, received[3]))
     globals_all = lax.all_to_all(chosen, "lo", 0, 0)
     received[1] = lax.ppermute(joined_late, CTX, routes[1])
-    count = ROUNDS + 2 + NGLOB
     nheads = width // HD
     block = jax.ShapeDtypeStruct((2 * width, length), BF16)
     square = jax.ShapeDtypeStruct((length, width), F32)
+    near_stats, near_sum = pl.pallas_call(
+        near_kernel,
+        out_shape=(square, square),
+        in_specs=[smem()] * 2 + vmem(5),
+        out_specs=tuple(vmem(2)),
+        scratch_shapes=[pltpu.VMEM((length, 5 * length), F32)],
+        compiler_params=limit(12),
+        cost_estimate=pl.CostEstimate(
+            flops=1_000_000_000, bytes_accessed=1_000_000, transcendentals=650_000
+        ),
+        name="near",
+    )(position[None], pair_active, joined, received[0], *received[2:])
+    globals_all, near_stats, near_sum = lax.optimization_barrier(
+        (globals_all, near_stats, near_sum)
+    )
     attended, sums, stats, gglob = pl.pallas_call(
         forward_kernel,
         out_shape=(
@@ -358,10 +413,10 @@
             square,
             square,
         ),
-        in_specs=[smem()] * 2 + vmem(9),
+        in_specs=[smem()] * 2 + vmem(7),
         out_specs=tuple(vmem(4)),
         scratch_shapes=[
-            pltpu.VMEM((nheads, length, count * length), F32),
+            pltpu.VMEM((nheads, length, (1 + NGLOB) * length), F32),
             pltpu.VMEM((length, width), F32),
         ],
         compiler_params=limit(20),
@@ -369,7 +424,10 @@
             flops=3_000_000_000, bytes_accessed=4_000_000, transcendentals=1_100_000
         ),
         name="forward",
-    )(position[None], pair_active, joined, *received, globals_all, portion_b, gatt)
+    )(
+        position[None], pair_active, joined, received[1], near_stats, near_sum,
+        globals_all, portion_b, gatt,
+    )
 
     shares = lax.all_to_all(sums, "lo", 0, 0)
     attended_all = lax.all_gather(attended, HEAD, axis=0)
@@ -396,7 +454,7 @@
     column = lax.all_to_all(jnp.broadcast_to(share[None], (his,) + share.shape), "hi", 0, 0)
     for n in (4, 2, 3, 1):
         returned[n] = lax.ppermute(terms[n], CTX, routes[n])
-    column, returned[2], returned[4] = lax.optimization_barrier((column, returned[2], returned[4]))
+    column, returned[4], returned[2] = lax.optimization_barrier((column, returned[4], returned[2]))
     share = jnp.sum(column.astype(F32), axis=0).astype(BF16)
     share, attended_all = lax.optimization_barrier((share, attended_all))
     totals = lax.all_to_all(jnp.broadcast_to(share[None], (los,) + share.shape), "lo", 0, 0)

time: 153 us -> 166 us (1.085)
  Pallas kernels: 16 us -> 31 us
  waiting for transfers between devices: 26.8 us -> 24.8 us
    pallas_call x1, Pallas kernels: 1.85 us -> 15.1 us  [local(): pl.pallas_call(pack_kernel, out_shape=(jax.ShapeDtypeStruct((2 * length,...]
    all_to_all x1, waiting for transfers between devices: 9.28 us -> 7.41 us  [local(): globals_all = lax.all_to_all(chosen, 'lo', 0, 0)]
    pallas_call x0 -> x1, Pallas kernels: none -> 1.86 us  [local(): pl.pallas_call(near_kernel, out_shape=(square, square), in_specs=[smem()]...]
  transfers between devices with their start and end apart: 18 -> 18, of which waited for: 8 -> 10; matrix products, arithmetic and copies ran while one was open for 1% -> 0% of each run, Pallas kernels for 5% -> 6%
where the time goes in v7:
time: 166 us; the launch traced here: 164 us
  starting transfers between devices  87.3 us (53%)
  Pallas kernels  31 us (19%)
  waiting for transfers between devices  24.8 us (15%)
  between operations  14.3 us (9%)
  local copies, waits for them, and re-layouts  6.14 us (4%)
    ppermute x4, starting transfers between devices, local(): returned[n] = lax.ppermute(terms[n], CTX, routes[n])  17.1 us
    pallas_call x1, Pallas kernels, local(): pl.pallas_call(pack_kernel, out_shape=(jax.ShapeDtypeStruct((2 * length,...  15.1 us
    all_to_all x1, starting transfers between devices, local(): column = lax.all_to_all(picked, 'hi', 0, 0)  12.4 us
    all_to_all x1, starting transfers between devices, local(): slices = lax.all_to_all(joined.reshape(los, step, width), 'lo', 0, 0)  8.61 us
    ppermute x2, starting transfers between devices, local(): received[n] = lax.ppermute(joined, CTX, routes[n])  8.4 us
    all_to_all x1, starting transfers between devices, local(): lax.all_to_all(jnp.broadcast_to(share[None], (his,) + share.shape), 'hi',...  8.13 us
    all_to_all x1, starting transfers between devices, local(): shares = lax.all_to_all(sums, 'lo', 0, 0)  7.43 us
    all_to_all x1, waiting for transfers between devices, local(): globals_all = lax.all_to_all(chosen, 'lo', 0, 0)  7.41 us
  transfers between devices with their start and end apart: 18, of which 10 were waited for; matrix products, arithmetic and copies ran while one was open for 0% of the time, Pallas kernels for 6%

profile of v7, /device:TPU:24, one launch (start us, length us, event | category | flops | bytes accessed | tf_op | source)
XLA Modules:
  0.0 163.7 jit_solution(16319728110387227278)
XLA Ops:
  7.2 0.0 all-gather.5.cloned.1.call-start
  7.2 15.1 %pack.1 = (bf16[512,128]{1,0:T(8,128)(2,1)}, bf16[10,128,128]{2,1,0:T(8,128)(2,1)}) custom-call(bf16[256,128]{1,0:T(8,128)(2,1)} %qk_ref.1, bf16[256,128]{1,0:T(8,128)(2,1)} %val_ref.1, bf16[256,128]{1,0:T(8,128)(2,1)} %gout_ref.1, bf16[128,1024]{1,0:T(8,128)(2,1)} %w_ref.3), custom_call_target="tpu_custom_call" | custom-call | tf_op jit(solution)/shard_map/pack/pallas_call | solution.py:325
  22.4 0.0 all-gather.5.cloned.1.call-update
  22.4 8.6 %all-to-all-start = ((bf16[16,32,128]{2,1,0:T(8,128)(2,1)}), bf16[16,32,128]{2,1,0:T(8,128)(2,1)S(1)}, u32[]{:S(2)}, u32[]{:S(2)}) async-start(bf16[16,32,128]{2,1,0:T(8,128)(2,1)} %bitcast.7), calls=%async_computation | async-start | bytes 262144 | tf_op jit(solution)/shard_map/all_to_all | solution.py:337
  31.0 3.8 %collective-permute-start = (bf16[512,128]{1,0:T(8,128)(2,1)}, bf16[512,128]{1,0:T(8,128)(2,1)S(1)}, u32[]{:S(2)}, u32[]{:S(2)}) collective-permute-start(bf16[512,128]{1,0:T(8,128)(2,1)} %get-tuple-element.62.own_ref), channel_id=1, source_target_pairs={{0,8},{8,0},{16,24},{24,16},{32,40},{40,32},{48,56},{56,48},{64,72... | collective-permute-start | bytes 393224 | tf_op jit(solution)/shard_map/ppermute | solution.py:345
  34.8 4.6 %collective-permute-start.1 = (bf16[512,128]{1,0:T(8,128)(2,1)}, bf16[512,128]{1,0:T(8,128)(2,1)S(1)}, u32[]{:S(2)}, u32[]{:S(2)}) collective-permute-start(bf16[512,128]{1,0:T(8,128)(2,1)} %get-tuple-element.62.own_ref), channel_id=1, source_target_pairs={{0,16},{8,24},{16,0},{24,8},{32,48},{40,56},{48,32},{56,40},{64,80... | collective-permute-start | bytes 393224 | tf_op jit(solution)/shard_map/ppermute | solution.py:345
  39.4 0.5 all-to-all-done.slices_ref
  39.9 0.7 copy-done.4
  40.6 1.2 pick.1
  41.8 1.8 %collective-permute-done.1.p2 = bf16[512,128]{1,0:T(8,128)(2,1)S(1)} collective-permute-done((bf16[512,128]{1,0:T(8,128)(2,1)}, bf16[512,128]{1,0:T(8,128)(2,1)S(1)}, u32[]{:S(2)}, u32[]{:S(2)}) %collective-permute-start.1) | collective-permute-done | bytes 131104 | tf_op jit(solution)/shard_map/ppermute | solution.py:345
  43.7 12.4 %all-to-all-start.1 = ((bf16[4,2,32,128]{3,2,1,0:T(8,128)(2,1)}), bf16[4,2,32,128]{3,2,1,0:T(8,128)(2,1)S(1)}, u32[]{:S(2)}, u32[]{:S(2)}) async-start(bf16[4,2,32,128]{3,2,1,0:T(8,128)(2,1)} %pick.1), calls=%async_computation.1 | async-start | bytes 131072 | tf_op jit(solution)/shard_map/all_to_all | solution.py:357
  56.1 4.0 %collective-permute-start.2 = (bf16[512,128]{1,0:T(8,128)(2,1)}, bf16[512,128]{1,0:T(8,128)(2,1)S(1)}, u32[]{:S(2)}, u32[]{:S(2)}) collective-permute-start(bf16[512,128]{1,0:T(8,128)(2,1)} %get-tuple-element.62.own_ref), channel_id=1, source_target_pairs={{0,64},{8,72},{16,80},{24,88},{32,96},{40,104},{48,112},{56,120},{... | collective-permute-start | bytes 393224 | tf_op jit(solution)/shard_map/ppermute | solution.py:359
  60.1 3.4 %collective-permute-start.3 = (bf16[512,128]{1,0:T(8,128)(2,1)}, bf16[512,128]{1,0:T(8,128)(2,1)S(1)}, u32[]{:S(2)}, u32[]{:S(2)}) collective-permute-start(bf16[512,128]{1,0:T(8,128)(2,1)} %get-tuple-element.62.own_ref), channel_id=1, source_target_pairs={{0,32},{8,40},{16,48},{24,56},{32,0},{40,8},{48,16},{56,24},{64,96... | collective-permute-start | bytes 393224 | tf_op jit(solution)/shard_map/ppermute | solution.py:359
  63.5 0.0 all-gather.5.cloned.1.call-done
  63.5 1.7 %copy-done = bf16[80,128,128]{2,1,0:T(8,128)(2,1)S(1)} copy-done((bf16[80,128,128]{2,1,0:T(8,128)(2,1)S(1)}, bf16[80,128,128]{2,1,0:T(8,128)(2,1)}, u32[]{:S(2)}) %copy-start) | copy-done | bytes 2621464
  65.3 0.9 copy-done.1
  66.2 0.3 cotangent.1
  66.6 1.3 collective-permute-done.2.p4
  67.9 2.0 %all-to-all-done.1.slices_ref = bf16[4,2,32,128]{3,2,1,0:T(8,128)(2,1)S(1)} async-done(((bf16[4,2,32,128]{3,2,1,0:T(8,128)(2,1)}), bf16[4,2,32,128]{3,2,1,0:T(8,128)(2,1)S(1)}, u32[]{:S(2)}, u32[]{:S(2)}) %all-to-all-start.1) | async-done | bytes 65568 | tf_op jit(solution)/shard_map/all_to_all | solution.py:357
  69.9 1.5 spread.1
  71.5 6.0 %all-to-all-start.2 = ((bf16[16,2,32,128]{3,2,1,0:T(8,128)(2,1)}), bf16[16,2,32,128]{3,2,1,0:T(8,128)(2,1)S(1)}, u32[]{:S(2)}, u32[]{:S(2)}) async-start(bf16[16,2,32,128]{3,2,1,0:T(8,128)(2,1)} %spread.1), calls=%async_computation.2 | async-start | bytes 524288 | tf_op jit(solution)/shard_map/all_to_all | solution.py:388
  77.5 0.7 collective-permute-start.4
  78.2 1.9 %near.1 = (f32[256,128]{1,0:T(8,128)S(1)}, f32[256,128]{1,0:T(8,128)S(1)}) custom-call(s32[1]{0:T(128)} %bitcast.pos_ref, s32[4,32]{1,0:T(4,128)S(1)} %copy-done.6, bf16[512,128]{1,0:T(8,128)(2,1)S(1)} %copy-done.3, bf16[512,128]{1,0:T(8,128)(2,1)S(1)} %collective-permute-done.p0, bf16[512,128]{1,0:T(8,128)(2,1)S(1)} %collective-permute-done.1.p2, ...), custom_call_target="tpu_custom_call" | custom-call | flops 1000000000 | bytes 1000000 | tf_op jit(solution)/shard_map/near/pallas_call | solution.py:393
  80.1 7.4 %all-to-all-done.2.glob_ref = bf16[16,2,32,128]{3,2,1,0:T(8,128)(2,1)S(1)} async-done(((bf16[16,2,32,128]{3,2,1,0:T(8,128)(2,1)}), bf16[16,2,32,128]{3,2,1,0:T(8,128)(2,1)S(1)}, u32[]{:S(2)}, u32[]{:S(2)}) %all-to-all-start.2) | async-done | bytes 262176 | tf_op jit(solution)/shard_map/all_to_all | solution.py:388
  87.5 4.5 %forward.1 = (f32[256,128]{1,0:T(8,128)}, bf16[16,128,128]{2,1,0:T(8,128)(2,1)}, f32[256,128]{1,0:T(8,128)S(1)}, f32[256,128]{1,0:T(8,128)S(1)}) custom-call(s32[1]{0:T(128)} %bitcast.pos_ref, s32[4,32]{1,0:T(4,128)S(1)} %copy-done.6, bf16[512,128]{1,0:T(8,128)(2,1)S(1)} %copy-done.3, bf16[512,128]{1,0:T(8,128)(2,1)S(1)} %collective-permute-done.4.p1, ...), custom_call_target="tpu_custom_call" | custom-call | flops 3000000000 | bytes 4000000 | tf_op jit(solution)/shard_map/forward/pallas_call | solution.py:408
  92.0 7.4 %all-to-all-start.3 = ((bf16[16,128,128]{2,1,0:T(8,128)(2,1)}), bf16[16,128,128]{2,1,0:T(8,128)(2,1)S(1)}, u32[]{:S(2)}, u32[]{:S(2)}) async-start(bf16[16,128,128]{2,1,0:T(8,128)(2,1)} %get-tuple-element.75), calls=%async_computation.3 | async-start | bytes 1048576 | tf_op jit(solution)/shard_map/all_to_all | solution.py:432
  99.4 0.0 all-gather.7.cloned.1.call-start
  99.5 0.7 all-gather.7.cloned.1.call-update
  100.2 3.9 %backward.1 = (bf16[256,256]{1,0:T(8,128)(2,1)S(1)}, bf16[256,256]{1,0:T(8,128)(2,1)S(1)}, bf16[256,256]{1,0:T(8,128)(2,1)S(1)}, bf16[256,256]{1,0:T(8,128)(2,1)...) custom-call(s32[1]{0:T(128)} %bitcast.pos_ref, s32[4,32]{1,0:T(4,128)S(1)} %copy-done.6, ...), custom_call_target="tpu_custom_call" | custom-call | flops 3000000000 | bytes 4000000 | tf_op jit(solution)/shard_map/backward/pallas_call | solution.py:434
  104.1 3.8 %collective-permute-start.5 = (bf16[256,256]{1,0:T(8,128)(2,1)S(1)}, bf16[256,256]{1,0:T(8,128)(2,1)S(1)}, u32[]{:S(2)}, u32[]{:S(2)}) collective-permute-start(bf16[256,256]{1,0:T(8,128)(2,1)S(1)} %get-tuple-element.78), channel_id=1, source_target_pairs={{0,8},{8,0},{16,24},{24,16},{32,40},{40,32},{48,56},{56,48},{64,72... | collective-permute-start | bytes 393224 | tf_op jit(solution)/shard_map/ppermute | solution.py:450
  107.9 3.8 %all-to-all-done.3 = bf16[16,128,128]{2,1,0:T(8,128)(2,1)S(1)} async-done(((bf16[16,128,128]{2,1,0:T(8,128)(2,1)}), bf16[16,128,128]{2,1,0:T(8,128)(2,1)S(1)}, u32[]{:S(2)}, u32[]{:S(2)}) %all-to-all-start.3) | async-done | bytes 524320 | tf_op jit(solution)/shard_map/all_to_all | solution.py:432
  111.7 0.1 reduce_sum.24
  111.8 0.7 broadcast_in_dim.10
  112.5 8.1 %all-to-all-start.4 = ((bf16[4,128,128]{2,1,0:T(8,128)(2,1)}), bf16[4,128,128]{2,1,0:T(8,128)(2,1)S(1)}, u32[]{:S(2)}, u32[]{:S(2)}) async-start(bf16[4,128,128]{2,1,0:T(8,128)(2,1)} %broadcast_in_dim.10), calls=%async_computation.4 | async-start | bytes 262144 | tf_op jit(solution)/shard_map/all_to_all | solution.py:454
  120.6 3.9 %collective-permute-start.6 = (bf16[256,256]{1,0:T(8,128)(2,1)S(1)}, bf16[256,256]{1,0:T(8,128)(2,1)S(1)}, u32[]{:S(2)}, u32[]{:S(2)}) collective-permute-start(bf16[256,256]{1,0:T(8,128)(2,1)S(1)} %get-tuple-element.85), channel_id=1, source_target_pairs={{0,64},{8,72},{16,80},{24,88},{32,96},{40,104},{48,112},{56,120},{... | collective-permute-start | bytes 393224 | tf_op jit(solution)/shard_map/ppermute | solution.py:456
  124.5 4.9 %collective-permute-start.7 = (bf16[256,256]{1,0:T(8,128)(2,1)S(1)}, bf16[256,256]{1,0:T(8,128)(2,1)S(1)}, u32[]{:S(2)}, u32[]{:S(2)}) collective-permute-start(bf16[256,256]{1,0:T(8,128)(2,1)S(1)} %get-tuple-element.86), channel_id=1, source_target_pairs={{0,16},{8,24},{16,0},{24,8},{32,48},{40,56},{48,32},{56,40},{64,80... | collective-permute-start | bytes 393224 | tf_op jit(solution)/shard_map/ppermute | solution.py:456
  129.3 2.2 %collective-permute-done.6.b4 = bf16[256,256]{1,0:T(8,128)(2,1)S(1)} collective-permute-done((bf16[256,256]{1,0:T(8,128)(2,1)S(1)}, bf16[256,256]{1,0:T(8,128)(2,1)S(1)}, u32[]{:S(2)}, u32[]{:S(2)}) %collective-permute-start.6) | collective-permute-done | bytes 131104 | tf_op jit(solution)/shard_map/ppermute | solution.py:456
  131.5 1.3 collective-permute-done.7.b2
  132.8 1.5 all-to-all-done.4
  134.4 0.0 all-gather.7.cloned.1.call-done
  134.4 0.9 broadcast_in_dim.11
  135.3 7.3 %all-to-all-start.5 = ((bf16[16,128,128]{2,1,0:T(8,128)(2,1)}), bf16[16,128,128]{2,1,0:T(8,128)(2,1)S(1)}, u32[]{:S(2)}, u32[]{:S(2)}) async-start(bf16[16,128,128]{2,1,0:T(8,128)(2,1)} %broadcast_in_dim.11), calls=%async_computation.5 | async-start | bytes 1048576 | tf_op jit(solution)/shard_map/all_to_all | solution.py:460
  142.6 0.7 collective-permute-start.8
  143.2 7.7 %collective-permute-start.9 = (bf16[256,256]{1,0:T(8,128)(2,1)S(1)}, bf16[256,256]{1,0:T(8,128)(2,1)S(1)}, u32[]{:S(2)}, u32[]{:S(2)}) collective-permute-start(bf16[256,256]{1,0:T(8,128)(2,1)S(1)} %get-tuple-element.94), channel_id=1, source_target_pairs={{0,32},{8,40},{16,48},{24,56},{32,0},{40,8},{48,16},{56,24},{64,96... | collective-permute-start | bytes 393224 | tf_op jit(solution)/shard_map/ppermute | solution.py:456
  151.0 1.2 copy-done.2
  152.2 0.9 project.1
  153.1 2.1 %collective-permute-done.9.b3 = bf16[256,256]{1,0:T(8,128)(2,1)S(1)} collective-permute-done((bf16[256,256]{1,0:T(8,128)(2,1)S(1)}, bf16[256,256]{1,0:T(8,128)(2,1)S(1)}, u32[]{:S(2)}, u32[]{:S(2)}) %collective-permute-start.9) | collective-permute-done | bytes 131104 | tf_op jit(solution)/shard_map/ppermute | solution.py:456
  155.3 1.6 finish.1
  (17 shorter events, 0.1 us)
Async XLA Ops:
  7.2 62.8 %copy-start.5 = (s32[2]{0:T(128)S(1)}, s32[2]{0:T(128)}, u32[]{:S(2)}) copy-start(s32[2]{0:T(128)} %ids_ref.5) | copy-start | bytes 28
  7.2 71.0 %copy-start.6 = (s32[4,32]{1,0:T(4,128)S(1)}, s32[4,32]{1,0:T(4,128)}, u32[]{:S(2)}) copy-start(s32[4,32]{1,0:T(4,128)} %pair_ref.5) | copy-start | bytes 1540
  7.2 56.3 %all-gather.5.cloned.1.call-start = ((), (), s32[]{:S(2)}) async-start(), calls=%async_computation.6 | async-start | bytes 2949120 | tf_op jit(solution)/shard_map/all_gather | solution.py:338
  22.3 55.1 %copy-start.3 = (bf16[512,128]{1,0:T(8,128)(2,1)S(1)}, bf16[512,128]{1,0:T(8,128)(2,1)}, u32[]{:S(2)}) copy-start(bf16[512,128]{1,0:T(8,128)(2,1)} %get-tuple-element.62.own_ref) | copy-start | bytes 393220
  22.4 17.6 %all-to-all-start = ((bf16[16,32,128]{2,1,0:T(8,128)(2,1)}), bf16[16,32,128]{2,1,0:T(8,128)(2,1)S(1)}, u32[]{:S(2)}, u32[]{:S(2)}) async-start(bf16[16,32,128]{2,1,0:T(8,128)(2,1)} %bitcast.7), calls=%async_computation | async-start | bytes 262144 | tf_op jit(solution)/shard_map/all_to_all | solution.py:337
  31.0 8.4 %collective-permute-start = (bf16[512,128]{1,0:T(8,128)(2,1)}, bf16[512,128]{1,0:T(8,128)(2,1)S(1)}, u32[]{:S(2)}, u32[]{:S(2)}) collective-permute-start(bf16[512,128]{1,0:T(8,128)(2,1)} %get-tuple-element.62.own_ref), channel_id=1, source_target_pairs={{0,8},{8,0},{16,24},{24,16},{32,40},{40,32},{48,56},{56,48},{64,72... | collective-permute-start | bytes 393224 | tf_op jit(solution)/shard_map/ppermute | solution.py:345
  34.8 8.8 %collective-permute-start.1 = (bf16[512,128]{1,0:T(8,128)(2,1)}, bf16[512,128]{1,0:T(8,128)(2,1)S(1)}, u32[]{:S(2)}, u32[]{:S(2)}) collective-permute-start(bf16[512,128]{1,0:T(8,128)(2,1)} %get-tuple-element.62.own_ref), channel_id=1, source_target_pairs={{0,16},{8,24},{16,0},{24,8},{32,48},{40,56},{48,32},{56,40},{64,80... | collective-permute-start | bytes 393224 | tf_op jit(solution)/shard_map/ppermute | solution.py:345
  39.9 0.7 copy-start.4
  43.7 26.3 %all-to-all-start.1 = ((bf16[4,2,32,128]{3,2,1,0:T(8,128)(2,1)}), bf16[4,2,32,128]{3,2,1,0:T(8,128)(2,1)S(1)}, u32[]{:S(2)}, u32[]{:S(2)}) async-start(bf16[4,2,32,128]{3,2,1,0:T(8,128)(2,1)} %pick.1), calls=%async_computation.1 | async-start | bytes 131072 | tf_op jit(solution)/shard_map/all_to_all | solution.py:357
  56.1 11.8 %collective-permute-start.2 = (bf16[512,128]{1,0:T(8,128)(2,1)}, bf16[512,128]{1,0:T(8,128)(2,1)S(1)}, u32[]{:S(2)}, u32[]{:S(2)}) collective-permute-start(bf16[512,128]{1,0:T(8,128)(2,1)} %get-tuple-element.62.own_ref), channel_id=1, source_target_pairs={{0,64},{8,72},{16,80},{24,88},{32,96},{40,104},{48,112},{56,120},{... | collective-permute-start | bytes 393224 | tf_op jit(solution)/shard_map/ppermute | solution.py:359
  60.1 11.4 %collective-permute-start.3 = (bf16[512,128]{1,0:T(8,128)(2,1)}, bf16[512,128]{1,0:T(8,128)(2,1)S(1)}, u32[]{:S(2)}, u32[]{:S(2)}) collective-permute-start(bf16[512,128]{1,0:T(8,128)(2,1)} %get-tuple-element.62.own_ref), channel_id=1, source_target_pairs={{0,32},{8,40},{16,48},{24,56},{32,0},{40,8},{48,16},{56,24},{64,96... | collective-permute-start | bytes 393224 | tf_op jit(solution)/shard_map/ppermute | solution.py:359
  63.5 1.7 %copy-start = (bf16[80,128,128]{2,1,0:T(8,128)(2,1)S(1)}, bf16[80,128,128]{2,1,0:T(8,128)(2,1)}, u32[]{:S(2)}) copy-start(bf16[80,128,128]{2,1,0:T(8,128)(2,1)} %all-gather.5.cloned.1.call-done) | copy-start | bytes 7864324
  65.3 0.9 copy-start.1
  71.5 16.0 %all-to-all-start.2 = ((bf16[16,2,32,128]{3,2,1,0:T(8,128)(2,1)}), bf16[16,2,32,128]{3,2,1,0:T(8,128)(2,1)S(1)}, u32[]{:S(2)}, u32[]{:S(2)}) async-start(bf16[16,2,32,128]{3,2,1,0:T(8,128)(2,1)} %spread.1), calls=%async_computation.2 | async-start | bytes 524288 | tf_op jit(solution)/shard_map/all_to_all | solution.py:388
  77.5 10.0 %collective-permute-start.4 = (bf16[512,128]{1,0:T(8,128)(2,1)S(1)}, bf16[512,128]{1,0:T(8,128)(2,1)S(1)}, u32[]{:S(2)}, u32[]{:S(2)}) collective-permute-start(bf16[512,128]{1,0:T(8,128)(2,1)S(1)} %copy-done.3), channel_id=1, source_target_pairs={{8,16},{16,8},{24,32},{32,24},{40,48},{48,40},{56,64},{64,56},{72,... | collective-permute-start | bytes 393224 | tf_op jit(solution)/shard_map/ppermute | solution.py:389
  92.0 19.7 %all-to-all-start.3 = ((bf16[16,128,128]{2,1,0:T(8,128)(2,1)}), bf16[16,128,128]{2,1,0:T(8,128)(2,1)S(1)}, u32[]{:S(2)}, u32[]{:S(2)}) async-start(bf16[16,128,128]{2,1,0:T(8,128)(2,1)} %get-tuple-element.75), calls=%async_computation.3 | async-start | bytes 1048576 | tf_op jit(solution)/shard_map/all_to_all | solution.py:432
  99.4 35.0 %all-gather.7.cloned.1.call-start = ((), (), s32[]{:S(2)}) async-start(), calls=%async_computation.7 | async-start | bytes 1179648 | tf_op jit(solution)/shard_map/all_gather | solution.py:433
  104.1 7.7 %collective-permute-start.5 = (bf16[256,256]{1,0:T(8,128)(2,1)S(1)}, bf16[256,256]{1,0:T(8,128)(2,1)S(1)}, u32[]{:S(2)}, u32[]{:S(2)}) collective-permute-start(bf16[256,256]{1,0:T(8,128)(2,1)S(1)} %get-tuple-element.78), channel_id=1, source_target_pairs={{0,8},{8,0},{16,24},{24,16},{32,40},{40,32},{48,56},{56,48},{64,72... | collective-permute-start | bytes 393224 | tf_op jit(solution)/shard_map/ppermute | solution.py:450
  112.5 21.9 %all-to-all-start.4 = ((bf16[4,128,128]{2,1,0:T(8,128)(2,1)}), bf16[4,128,128]{2,1,0:T(8,128)(2,1)S(1)}, u32[]{:S(2)}, u32[]{:S(2)}) async-start(bf16[4,128,128]{2,1,0:T(8,128)(2,1)} %broadcast_in_dim.10), calls=%async_computation.4 | async-start | bytes 262144 | tf_op jit(solution)/shard_map/all_to_all | solution.py:454
  120.6 10.9 %collective-permute-start.6 = (bf16[256,256]{1,0:T(8,128)(2,1)S(1)}, bf16[256,256]{1,0:T(8,128)(2,1)S(1)}, u32[]{:S(2)}, u32[]{:S(2)}) collective-permute-start(bf16[256,256]{1,0:T(8,128)(2,1)S(1)} %get-tuple-element.85), channel_id=1, source_target_pairs={{0,64},{8,72},{16,80},{24,88},{32,96},{40,104},{48,112},{56,120},{... | collective-permute-start | bytes 393224 | tf_op jit(solution)/shard_map/ppermute | solution.py:456
  124.5 8.4 %collective-permute-start.7 = (bf16[256,256]{1,0:T(8,128)(2,1)S(1)}, bf16[256,256]{1,0:T(8,128)(2,1)S(1)}, u32[]{:S(2)}, u32[]{:S(2)}) collective-permute-start(bf16[256,256]{1,0:T(8,128)(2,1)S(1)} %get-tuple-element.86), channel_id=1, source_target_pairs={{0,16},{8,24},{16,0},{24,8},{32,48},{40,56},{48,32},{56,40},{64,80... | collective-permute-start | bytes 393224 | tf_op jit(solution)/shard_map/ppermute | solution.py:456
  135.3 20.0 %all-to-all-start.5 = ((bf16[16,128,128]{2,1,0:T(8,128)(2,1)}), bf16[16,128,128]{2,1,0:T(8,128)(2,1)S(1)}, u32[]{:S(2)}, u32[]{:S(2)}) async-start(bf16[16,128,128]{2,1,0:T(8,128)(2,1)} %broadcast_in_dim.11), calls=%async_computation.5 | async-start | bytes 1048576 | tf_op jit(solution)/shard_map/all_to_all | solution.py:460
  142.6 10.6 %collective-permute-start.8 = (bf16[256,256]{1,0:T(8,128)(2,1)S(1)}, bf16[256,256]{1,0:T(8,128)(2,1)S(1)}, u32[]{:S(2)}, u32[]{:S(2)}) collective-permute-start(bf16[256,256]{1,0:T(8,128)(2,1)S(1)} %get-tuple-element.92), channel_id=1, source_target_pairs={{8,16},{16,8},{24,32},{32,24},{40,48},{48,40},{56,64},{64,56},{72,... | collective-permute-start | bytes 393224 | tf_op jit(solution)/shard_map/ppermute | solution.py:456
  143.2 12.0 %collective-permute-start.9 = (bf16[256,256]{1,0:T(8,128)(2,1)S(1)}, bf16[256,256]{1,0:T(8,128)(2,1)S(1)}, u32[]{:S(2)}, u32[]{:S(2)}) collective-permute-start(bf16[256,256]{1,0:T(8,128)(2,1)S(1)} %get-tuple-element.94), channel_id=1, source_target_pairs={{0,32},{8,40},{16,48},{24,56},{32,0},{40,8},{48,16},{56,24},{64,96... | collective-permute-start | bytes 393224 | tf_op jit(solution)/shard_map/ppermute | solution.py:456
  151.0 1.2 copy-start.2
Sparse Core Ops, SparseCore 0:
  22.5 37.0 all-gather.4
  102.4 27.3 all-gather.6

commit v8 on v7

--- a/solution.py
+++ b/solution.py
@@ -15,7 +15,6 @@
 HEAD = "head"
 PATCH = 16
 NT = (((1,), (1,)), ((), ()))
-TN = (((0,), (0,)), ((), ()))
 NN = (((1,), (0,)), ((), ()))
 F32 = jnp.float32
 BF16 = jnp.bfloat16
@@ -142,9 +141,9 @@
 
     attended = out_ref[...]
     att_ref[...] = attended
-    attended_b = attended.astype(BF16)
+    attended_t = attended.T.astype(BF16)
     for c in range(pieces):
-        part = dot(attended_b, gout_ref[c], TN).astype(BF16)
+        part = dot(attended_t, gout_ref[c], NN).astype(BF16)
         n = width // HD
         sums_ref[c * n:(c + 1) * n, 0:HD, :] = part.reshape(n, HD, 128)
 
@@ -261,18 +260,14 @@
         copy.wait()
 
 
-def pack_kernel(qk_ref, val_ref, gout_ref, w_ref, joined_ref, share_ref, sems):
-    length = qk_ref.shape[0]
+def pack_kernel(qk_ref, val_ref, gout_ref, w_ref, joined_ref, share_ref):
+    length, width = qk_ref.shape
     blocks = length // 128
-    pairs = [
-        (qk_ref, joined_ref.at[pl.ds(0, length)]),
-        (val_ref, joined_ref.at[pl.ds(length, length)]),
-    ]
-    for b in range(blocks):
-        pairs.append((gout_ref.at[pl.ds(b * 128, 128)], share_ref.at[b]))
+    joined_ref[:length] = qk_ref[...]
+    joined_ref[length:] = val_ref[...]
+    share_ref[0:blocks] = gout_ref[...].reshape(blocks, 128, width)
     for c in range(w_ref.shape[1] // 128):
-        pairs.append((w_ref.at[:, pl.ds(c * 128, 128)], share_ref.at[blocks + c]))
-    copy_all([pltpu.make_async_copy(a, b, sems.at[n]) for n, (a, b) in enumerate(pairs)])
+        share_ref[blocks + c] = w_ref[:, c * 128:(c + 1) * 128]
 
 
 def pick_kernel(ids_ref, slices_ref, out_ref, sems):
@@ -328,9 +323,8 @@
             jax.ShapeDtypeStruct((2 * length, width), BF16),
             jax.ShapeDtypeStruct((length // 128 + pieces, 128, width), BF16),
         ),
-        in_specs=[anywhere()] * 4,
-        out_specs=(anywhere(), anywhere()),
-        scratch_shapes=[pltpu.SemaphoreType.DMA((2 + length // 128 + pieces,))],
+        in_specs=vmem(4),
+        out_specs=tuple(vmem(2)),
         name="pack",
     )(qk_vectors, token_values, grad_output, out_weight)
 
@@ -341,9 +335,8 @@
     routes.append([(i, j) for i, j in enumerate(other) if 0 <= j < devices])
     routes += [[(i, i ^ (1 << k)) for i in range(devices)] for k in range(1, ROUNDS)]
     received = [None] * len(routes)
-    for n in (0, 2):
+    for n in (4, 0):
         received[n] = lax.ppermute(joined, CTX, routes[n])
-    slices, received[0] = lax.optimization_barrier((slices, received[0]))
     picked = pl.pallas_call(
         pick_kernel,
         out_shape=jax.ShapeDtypeStruct((his, NGLOB, step, width), BF16),
@@ -353,9 +346,11 @@
         compiler_params=limit(1),
         name="pick",
     )(global_ids, slices)
-    picked, joined_late, received[2] = lax.optimization_barrier((picked, joined, received[2]))
+    picked, joined_late, received[4], received[0] = lax.optimization_barrier(
+        (picked, joined, received[4], received[0])
+    )
     column = lax.all_to_all(picked, "hi", 0, 0)
-    for n in (4, 3):
+    for n in (3, 2):
         received[n] = lax.ppermute(joined_late, CTX, routes[n])
     portion_b, gatt, weight_cols = pl.pallas_call(
         cotangent_kernel,
@@ -372,8 +367,8 @@
         ),
         name="cotangent",
     )(lax.axis_index(HEAD)[None], portion, out_weight)
-    column, received[4], portion_b, gatt, weight_cols = lax.optimization_barrier(
-        (column, received[4], portion_b, gatt, weight_cols)
+    column, portion_b, gatt, weight_cols = lax.optimization_barrier(
+        (column, portion_b, gatt, weight_cols)
     )
     chosen = pl.pallas_call(
         spread_kernel,
@@ -384,7 +379,9 @@
         compiler_params=limit(1),
         name="spread",
     )(global_ids, column)
-    chosen, joined_late, received[3] = lax.optimization_barrier((chosen, joined, received[3]))
+    chosen, joined_late, received[3], received[2] = lax.optimization_barrier(
+        (chosen, joined, received[3], received[2])
+    )
     globals_all = lax.all_to_all(chosen, "lo", 0, 0)
     received[1] = lax.ppermute(joined_late, CTX, routes[1])
     nheads = width // HD
@@ -442,7 +439,7 @@
         out_specs=tuple(vmem(7)),
         compiler_params=limit(10),
         cost_estimate=pl.CostEstimate(
-            flops=3_000_000_000, bytes_accessed=4_000_000, transcendentals=800_000
+            flops=1_000_000, bytes_accessed=10_000, transcendentals=0
         ),
         name="backward",
     )(position[None], pair_active, joined, *received, stats, gatt, gglob)
@@ -454,9 +451,10 @@
     column = lax.all_to_all(jnp.broadcast_to(share[None], (his,) + share.shape), "hi", 0, 0)
     for n in (4, 2, 3, 1):
         returned[n] = lax.ppermute(terms[n], CTX, routes[n])
-    column, returned[4], returned[2] = lax.optimization_barrier((column, returned[4], returned[2]))
     share = jnp.sum(column.astype(F32), axis=0).astype(BF16)
-    share, attended_all = lax.optimization_barrier((share, attended_all))
+    share, returned[4], returned[2], attended_all = lax.optimization_barrier(
+        (share, returned[4], returned[2], attended_all)
+    )
     totals = lax.all_to_all(jnp.broadcast_to(share[None], (los,) + share.shape), "lo", 0, 0)
 
     projected = pl.pallas_call(
@@ -470,6 +468,9 @@
         ),
         name="project",
     )(attended_all, weight_cols)
+    totals, returned[3], returned[1] = lax.optimization_barrier(
+        (totals, returned[3], returned[1])
+    )
     gqk, gval, gweight = pl.pallas_call(
         finish_kernel,
         out_shape=(

time: 166 us -> 153 us (0.922)
  Pallas kernels: 31 us -> 18.1 us
  starting transfers between devices: 87.3 us -> 82.5 us
  waiting for transfers between devices: 24.8 us -> 28.6 us
    pallas_call x1, Pallas kernels: 15.1 us -> 1.85 us  [local(): pl.pallas_call(pack_kernel, out_shape=(jax.ShapeDtypeStruct((2 * length,...]
    all_to_all x1, waiting for transfers between devices: 1.52 us -> 6.73 us  [local(): lax.all_to_all(jnp.broadcast_to(share[None], (his,) + share.shape), 'hi',...]
    ppermute x4, starting transfers between devices: 17.1 us -> 13 us  [local(): returned[n] = lax.ppermute(terms[n], CTX, routes[n])]
    all_to_all x1, waiting for transfers between devices: 0.01 us -> 1.76 us  [local(): lax.all_to_all(jnp.broadcast_to(share[None], (los,) + share.shape), 'lo',...]
    ppermute x4, waiting for transfers between devices: 5.61 us -> 3.88 us  [local(): returned[n] = lax.ppermute(terms[n], CTX, routes[n])]
  transfers between devices with their start and end apart: 18 -> 18, of which waited for: 10 -> 8; matrix products, arithmetic and copies ran while one was open for 0% -> 1% of each run, Pallas kernels for 6% -> 7%
where the time goes in v8:
time: 153 us; the launch traced here: 150 us
  starting transfers between devices  82.5 us (54%)
  waiting for transfers between devices  28.6 us (19%)
  Pallas kernels  18.1 us (12%)
  between operations  14.3 us (9%)
  local copies, waits for them, and re-layouts  6.14 us (4%)
    ppermute x4, starting transfers between devices, local(): returned[n] = lax.ppermute(terms[n], CTX, routes[n])  13 us
    all_to_all x1, starting transfers between devices, local(): column = lax.all_to_all(picked, 'hi', 0, 0)  12.4 us
    all_to_all x1, starting transfers between devices, local(): slices = lax.all_to_all(joined.reshape(los, step, width), 'lo', 0, 0)  8.61 us
    all_to_all x1, starting transfers between devices, local(): lax.all_to_all(jnp.broadcast_to(share[None], (his,) + share.shape), 'hi',...  8.31 us
    ppermute x2, starting transfers between devices, local(): received[n] = lax.ppermute(joined, CTX, routes[n])  8.1 us
    ppermute x2, starting transfers between devices, local(): received[n] = lax.ppermute(joined_late, CTX, routes[n])  8.09 us
    all_to_all x1, starting transfers between devices, local(): shares = lax.all_to_all(sums, 'lo', 0, 0)  7.43 us
    all_to_all x1, waiting for transfers between devices, local(): globals_all = lax.all_to_all(chosen, 'lo', 0, 0)  7.41 us
  transfers between devices with their start and end apart: 18, of which 8 were waited for; matrix products, arithmetic and copies ran while one was open for 1% of the time, Pallas kernels for 7%

profile of v8, /device:TPU:24, one launch (start us, length us, event | category | flops | bytes accessed | tf_op | source)
XLA Modules:
  0.0 149.7 jit_solution(18168069712084251385)
XLA Ops:
  7.2 0.0 all-gather.5.cloned.1.call-start
  7.2 1.8 %pack.1 = (bf16[512,128]{1,0:T(8,128)(2,1)}, bf16[10,128,128]{2,1,0:T(8,128)(2,1)}) custom-call(bf16[256,128]{1,0:T(8,128)(2,1)} %qk_ref.1, bf16[256,128]{1,0:T(8,128)(2,1)} %val_ref.1, bf16[256,128]{1,0:T(8,128)(2,1)} %gout_ref.1, bf16[128,1024]{1,0:T(8,128)(2,1)} %w_ref.3), custom_call_target="tpu_custom_call" | custom-call | tf_op jit(solution)/shard_map/pack/pallas_call | solution.py:320
  9.1 0.0 all-gather.5.cloned.1.call-update
  9.1 8.6 %all-to-all-start = ((bf16[16,32,128]{2,1,0:T(8,128)(2,1)}), bf16[16,32,128]{2,1,0:T(8,128)(2,1)S(1)}, u32[]{:S(2)}, u32[]{:S(2)}) async-start(bf16[16,32,128]{2,1,0:T(8,128)(2,1)} %bitcast.7), calls=%async_computation | async-start | bytes 262144 | tf_op jit(solution)/shard_map/all_to_all | solution.py:331
  17.7 4.7 %collective-permute-start = (bf16[512,128]{1,0:T(8,128)(2,1)}, bf16[512,128]{1,0:T(8,128)(2,1)S(1)}, u32[]{:S(2)}, u32[]{:S(2)}) collective-permute-start(bf16[512,128]{1,0:T(8,128)(2,1)} %get-tuple-element.62.own_ref), channel_id=1, source_target_pairs={{0,64},{8,72},{16,80},{24,88},{32,96},{40,104},{48,112},{56,120},{... | collective-permute-start | bytes 393224 | tf_op jit(solution)/shard_map/ppermute | solution.py:339
  22.4 3.4 %collective-permute-start.1 = (bf16[512,128]{1,0:T(8,128)(2,1)}, bf16[512,128]{1,0:T(8,128)(2,1)S(1)}, u32[]{:S(2)}, u32[]{:S(2)}) collective-permute-start(bf16[512,128]{1,0:T(8,128)(2,1)} %get-tuple-element.62.own_ref), channel_id=1, source_target_pairs={{0,8},{8,0},{16,24},{24,16},{32,40},{40,32},{48,56},{56,48},{64,72... | collective-permute-start | bytes 393224 | tf_op jit(solution)/shard_map/ppermute | solution.py:339
  25.8 1.2 all-to-all-done.slices_ref
  27.0 0.7 copy-done.4
  27.6 1.2 pick.1
  28.9 0.8 collective-permute-done.p4
  29.7 0.0 collective-permute-done.1.p0
  29.7 12.4 %all-to-all-start.1 = ((bf16[4,2,32,128]{3,2,1,0:T(8,128)(2,1)}), bf16[4,2,32,128]{3,2,1,0:T(8,128)(2,1)S(1)}, u32[]{:S(2)}, u32[]{:S(2)}) async-start(bf16[4,2,32,128]{3,2,1,0:T(8,128)(2,1)} %pick.1), calls=%async_computation.1 | async-start | bytes 131072 | tf_op jit(solution)/shard_map/all_to_all | solution.py:352
  42.0 3.2 %collective-permute-start.2 = (bf16[512,128]{1,0:T(8,128)(2,1)}, bf16[512,128]{1,0:T(8,128)(2,1)S(1)}, u32[]{:S(2)}, u32[]{:S(2)}) collective-permute-start(bf16[512,128]{1,0:T(8,128)(2,1)} %get-tuple-element.62.own_ref), channel_id=1, source_target_pairs={{0,32},{8,40},{16,48},{24,56},{32,0},{40,8},{48,16},{56,24},{64,96... | collective-permute-start | bytes 393224 | tf_op jit(solution)/shard_map/ppermute | solution.py:354
  45.3 4.9 %collective-permute-start.3 = (bf16[512,128]{1,0:T(8,128)(2,1)}, bf16[512,128]{1,0:T(8,128)(2,1)S(1)}, u32[]{:S(2)}, u32[]{:S(2)}) collective-permute-start(bf16[512,128]{1,0:T(8,128)(2,1)} %get-tuple-element.62.own_ref), channel_id=1, source_target_pairs={{0,16},{8,24},{16,0},{24,8},{32,48},{40,56},{48,32},{56,40},{64,80... | collective-permute-start | bytes 393224 | tf_op jit(solution)/shard_map/ppermute | solution.py:354
  50.2 0.0 all-gather.5.cloned.1.call-done
  50.2 1.7 %copy-done = bf16[80,128,128]{2,1,0:T(8,128)(2,1)S(1)} copy-done((bf16[80,128,128]{2,1,0:T(8,128)(2,1)S(1)}, bf16[80,128,128]{2,1,0:T(8,128)(2,1)}, u32[]{:S(2)}) %copy-start) | copy-done | bytes 2621464
  51.9 0.9 copy-done.1
  52.9 0.3 cotangent.1
  53.2 2.0 %all-to-all-done.1.slices_ref = bf16[4,2,32,128]{3,2,1,0:T(8,128)(2,1)S(1)} async-done(((bf16[4,2,32,128]{3,2,1,0:T(8,128)(2,1)}), bf16[4,2,32,128]{3,2,1,0:T(8,128)(2,1)S(1)}, u32[]{:S(2)}, u32[]{:S(2)}) %all-to-all-start.1) | async-done | bytes 65568 | tf_op jit(solution)/shard_map/all_to_all | solution.py:352
  55.3 1.5 %spread.1 = bf16[16,2,32,128]{3,2,1,0:T(8,128)(2,1)} custom-call(s32[2]{0:T(128)S(1)} %copy-done.4, bf16[4,2,32,128]{3,2,1,0:T(8,128)(2,1)S(1)} %all-to-all-done.1.slices_ref), custom_call_target="tpu_custom_call" | custom-call | tf_op jit(solution)/shard_map/spread/pallas_call | solution.py:373
  56.8 5.9 %all-to-all-start.2 = ((bf16[16,2,32,128]{3,2,1,0:T(8,128)(2,1)}), bf16[16,2,32,128]{3,2,1,0:T(8,128)(2,1)S(1)}, u32[]{:S(2)}, u32[]{:S(2)}) async-start(bf16[16,2,32,128]{3,2,1,0:T(8,128)(2,1)} %spread.1), calls=%async_computation.2 | async-start | bytes 524288 | tf_op jit(solution)/shard_map/all_to_all | solution.py:385
  62.8 0.7 collective-permute-start.4
  63.5 1.9 %near.1 = (f32[256,128]{1,0:T(8,128)S(1)}, f32[256,128]{1,0:T(8,128)S(1)}) custom-call(s32[1]{0:T(128)} %bitcast.pos_ref, s32[4,32]{1,0:T(4,128)S(1)} %copy-done.6, bf16[512,128]{1,0:T(8,128)(2,1)S(1)} %copy-done.3, bf16[512,128]{1,0:T(8,128)(2,1)S(1)} %collective-permute-done.1.p0, bf16[512,128]{1,0:T(8,128)(2,1)S(1)} %collective-permute-done.3.p2, ...), custom_call_target="tpu_custom_call" | custom-call | flops 1000000000 | bytes 1000000 | tf_op jit(solution)/shard_map/near/pallas_call | solution.py:390
  65.3 7.4 %all-to-all-done.2.glob_ref = bf16[16,2,32,128]{3,2,1,0:T(8,128)(2,1)S(1)} async-done(((bf16[16,2,32,128]{3,2,1,0:T(8,128)(2,1)}), bf16[16,2,32,128]{3,2,1,0:T(8,128)(2,1)S(1)}, u32[]{:S(2)}, u32[]{:S(2)}) %all-to-all-start.2) | async-done | bytes 262176 | tf_op jit(solution)/shard_map/all_to_all | solution.py:385
  72.7 4.8 %forward.1 = (f32[256,128]{1,0:T(8,128)}, bf16[16,128,128]{2,1,0:T(8,128)(2,1)}, f32[256,128]{1,0:T(8,128)S(1)}, f32[256,128]{1,0:T(8,128)S(1)}) custom-call(s32[1]{0:T(128)} %bitcast.pos_ref, s32[4,32]{1,0:T(4,128)S(1)} %copy-done.6, bf16[512,128]{1,0:T(8,128)(2,1)S(1)} %copy-done.3, bf16[512,128]{1,0:T(8,128)(2,1)S(1)} %collective-permute-done.4.p1, ...), custom_call_target="tpu_custom_call" | custom-call | flops 3000000000 | bytes 4000000 | tf_op jit(solution)/shard_map/forward/pallas_call | solution.py:405
  77.6 7.4 %all-to-all-start.3 = ((bf16[16,128,128]{2,1,0:T(8,128)(2,1)}), bf16[16,128,128]{2,1,0:T(8,128)(2,1)S(1)}, u32[]{:S(2)}, u32[]{:S(2)}) async-start(bf16[16,128,128]{2,1,0:T(8,128)(2,1)} %get-tuple-element.75), calls=%async_computation.3 | async-start | bytes 1048576 | tf_op jit(solution)/shard_map/all_to_all | solution.py:429
  85.0 0.0 all-gather.7.cloned.1.call-start
  85.1 0.7 all-gather.7.cloned.1.call-update
  85.8 0.0 copy-start.5
  85.8 3.9 %backward.1 = (bf16[256,256]{1,0:T(8,128)(2,1)S(1)}, bf16[256,256]{1,0:T(8,128)(2,1)S(1)}, bf16[256,256]{1,0:T(8,128)(2,1)S(1)}, bf16[256,256]{1,0:T(8,128)(2,1)...) custom-call(s32[1]{0:T(128)} %bitcast.pos_ref, s32[4,32]{1,0:T(4,128)S(1)} %copy-done.6, ...), custom_call_target="tpu_custom_call" | custom-call | flops 1000000 | bytes 10000 | tf_op jit(solution)/shard_map/backward/pallas_call | solution.py:431
  89.7 3.8 %collective-permute-start.5 = (bf16[256,256]{1,0:T(8,128)(2,1)S(1)}, bf16[256,256]{1,0:T(8,128)(2,1)S(1)}, u32[]{:S(2)}, u32[]{:S(2)}) collective-permute-start(bf16[256,256]{1,0:T(8,128)(2,1)S(1)} %get-tuple-element.78), channel_id=1, source_target_pairs={{0,8},{8,0},{16,24},{24,16},{32,40},{40,32},{48,56},{56,48},{64,72... | collective-permute-start | bytes 393224 | tf_op jit(solution)/shard_map/ppermute | solution.py:447
  93.5 4.1 %all-to-all-done.3 = bf16[16,128,128]{2,1,0:T(8,128)(2,1)S(1)} async-done(((bf16[16,128,128]{2,1,0:T(8,128)(2,1)}), bf16[16,128,128]{2,1,0:T(8,128)(2,1)S(1)}, u32[]{:S(2)}, u32[]{:S(2)}) %all-to-all-start.3) | async-done | bytes 524320 | tf_op jit(solution)/shard_map/all_to_all | solution.py:429
  97.6 0.1 reduce_sum.24
  97.7 0.7 broadcast_in_dim.10
  98.3 8.3 %all-to-all-start.4 = ((bf16[4,128,128]{2,1,0:T(8,128)(2,1)}), bf16[4,128,128]{2,1,0:T(8,128)(2,1)S(1)}, u32[]{:S(2)}, u32[]{:S(2)}) async-start(bf16[4,128,128]{2,1,0:T(8,128)(2,1)} %broadcast_in_dim.10), calls=%async_computation.4 | async-start | bytes 262144 | tf_op jit(solution)/shard_map/all_to_all | solution.py:451
  106.7 3.6 %collective-permute-start.6 = (bf16[256,256]{1,0:T(8,128)(2,1)S(1)}, bf16[256,256]{1,0:T(8,128)(2,1)S(1)}, u32[]{:S(2)}, u32[]{:S(2)}) collective-permute-start(bf16[256,256]{1,0:T(8,128)(2,1)S(1)} %get-tuple-element.85), channel_id=1, source_target_pairs={{0,64},{8,72},{16,80},{24,88},{32,96},{40,104},{48,112},{56,120},{... | collective-permute-start | bytes 393224 | tf_op jit(solution)/shard_map/ppermute | solution.py:453
  110.3 4.9 %collective-permute-start.7 = (bf16[256,256]{1,0:T(8,128)(2,1)S(1)}, bf16[256,256]{1,0:T(8,128)(2,1)S(1)}, u32[]{:S(2)}, u32[]{:S(2)}) collective-permute-start(bf16[256,256]{1,0:T(8,128)(2,1)S(1)} %get-tuple-element.86), channel_id=1, source_target_pairs={{0,16},{8,24},{16,0},{24,8},{32,48},{40,56},{48,32},{56,40},{64,80... | collective-permute-start | bytes 393224 | tf_op jit(solution)/shard_map/ppermute | solution.py:453
  115.2 6.7 %all-to-all-done.4 = bf16[4,128,128]{2,1,0:T(8,128)(2,1)S(1)} async-done(((bf16[4,128,128]{2,1,0:T(8,128)(2,1)}), bf16[4,128,128]{2,1,0:T(8,128)(2,1)S(1)}, u32[]{:S(2)}, u32[]{:S(2)}) %all-to-all-start.4) | async-done | bytes 131104 | tf_op jit(solution)/shard_map/all_to_all | solution.py:451
  121.9 0.0 all-gather.7.cloned.1.call-done
  122.0 0.9 broadcast_in_dim.11
  122.9 6.1 %all-to-all-start.5 = ((bf16[16,128,128]{2,1,0:T(8,128)(2,1)}), bf16[16,128,128]{2,1,0:T(8,128)(2,1)S(1)}, u32[]{:S(2)}, u32[]{:S(2)}) async-start(bf16[16,128,128]{2,1,0:T(8,128)(2,1)} %broadcast_in_dim.11), calls=%async_computation.5 | async-start | bytes 1048576 | tf_op jit(solution)/shard_map/all_to_all | solution.py:458
  129.0 3.8 %collective-permute-start.8 = (bf16[256,256]{1,0:T(8,128)(2,1)S(1)}, bf16[256,256]{1,0:T(8,128)(2,1)S(1)}, u32[]{:S(2)}, u32[]{:S(2)}) collective-permute-start(bf16[256,256]{1,0:T(8,128)(2,1)S(1)} %get-tuple-element.92), channel_id=1, source_target_pairs={{0,32},{8,40},{16,48},{24,56},{32,0},{40,8},{48,16},{56,24},{64,96... | collective-permute-start | bytes 393224 | tf_op jit(solution)/shard_map/ppermute | solution.py:453
  132.8 0.7 collective-permute-start.9
  133.5 1.2 copy-done.2
  134.8 0.9 project.1
  135.7 3.9 %collective-permute-done.8.b3 = bf16[256,256]{1,0:T(8,128)(2,1)S(1)} collective-permute-done((bf16[256,256]{1,0:T(8,128)(2,1)S(1)}, bf16[256,256]{1,0:T(8,128)(2,1)S(1)}, u32[]{:S(2)}, u32[]{:S(2)}) %collective-permute-start.8) | collective-permute-done | bytes 131104 | tf_op jit(solution)/shard_map/ppermute | solution.py:453
  139.5 1.8 %all-to-all-done.5.total_ref = bf16[16,128,128]{2,1,0:T(8,128)(2,1)S(1)} async-done(((bf16[16,128,128]{2,1,0:T(8,128)(2,1)}), bf16[16,128,128]{2,1,0:T(8,128)(2,1)S(1)}, u32[]{:S(2)}, u32[]{:S(2)}) %all-to-all-start.5) | async-done | bytes 524320 | tf_op jit(solution)/shard_map/all_to_all | solution.py:458
  141.3 1.6 %finish.1 = (bf16[256,128]{1,0:T(8,128)(2,1)}, bf16[256,128]{1,0:T(8,128)(2,1)}, f32[128,1024]{1,0:T(8,128)}) custom-call(s32[1]{0:T(128)} %bitcast.pos_ref, s32[2]{0:T(128)S(1)} %copy-done.5, bf16[256,256]{1,0:T(8,128)(2,1)S(1)} %collective-permute-done.5.b0, bf16[256,256]{1,0:T(8,128)(2,1)S(1)} %collective-permute-done.9.b1, ...), custom_call_target="tpu_custom_call" | custom-call | flops 2000000 | bytes 2500000 | tf_op jit(solution)/shard_map/finish/pallas_call | solution.py:474
  (17 shorter events, 0.1 us)
Async XLA Ops:
  7.2 56.3 %copy-start.6 = (s32[4,32]{1,0:T(4,128)S(1)}, s32[4,32]{1,0:T(4,128)}, u32[]{:S(2)}) copy-start(s32[4,32]{1,0:T(4,128)} %pair_ref.5) | copy-start | bytes 1540
  7.2 43.0 %all-gather.5.cloned.1.call-start = ((), (), s32[]{:S(2)}) async-start(), calls=%async_computation.6 | async-start | bytes 2949120 | tf_op jit(solution)/shard_map/all_gather | solution.py:332
  9.1 53.7 %copy-start.3 = (bf16[512,128]{1,0:T(8,128)(2,1)S(1)}, bf16[512,128]{1,0:T(8,128)(2,1)}, u32[]{:S(2)}) copy-start(bf16[512,128]{1,0:T(8,128)(2,1)} %get-tuple-element.62.own_ref) | copy-start | bytes 393220
  9.1 17.9 %all-to-all-start = ((bf16[16,32,128]{2,1,0:T(8,128)(2,1)}), bf16[16,32,128]{2,1,0:T(8,128)(2,1)S(1)}, u32[]{:S(2)}, u32[]{:S(2)}) async-start(bf16[16,32,128]{2,1,0:T(8,128)(2,1)} %bitcast.7), calls=%async_computation | async-start | bytes 262144 | tf_op jit(solution)/shard_map/all_to_all | solution.py:331
  17.7 11.9 %collective-permute-start = (bf16[512,128]{1,0:T(8,128)(2,1)}, bf16[512,128]{1,0:T(8,128)(2,1)S(1)}, u32[]{:S(2)}, u32[]{:S(2)}) collective-permute-start(bf16[512,128]{1,0:T(8,128)(2,1)} %get-tuple-element.62.own_ref), channel_id=1, source_target_pairs={{0,64},{8,72},{16,80},{24,88},{32,96},{40,104},{48,112},{56,120},{... | collective-permute-start | bytes 393224 | tf_op jit(solution)/shard_map/ppermute | solution.py:339
  22.4 7.2 %collective-permute-start.1 = (bf16[512,128]{1,0:T(8,128)(2,1)}, bf16[512,128]{1,0:T(8,128)(2,1)S(1)}, u32[]{:S(2)}, u32[]{:S(2)}) collective-permute-start(bf16[512,128]{1,0:T(8,128)(2,1)} %get-tuple-element.62.own_ref), channel_id=1, source_target_pairs={{0,8},{8,0},{16,24},{24,16},{32,40},{40,32},{48,56},{56,48},{64,72... | collective-permute-start | bytes 393224 | tf_op jit(solution)/shard_map/ppermute | solution.py:339
  27.0 0.7 copy-start.4
  29.7 25.6 %all-to-all-start.1 = ((bf16[4,2,32,128]{3,2,1,0:T(8,128)(2,1)}), bf16[4,2,32,128]{3,2,1,0:T(8,128)(2,1)S(1)}, u32[]{:S(2)}, u32[]{:S(2)}) async-start(bf16[4,2,32,128]{3,2,1,0:T(8,128)(2,1)} %pick.1), calls=%async_computation.1 | async-start | bytes 131072 | tf_op jit(solution)/shard_map/all_to_all | solution.py:352
  42.0 14.8 %collective-permute-start.2 = (bf16[512,128]{1,0:T(8,128)(2,1)}, bf16[512,128]{1,0:T(8,128)(2,1)S(1)}, u32[]{:S(2)}, u32[]{:S(2)}) collective-permute-start(bf16[512,128]{1,0:T(8,128)(2,1)} %get-tuple-element.62.own_ref), channel_id=1, source_target_pairs={{0,32},{8,40},{16,48},{24,56},{32,0},{40,8},{48,16},{56,24},{64,96... | collective-permute-start | bytes 393224 | tf_op jit(solution)/shard_map/ppermute | solution.py:354
  45.3 11.6 %collective-permute-start.3 = (bf16[512,128]{1,0:T(8,128)(2,1)}, bf16[512,128]{1,0:T(8,128)(2,1)S(1)}, u32[]{:S(2)}, u32[]{:S(2)}) collective-permute-start(bf16[512,128]{1,0:T(8,128)(2,1)} %get-tuple-element.62.own_ref), channel_id=1, source_target_pairs={{0,16},{8,24},{16,0},{24,8},{32,48},{40,56},{48,32},{56,40},{64,80... | collective-permute-start | bytes 393224 | tf_op jit(solution)/shard_map/ppermute | solution.py:354
  50.2 1.7 %copy-start = (bf16[80,128,128]{2,1,0:T(8,128)(2,1)S(1)}, bf16[80,128,128]{2,1,0:T(8,128)(2,1)}, u32[]{:S(2)}) copy-start(bf16[80,128,128]{2,1,0:T(8,128)(2,1)} %all-gather.5.cloned.1.call-done) | copy-start | bytes 7864324
  51.9 0.9 copy-start.1
  56.8 15.9 %all-to-all-start.2 = ((bf16[16,2,32,128]{3,2,1,0:T(8,128)(2,1)}), bf16[16,2,32,128]{3,2,1,0:T(8,128)(2,1)S(1)}, u32[]{:S(2)}, u32[]{:S(2)}) async-start(bf16[16,2,32,128]{3,2,1,0:T(8,128)(2,1)} %spread.1), calls=%async_computation.2 | async-start | bytes 524288 | tf_op jit(solution)/shard_map/all_to_all | solution.py:385
  62.8 10.0 %collective-permute-start.4 = (bf16[512,128]{1,0:T(8,128)(2,1)S(1)}, bf16[512,128]{1,0:T(8,128)(2,1)S(1)}, u32[]{:S(2)}, u32[]{:S(2)}) collective-permute-start(bf16[512,128]{1,0:T(8,128)(2,1)S(1)} %copy-done.3), channel_id=1, source_target_pairs={{8,16},{16,8},{24,32},{32,24},{40,48},{48,40},{56,64},{64,56},{72,... | collective-permute-start | bytes 393224 | tf_op jit(solution)/shard_map/ppermute | solution.py:386
  77.6 20.0 %all-to-all-start.3 = ((bf16[16,128,128]{2,1,0:T(8,128)(2,1)}), bf16[16,128,128]{2,1,0:T(8,128)(2,1)S(1)}, u32[]{:S(2)}, u32[]{:S(2)}) async-start(bf16[16,128,128]{2,1,0:T(8,128)(2,1)} %get-tuple-element.75), calls=%async_computation.3 | async-start | bytes 1048576 | tf_op jit(solution)/shard_map/all_to_all | solution.py:429
  85.0 37.0 %all-gather.7.cloned.1.call-start = ((), (), s32[]{:S(2)}) async-start(), calls=%async_computation.7 | async-start | bytes 1179648 | tf_op jit(solution)/shard_map/all_gather | solution.py:430
  85.8 55.5 %copy-start.5 = (s32[2]{0:T(128)S(1)}, s32[2]{0:T(128)}, u32[]{:S(2)}) copy-start(s32[2]{0:T(128)} %ids_ref.5) | copy-start | bytes 28
  89.7 8.0 %collective-permute-start.5 = (bf16[256,256]{1,0:T(8,128)(2,1)S(1)}, bf16[256,256]{1,0:T(8,128)(2,1)S(1)}, u32[]{:S(2)}, u32[]{:S(2)}) collective-permute-start(bf16[256,256]{1,0:T(8,128)(2,1)S(1)} %get-tuple-element.78), channel_id=1, source_target_pairs={{0,8},{8,0},{16,24},{24,16},{32,40},{40,32},{48,56},{56,48},{64,72... | collective-permute-start | bytes 393224 | tf_op jit(solution)/shard_map/ppermute | solution.py:447
  98.3 23.6 %all-to-all-start.4 = ((bf16[4,128,128]{2,1,0:T(8,128)(2,1)}), bf16[4,128,128]{2,1,0:T(8,128)(2,1)S(1)}, u32[]{:S(2)}, u32[]{:S(2)}) async-start(bf16[4,128,128]{2,1,0:T(8,128)(2,1)} %broadcast_in_dim.10), calls=%async_computation.4 | async-start | bytes 262144 | tf_op jit(solution)/shard_map/all_to_all | solution.py:451
  106.7 15.3 %collective-permute-start.6 = (bf16[256,256]{1,0:T(8,128)(2,1)S(1)}, bf16[256,256]{1,0:T(8,128)(2,1)S(1)}, u32[]{:S(2)}, u32[]{:S(2)}) collective-permute-start(bf16[256,256]{1,0:T(8,128)(2,1)S(1)} %get-tuple-element.85), channel_id=1, source_target_pairs={{0,64},{8,72},{16,80},{24,88},{32,96},{40,104},{48,112},{56,120},{... | collective-permute-start | bytes 393224 | tf_op jit(solution)/shard_map/ppermute | solution.py:453
  110.3 11.7 %collective-permute-start.7 = (bf16[256,256]{1,0:T(8,128)(2,1)S(1)}, bf16[256,256]{1,0:T(8,128)(2,1)S(1)}, u32[]{:S(2)}, u32[]{:S(2)}) collective-permute-start(bf16[256,256]{1,0:T(8,128)(2,1)S(1)} %get-tuple-element.86), channel_id=1, source_target_pairs={{0,16},{8,24},{16,0},{24,8},{32,48},{40,56},{48,32},{56,40},{64,80... | collective-permute-start | bytes 393224 | tf_op jit(solution)/shard_map/ppermute | solution.py:453
  122.9 18.4 %all-to-all-start.5 = ((bf16[16,128,128]{2,1,0:T(8,128)(2,1)}), bf16[16,128,128]{2,1,0:T(8,128)(2,1)S(1)}, u32[]{:S(2)}, u32[]{:S(2)}) async-start(bf16[16,128,128]{2,1,0:T(8,128)(2,1)} %broadcast_in_dim.11), calls=%async_computation.5 | async-start | bytes 1048576 | tf_op jit(solution)/shard_map/all_to_all | solution.py:458
  129.0 10.5 %collective-permute-start.8 = (bf16[256,256]{1,0:T(8,128)(2,1)S(1)}, bf16[256,256]{1,0:T(8,128)(2,1)S(1)}, u32[]{:S(2)}, u32[]{:S(2)}) collective-permute-start(bf16[256,256]{1,0:T(8,128)(2,1)S(1)} %get-tuple-element.92), channel_id=1, source_target_pairs={{0,32},{8,40},{16,48},{24,56},{32,0},{40,8},{48,16},{56,24},{64,96... | collective-permute-start | bytes 393224 | tf_op jit(solution)/shard_map/ppermute | solution.py:453
  132.8 6.7 %collective-permute-start.9 = (bf16[256,256]{1,0:T(8,128)(2,1)S(1)}, bf16[256,256]{1,0:T(8,128)(2,1)S(1)}, u32[]{:S(2)}, u32[]{:S(2)}) collective-permute-start(bf16[256,256]{1,0:T(8,128)(2,1)S(1)} %get-tuple-element.93), channel_id=1, source_target_pairs={{8,16},{16,8},{24,32},{32,24},{40,48},{48,40},{56,64},{64,56},{72,... | collective-permute-start | bytes 393224 | tf_op jit(solution)/shard_map/ppermute | solution.py:453
  133.5 1.2 copy-start.2
Sparse Core Ops, SparseCore 0:
  10.7 37.0 all-gather.4
  88.0 27.6 all-gather.6

commit v9 on v8

--- a/solution.py
+++ b/solution.py
@@ -16,6 +16,7 @@
 PATCH = 16
 NT = (((1,), (1,)), ((), ()))
 NN = (((1,), (0,)), ((), ()))
+TN = (((0,), (0,)), ((), ()))
 F32 = jnp.float32
 BF16 = jnp.bfloat16
 MASKED = -1e30
@@ -41,26 +42,43 @@
     return bias + [zero] * NGLOB
 
 
-def cotangent_kernel(head_ref, all_ref, w_ref, out_ref, gatt_ref, cols_ref):
+def cotangent_kernel(head_ref, all_ref, w_hbm, out_ref, gatt_ref, cols_ref, w_ref, sems):
     pieces, length, width = out_ref.shape
     blocks = length // 128
+    copies = [pltpu.make_async_copy(w_hbm, w_ref, sems.at[0])]
+    for c in range(pieces):
+        for b in range(blocks):
+            copies.append(pltpu.make_async_copy(
+                all_ref.at[c, b], out_ref.at[c, pl.ds(b * 128, 128)], sems.at[len(copies)]
+            ))
+    late = len(copies)
+    for c in range(pieces):
+        copies.append(pltpu.make_async_copy(
+            all_ref.at[c, blocks + head_ref[0]], cols_ref.at[c], sems.at[len(copies)]
+        ))
+    for copy in copies:
+        copy.start()
+    for copy in copies[:late]:
+        copy.wait()
     gatt = jnp.zeros((length, width), F32)
     for c in range(pieces):
-        part = all_ref[c, 0:blocks].reshape(length, width)
-        out_ref[c] = part
-        gatt = gatt + dot(part, w_ref[:, c * width:(c + 1) * width], NT)
-        cols_ref[c] = all_ref[c, blocks + head_ref[0]]
+        gatt = gatt + dot(out_ref[c], w_ref[:, c * width:(c + 1) * width], NT)
     gatt_ref[...] = gatt.astype(BF16)
+    for copy in copies[late:]:
+        copy.wait()
 
 
 def near_kernel(
-    pos_ref, pair_ref, own_ref, p0, p2, p3, p4, stats_ref, sum_ref, score_ref,
+    pos_ref, pair_ref, own_ref, p0, p2, p3, p4, gatt_ref,
+    stats_ref, sum_ref, turned_ref, score_ref,
 ):
     length = own_ref.shape[0] // 2
     width = own_ref.shape[1]
     nheads = width // HD
     base2 = 1.0 / math.sqrt(HD) / math.log(2.0)
     bias = block_bias(pos_ref, pair_ref)
+    turned_ref[:width] = own_ref[:length].astype(F32).T.astype(BF16)
+    turned_ref[width:] = gatt_ref[...].astype(F32).T.astype(BF16)
     blocks = ((own_ref, bias[0]), (p0, bias[1]), (p2, bias[3]), (p3, bias[4]), (p4, bias[5]))
     query = own_ref[:length]
     lane = lax.broadcasted_iota(jnp.int32, (1, width), 1)
@@ -89,7 +107,7 @@
 
 
 def forward_kernel(
-    pos_ref, pair_ref, own_ref, p1, near_ref, sum_ref, glob_ref, gout_ref, gatt_ref,
+    pos_ref, pair_ref, own_ref, p1, near_ref, sum_ref, turned_ref, glob_ref, gout_ref, gatt_ref,
     att_ref, sums_ref, stats_ref, gquery_ref,
     score_ref, out_ref,
 ):
@@ -141,15 +159,15 @@
 
     attended = out_ref[...]
     att_ref[...] = attended
-    attended_t = attended.T.astype(BF16)
+    attended_b = attended.astype(BF16)
     for c in range(pieces):
-        part = dot(attended_t, gout_ref[c], NN).astype(BF16)
+        part = dot(attended_b, gout_ref[c], TN).astype(BF16)
         n = width // HD
         sums_ref[c * n:(c + 1) * n, 0:HD, :] = part.reshape(n, HD, 128)
 
     product = gatt_b.astype(F32) * attended
-    query_t = query.astype(F32).T.astype(BF16)
-    gatt_t = gatt_b.astype(F32).T.astype(BF16)
+    query_t = turned_ref[:width]
+    gatt_t = turned_ref[width:]
     for h in range(nheads):
         gatt_h = jnp.where(head == h, gatt_b, jnp.zeros_like(gatt_b))
         row_dot = jnp.sum(jnp.where(head == h, product, 0.0), axis=1, keepdims=True)
@@ -180,7 +198,7 @@
 
 
 def backward_kernel(
-    pos_ref, pair_ref, own_ref, p0, p1, p2, p3, p4, stats_ref, gatt_ref, gglob_ref,
+    pos_ref, pair_ref, own_ref, p0, p1, p2, p3, p4, stats_ref, turned_ref, gatt_ref, gglob_ref,
     r0, r1, r2, r3, r4, gquery_ref, gown_ref,
 ):
     length = own_ref.shape[0] // 2
@@ -192,8 +210,8 @@
     query = own_ref[:length]
     gatt_b = gatt_ref[...]
     head = lax.broadcasted_iota(jnp.int32, (1, width), 1) // HD
-    query_t = query.astype(F32).T.astype(BF16)
-    gatt_t = gatt_b.astype(F32).T.astype(BF16)
+    query_t = turned_ref[:width]
+    gatt_t = turned_ref[width:]
     blocks = (own_ref, p0, p1, p2, p3, p4)
     outs = (gown_ref, r0, r1, r2, r3, r4)
     result = gglob_ref[...]
@@ -292,6 +310,10 @@
     copy_all(copies)
 
 
+def hbm():
+    return pl.BlockSpec(memory_space=pltpu.HBM)
+
+
 def anywhere():
     return pl.BlockSpec(memory_space=pl.ANY)
 
@@ -359,9 +381,13 @@
             jax.ShapeDtypeStruct((length, width), BF16),
             jax.ShapeDtypeStruct((pieces, width, 128), BF16),
         ),
-        in_specs=[smem()] + vmem(2),
+        in_specs=[smem(), hbm(), hbm()],
         out_specs=tuple(vmem(3)),
-        compiler_params=limit(8),
+        scratch_shapes=[
+            pltpu.VMEM((width, pieces * width), BF16),
+            pltpu.SemaphoreType.DMA((1 + pieces * (length // 128 + 1),)),
+        ],
+        compiler_params=limit(58),
         cost_estimate=pl.CostEstimate(
             flops=600_000_000, bytes_accessed=4_000_000, transcendentals=0
         ),
@@ -387,20 +413,20 @@
     nheads = width // HD
     block = jax.ShapeDtypeStruct((2 * width, length), BF16)
     square = jax.ShapeDtypeStruct((length, width), F32)
-    near_stats, near_sum = pl.pallas_call(
+    near_stats, near_sum, turned = pl.pallas_call(
         near_kernel,
-        out_shape=(square, square),
-        in_specs=[smem()] * 2 + vmem(5),
-        out_specs=tuple(vmem(2)),
+        out_shape=(square, square, block),
+        in_specs=[smem()] * 2 + vmem(6),
+        out_specs=tuple(vmem(3)),
         scratch_shapes=[pltpu.VMEM((length, 5 * length), F32)],
         compiler_params=limit(12),
         cost_estimate=pl.CostEstimate(
             flops=1_000_000_000, bytes_accessed=1_000_000, transcendentals=650_000
         ),
         name="near",
-    )(position[None], pair_active, joined, received[0], *received[2:])
-    globals_all, near_stats, near_sum = lax.optimization_barrier(
-        (globals_all, near_stats, near_sum)
+    )(position[None], pair_active, joined, received[0], *received[2:], gatt)
+    globals_all, near_stats, near_sum, turned = lax.optimization_barrier(
+        (globals_all, near_stats, near_sum, turned)
     )
     attended, sums, stats, gglob = pl.pallas_call(
         forward_kernel,
@@ -410,7 +436,7 @@
             square,
             square,
         ),
-        in_specs=[smem()] * 2 + vmem(7),
+        in_specs=[smem()] * 2 + vmem(8),
         out_specs=tuple(vmem(4)),
         scratch_shapes=[
             pltpu.VMEM((nheads, length, (1 + NGLOB) * length), F32),
@@ -422,7 +448,7 @@
         ),
         name="forward",
     )(
-        position[None], pair_active, joined, received[1], near_stats, near_sum,
+        position[None], pair_active, joined, received[1], near_stats, near_sum, turned,
         globals_all, portion_b, gatt,
     )
 
@@ -435,21 +461,22 @@
             square,
             jax.ShapeDtypeStruct((2 * width, length), F32),
         ),
-        in_specs=[smem()] * 2 + vmem(9),
+        in_specs=[smem()] * 2 + vmem(10),
         out_specs=tuple(vmem(7)),
         compiler_params=limit(10),
         cost_estimate=pl.CostEstimate(
             flops=1_000_000, bytes_accessed=10_000, transcendentals=0
         ),
         name="backward",
-    )(position[None], pair_active, joined, *received, stats, gatt, gglob)
+    )(position[None], pair_active, joined, *received, stats, turned, gatt, gglob)
     returned = [None] * len(routes)
-    returned[0] = lax.ppermute(terms[0], CTX, routes[0])
+    for n in (1, 0):
+        returned[n] = lax.ppermute(terms[n], CTX, routes[n])
     shares, *terms = lax.optimization_barrier((shares, *terms))
     share = jnp.sum(shares.astype(F32), axis=0).astype(BF16)
-    share, returned[0] = lax.optimization_barrier((share, returned[0]))
+    share, returned[1], returned[0] = lax.optimization_barrier((share, returned[1], returned[0]))
     column = lax.all_to_all(jnp.broadcast_to(share[None], (his,) + share.shape), "hi", 0, 0)
-    for n in (4, 2, 3, 1):
+    for n in (4, 2, 3):
         returned[n] = lax.ppermute(terms[n], CTX, routes[n])
     share = jnp.sum(column.astype(F32), axis=0).astype(BF16)
     share, returned[4], returned[2], attended_all = lax.optimization_barrier(
@@ -468,9 +495,6 @@
         ),
         name="project",
     )(attended_all, weight_cols)
-    totals, returned[3], returned[1] = lax.optimization_barrier(
-        (totals, returned[3], returned[1])
-    )
     gqk, gval, gweight = pl.pallas_call(
         finish_kernel,
         out_shape=(

time: 153 us -> 153 us (level); the launches traced: 150 us -> 152 us
  starting transfers between devices: 82.5 us -> 85.4 us
  local copies, waits for them, and re-layouts: 6.14 us -> 4.31 us
  Pallas kernels: 18.1 us -> 19.8 us
    ppermute x4 -> x5, starting transfers between devices: 13 us -> 18.1 us  [local(): returned[n] = lax.ppermute(terms[n], CTX, routes[n])]
    ppermute x1 -> x0, starting transfers between devices: 3.83 us -> none  [local(): returned[0] = lax.ppermute(terms[0], CTX, routes[0])]
    all_to_all x1, waiting for transfers between devices: 4.08 us -> 0.73 us  [local(): shares = lax.all_to_all(sums, 'lo', 0, 0)]
    pallas_call x1, Pallas kernels: 0.34 us -> 2.46 us  [local(): pl.pallas_call(cotangent_kernel, out_shape=(jax.ShapeDtypeStruct((pieces,...]
    all_to_all x1, starting transfers between devices: 8.31 us -> 10.2 us  [local(): lax.all_to_all(jnp.broadcast_to(share[None], (his,) + share.shape), 'hi',...]
    unnamed x14 -> x18, local copies, waits for them, and re-layouts: 4.57 us -> 2.74 us
    all_to_all x1, waiting for transfers between devices: 1.76 us -> 3.35 us  [local(): lax.all_to_all(jnp.broadcast_to(share[None], (los,) + share.shape), 'lo',...]
    ppermute x4 -> x5, waiting for transfers between devices: 3.88 us -> 5.06 us  [local(): returned[n] = lax.ppermute(terms[n], CTX, routes[n])]
  transfers between devices with their start and end apart: 18 -> 18, of which waited for: 8 -> 9; matrix products, arithmetic and copies ran while one was open for 1% -> 1% of each run, Pallas kernels for 7% -> 8%
where the time goes in v9:
time: 153 us; the launch traced here: 152 us
  starting transfers between devices  85.4 us (56%)
  waiting for transfers between devices  27.7 us (18%)
  Pallas kernels  19.8 us (13%)
  between operations  14.3 us (9%)
  local copies, waits for them, and re-layouts  4.31 us (3%)
    ppermute x5, starting transfers between devices, local(): returned[n] = lax.ppermute(terms[n], CTX, routes[n])  18.1 us
    all_to_all x1, starting transfers between devices, local(): column = lax.all_to_all(picked, 'hi', 0, 0)  12.4 us
    all_to_all x1, starting transfers between devices, local(): lax.all_to_all(jnp.broadcast_to(share[None], (his,) + share.shape), 'hi',...  10.2 us
    all_to_all x1, starting transfers between devices, local(): slices = lax.all_to_all(joined.reshape(los, step, width), 'lo', 0, 0)  8.61 us
    ppermute x2, starting transfers between devices, local(): received[n] = lax.ppermute(joined, CTX, routes[n])  8.1 us
    ppermute x2, starting transfers between devices, local(): received[n] = lax.ppermute(joined_late, CTX, routes[n])  8.09 us
    all_to_all x1, starting transfers between devices, local(): shares = lax.all_to_all(sums, 'lo', 0, 0)  7.55 us
    all_to_all x1, waiting for transfers between devices, local(): lax.all_to_all(jnp.broadcast_to(share[None], (his,) + share.shape), 'hi',...  6.71 us
  transfers between devices with their start and end apart: 18, of which 9 were waited for; matrix products, arithmetic and copies ran while one was open for 1% of the time, Pallas kernels for 8%

profile of v9, /device:TPU:24, one launch (start us, length us, event | category | flops | bytes accessed | tf_op | source)
XLA Modules:
  0.0 151.6 jit_solution(15013309933058189063)
XLA Ops:
  7.2 0.0 copy-start.6
  7.2 0.0 all-gather.5.cloned.1.call-start
  7.2 1.8 %pack.1 = (bf16[512,128]{1,0:T(8,128)(2,1)}, bf16[10,128,128]{2,1,0:T(8,128)(2,1)}) custom-call(bf16[256,128]{1,0:T(8,128)(2,1)} %qk_ref.1, bf16[256,128]{1,0:T(8,128)(2,1)} %val_ref.1, bf16[256,128]{1,0:T(8,128)(2,1)} %gout_ref.1, bf16[128,1024]{1,0:T(8,128)(2,1)} %w_hbm.1), custom_call_target="tpu_custom_call" | custom-call | tf_op jit(solution)/shard_map/pack/pallas_call | solution.py:342
  9.1 0.0 all-gather.5.cloned.1.call-update
  9.1 8.6 %all-to-all-start = ((bf16[16,32,128]{2,1,0:T(8,128)(2,1)}), bf16[16,32,128]{2,1,0:T(8,128)(2,1)S(1)}, u32[]{:S(2)}, u32[]{:S(2)}) async-start(bf16[16,32,128]{2,1,0:T(8,128)(2,1)} %bitcast.6), calls=%async_computation | async-start | bytes 262144 | tf_op jit(solution)/shard_map/all_to_all | solution.py:353
  17.7 4.7 %collective-permute-start = (bf16[512,128]{1,0:T(8,128)(2,1)}, bf16[512,128]{1,0:T(8,128)(2,1)S(1)}, u32[]{:S(2)}, u32[]{:S(2)}) collective-permute-start(bf16[512,128]{1,0:T(8,128)(2,1)} %get-tuple-element.61.own_ref), channel_id=1, source_target_pairs={{0,64},{8,72},{16,80},{24,88},{32,96},{40,104},{48,112},{56,120},{... | collective-permute-start | bytes 393224 | tf_op jit(solution)/shard_map/ppermute | solution.py:361
  22.5 3.4 %collective-permute-start.1 = (bf16[512,128]{1,0:T(8,128)(2,1)}, bf16[512,128]{1,0:T(8,128)(2,1)S(1)}, u32[]{:S(2)}, u32[]{:S(2)}) collective-permute-start(bf16[512,128]{1,0:T(8,128)(2,1)} %get-tuple-element.61.own_ref), channel_id=1, source_target_pairs={{0,8},{8,0},{16,24},{24,16},{32,40},{40,32},{48,56},{56,48},{64,72... | collective-permute-start | bytes 393224 | tf_op jit(solution)/shard_map/ppermute | solution.py:361
  25.8 1.2 all-to-all-done.slices_ref
  27.0 0.7 copy-done.5
  27.6 1.2 pick.1
  28.9 0.8 collective-permute-done.p4
  29.7 12.4 %all-to-all-start.1 = ((bf16[4,2,32,128]{3,2,1,0:T(8,128)(2,1)}), bf16[4,2,32,128]{3,2,1,0:T(8,128)(2,1)S(1)}, u32[]{:S(2)}, u32[]{:S(2)}) async-start(bf16[4,2,32,128]{3,2,1,0:T(8,128)(2,1)} %pick.1), calls=%async_computation.1 | async-start | bytes 131072 | tf_op jit(solution)/shard_map/all_to_all | solution.py:374
  42.1 3.2 %collective-permute-start.2 = (bf16[512,128]{1,0:T(8,128)(2,1)}, bf16[512,128]{1,0:T(8,128)(2,1)S(1)}, u32[]{:S(2)}, u32[]{:S(2)}) collective-permute-start(bf16[512,128]{1,0:T(8,128)(2,1)} %get-tuple-element.61.own_ref), channel_id=1, source_target_pairs={{0,32},{8,40},{16,48},{24,56},{32,0},{40,8},{48,16},{56,24},{64,96... | collective-permute-start | bytes 393224 | tf_op jit(solution)/shard_map/ppermute | solution.py:376
  45.3 4.9 %collective-permute-start.3 = (bf16[512,128]{1,0:T(8,128)(2,1)}, bf16[512,128]{1,0:T(8,128)(2,1)S(1)}, u32[]{:S(2)}, u32[]{:S(2)}) collective-permute-start(bf16[512,128]{1,0:T(8,128)(2,1)} %get-tuple-element.61.own_ref), channel_id=1, source_target_pairs={{0,16},{8,24},{16,0},{24,8},{32,48},{40,56},{48,32},{56,40},{64,80... | collective-permute-start | bytes 393224 | tf_op jit(solution)/shard_map/ppermute | solution.py:376
  50.2 0.0 all-gather.5.cloned.1.call-done
  50.2 2.5 %cotangent.1 = (bf16[8,256,128]{2,1,0:T(8,128)(2,1)}, bf16[256,128]{1,0:T(8,128)(2,1)}, bf16[8,128,128]{2,1,0:T(8,128)(2,1)}) custom-call(s32[1]{0:T(128)} %bitcast.2.head_ref, bf16[8,10,128,128]{3,2,1,0:T(8,128)(2,1)} %bitcast.7, bf16[128,1024]{1,0:T(8,128)(2,1)} %w_hbm.1), custom_call_target="tpu_custom_call" | custom-call | flops 600000000 | bytes 4000000 | tf_op jit(solution)/shard_map/cotangent/pallas_call | solution.py:377
  52.7 0.0 copy-start.8
  52.7 2.6 %all-to-all-done.1.slices_ref = bf16[4,2,32,128]{3,2,1,0:T(8,128)(2,1)S(1)} async-done(((bf16[4,2,32,128]{3,2,1,0:T(8,128)(2,1)}), bf16[4,2,32,128]{3,2,1,0:T(8,128)(2,1)S(1)}, u32[]{:S(2)}, u32[]{:S(2)}) %all-to-all-start.1) | async-done | bytes 65568 | tf_op jit(solution)/shard_map/all_to_all | solution.py:374
  55.3 1.6 %spread.1 = bf16[16,2,32,128]{3,2,1,0:T(8,128)(2,1)} custom-call(s32[2]{0:T(128)S(1)} %copy-done.6, bf16[4,2,32,128]{3,2,1,0:T(8,128)(2,1)S(1)} %all-to-all-done.1.slices_ref), custom_call_target="tpu_custom_call" | custom-call | tf_op jit(solution)/shard_map/spread/pallas_call | solution.py:399
  56.9 5.9 %all-to-all-start.2 = ((bf16[16,2,32,128]{3,2,1,0:T(8,128)(2,1)}), bf16[16,2,32,128]{3,2,1,0:T(8,128)(2,1)S(1)}, u32[]{:S(2)}, u32[]{:S(2)}) async-start(bf16[16,2,32,128]{3,2,1,0:T(8,128)(2,1)} %spread.1), calls=%async_computation.2 | async-start | bytes 524288 | tf_op jit(solution)/shard_map/all_to_all | solution.py:411
  62.8 0.7 collective-permute-start.4
  63.5 0.8 copy-done.3
  64.3 1.9 %near.1 = (f32[256,128]{1,0:T(8,128)S(1)}, f32[256,128]{1,0:T(8,128)S(1)}, bf16[256,256]{1,0:T(8,128)(2,1)S(1)}) custom-call(s32[1]{0:T(128)} %bitcast.pos_ref, s32[4,32]{1,0:T(4,128)S(1)} %copy-done.7, bf16[512,128]{1,0:T(8,128)(2,1)S(1)} %copy-done.1, bf16[512,128]{1,0:T(8,128)(2,1)S(1)} %collective-permute-done.1.p0, ...), custom_call_target="tpu_custom_call" | custom-call | flops 1000000000 | bytes 1000000 | tf_op jit(solution)/shard_map/near/pallas_call | solution.py:416
  66.2 6.6 %all-to-all-done.2.glob_ref = bf16[16,2,32,128]{3,2,1,0:T(8,128)(2,1)S(1)} async-done(((bf16[16,2,32,128]{3,2,1,0:T(8,128)(2,1)}), bf16[16,2,32,128]{3,2,1,0:T(8,128)(2,1)S(1)}, u32[]{:S(2)}, u32[]{:S(2)}) %all-to-all-start.2) | async-done | bytes 262176 | tf_op jit(solution)/shard_map/all_to_all | solution.py:411
  72.8 4.5 %forward.1 = (f32[256,128]{1,0:T(8,128)}, bf16[16,128,128]{2,1,0:T(8,128)(2,1)}, f32[256,128]{1,0:T(8,128)S(1)}, f32[256,128]{1,0:T(8,128)S(1)}) custom-call(s32[1]{0:T(128)} %bitcast.pos_ref, s32[4,32]{1,0:T(4,128)S(1)} %copy-done.7, bf16[512,128]{1,0:T(8,128)(2,1)S(1)} %copy-done.1, bf16[512,128]{1,0:T(8,128)(2,1)S(1)} %collective-permute-done.4.p1, ...), custom_call_target="tpu_custom_call" | custom-call | flops 3000000000 | bytes 4000000 | tf_op jit(solution)/shard_map/forward/pallas_call | solution.py:431
  77.3 7.5 %all-to-all-start.3 = ((bf16[16,128,128]{2,1,0:T(8,128)(2,1)}), bf16[16,128,128]{2,1,0:T(8,128)(2,1)S(1)}, u32[]{:S(2)}, u32[]{:S(2)}) async-start(bf16[16,128,128]{2,1,0:T(8,128)(2,1)} %get-tuple-element.76), calls=%async_computation.3 | async-start | bytes 1048576 | tf_op jit(solution)/shard_map/all_to_all | solution.py:455
  84.8 0.0 all-gather.7.cloned.1.call-start
  84.9 0.7 all-gather.7.cloned.1.call-update
  85.6 3.9 %backward.1 = (bf16[256,256]{1,0:T(8,128)(2,1)S(1)}, bf16[256,256]{1,0:T(8,128)(2,1)S(1)}, bf16[256,256]{1,0:T(8,128)(2,1)S(1)}, bf16[256,256]{1,0:T(8,128)(2,1)...) custom-call(s32[1]{0:T(128)} %bitcast.pos_ref, s32[4,32]{1,0:T(4,128)S(1)} %copy-done.7, ...), custom_call_target="tpu_custom_call" | custom-call | flops 1000000 | bytes 10000 | tf_op jit(solution)/shard_map/backward/pallas_call | solution.py:457
  89.4 0.7 collective-permute-start.5
  90.1 6.5 %collective-permute-start.6 = (bf16[256,256]{1,0:T(8,128)(2,1)S(1)}, bf16[256,256]{1,0:T(8,128)(2,1)S(1)}, u32[]{:S(2)}, u32[]{:S(2)}) collective-permute-start(bf16[256,256]{1,0:T(8,128)(2,1)S(1)} %get-tuple-element.79), channel_id=1, source_target_pairs={{0,8},{8,0},{16,24},{24,16},{32,40},{40,32},{48,56},{56,48},{64,72... | collective-permute-start | bytes 393224 | tf_op jit(solution)/shard_map/ppermute | solution.py:474
  96.7 0.7 all-to-all-done.3
  97.4 0.1 reduce_sum.24
  97.5 2.1 %collective-permute-done.6.b0 = bf16[256,256]{1,0:T(8,128)(2,1)S(1)} collective-permute-done((bf16[256,256]{1,0:T(8,128)(2,1)S(1)}, bf16[256,256]{1,0:T(8,128)(2,1)S(1)}, u32[]{:S(2)}, u32[]{:S(2)}) %collective-permute-start.6) | collective-permute-done | bytes 131104 | tf_op jit(solution)/shard_map/ppermute | solution.py:474
  99.6 0.7 broadcast_in_dim.10
  100.3 10.2 %all-to-all-start.4 = ((bf16[4,128,128]{2,1,0:T(8,128)(2,1)}), bf16[4,128,128]{2,1,0:T(8,128)(2,1)S(1)}, u32[]{:S(2)}, u32[]{:S(2)}) async-start(bf16[4,128,128]{2,1,0:T(8,128)(2,1)} %broadcast_in_dim.10), calls=%async_computation.4 | async-start | bytes 262144 | tf_op jit(solution)/shard_map/all_to_all | solution.py:478
  110.4 4.3 %collective-permute-start.7 = (bf16[256,256]{1,0:T(8,128)(2,1)S(1)}, bf16[256,256]{1,0:T(8,128)(2,1)S(1)}, u32[]{:S(2)}, u32[]{:S(2)}) collective-permute-start(bf16[256,256]{1,0:T(8,128)(2,1)S(1)} %get-tuple-element.86), channel_id=1, source_target_pairs={{0,64},{8,72},{16,80},{24,88},{32,96},{40,104},{48,112},{56,120},{... | collective-permute-start | bytes 393224 | tf_op jit(solution)/shard_map/ppermute | solution.py:480
  114.7 2.8 %collective-permute-start.8 = (bf16[256,256]{1,0:T(8,128)(2,1)S(1)}, bf16[256,256]{1,0:T(8,128)(2,1)S(1)}, u32[]{:S(2)}, u32[]{:S(2)}) collective-permute-start(bf16[256,256]{1,0:T(8,128)(2,1)S(1)} %get-tuple-element.87), channel_id=1, source_target_pairs={{0,16},{8,24},{16,0},{24,8},{32,48},{40,56},{48,32},{56,40},{64,80... | collective-permute-start | bytes 393224 | tf_op jit(solution)/shard_map/ppermute | solution.py:480
  117.5 6.7 %all-to-all-done.4 = bf16[4,128,128]{2,1,0:T(8,128)(2,1)S(1)} async-done(((bf16[4,128,128]{2,1,0:T(8,128)(2,1)}), bf16[4,128,128]{2,1,0:T(8,128)(2,1)S(1)}, u32[]{:S(2)}, u32[]{:S(2)}) %all-to-all-start.4) | async-done | bytes 131104 | tf_op jit(solution)/shard_map/all_to_all | solution.py:478
  124.2 0.0 all-gather.7.cloned.1.call-done
  124.3 0.9 broadcast_in_dim.11
  125.2 5.7 %all-to-all-start.5 = ((bf16[16,128,128]{2,1,0:T(8,128)(2,1)}), bf16[16,128,128]{2,1,0:T(8,128)(2,1)S(1)}, u32[]{:S(2)}, u32[]{:S(2)}) async-start(bf16[16,128,128]{2,1,0:T(8,128)(2,1)} %broadcast_in_dim.11), calls=%async_computation.5 | async-start | bytes 1048576 | tf_op jit(solution)/shard_map/all_to_all | solution.py:485
  130.9 3.8 %collective-permute-start.9 = (bf16[256,256]{1,0:T(8,128)(2,1)S(1)}, bf16[256,256]{1,0:T(8,128)(2,1)S(1)}, u32[]{:S(2)}, u32[]{:S(2)}) collective-permute-start(bf16[256,256]{1,0:T(8,128)(2,1)S(1)} %get-tuple-element.94), channel_id=1, source_target_pairs={{0,32},{8,40},{16,48},{24,56},{32,0},{40,8},{48,16},{56,24},{64,96... | collective-permute-start | bytes 393224 | tf_op jit(solution)/shard_map/ppermute | solution.py:480
  134.8 1.2 copy-done
  136.0 0.9 project.1
  136.9 2.9 %collective-permute-done.9.b3 = bf16[256,256]{1,0:T(8,128)(2,1)S(1)} collective-permute-done((bf16[256,256]{1,0:T(8,128)(2,1)S(1)}, bf16[256,256]{1,0:T(8,128)(2,1)S(1)}, u32[]{:S(2)}, u32[]{:S(2)}) %collective-permute-start.9) | collective-permute-done | bytes 131104 | tf_op jit(solution)/shard_map/ppermute | solution.py:480
  139.9 3.4 %all-to-all-done.5.total_ref = bf16[16,128,128]{2,1,0:T(8,128)(2,1)S(1)} async-done(((bf16[16,128,128]{2,1,0:T(8,128)(2,1)}), bf16[16,128,128]{2,1,0:T(8,128)(2,1)S(1)}, u32[]{:S(2)}, u32[]{:S(2)}) %all-to-all-start.5) | async-done | bytes 524320 | tf_op jit(solution)/shard_map/all_to_all | solution.py:485
  143.2 1.6 %finish.1 = (bf16[256,128]{1,0:T(8,128)(2,1)}, bf16[256,128]{1,0:T(8,128)(2,1)}, f32[128,1024]{1,0:T(8,128)}) custom-call(s32[1]{0:T(128)} %bitcast.pos_ref, s32[2]{0:T(128)S(1)} %copy-done.6, bf16[256,256]{1,0:T(8,128)(2,1)S(1)} %collective-permute-done.6.b0, bf16[256,256]{1,0:T(8,128)(2,1)S(1)} %collective-permute-done.5.b1, ...), custom_call_target="tpu_custom_call" | custom-call | flops 2000000 | bytes 2500000 | tf_op jit(solution)/shard_map/finish/pallas_call | solution.py:498
  (21 shorter events, 0.1 us)
Async XLA Ops:
  7.2 48.1 %copy-start.6 = (s32[2]{0:T(128)S(1)}, s32[2]{0:T(128)}, u32[]{:S(2)}) copy-start(s32[2]{0:T(128)} %ids_ref.5) | copy-start | bytes 28
  7.2 56.3 %copy-start.7 = (s32[4,32]{1,0:T(4,128)S(1)}, s32[4,32]{1,0:T(4,128)}, u32[]{:S(2)}) copy-start(s32[4,32]{1,0:T(4,128)} %pair_ref.5) | copy-start | bytes 1540
  7.2 43.0 %all-gather.5.cloned.1.call-start = ((), (), s32[]{:S(2)}) async-start(), calls=%async_computation.6 | async-start | bytes 2949120 | tf_op jit(solution)/shard_map/all_gather | solution.py:354
  9.1 53.7 %copy-start.1 = (bf16[512,128]{1,0:T(8,128)(2,1)S(1)}, bf16[512,128]{1,0:T(8,128)(2,1)}, u32[]{:S(2)}) copy-start(bf16[512,128]{1,0:T(8,128)(2,1)} %get-tuple-element.61.own_ref) | copy-start | bytes 393220
  9.1 17.9 %all-to-all-start = ((bf16[16,32,128]{2,1,0:T(8,128)(2,1)}), bf16[16,32,128]{2,1,0:T(8,128)(2,1)S(1)}, u32[]{:S(2)}, u32[]{:S(2)}) async-start(bf16[16,32,128]{2,1,0:T(8,128)(2,1)} %bitcast.6), calls=%async_computation | async-start | bytes 262144 | tf_op jit(solution)/shard_map/all_to_all | solution.py:353
  17.7 11.9 %collective-permute-start = (bf16[512,128]{1,0:T(8,128)(2,1)}, bf16[512,128]{1,0:T(8,128)(2,1)S(1)}, u32[]{:S(2)}, u32[]{:S(2)}) collective-permute-start(bf16[512,128]{1,0:T(8,128)(2,1)} %get-tuple-element.61.own_ref), channel_id=1, source_target_pairs={{0,64},{8,72},{16,80},{24,88},{32,96},{40,104},{48,112},{56,120},{... | collective-permute-start | bytes 393224 | tf_op jit(solution)/shard_map/ppermute | solution.py:361
  22.5 7.2 %collective-permute-start.1 = (bf16[512,128]{1,0:T(8,128)(2,1)}, bf16[512,128]{1,0:T(8,128)(2,1)S(1)}, u32[]{:S(2)}, u32[]{:S(2)}) collective-permute-start(bf16[512,128]{1,0:T(8,128)(2,1)} %get-tuple-element.61.own_ref), channel_id=1, source_target_pairs={{0,8},{8,0},{16,24},{24,16},{32,40},{40,32},{48,56},{56,48},{64,72... | collective-permute-start | bytes 393224 | tf_op jit(solution)/shard_map/ppermute | solution.py:361
  27.0 0.7 copy-start.5
  29.7 25.6 %all-to-all-start.1 = ((bf16[4,2,32,128]{3,2,1,0:T(8,128)(2,1)}), bf16[4,2,32,128]{3,2,1,0:T(8,128)(2,1)S(1)}, u32[]{:S(2)}, u32[]{:S(2)}) async-start(bf16[4,2,32,128]{3,2,1,0:T(8,128)(2,1)} %pick.1), calls=%async_computation.1 | async-start | bytes 131072 | tf_op jit(solution)/shard_map/all_to_all | solution.py:374
  42.1 14.8 %collective-permute-start.2 = (bf16[512,128]{1,0:T(8,128)(2,1)}, bf16[512,128]{1,0:T(8,128)(2,1)S(1)}, u32[]{:S(2)}, u32[]{:S(2)}) collective-permute-start(bf16[512,128]{1,0:T(8,128)(2,1)} %get-tuple-element.61.own_ref), channel_id=1, source_target_pairs={{0,32},{8,40},{16,48},{24,56},{32,0},{40,8},{48,16},{56,24},{64,96... | collective-permute-start | bytes 393224 | tf_op jit(solution)/shard_map/ppermute | solution.py:376
  45.3 11.6 %collective-permute-start.3 = (bf16[512,128]{1,0:T(8,128)(2,1)}, bf16[512,128]{1,0:T(8,128)(2,1)S(1)}, u32[]{:S(2)}, u32[]{:S(2)}) collective-permute-start(bf16[512,128]{1,0:T(8,128)(2,1)} %get-tuple-element.61.own_ref), channel_id=1, source_target_pairs={{0,16},{8,24},{16,0},{24,8},{32,48},{40,56},{48,32},{56,40},{64,80... | collective-permute-start | bytes 393224 | tf_op jit(solution)/shard_map/ppermute | solution.py:376
  52.7 20.1 %copy-start.4 = (bf16[256,128]{1,0:T(8,128)(2,1)S(1)}, bf16[256,128]{1,0:T(8,128)(2,1)}, u32[]{:S(2)}) copy-start(bf16[256,128]{1,0:T(8,128)(2,1)} %get-tuple-element.67.gatt_ref) | copy-start | bytes 196612
  52.7 20.1 %copy-start.8 = (bf16[8,256,128]{2,1,0:T(8,128)(2,1)S(1)}, bf16[8,256,128]{2,1,0:T(8,128)(2,1)}, u32[]{:S(2)}) copy-start(bf16[8,256,128]{2,1,0:T(8,128)(2,1)} %get-tuple-element.75.gout_ref) | copy-start | bytes 1572868
  56.9 15.9 %all-to-all-start.2 = ((bf16[16,2,32,128]{3,2,1,0:T(8,128)(2,1)}), bf16[16,2,32,128]{3,2,1,0:T(8,128)(2,1)S(1)}, u32[]{:S(2)}, u32[]{:S(2)}) async-start(bf16[16,2,32,128]{3,2,1,0:T(8,128)(2,1)} %spread.1), calls=%async_computation.2 | async-start | bytes 524288 | tf_op jit(solution)/shard_map/all_to_all | solution.py:411
  62.8 10.0 %collective-permute-start.4 = (bf16[512,128]{1,0:T(8,128)(2,1)S(1)}, bf16[512,128]{1,0:T(8,128)(2,1)S(1)}, u32[]{:S(2)}, u32[]{:S(2)}) collective-permute-start(bf16[512,128]{1,0:T(8,128)(2,1)S(1)} %copy-done.1), channel_id=1, source_target_pairs={{8,16},{16,8},{24,32},{32,24},{40,48},{48,40},{56,64},{64,56},{72,... | collective-permute-start | bytes 393224 | tf_op jit(solution)/shard_map/ppermute | solution.py:412
  63.5 0.8 copy-start.3
  77.3 57.5 %copy-start.2 = (bf16[8,128,128]{2,1,0:T(8,128)(2,1)S(1)}, bf16[8,128,128]{2,1,0:T(8,128)(2,1)}, u32[]{:S(2)}) copy-start(bf16[8,128,128]{2,1,0:T(8,128)(2,1)} %get-tuple-element.90.w_ref) | copy-start | bytes 786436
  77.3 20.1 %all-to-all-start.3 = ((bf16[16,128,128]{2,1,0:T(8,128)(2,1)}), bf16[16,128,128]{2,1,0:T(8,128)(2,1)S(1)}, u32[]{:S(2)}, u32[]{:S(2)}) async-start(bf16[16,128,128]{2,1,0:T(8,128)(2,1)} %get-tuple-element.76), calls=%async_computation.3 | async-start | bytes 1048576 | tf_op jit(solution)/shard_map/all_to_all | solution.py:455
  84.8 39.4 %all-gather.7.cloned.1.call-start = ((), (), s32[]{:S(2)}) async-start(), calls=%async_computation.7 | async-start | bytes 1179648 | tf_op jit(solution)/shard_map/all_gather | solution.py:456
  89.4 8.0 %collective-permute-start.5 = (bf16[256,256]{1,0:T(8,128)(2,1)S(1)}, bf16[256,256]{1,0:T(8,128)(2,1)S(1)}, u32[]{:S(2)}, u32[]{:S(2)}) collective-permute-start(bf16[256,256]{1,0:T(8,128)(2,1)S(1)} %get-tuple-element.80), channel_id=1, source_target_pairs={{8,16},{16,8},{24,32},{32,24},{40,48},{48,40},{56,64},{64,56},{72,... | collective-permute-start | bytes 393224 | tf_op jit(solution)/shard_map/ppermute | solution.py:474
  90.1 9.5 %collective-permute-start.6 = (bf16[256,256]{1,0:T(8,128)(2,1)S(1)}, bf16[256,256]{1,0:T(8,128)(2,1)S(1)}, u32[]{:S(2)}, u32[]{:S(2)}) collective-permute-start(bf16[256,256]{1,0:T(8,128)(2,1)S(1)} %get-tuple-element.79), channel_id=1, source_target_pairs={{0,8},{8,0},{16,24},{24,16},{32,40},{40,32},{48,56},{56,48},{64,72... | collective-permute-start | bytes 393224 | tf_op jit(solution)/shard_map/ppermute | solution.py:474
  100.3 24.0 %all-to-all-start.4 = ((bf16[4,128,128]{2,1,0:T(8,128)(2,1)}), bf16[4,128,128]{2,1,0:T(8,128)(2,1)S(1)}, u32[]{:S(2)}, u32[]{:S(2)}) async-start(bf16[4,128,128]{2,1,0:T(8,128)(2,1)} %broadcast_in_dim.10), calls=%async_computation.4 | async-start | bytes 262144 | tf_op jit(solution)/shard_map/all_to_all | solution.py:478
  110.4 13.9 %collective-permute-start.7 = (bf16[256,256]{1,0:T(8,128)(2,1)S(1)}, bf16[256,256]{1,0:T(8,128)(2,1)S(1)}, u32[]{:S(2)}, u32[]{:S(2)}) collective-permute-start(bf16[256,256]{1,0:T(8,128)(2,1)S(1)} %get-tuple-element.86), channel_id=1, source_target_pairs={{0,64},{8,72},{16,80},{24,88},{32,96},{40,104},{48,112},{56,120},{... | collective-permute-start | bytes 393224 | tf_op jit(solution)/shard_map/ppermute | solution.py:480
  114.7 9.6 %collective-permute-start.8 = (bf16[256,256]{1,0:T(8,128)(2,1)S(1)}, bf16[256,256]{1,0:T(8,128)(2,1)S(1)}, u32[]{:S(2)}, u32[]{:S(2)}) collective-permute-start(bf16[256,256]{1,0:T(8,128)(2,1)S(1)} %get-tuple-element.87), channel_id=1, source_target_pairs={{0,16},{8,24},{16,0},{24,8},{32,48},{40,56},{48,32},{56,40},{64,80... | collective-permute-start | bytes 393224 | tf_op jit(solution)/shard_map/ppermute | solution.py:480
  125.2 18.0 %all-to-all-start.5 = ((bf16[16,128,128]{2,1,0:T(8,128)(2,1)}), bf16[16,128,128]{2,1,0:T(8,128)(2,1)S(1)}, u32[]{:S(2)}, u32[]{:S(2)}) async-start(bf16[16,128,128]{2,1,0:T(8,128)(2,1)} %broadcast_in_dim.11), calls=%async_computation.5 | async-start | bytes 1048576 | tf_op jit(solution)/shard_map/all_to_all | solution.py:485
  130.9 8.9 %collective-permute-start.9 = (bf16[256,256]{1,0:T(8,128)(2,1)S(1)}, bf16[256,256]{1,0:T(8,128)(2,1)S(1)}, u32[]{:S(2)}, u32[]{:S(2)}) collective-permute-start(bf16[256,256]{1,0:T(8,128)(2,1)S(1)} %get-tuple-element.94), channel_id=1, source_target_pairs={{0,32},{8,40},{16,48},{24,56},{32,0},{40,8},{48,16},{56,24},{64,96... | collective-permute-start | bytes 393224 | tf_op jit(solution)/shard_map/ppermute | solution.py:480
  134.8 1.2 copy-start
Sparse Core Ops, SparseCore 0:
  10.7 37.0 all-gather.4
  87.8 27.6 all-gather.6

commit v10 on v9

--- a/solution.py
+++ b/solution.py
@@ -42,7 +42,9 @@
     return bias + [zero] * NGLOB
 
 
-def cotangent_kernel(head_ref, all_ref, w_hbm, out_ref, gatt_ref, cols_ref, w_ref, sems):
+def cotangent_kernel(
+    head_ref, all_ref, w_hbm, out_ref, gatt_ref, gattt_ref, cols_ref, w_ref, sems
+):
     pieces, length, width = out_ref.shape
     blocks = length // 128
     copies = [pltpu.make_async_copy(w_hbm, w_ref, sems.at[0])]
@@ -64,21 +66,20 @@
     for c in range(pieces):
         gatt = gatt + dot(out_ref[c], w_ref[:, c * width:(c + 1) * width], NT)
     gatt_ref[...] = gatt.astype(BF16)
+    gattt_ref[...] = gatt.T.astype(BF16)
     for copy in copies[late:]:
         copy.wait()
 
 
 def near_kernel(
-    pos_ref, pair_ref, own_ref, p0, p2, p3, p4, gatt_ref,
-    stats_ref, sum_ref, turned_ref, score_ref,
+    pos_ref, pair_ref, own_ref, p0, p2, p3, p4, stats_ref, sum_ref, turned_ref, score_ref,
 ):
     length = own_ref.shape[0] // 2
     width = own_ref.shape[1]
     nheads = width // HD
     base2 = 1.0 / math.sqrt(HD) / math.log(2.0)
     bias = block_bias(pos_ref, pair_ref)
-    turned_ref[:width] = own_ref[:length].astype(F32).T.astype(BF16)
-    turned_ref[width:] = gatt_ref[...].astype(F32).T.astype(BF16)
+    turned_ref[...] = own_ref[:length].astype(F32).T.astype(BF16)
     blocks = ((own_ref, bias[0]), (p0, bias[1]), (p2, bias[3]), (p3, bias[4]), (p4, bias[5]))
     query = own_ref[:length]
     lane = lax.broadcasted_iota(jnp.int32, (1, width), 1)
@@ -107,7 +108,8 @@
 
 
 def forward_kernel(
-    pos_ref, pair_ref, own_ref, p1, near_ref, sum_ref, turned_ref, glob_ref, gout_ref, gatt_ref,
+    pos_ref, pair_ref, own_ref, p1, near_ref, sum_ref, turned_ref, gattt_ref, glob_ref, gout_ref,
+    gatt_ref,
     att_ref, sums_ref, stats_ref, gquery_ref,
     score_ref, out_ref,
 ):
@@ -166,8 +168,8 @@
         sums_ref[c * n:(c + 1) * n, 0:HD, :] = part.reshape(n, HD, 128)
 
     product = gatt_b.astype(F32) * attended
-    query_t = turned_ref[:width]
-    gatt_t = turned_ref[width:]
+    query_t = turned_ref[...]
+    gatt_t = gattt_ref[...]
     for h in range(nheads):
         gatt_h = jnp.where(head == h, gatt_b, jnp.zeros_like(gatt_b))
         row_dot = jnp.sum(jnp.where(head == h, product, 0.0), axis=1, keepdims=True)
@@ -198,8 +200,7 @@
 
 
 def backward_kernel(
-    pos_ref, pair_ref, own_ref, p0, p1, p2, p3, p4, stats_ref, turned_ref, gatt_ref, gglob_ref,
-    r0, r1, r2, r3, r4, gquery_ref, gown_ref,
+    slots, pos_ref, pair_ref, own_ref, stats_ref, turned_ref, gattt_ref, gatt_ref, gsum_ref, *refs
 ):
     length = own_ref.shape[0] // 2
     width = own_ref.shape[1]
@@ -207,14 +208,17 @@
     scaling = 1.0 / math.sqrt(HD)
     base2 = scaling / math.log(2.0)
     bias = block_bias(pos_ref, pair_ref)
+    inputs = sum(slot > 0 for slot in slots)
+    blocks = list(refs[:inputs])
+    outs, gquery_ref = refs[inputs:-1], refs[-1]
+    if 0 in slots:
+        blocks.insert(slots.index(0), own_ref)
     query = own_ref[:length]
     gatt_b = gatt_ref[...]
     head = lax.broadcasted_iota(jnp.int32, (1, width), 1) // HD
-    query_t = turned_ref[:width]
-    gatt_t = turned_ref[width:]
-    blocks = (own_ref, p0, p1, p2, p3, p4)
-    outs = (gown_ref, r0, r1, r2, r3, r4)
-    result = gglob_ref[...]
+    query_t = turned_ref[...]
+    gatt_t = gattt_ref[...]
+    result = gsum_ref[...]
     for h in range(nheads):
         query_h = jnp.where(head == h, query, jnp.zeros_like(query))
         gatt_h = jnp.where(head == h, gatt_b, jnp.zeros_like(gatt_b))
@@ -223,20 +227,19 @@
         qt = query_t[h * HD:(h + 1) * HD]
         gt = gatt_t[h * HD:(h + 1) * HD]
         acc = jnp.zeros((length, width), F32)
-        for b in (1, 2, 3, 4, 5, 0):
-            keys = blocks[b][:length]
-            s = dot(query_h, keys, NT) * base2 + (bias[b] - log_total)
+        for slot, ref, o in zip(slots, blocks, outs):
+            keys = ref[:length]
+            s = dot(query_h, keys, NT) * base2 + (bias[slot] - log_total)
             weights = jnp.exp2(s)
-            gw = dot(gatt_h, blocks[b][length:], NT)
+            gw = dot(gatt_h, ref[length:], NT)
             gs = (weights * (gw - row_dot)).astype(BF16)
             acc = acc + dot(gs, keys, NN)
             gk = dot(qt, gs, NN) * scaling
             gv = dot(gt, weights.astype(BF16), NN)
-            o = outs[b]
             o[h * HD:(h + 1) * HD, :] = gk.astype(o.dtype)
             o[width + h * HD:width + (h + 1) * HD, :] = gv.astype(o.dtype)
         result = result + jnp.where(head == h, acc, 0.0)
-    gquery_ref[...] = result * scaling
+    gquery_ref[...] = result
 
 
 def project_kernel(att_ref, w_ref, projected_ref):
@@ -263,7 +266,7 @@
             term = total_ref[at:at + rows, HD:2 * HD, :].reshape(2 * width, 128).astype(F32)
             acc = acc + jnp.where(ids_ref[g] == pos_ref[0], term, 0.0)
         tokens = slice(a * 128, (a + 1) * 128)
-        gqk_ref[tokens, :] = (gquery_ref[tokens, :] + acc[:width].T).astype(BF16)
+        gqk_ref[tokens, :] = (gquery_ref[tokens, :] / math.sqrt(HD) + acc[:width].T).astype(BF16)
         gval_ref[tokens, :] = acc[width:].T.astype(BF16)
     n = width // HD
     for c in range(gweight_ref.shape[1] // 128):
@@ -374,15 +377,16 @@
     column = lax.all_to_all(picked, "hi", 0, 0)
     for n in (3, 2):
         received[n] = lax.ppermute(joined_late, CTX, routes[n])
-    portion_b, gatt, weight_cols = pl.pallas_call(
+    portion_b, gatt, gatt_t, weight_cols = pl.pallas_call(
         cotangent_kernel,
         out_shape=(
             jax.ShapeDtypeStruct((pieces, length, width), BF16),
             jax.ShapeDtypeStruct((length, width), BF16),
+            jax.ShapeDtypeStruct((width, length), BF16),
             jax.ShapeDtypeStruct((pieces, width, 128), BF16),
         ),
         in_specs=[smem(), hbm(), hbm()],
-        out_specs=tuple(vmem(3)),
+        out_specs=tuple(vmem(4)),
         scratch_shapes=[
             pltpu.VMEM((width, pieces * width), BF16),
             pltpu.SemaphoreType.DMA((1 + pieces * (length // 128 + 1),)),
@@ -393,8 +397,8 @@
         ),
         name="cotangent",
     )(lax.axis_index(HEAD)[None], portion, out_weight)
-    column, portion_b, gatt, weight_cols = lax.optimization_barrier(
-        (column, portion_b, gatt, weight_cols)
+    column, portion_b, gatt, gatt_t, weight_cols = lax.optimization_barrier(
+        (column, portion_b, gatt, gatt_t, weight_cols)
     )
     chosen = pl.pallas_call(
         spread_kernel,
@@ -415,8 +419,8 @@
     square = jax.ShapeDtypeStruct((length, width), F32)
     near_stats, near_sum, turned = pl.pallas_call(
         near_kernel,
-        out_shape=(square, square, block),
-        in_specs=[smem()] * 2 + vmem(6),
+        out_shape=(square, square, jax.ShapeDtypeStruct((width, length), BF16)),
+        in_specs=[smem()] * 2 + vmem(5),
         out_specs=tuple(vmem(3)),
         scratch_shapes=[pltpu.VMEM((length, 5 * length), F32)],
         compiler_params=limit(12),
@@ -424,7 +428,7 @@
             flops=1_000_000_000, bytes_accessed=1_000_000, transcendentals=650_000
         ),
         name="near",
-    )(position[None], pair_active, joined, received[0], *received[2:], gatt)
+    )(position[None], pair_active, joined, received[0], *received[2:])
     globals_all, near_stats, near_sum, turned = lax.optimization_barrier(
         (globals_all, near_stats, near_sum, turned)
     )
@@ -436,7 +440,7 @@
             square,
             square,
         ),
-        in_specs=[smem()] * 2 + vmem(8),
+        in_specs=[smem()] * 2 + vmem(9),
         out_specs=tuple(vmem(4)),
         scratch_shapes=[
             pltpu.VMEM((nheads, length, (1 + NGLOB) * length), F32),
@@ -448,34 +452,38 @@
         ),
         name="forward",
     )(
-        position[None], pair_active, joined, received[1], near_stats, near_sum, turned,
+        position[None], pair_active, joined, received[1], near_stats, near_sum, turned, gatt_t,
         globals_all, portion_b, gatt,
     )
 
     shares = lax.all_to_all(sums, "lo", 0, 0)
     attended_all = lax.all_gather(attended, HEAD, axis=0)
-    *terms, gquery, gown = pl.pallas_call(
-        backward_kernel,
-        out_shape=(
-            block, block, block, block, block,
-            square,
-            jax.ShapeDtypeStruct((2 * width, length), F32),
-        ),
-        in_specs=[smem()] * 2 + vmem(10),
-        out_specs=tuple(vmem(7)),
-        compiler_params=limit(10),
-        cost_estimate=pl.CostEstimate(
-            flops=1_000_000, bytes_accessed=10_000, transcendentals=0
-        ),
-        name="backward",
-    )(position[None], pair_active, joined, *received, stats, turned, gatt, gglob)
+    def backward(slots, name, gsum):
+        inputs = [received[slot - 1] for slot in slots if slot > 0]
+        shapes = [block if slot > 0 else whole for slot in slots] + [square]
+        return pl.pallas_call(
+            functools.partial(backward_kernel, slots),
+            out_shape=tuple(shapes),
+            in_specs=[smem()] * 2 + vmem(6 + len(inputs)),
+            out_specs=tuple(vmem(len(shapes))),
+            compiler_params=limit(10),
+            cost_estimate=pl.CostEstimate(
+                flops=1_000_000, bytes_accessed=10_000, transcendentals=0
+            ),
+            name=name,
+        )(position[None], pair_active, joined, stats, turned, gatt_t, gatt, gsum, *inputs)
+
+    whole = jax.ShapeDtypeStruct((2 * width, length), F32)
+    terms = [None] * len(routes)
+    terms[0], terms[1], terms[4], gquery = backward((1, 2, 5), "backward", gglob)
     returned = [None] * len(routes)
     for n in (1, 0):
         returned[n] = lax.ppermute(terms[n], CTX, routes[n])
-    shares, *terms = lax.optimization_barrier((shares, *terms))
+    shares, terms[4], gquery = lax.optimization_barrier((shares, terms[4], gquery))
     share = jnp.sum(shares.astype(F32), axis=0).astype(BF16)
     share, returned[1], returned[0] = lax.optimization_barrier((share, returned[1], returned[0]))
     column = lax.all_to_all(jnp.broadcast_to(share[None], (his,) + share.shape), "hi", 0, 0)
+    terms[2], terms[3], gown, gquery = backward((3, 4, 0), "backward_rest", gquery)
     for n in (4, 2, 3):
         returned[n] = lax.ppermute(terms[n], CTX, routes[n])
     share = jnp.sum(column.astype(F32), axis=0).astype(BF16)

time: 153 us -> 153 us (level)
  waiting for transfers between devices: 27.7 us -> 31.4 us
  starting transfers between devices: 85.4 us -> 81.8 us
    ppermute x2, waiting for transfers between devices: 0.78 us -> 3.19 us  [local(): received[n] = lax.ppermute(joined, CTX, routes[n])]
    all_to_all x1, starting transfers between devices: 5.74 us -> 3.82 us  [local(): lax.all_to_all(jnp.broadcast_to(share[None], (los,) + share.shape), 'lo',...]
    pallas_call x2 -> x3, Pallas kernels: 5.73 us -> 6.4 us  [the longest x2 4.53 us: backward(): pl.pallas_call(functools.partial(backward_kernel, slots), out_shape=tuple...]
where the time goes in v10:
time: 153 us; the launch traced here: 152 us
  starting transfers between devices  81.8 us (53%)
  waiting for transfers between devices  31.4 us (21%)
  Pallas kernels  20.6 us (13%)
  between operations  14.4 us (9%)
  local copies, waits for them, and re-layouts  3.48 us (2%)
    ppermute x5, starting transfers between devices, local(): returned[n] = lax.ppermute(terms[n], CTX, routes[n])  18.1 us
    all_to_all x1, starting transfers between devices, local(): column = lax.all_to_all(picked, 'hi', 0, 0)  12.4 us
    all_to_all x1, starting transfers between devices, local(): lax.all_to_all(jnp.broadcast_to(share[None], (his,) + share.shape), 'hi',...  8.99 us
    all_to_all x1, starting transfers between devices, local(): slices = lax.all_to_all(joined.reshape(los, step, width), 'lo', 0, 0)  8.61 us
    ppermute x2, starting transfers between devices, local(): received[n] = lax.ppermute(joined, CTX, routes[n])  8.1 us
    all_to_all x1, starting transfers between devices, local(): shares = lax.all_to_all(sums, 'lo', 0, 0)  7.42 us
    all_to_all x1, waiting for transfers between devices, local(): globals_all = lax.all_to_all(chosen, 'lo', 0, 0)  7.4 us
    ppermute x2, starting transfers between devices, local(): received[n] = lax.ppermute(joined_late, CTX, routes[n])  7.03 us
  transfers between devices with their start and end apart: 18, of which 9 were waited for; matrix products, arithmetic and copies ran while one was open for 1% of the time, Pallas kernels for 8%

profile of v10, /device:TPU:24, one launch (start us, length us, event | category | flops | bytes accessed | tf_op | source)
XLA Modules:
  0.0 151.7 jit_solution(1887154923590551937)
XLA Ops:
  7.2 0.0 all-gather.5.cloned.1.call-start
  7.2 1.8 %pack.1 = (bf16[512,128]{1,0:T(8,128)(2,1)}, bf16[10,128,128]{2,1,0:T(8,128)(2,1)}) custom-call(bf16[256,128]{1,0:T(8,128)(2,1)} %qk_ref.1, bf16[256,128]{1,0:T(8,128)(2,1)} %val_ref.1, bf16[256,128]{1,0:T(8,128)(2,1)} %gout_ref.1, bf16[128,1024]{1,0:T(8,128)(2,1)} %w_hbm.1), custom_call_target="tpu_custom_call" | custom-call | tf_op jit(solution)/shard_map/pack/pallas_call | solution.py:345
  9.1 0.0 all-gather.5.cloned.1.call-update
  9.1 8.6 %all-to-all-start = ((bf16[16,32,128]{2,1,0:T(8,128)(2,1)}), bf16[16,32,128]{2,1,0:T(8,128)(2,1)S(1)}, u32[]{:S(2)}, u32[]{:S(2)}) async-start(bf16[16,32,128]{2,1,0:T(8,128)(2,1)} %bitcast.5), calls=%async_computation | async-start | bytes 262144 | tf_op jit(solution)/shard_map/all_to_all | solution.py:356
  17.7 3.8 %collective-permute-start.1 = (bf16[512,128]{1,0:T(8,128)(2,1)}, bf16[512,128]{1,0:T(8,128)(2,1)S(1)}, u32[]{:S(2)}, u32[]{:S(2)}) collective-permute-start(bf16[512,128]{1,0:T(8,128)(2,1)} %get-tuple-element.64.own_ref), channel_id=1, source_target_pairs={{0,8},{8,0},{16,24},{24,16},{32,40},{40,32},{48,56},{56,48},{64,72... | collective-permute-start | bytes 393224 | tf_op jit(solution)/shard_map/ppermute | solution.py:364
  21.6 4.3 %collective-permute-start = (bf16[512,128]{1,0:T(8,128)(2,1)}, bf16[512,128]{1,0:T(8,128)(2,1)S(1)}, u32[]{:S(2)}, u32[]{:S(2)}) collective-permute-start(bf16[512,128]{1,0:T(8,128)(2,1)} %get-tuple-element.64.own_ref), channel_id=1, source_target_pairs={{0,64},{8,72},{16,80},{24,88},{32,96},{40,104},{48,112},{56,120},{... | collective-permute-start | bytes 393224 | tf_op jit(solution)/shard_map/ppermute | solution.py:364
  25.8 0.8 all-to-all-done.slices_ref
  26.7 0.7 copy-done.6
  27.3 1.2 pick.1
  28.6 3.2 %collective-permute-done.p4.refs_2_ = bf16[512,128]{1,0:T(8,128)(2,1)S(1)} collective-permute-done((bf16[512,128]{1,0:T(8,128)(2,1)}, bf16[512,128]{1,0:T(8,128)(2,1)S(1)}, u32[]{:S(2)}, u32[]{:S(2)}) %collective-permute-start) | collective-permute-done | bytes 131104 | tf_op jit(solution)/shard_map/ppermute | solution.py:364
  31.8 12.4 %all-to-all-start.1 = ((bf16[4,2,32,128]{3,2,1,0:T(8,128)(2,1)}), bf16[4,2,32,128]{3,2,1,0:T(8,128)(2,1)S(1)}, u32[]{:S(2)}, u32[]{:S(2)}) async-start(bf16[4,2,32,128]{3,2,1,0:T(8,128)(2,1)} %pick.1), calls=%async_computation.1 | async-start | bytes 131072 | tf_op jit(solution)/shard_map/all_to_all | solution.py:377
  44.1 4.6 %collective-permute-start.3 = (bf16[512,128]{1,0:T(8,128)(2,1)}, bf16[512,128]{1,0:T(8,128)(2,1)S(1)}, u32[]{:S(2)}, u32[]{:S(2)}) collective-permute-start(bf16[512,128]{1,0:T(8,128)(2,1)} %get-tuple-element.64.own_ref), channel_id=1, source_target_pairs={{0,16},{8,24},{16,0},{24,8},{32,48},{40,56},{48,32},{56,40},{64,80... | collective-permute-start | bytes 393224 | tf_op jit(solution)/shard_map/ppermute | solution.py:379
  48.7 2.5 %collective-permute-start.2 = (bf16[512,128]{1,0:T(8,128)(2,1)}, bf16[512,128]{1,0:T(8,128)(2,1)S(1)}, u32[]{:S(2)}, u32[]{:S(2)}) collective-permute-start(bf16[512,128]{1,0:T(8,128)(2,1)} %get-tuple-element.64.own_ref), channel_id=1, source_target_pairs={{0,32},{8,40},{16,48},{24,56},{32,0},{40,8},{48,16},{56,24},{64,96... | collective-permute-start | bytes 393224 | tf_op jit(solution)/shard_map/ppermute | solution.py:379
  51.2 0.0 all-gather.5.cloned.1.call-done
  51.2 2.6 %cotangent.1 = (bf16[8,256,128]{2,1,0:T(8,128)(2,1)}, bf16[256,128]{1,0:T(8,128)(2,1)}, bf16[128,256]{1,0:T(8,128)(2,1)}, bf16[8,128,128]{2,1,0:T(8,128)(2,1)}) custom-call(s32[1]{0:T(128)} %bitcast.2.head_ref, bf16[8,10,128,128]{3,2,1,0:T(8,128)(2,1)} %bitcast.7, bf16[128,1024]{1,0:T(8,128)(2,1)} %w_hbm.1), custom_call_target="tpu_custom_call" | custom-call | flops 600000000 | bytes 4000000 | tf_op jit(solution)/shard_map/cotangent/pallas_call | solution.py:380
  53.8 0.0 copy-start.2
  53.8 0.0 copy-start.3
  53.8 3.5 %all-to-all-done.1.slices_ref = bf16[4,2,32,128]{3,2,1,0:T(8,128)(2,1)S(1)} async-done(((bf16[4,2,32,128]{3,2,1,0:T(8,128)(2,1)}), bf16[4,2,32,128]{3,2,1,0:T(8,128)(2,1)S(1)}, u32[]{:S(2)}, u32[]{:S(2)}) %all-to-all-start.1) | async-done | bytes 65568 | tf_op jit(solution)/shard_map/all_to_all | solution.py:377
  57.4 1.6 %spread.1 = bf16[16,2,32,128]{3,2,1,0:T(8,128)(2,1)} custom-call(s32[2]{0:T(128)S(1)} %copy-done.7, bf16[4,2,32,128]{3,2,1,0:T(8,128)(2,1)S(1)} %all-to-all-done.1.slices_ref), custom_call_target="tpu_custom_call" | custom-call | tf_op jit(solution)/shard_map/spread/pallas_call | solution.py:403
  59.0 6.6 %all-to-all-start.2 = ((bf16[16,2,32,128]{3,2,1,0:T(8,128)(2,1)}), bf16[16,2,32,128]{3,2,1,0:T(8,128)(2,1)S(1)}, u32[]{:S(2)}, u32[]{:S(2)}) async-start(bf16[16,2,32,128]{3,2,1,0:T(8,128)(2,1)} %spread.1), calls=%async_computation.2 | async-start | bytes 524288 | tf_op jit(solution)/shard_map/all_to_all | solution.py:415
  65.5 0.7 collective-permute-start.4
  66.2 1.9 %near.1 = (f32[256,128]{1,0:T(8,128)S(1)}, f32[256,128]{1,0:T(8,128)S(1)}, bf16[128,256]{1,0:T(8,128)(2,1)S(1)}) custom-call(s32[1]{0:T(128)} %bitcast.pos_ref, s32[4,32]{1,0:T(4,128)S(1)} %copy-done.5, bf16[512,128]{1,0:T(8,128)(2,1)S(1)} %copy-done, bf16[512,128]{1,0:T(8,128)(2,1)S(1)} %collective-permute-done.1.p0.refs_0_, ...), custom_call_target="tpu_custom_call" | custom-call | flops 1000000000 | bytes 1000000 | tf_op jit(solution)/shard_map/near/pallas_call | solution.py:420
  68.1 7.4 %all-to-all-done.2.glob_ref = bf16[16,2,32,128]{3,2,1,0:T(8,128)(2,1)S(1)} async-done(((bf16[16,2,32,128]{3,2,1,0:T(8,128)(2,1)}), bf16[16,2,32,128]{3,2,1,0:T(8,128)(2,1)S(1)}, u32[]{:S(2)}, u32[]{:S(2)}) %all-to-all-start.2) | async-done | bytes 262176 | tf_op jit(solution)/shard_map/all_to_all | solution.py:415
  75.5 4.5 %forward.1 = (f32[256,128]{1,0:T(8,128)}, bf16[16,128,128]{2,1,0:T(8,128)(2,1)}, f32[256,128]{1,0:T(8,128)S(1)}, f32[256,128]{1,0:T(8,128)S(1)}) custom-call(s32[1]{0:T(128)} %bitcast.pos_ref, s32[4,32]{1,0:T(4,128)S(1)} %copy-done.5, bf16[512,128]{1,0:T(8,128)(2,1)S(1)} %copy-done, bf16[512,128]{1,0:T(8,128)(2,1)S(1)} %collective-permute-done.4.p1.refs_1_, ...), custom_call_target="tpu_custom_call" | custom-call | flops 3000000000 | bytes 4000000 | tf_op jit(solution)/shard_map/forward/pallas_call | solution.py:435
  80.0 7.4 %all-to-all-start.3 = ((bf16[16,128,128]{2,1,0:T(8,128)(2,1)}), bf16[16,128,128]{2,1,0:T(8,128)(2,1)S(1)}, u32[]{:S(2)}, u32[]{:S(2)}) async-start(bf16[16,128,128]{2,1,0:T(8,128)(2,1)} %get-tuple-element.80), calls=%async_computation.3 | async-start | bytes 1048576 | tf_op jit(solution)/shard_map/all_to_all | solution.py:459
  87.4 0.0 all-gather.7.cloned.1.call-start
  87.5 0.7 all-gather.7.cloned.1.call-update
  88.2 2.3 %backward.1 = (bf16[256,256]{1,0:T(8,128)(2,1)S(1)}, bf16[256,256]{1,0:T(8,128)(2,1)S(1)}, bf16[256,256]{1,0:T(8,128)(2,1)S(1)}, f32[256,128]{1,0:T(8,128)S(1)}) custom-call(s32[1]{0:T(128)} %bitcast.pos_ref, s32[4,32]{1,0:T(4,128)S(1)} %copy-done.5, bf16[512,128]{1,0:T(8,128)(2,1)S(1)} %copy-done, f32[256,128]{1,0:T(8,128)S(1)} %get-tuple-element.81.stats_ref, ...), custom_call_target="tpu_custom_call" | custom-call | flops 1000000 | bytes 10000 | tf_op jit(solution)/shard_map/backward/pallas_call | solution.py:464
  90.5 0.7 collective-permute-start.5
  91.1 6.5 %collective-permute-start.6 = (bf16[256,256]{1,0:T(8,128)(2,1)S(1)}, bf16[256,256]{1,0:T(8,128)(2,1)S(1)}, u32[]{:S(2)}, u32[]{:S(2)}) collective-permute-start(bf16[256,256]{1,0:T(8,128)(2,1)S(1)} %get-tuple-element.87), channel_id=1, source_target_pairs={{0,8},{8,0},{16,24},{24,16},{32,40},{40,32},{48,56},{56,48},{64,72... | collective-permute-start | bytes 393224 | tf_op jit(solution)/shard_map/ppermute | solution.py:481
  97.7 2.0 %all-to-all-done.3 = bf16[16,128,128]{2,1,0:T(8,128)(2,1)S(1)} async-done(((bf16[16,128,128]{2,1,0:T(8,128)(2,1)}), bf16[16,128,128]{2,1,0:T(8,128)(2,1)S(1)}, u32[]{:S(2)}, u32[]{:S(2)}) %all-to-all-start.3) | async-done | bytes 524320 | tf_op jit(solution)/shard_map/all_to_all | solution.py:459
  99.7 0.1 reduce_sum.24
  99.8 0.8 collective-permute-done.6.b0
  100.6 0.7 broadcast_in_dim.10
  101.3 9.0 %all-to-all-start.4 = ((bf16[4,128,128]{2,1,0:T(8,128)(2,1)}), bf16[4,128,128]{2,1,0:T(8,128)(2,1)S(1)}, u32[]{:S(2)}, u32[]{:S(2)}) async-start(bf16[4,128,128]{2,1,0:T(8,128)(2,1)} %broadcast_in_dim.10), calls=%async_computation.4 | async-start | bytes 262144 | tf_op jit(solution)/shard_map/all_to_all | solution.py:485
  110.3 4.3 %collective-permute-start.7 = (bf16[256,256]{1,0:T(8,128)(2,1)S(1)}, bf16[256,256]{1,0:T(8,128)(2,1)S(1)}, u32[]{:S(2)}, u32[]{:S(2)}) collective-permute-start(bf16[256,256]{1,0:T(8,128)(2,1)S(1)} %get-tuple-element.89), channel_id=1, source_target_pairs={{0,64},{8,72},{16,80},{24,88},{32,96},{40,104},{48,112},{56,120},{... | collective-permute-start | bytes 393224 | tf_op jit(solution)/shard_map/ppermute | solution.py:488
  114.5 2.3 %backward_rest.1 = (bf16[256,256]{1,0:T(8,128)(2,1)S(1)}, bf16[256,256]{1,0:T(8,128)(2,1)S(1)}, f32[256,256]{1,0:T(8,128)S(1)}, f32[256,128]{1,0:T(8,128)S(1)}) custom-call(s32[1]{0:T(128)} %bitcast.pos_ref, s32[4,32]{1,0:T(4,128)S(1)} %copy-done.5, bf16[512,128]{1,0:T(8,128)(2,1)S(1)} %copy-done, f32[256,128]{1,0:T(8,128)S(1)} %get-tuple-element.81.stats_ref, ...), custom_call_target="tpu_custom_call" | custom-call | flops 1000000 | bytes 10000 | tf_op jit(solution)/shard_map/backward_rest/pallas_call | solution.py:464
  116.8 2.8 %collective-permute-start.8 = (bf16[256,256]{1,0:T(8,128)(2,1)S(1)}, bf16[256,256]{1,0:T(8,128)(2,1)S(1)}, u32[]{:S(2)}, u32[]{:S(2)}) collective-permute-start(bf16[256,256]{1,0:T(8,128)(2,1)S(1)} %get-tuple-element.91), channel_id=1, source_target_pairs={{0,16},{8,24},{16,0},{24,8},{32,48},{40,56},{48,32},{56,40},{64,80... | collective-permute-start | bytes 393224 | tf_op jit(solution)/shard_map/ppermute | solution.py:488
  119.6 6.6 %all-to-all-done.4 = bf16[4,128,128]{2,1,0:T(8,128)(2,1)S(1)} async-done(((bf16[4,128,128]{2,1,0:T(8,128)(2,1)}), bf16[4,128,128]{2,1,0:T(8,128)(2,1)S(1)}, u32[]{:S(2)}, u32[]{:S(2)}) %all-to-all-start.4) | async-done | bytes 131104 | tf_op jit(solution)/shard_map/all_to_all | solution.py:485
  126.2 0.0 all-gather.7.cloned.1.call-done
  126.3 0.9 broadcast_in_dim.11
  127.2 3.8 %all-to-all-start.5 = ((bf16[16,128,128]{2,1,0:T(8,128)(2,1)}), bf16[16,128,128]{2,1,0:T(8,128)(2,1)S(1)}, u32[]{:S(2)}, u32[]{:S(2)}) async-start(bf16[16,128,128]{2,1,0:T(8,128)(2,1)} %broadcast_in_dim.11), calls=%async_computation.5 | async-start | bytes 1048576 | tf_op jit(solution)/shard_map/all_to_all | solution.py:493
  131.0 3.8 %collective-permute-start.9 = (bf16[256,256]{1,0:T(8,128)(2,1)S(1)}, bf16[256,256]{1,0:T(8,128)(2,1)S(1)}, u32[]{:S(2)}, u32[]{:S(2)}) collective-permute-start(bf16[256,256]{1,0:T(8,128)(2,1)S(1)} %get-tuple-element.98), channel_id=1, source_target_pairs={{0,32},{8,40},{16,48},{24,56},{32,0},{40,8},{48,16},{56,24},{64,96... | collective-permute-start | bytes 393224 | tf_op jit(solution)/shard_map/ppermute | solution.py:488
  134.9 1.2 copy-done.1
  136.1 0.9 project.1
  137.0 2.9 %collective-permute-done.9.b3 = bf16[256,256]{1,0:T(8,128)(2,1)S(1)} collective-permute-done((bf16[256,256]{1,0:T(8,128)(2,1)S(1)}, bf16[256,256]{1,0:T(8,128)(2,1)S(1)}, u32[]{:S(2)}, u32[]{:S(2)}) %collective-permute-start.9) | collective-permute-done | bytes 131104 | tf_op jit(solution)/shard_map/ppermute | solution.py:488
  139.9 3.4 %all-to-all-done.5.total_ref = bf16[16,128,128]{2,1,0:T(8,128)(2,1)S(1)} async-done(((bf16[16,128,128]{2,1,0:T(8,128)(2,1)}), bf16[16,128,128]{2,1,0:T(8,128)(2,1)S(1)}, u32[]{:S(2)}, u32[]{:S(2)}) %all-to-all-start.5) | async-done | bytes 524320 | tf_op jit(solution)/shard_map/all_to_all | solution.py:493
  143.3 1.6 %finish.1 = (bf16[256,128]{1,0:T(8,128)(2,1)}, bf16[256,128]{1,0:T(8,128)(2,1)}, f32[128,1024]{1,0:T(8,128)}) custom-call(s32[1]{0:T(128)} %bitcast.pos_ref, s32[2]{0:T(128)S(1)} %copy-done.7, bf16[256,256]{1,0:T(8,128)(2,1)S(1)} %collective-permute-done.6.b0, bf16[256,256]{1,0:T(8,128)(2,1)S(1)} %collective-permute-done.5.b1, ...), custom_call_target="tpu_custom_call" | custom-call | flops 2000000 | bytes 2500000 | tf_op jit(solution)/shard_map/finish/pallas_call | solution.py:506
  (22 shorter events, 0.1 us)
Async XLA Ops:
  7.2 50.2 %copy-start.7 = (s32[2]{0:T(128)S(1)}, s32[2]{0:T(128)}, u32[]{:S(2)}) copy-start(s32[2]{0:T(128)} %ids_ref.5) | copy-start | bytes 28
  7.2 59.0 %copy-start.5 = (s32[4,32]{1,0:T(4,128)S(1)}, s32[4,32]{1,0:T(4,128)}, u32[]{:S(2)}) copy-start(s32[4,32]{1,0:T(4,128)} %pair_ref.7) | copy-start | bytes 1540
  7.2 44.0 %all-gather.5.cloned.1.call-start = ((), (), s32[]{:S(2)}) async-start(), calls=%async_computation.6 | async-start | bytes 2949120 | tf_op jit(solution)/shard_map/all_gather | solution.py:357
  9.1 56.5 %copy-start = (bf16[512,128]{1,0:T(8,128)(2,1)S(1)}, bf16[512,128]{1,0:T(8,128)(2,1)}, u32[]{:S(2)}) copy-start(bf16[512,128]{1,0:T(8,128)(2,1)} %get-tuple-element.64.own_ref) | copy-start | bytes 393220
  9.1 17.6 %all-to-all-start = ((bf16[16,32,128]{2,1,0:T(8,128)(2,1)}), bf16[16,32,128]{2,1,0:T(8,128)(2,1)S(1)}, u32[]{:S(2)}, u32[]{:S(2)}) async-start(bf16[16,32,128]{2,1,0:T(8,128)(2,1)} %bitcast.5), calls=%async_computation | async-start | bytes 262144 | tf_op jit(solution)/shard_map/all_to_all | solution.py:356
  17.7 10.8 %collective-permute-start.1 = (bf16[512,128]{1,0:T(8,128)(2,1)}, bf16[512,128]{1,0:T(8,128)(2,1)S(1)}, u32[]{:S(2)}, u32[]{:S(2)}) collective-permute-start(bf16[512,128]{1,0:T(8,128)(2,1)} %get-tuple-element.64.own_ref), channel_id=1, source_target_pairs={{0,8},{8,0},{16,24},{24,16},{32,40},{40,32},{48,56},{56,48},{64,72... | collective-permute-start | bytes 393224 | tf_op jit(solution)/shard_map/ppermute | solution.py:364
  21.6 10.2 %collective-permute-start = (bf16[512,128]{1,0:T(8,128)(2,1)}, bf16[512,128]{1,0:T(8,128)(2,1)S(1)}, u32[]{:S(2)}, u32[]{:S(2)}) collective-permute-start(bf16[512,128]{1,0:T(8,128)(2,1)} %get-tuple-element.64.own_ref), channel_id=1, source_target_pairs={{0,64},{8,72},{16,80},{24,88},{32,96},{40,104},{48,112},{56,120},{... | collective-permute-start | bytes 393224 | tf_op jit(solution)/shard_map/ppermute | solution.py:364
  26.7 0.7 copy-start.6
  31.8 25.6 %all-to-all-start.1 = ((bf16[4,2,32,128]{3,2,1,0:T(8,128)(2,1)}), bf16[4,2,32,128]{3,2,1,0:T(8,128)(2,1)S(1)}, u32[]{:S(2)}, u32[]{:S(2)}) async-start(bf16[4,2,32,128]{3,2,1,0:T(8,128)(2,1)} %pick.1), calls=%async_computation.1 | async-start | bytes 131072 | tf_op jit(solution)/shard_map/all_to_all | solution.py:377
  44.1 14.8 %collective-permute-start.3 = (bf16[512,128]{1,0:T(8,128)(2,1)}, bf16[512,128]{1,0:T(8,128)(2,1)S(1)}, u32[]{:S(2)}, u32[]{:S(2)}) collective-permute-start(bf16[512,128]{1,0:T(8,128)(2,1)} %get-tuple-element.64.own_ref), channel_id=1, source_target_pairs={{0,16},{8,24},{16,0},{24,8},{32,48},{40,56},{48,32},{56,40},{64,80... | collective-permute-start | bytes 393224 | tf_op jit(solution)/shard_map/ppermute | solution.py:379
  48.7 10.2 %collective-permute-start.2 = (bf16[512,128]{1,0:T(8,128)(2,1)}, bf16[512,128]{1,0:T(8,128)(2,1)S(1)}, u32[]{:S(2)}, u32[]{:S(2)}) collective-permute-start(bf16[512,128]{1,0:T(8,128)(2,1)} %get-tuple-element.64.own_ref), channel_id=1, source_target_pairs={{0,32},{8,40},{16,48},{24,56},{32,0},{40,8},{48,16},{56,24},{64,96... | collective-permute-start | bytes 393224 | tf_op jit(solution)/shard_map/ppermute | solution.py:379
  53.8 21.7 %copy-start.2 = (bf16[256,128]{1,0:T(8,128)(2,1)S(1)}, bf16[256,128]{1,0:T(8,128)(2,1)}, u32[]{:S(2)}) copy-start(bf16[256,128]{1,0:T(8,128)(2,1)} %get-tuple-element.79.gatt_ref) | copy-start | bytes 196612
  53.8 21.7 %copy-start.3 = (bf16[128,256]{1,0:T(8,128)(2,1)S(1)}, bf16[128,256]{1,0:T(8,128)(2,1)}, u32[]{:S(2)}) copy-start(bf16[128,256]{1,0:T(8,128)(2,1)} %get-tuple-element.76.gattt_ref) | copy-start | bytes 196612
  53.8 21.7 %copy-start.8 = (bf16[8,256,128]{2,1,0:T(8,128)(2,1)S(1)}, bf16[8,256,128]{2,1,0:T(8,128)(2,1)}, u32[]{:S(2)}) copy-start(bf16[8,256,128]{2,1,0:T(8,128)(2,1)} %get-tuple-element.78.gout_ref) | copy-start | bytes 1572868
  59.0 16.6 %all-to-all-start.2 = ((bf16[16,2,32,128]{3,2,1,0:T(8,128)(2,1)}), bf16[16,2,32,128]{3,2,1,0:T(8,128)(2,1)S(1)}, u32[]{:S(2)}, u32[]{:S(2)}) async-start(bf16[16,2,32,128]{3,2,1,0:T(8,128)(2,1)} %spread.1), calls=%async_computation.2 | async-start | bytes 524288 | tf_op jit(solution)/shard_map/all_to_all | solution.py:415
  65.5 10.0 %collective-permute-start.4 = (bf16[512,128]{1,0:T(8,128)(2,1)S(1)}, bf16[512,128]{1,0:T(8,128)(2,1)S(1)}, u32[]{:S(2)}, u32[]{:S(2)}) collective-permute-start(bf16[512,128]{1,0:T(8,128)(2,1)S(1)} %copy-done), channel_id=1, source_target_pairs={{8,16},{16,8},{24,32},{32,24},{40,48},{48,40},{56,64},{64,56},{72,... | collective-permute-start | bytes 393224 | tf_op jit(solution)/shard_map/ppermute | solution.py:416
  80.0 19.7 %all-to-all-start.3 = ((bf16[16,128,128]{2,1,0:T(8,128)(2,1)}), bf16[16,128,128]{2,1,0:T(8,128)(2,1)S(1)}, u32[]{:S(2)}, u32[]{:S(2)}) async-start(bf16[16,128,128]{2,1,0:T(8,128)(2,1)} %get-tuple-element.80), calls=%async_computation.3 | async-start | bytes 1048576 | tf_op jit(solution)/shard_map/all_to_all | solution.py:459
  87.4 47.4 %copy-start.4 = (bf16[8,128,128]{2,1,0:T(8,128)(2,1)S(1)}, bf16[8,128,128]{2,1,0:T(8,128)(2,1)}, u32[]{:S(2)}) copy-start(bf16[8,128,128]{2,1,0:T(8,128)(2,1)} %get-tuple-element.94.w_ref) | copy-start | bytes 786436
  87.4 38.8 %all-gather.7.cloned.1.call-start = ((), (), s32[]{:S(2)}) async-start(), calls=%async_computation.7 | async-start | bytes 1179648 | tf_op jit(solution)/shard_map/all_gather | solution.py:460
  90.5 9.3 %collective-permute-start.5 = (bf16[256,256]{1,0:T(8,128)(2,1)S(1)}, bf16[256,256]{1,0:T(8,128)(2,1)S(1)}, u32[]{:S(2)}, u32[]{:S(2)}) collective-permute-start(bf16[256,256]{1,0:T(8,128)(2,1)S(1)} %get-tuple-element.86), channel_id=1, source_target_pairs={{8,16},{16,8},{24,32},{32,24},{40,48},{48,40},{56,64},{64,56},{72,... | collective-permute-start | bytes 393224 | tf_op jit(solution)/shard_map/ppermute | solution.py:481
  91.1 9.5 %collective-permute-start.6 = (bf16[256,256]{1,0:T(8,128)(2,1)S(1)}, bf16[256,256]{1,0:T(8,128)(2,1)S(1)}, u32[]{:S(2)}, u32[]{:S(2)}) collective-permute-start(bf16[256,256]{1,0:T(8,128)(2,1)S(1)} %get-tuple-element.87), channel_id=1, source_target_pairs={{0,8},{8,0},{16,24},{24,16},{32,40},{40,32},{48,56},{56,48},{64,72... | collective-permute-start | bytes 393224 | tf_op jit(solution)/shard_map/ppermute | solution.py:481
  101.3 24.9 %all-to-all-start.4 = ((bf16[4,128,128]{2,1,0:T(8,128)(2,1)}), bf16[4,128,128]{2,1,0:T(8,128)(2,1)S(1)}, u32[]{:S(2)}, u32[]{:S(2)}) async-start(bf16[4,128,128]{2,1,0:T(8,128)(2,1)} %broadcast_in_dim.10), calls=%async_computation.4 | async-start | bytes 262144 | tf_op jit(solution)/shard_map/all_to_all | solution.py:485
  110.3 16.0 %collective-permute-start.7 = (bf16[256,256]{1,0:T(8,128)(2,1)S(1)}, bf16[256,256]{1,0:T(8,128)(2,1)S(1)}, u32[]{:S(2)}, u32[]{:S(2)}) collective-permute-start(bf16[256,256]{1,0:T(8,128)(2,1)S(1)} %get-tuple-element.89), channel_id=1, source_target_pairs={{0,64},{8,72},{16,80},{24,88},{32,96},{40,104},{48,112},{56,120},{... | collective-permute-start | bytes 393224 | tf_op jit(solution)/shard_map/ppermute | solution.py:488
  116.8 9.5 %collective-permute-start.8 = (bf16[256,256]{1,0:T(8,128)(2,1)S(1)}, bf16[256,256]{1,0:T(8,128)(2,1)S(1)}, u32[]{:S(2)}, u32[]{:S(2)}) collective-permute-start(bf16[256,256]{1,0:T(8,128)(2,1)S(1)} %get-tuple-element.91), channel_id=1, source_target_pairs={{0,16},{8,24},{16,0},{24,8},{32,48},{40,56},{48,32},{56,40},{64,80... | collective-permute-start | bytes 393224 | tf_op jit(solution)/shard_map/ppermute | solution.py:488
  127.2 16.1 %all-to-all-start.5 = ((bf16[16,128,128]{2,1,0:T(8,128)(2,1)}), bf16[16,128,128]{2,1,0:T(8,128)(2,1)S(1)}, u32[]{:S(2)}, u32[]{:S(2)}) async-start(bf16[16,128,128]{2,1,0:T(8,128)(2,1)} %broadcast_in_dim.11), calls=%async_computation.5 | async-start | bytes 1048576 | tf_op jit(solution)/shard_map/all_to_all | solution.py:493
  131.0 8.9 %collective-permute-start.9 = (bf16[256,256]{1,0:T(8,128)(2,1)S(1)}, bf16[256,256]{1,0:T(8,128)(2,1)S(1)}, u32[]{:S(2)}, u32[]{:S(2)}) collective-permute-start(bf16[256,256]{1,0:T(8,128)(2,1)S(1)} %get-tuple-element.98), channel_id=1, source_target_pairs={{0,32},{8,40},{16,48},{24,56},{32,0},{40,8},{48,16},{56,24},{64,96... | collective-permute-start | bytes 393224 | tf_op jit(solution)/shard_map/ppermute | solution.py:488
  134.9 1.2 copy-start.1
Sparse Core Ops, SparseCore 0:
  10.7 37.0 all-gather.4
  90.4 26.4 all-gather.6

commit v11 on v10

--- a/solution.py
+++ b/solution.py
@@ -162,8 +162,10 @@
     attended = out_ref[...]
     att_ref[...] = attended
     attended_b = attended.astype(BF16)
+    every = jnp.concatenate([gout_ref[c] for c in range(pieces)], axis=1)
+    update = dot(attended_b, every, TN).astype(BF16)
     for c in range(pieces):
-        part = dot(attended_b, gout_ref[c], TN).astype(BF16)
+        part = update[:, c * 128:(c + 1) * 128]
         n = width // HD
         sums_ref[c * n:(c + 1) * n, 0:HD, :] = part.reshape(n, HD, 128)
 
@@ -371,8 +373,8 @@
         compiler_params=limit(1),
         name="pick",
     )(global_ids, slices)
-    picked, joined_late, received[4], received[0] = lax.optimization_barrier(
-        (picked, joined, received[4], received[0])
+    picked, joined_late, received[0], received[4] = lax.optimization_barrier(
+        (picked, joined, received[0], received[4])
     )
     column = lax.all_to_all(picked, "hi", 0, 0)
     for n in (3, 2):
@@ -409,8 +411,8 @@
         compiler_params=limit(1),
         name="spread",
     )(global_ids, column)
-    chosen, joined_late, received[3], received[2] = lax.optimization_barrier(
-        (chosen, joined, received[3], received[2])
+    chosen, joined_late, received[2], received[3] = lax.optimization_barrier(
+        (chosen, joined, received[2], received[3])
     )
     globals_all = lax.all_to_all(chosen, "lo", 0, 0)
     received[1] = lax.ppermute(joined_late, CTX, routes[1])

time: 153 us -> 151 us (0.987)
  waiting for transfers between devices: 31.4 us -> 28.1 us
  starting transfers between devices: 81.8 us -> 83.4 us
    ppermute x2, waiting for transfers between devices: 3.19 us -> 0.78 us  [local(): received[n] = lax.ppermute(joined, CTX, routes[n])]
where the time goes in v11:
time: 151 us; the launch traced here: 150 us
  starting transfers between devices  83.4 us (55%)
  waiting for transfers between devices  28.1 us (19%)
  Pallas kernels  20.5 us (14%)
  between operations  14.4 us (10%)
  local copies, waits for them, and re-layouts  3.48 us (2%)
    ppermute x5, starting transfers between devices, local(): returned[n] = lax.ppermute(terms[n], CTX, routes[n])  18 us
    all_to_all x1, starting transfers between devices, local(): column = lax.all_to_all(picked, 'hi', 0, 0)  12.4 us
    all_to_all x1, starting transfers between devices, local(): lax.all_to_all(jnp.broadcast_to(share[None], (his,) + share.shape), 'hi',...  10.3 us
    all_to_all x1, starting transfers between devices, local(): slices = lax.all_to_all(joined.reshape(los, step, width), 'lo', 0, 0)  8.61 us
    ppermute x2, starting transfers between devices, local(): received[n] = lax.ppermute(joined, CTX, routes[n])  8.1 us
    ppermute x2, starting transfers between devices, local(): received[n] = lax.ppermute(joined_late, CTX, routes[n])  8.09 us
    all_to_all x1, starting transfers between devices, local(): shares = lax.all_to_all(sums, 'lo', 0, 0)  7.42 us
    all_to_all x1, waiting for transfers between devices, local(): globals_all = lax.all_to_all(chosen, 'lo', 0, 0)  7.4 us
  transfers between devices with their start and end apart: 18, of which 9 were waited for; matrix products, arithmetic and copies ran while one was open for 1% of the time, Pallas kernels for 8%

profile of v11, /device:TPU:24, one launch (start us, length us, event | category | flops | bytes accessed | tf_op | source)
XLA Modules:
  0.0 149.9 jit_solution(2689065071595624081)
XLA Ops:
  7.2 0.0 all-gather.5.cloned.1.call-start
  7.2 1.8 %pack.1 = (bf16[512,128]{1,0:T(8,128)(2,1)}, bf16[10,128,128]{2,1,0:T(8,128)(2,1)}) custom-call(bf16[256,128]{1,0:T(8,128)(2,1)} %qk_ref.1, bf16[256,128]{1,0:T(8,128)(2,1)} %val_ref.1, bf16[256,128]{1,0:T(8,128)(2,1)} %gout_ref.1, bf16[128,1024]{1,0:T(8,128)(2,1)} %w_hbm.1), custom_call_target="tpu_custom_call" | custom-call | tf_op jit(solution)/shard_map/pack/pallas_call | solution.py:347
  9.1 0.0 all-gather.5.cloned.1.call-update
  9.1 8.6 %all-to-all-start = ((bf16[16,32,128]{2,1,0:T(8,128)(2,1)}), bf16[16,32,128]{2,1,0:T(8,128)(2,1)S(1)}, u32[]{:S(2)}, u32[]{:S(2)}) async-start(bf16[16,32,128]{2,1,0:T(8,128)(2,1)} %bitcast.5), calls=%async_computation | async-start | bytes 262144 | tf_op jit(solution)/shard_map/all_to_all | solution.py:358
  17.7 4.7 %collective-permute-start.1 = (bf16[512,128]{1,0:T(8,128)(2,1)}, bf16[512,128]{1,0:T(8,128)(2,1)S(1)}, u32[]{:S(2)}, u32[]{:S(2)}) collective-permute-start(bf16[512,128]{1,0:T(8,128)(2,1)} %get-tuple-element.64.own_ref), channel_id=1, source_target_pairs={{0,64},{8,72},{16,80},{24,88},{32,96},{40,104},{48,112},{56,120},{... | collective-permute-start | bytes 393224 | tf_op jit(solution)/shard_map/ppermute | solution.py:366
  22.5 3.4 %collective-permute-start = (bf16[512,128]{1,0:T(8,128)(2,1)}, bf16[512,128]{1,0:T(8,128)(2,1)S(1)}, u32[]{:S(2)}, u32[]{:S(2)}) collective-permute-start(bf16[512,128]{1,0:T(8,128)(2,1)} %get-tuple-element.64.own_ref), channel_id=1, source_target_pairs={{0,8},{8,0},{16,24},{24,16},{32,40},{40,32},{48,56},{56,48},{64,72... | collective-permute-start | bytes 393224 | tf_op jit(solution)/shard_map/ppermute | solution.py:366
  25.8 1.2 all-to-all-done.slices_ref
  27.0 0.7 copy-done.6
  27.6 1.2 pick.1
  28.9 0.8 collective-permute-done.1.p4.refs_2_
  29.7 12.4 %all-to-all-start.1 = ((bf16[4,2,32,128]{3,2,1,0:T(8,128)(2,1)}), bf16[4,2,32,128]{3,2,1,0:T(8,128)(2,1)S(1)}, u32[]{:S(2)}, u32[]{:S(2)}) async-start(bf16[4,2,32,128]{3,2,1,0:T(8,128)(2,1)} %pick.1), calls=%async_computation.1 | async-start | bytes 131072 | tf_op jit(solution)/shard_map/all_to_all | solution.py:379
  42.1 3.2 %collective-permute-start.3 = (bf16[512,128]{1,0:T(8,128)(2,1)}, bf16[512,128]{1,0:T(8,128)(2,1)S(1)}, u32[]{:S(2)}, u32[]{:S(2)}) collective-permute-start(bf16[512,128]{1,0:T(8,128)(2,1)} %get-tuple-element.64.own_ref), channel_id=1, source_target_pairs={{0,32},{8,40},{16,48},{24,56},{32,0},{40,8},{48,16},{56,24},{64,96... | collective-permute-start | bytes 393224 | tf_op jit(solution)/shard_map/ppermute | solution.py:381
  45.3 4.9 %collective-permute-start.2 = (bf16[512,128]{1,0:T(8,128)(2,1)}, bf16[512,128]{1,0:T(8,128)(2,1)S(1)}, u32[]{:S(2)}, u32[]{:S(2)}) collective-permute-start(bf16[512,128]{1,0:T(8,128)(2,1)} %get-tuple-element.64.own_ref), channel_id=1, source_target_pairs={{0,16},{8,24},{16,0},{24,8},{32,48},{40,56},{48,32},{56,40},{64,80... | collective-permute-start | bytes 393224 | tf_op jit(solution)/shard_map/ppermute | solution.py:381
  50.2 0.0 all-gather.5.cloned.1.call-done
  50.2 2.6 %cotangent.1 = (bf16[8,256,128]{2,1,0:T(8,128)(2,1)}, bf16[256,128]{1,0:T(8,128)(2,1)}, bf16[128,256]{1,0:T(8,128)(2,1)}, bf16[8,128,128]{2,1,0:T(8,128)(2,1)}) custom-call(s32[1]{0:T(128)} %bitcast.2.head_ref, bf16[8,10,128,128]{3,2,1,0:T(8,128)(2,1)} %bitcast.7, bf16[128,1024]{1,0:T(8,128)(2,1)} %w_hbm.1), custom_call_target="tpu_custom_call" | custom-call | flops 600000000 | bytes 4000000 | tf_op jit(solution)/shard_map/cotangent/pallas_call | solution.py:382
  52.8 0.0 copy-start.3
  52.8 0.0 copy-start.8
  52.8 2.5 %all-to-all-done.1.slices_ref = bf16[4,2,32,128]{3,2,1,0:T(8,128)(2,1)S(1)} async-done(((bf16[4,2,32,128]{3,2,1,0:T(8,128)(2,1)}), bf16[4,2,32,128]{3,2,1,0:T(8,128)(2,1)S(1)}, u32[]{:S(2)}, u32[]{:S(2)}) %all-to-all-start.1) | async-done | bytes 65568 | tf_op jit(solution)/shard_map/all_to_all | solution.py:379
  55.3 1.6 %spread.1 = bf16[16,2,32,128]{3,2,1,0:T(8,128)(2,1)} custom-call(s32[2]{0:T(128)S(1)} %copy-done.7, bf16[4,2,32,128]{3,2,1,0:T(8,128)(2,1)S(1)} %all-to-all-done.1.slices_ref), custom_call_target="tpu_custom_call" | custom-call | tf_op jit(solution)/shard_map/spread/pallas_call | solution.py:405
  56.9 5.9 %all-to-all-start.2 = ((bf16[16,2,32,128]{3,2,1,0:T(8,128)(2,1)}), bf16[16,2,32,128]{3,2,1,0:T(8,128)(2,1)S(1)}, u32[]{:S(2)}, u32[]{:S(2)}) async-start(bf16[16,2,32,128]{3,2,1,0:T(8,128)(2,1)} %spread.1), calls=%async_computation.2 | async-start | bytes 524288 | tf_op jit(solution)/shard_map/all_to_all | solution.py:417
  62.8 0.7 collective-permute-start.4
  63.5 1.9 %near.1 = (f32[256,128]{1,0:T(8,128)S(1)}, f32[256,128]{1,0:T(8,128)S(1)}, bf16[128,256]{1,0:T(8,128)(2,1)S(1)}) custom-call(s32[1]{0:T(128)} %bitcast.pos_ref, s32[4,32]{1,0:T(4,128)S(1)} %copy-done.5, bf16[512,128]{1,0:T(8,128)(2,1)S(1)} %copy-done, bf16[512,128]{1,0:T(8,128)(2,1)S(1)} %collective-permute-done.p0.refs_0_, ...), custom_call_target="tpu_custom_call" | custom-call | flops 1000000000 | bytes 1000000 | tf_op jit(solution)/shard_map/near/pallas_call | solution.py:422
  65.4 7.4 %all-to-all-done.2.glob_ref = bf16[16,2,32,128]{3,2,1,0:T(8,128)(2,1)S(1)} async-done(((bf16[16,2,32,128]{3,2,1,0:T(8,128)(2,1)}), bf16[16,2,32,128]{3,2,1,0:T(8,128)(2,1)S(1)}, u32[]{:S(2)}, u32[]{:S(2)}) %all-to-all-start.2) | async-done | bytes 262176 | tf_op jit(solution)/shard_map/all_to_all | solution.py:417
  72.8 4.4 %forward.1 = (f32[256,128]{1,0:T(8,128)}, bf16[16,128,128]{2,1,0:T(8,128)(2,1)}, f32[256,128]{1,0:T(8,128)S(1)}, f32[256,128]{1,0:T(8,128)S(1)}) custom-call(s32[1]{0:T(128)} %bitcast.pos_ref, s32[4,32]{1,0:T(4,128)S(1)} %copy-done.5, bf16[512,128]{1,0:T(8,128)(2,1)S(1)} %copy-done, bf16[512,128]{1,0:T(8,128)(2,1)S(1)} %collective-permute-done.4.p1.refs_1_, ...), custom_call_target="tpu_custom_call" | custom-call | flops 3000000000 | bytes 4000000 | tf_op jit(solution)/shard_map/forward/pallas_call | solution.py:437
  77.2 7.4 %all-to-all-start.3 = ((bf16[16,128,128]{2,1,0:T(8,128)(2,1)}), bf16[16,128,128]{2,1,0:T(8,128)(2,1)S(1)}, u32[]{:S(2)}, u32[]{:S(2)}) async-start(bf16[16,128,128]{2,1,0:T(8,128)(2,1)} %get-tuple-element.80), calls=%async_computation.3 | async-start | bytes 1048576 | tf_op jit(solution)/shard_map/all_to_all | solution.py:461
  84.6 0.0 all-gather.7.cloned.1.call-start
  84.7 0.7 all-gather.7.cloned.1.call-update
  85.4 2.3 %backward.1 = (bf16[256,256]{1,0:T(8,128)(2,1)S(1)}, bf16[256,256]{1,0:T(8,128)(2,1)S(1)}, bf16[256,256]{1,0:T(8,128)(2,1)S(1)}, f32[256,128]{1,0:T(8,128)S(1)}) custom-call(s32[1]{0:T(128)} %bitcast.pos_ref, s32[4,32]{1,0:T(4,128)S(1)} %copy-done.5, bf16[512,128]{1,0:T(8,128)(2,1)S(1)} %copy-done, f32[256,128]{1,0:T(8,128)S(1)} %get-tuple-element.81.stats_ref, ...), custom_call_target="tpu_custom_call" | custom-call | flops 1000000 | bytes 10000 | tf_op jit(solution)/shard_map/backward/pallas_call | solution.py:466
  87.7 0.7 collective-permute-start.5
  88.3 6.5 %collective-permute-start.6 = (bf16[256,256]{1,0:T(8,128)(2,1)S(1)}, bf16[256,256]{1,0:T(8,128)(2,1)S(1)}, u32[]{:S(2)}, u32[]{:S(2)}) collective-permute-start(bf16[256,256]{1,0:T(8,128)(2,1)S(1)} %get-tuple-element.87), channel_id=1, source_target_pairs={{0,8},{8,0},{16,24},{24,16},{32,40},{40,32},{48,56},{56,48},{64,72... | collective-permute-start | bytes 393224 | tf_op jit(solution)/shard_map/ppermute | solution.py:483
  94.9 2.3 %all-to-all-done.3 = bf16[16,128,128]{2,1,0:T(8,128)(2,1)S(1)} async-done(((bf16[16,128,128]{2,1,0:T(8,128)(2,1)}), bf16[16,128,128]{2,1,0:T(8,128)(2,1)S(1)}, u32[]{:S(2)}, u32[]{:S(2)}) %all-to-all-start.3) | async-done | bytes 524320 | tf_op jit(solution)/shard_map/all_to_all | solution.py:461
  97.2 0.1 reduce_sum.24
  97.3 0.5 collective-permute-done.6.b0
  97.8 0.7 broadcast_in_dim.10
  98.5 10.3 %all-to-all-start.4 = ((bf16[4,128,128]{2,1,0:T(8,128)(2,1)}), bf16[4,128,128]{2,1,0:T(8,128)(2,1)S(1)}, u32[]{:S(2)}, u32[]{:S(2)}) async-start(bf16[4,128,128]{2,1,0:T(8,128)(2,1)} %broadcast_in_dim.10), calls=%async_computation.4 | async-start | bytes 262144 | tf_op jit(solution)/shard_map/all_to_all | solution.py:487
  108.7 4.1 %collective-permute-start.7 = (bf16[256,256]{1,0:T(8,128)(2,1)S(1)}, bf16[256,256]{1,0:T(8,128)(2,1)S(1)}, u32[]{:S(2)}, u32[]{:S(2)}) collective-permute-start(bf16[256,256]{1,0:T(8,128)(2,1)S(1)} %get-tuple-element.89), channel_id=1, source_target_pairs={{0,64},{8,72},{16,80},{24,88},{32,96},{40,104},{48,112},{56,120},{... | collective-permute-start | bytes 393224 | tf_op jit(solution)/shard_map/ppermute | solution.py:490
  112.9 2.3 %backward_rest.1 = (bf16[256,256]{1,0:T(8,128)(2,1)S(1)}, bf16[256,256]{1,0:T(8,128)(2,1)S(1)}, f32[256,256]{1,0:T(8,128)S(1)}, f32[256,128]{1,0:T(8,128)S(1)}) custom-call(s32[1]{0:T(128)} %bitcast.pos_ref, s32[4,32]{1,0:T(4,128)S(1)} %copy-done.5, bf16[512,128]{1,0:T(8,128)(2,1)S(1)} %copy-done, f32[256,128]{1,0:T(8,128)S(1)} %get-tuple-element.81.stats_ref, ...), custom_call_target="tpu_custom_call" | custom-call | flops 1000000 | bytes 10000 | tf_op jit(solution)/shard_map/backward_rest/pallas_call | solution.py:466
  115.1 2.8 %collective-permute-start.8 = (bf16[256,256]{1,0:T(8,128)(2,1)S(1)}, bf16[256,256]{1,0:T(8,128)(2,1)S(1)}, u32[]{:S(2)}, u32[]{:S(2)}) collective-permute-start(bf16[256,256]{1,0:T(8,128)(2,1)S(1)} %get-tuple-element.91), channel_id=1, source_target_pairs={{0,16},{8,24},{16,0},{24,8},{32,48},{40,56},{48,32},{56,40},{64,80... | collective-permute-start | bytes 393224 | tf_op jit(solution)/shard_map/ppermute | solution.py:490
  118.0 6.4 %all-to-all-done.4 = bf16[4,128,128]{2,1,0:T(8,128)(2,1)S(1)} async-done(((bf16[4,128,128]{2,1,0:T(8,128)(2,1)}), bf16[4,128,128]{2,1,0:T(8,128)(2,1)S(1)}, u32[]{:S(2)}, u32[]{:S(2)}) %all-to-all-start.4) | async-done | bytes 131104 | tf_op jit(solution)/shard_map/all_to_all | solution.py:487
  124.4 0.0 all-gather.7.cloned.1.call-done
  124.4 0.9 broadcast_in_dim.11
  125.3 3.9 %all-to-all-start.5 = ((bf16[16,128,128]{2,1,0:T(8,128)(2,1)}), bf16[16,128,128]{2,1,0:T(8,128)(2,1)S(1)}, u32[]{:S(2)}, u32[]{:S(2)}) async-start(bf16[16,128,128]{2,1,0:T(8,128)(2,1)} %broadcast_in_dim.11), calls=%async_computation.5 | async-start | bytes 1048576 | tf_op jit(solution)/shard_map/all_to_all | solution.py:495
  129.2 3.8 %collective-permute-start.9 = (bf16[256,256]{1,0:T(8,128)(2,1)S(1)}, bf16[256,256]{1,0:T(8,128)(2,1)S(1)}, u32[]{:S(2)}, u32[]{:S(2)}) collective-permute-start(bf16[256,256]{1,0:T(8,128)(2,1)S(1)} %get-tuple-element.98), channel_id=1, source_target_pairs={{0,32},{8,40},{16,48},{24,56},{32,0},{40,8},{48,16},{56,24},{64,96... | collective-permute-start | bytes 393224 | tf_op jit(solution)/shard_map/ppermute | solution.py:490
  133.1 1.2 copy-done.1
  134.3 0.9 project.1
  135.2 2.9 %collective-permute-done.9.b3 = bf16[256,256]{1,0:T(8,128)(2,1)S(1)} collective-permute-done((bf16[256,256]{1,0:T(8,128)(2,1)S(1)}, bf16[256,256]{1,0:T(8,128)(2,1)S(1)}, u32[]{:S(2)}, u32[]{:S(2)}) %collective-permute-start.9) | collective-permute-done | bytes 131104 | tf_op jit(solution)/shard_map/ppermute | solution.py:490
  138.2 3.4 %all-to-all-done.5.total_ref = bf16[16,128,128]{2,1,0:T(8,128)(2,1)S(1)} async-done(((bf16[16,128,128]{2,1,0:T(8,128)(2,1)}), bf16[16,128,128]{2,1,0:T(8,128)(2,1)S(1)}, u32[]{:S(2)}, u32[]{:S(2)}) %all-to-all-start.5) | async-done | bytes 524320 | tf_op jit(solution)/shard_map/all_to_all | solution.py:495
  141.5 1.6 %finish.1 = (bf16[256,128]{1,0:T(8,128)(2,1)}, bf16[256,128]{1,0:T(8,128)(2,1)}, f32[128,1024]{1,0:T(8,128)}) custom-call(s32[1]{0:T(128)} %bitcast.pos_ref, s32[2]{0:T(128)S(1)} %copy-done.7, bf16[256,256]{1,0:T(8,128)(2,1)S(1)} %collective-permute-done.6.b0, bf16[256,256]{1,0:T(8,128)(2,1)S(1)} %collective-permute-done.5.b1, ...), custom_call_target="tpu_custom_call" | custom-call | flops 2000000 | bytes 2500000 | tf_op jit(solution)/shard_map/finish/pallas_call | solution.py:508
  (22 shorter events, 0.1 us)
Async XLA Ops:
  7.2 48.1 %copy-start.7 = (s32[2]{0:T(128)S(1)}, s32[2]{0:T(128)}, u32[]{:S(2)}) copy-start(s32[2]{0:T(128)} %ids_ref.5) | copy-start | bytes 28
  7.2 56.3 %copy-start.5 = (s32[4,32]{1,0:T(4,128)S(1)}, s32[4,32]{1,0:T(4,128)}, u32[]{:S(2)}) copy-start(s32[4,32]{1,0:T(4,128)} %pair_ref.7) | copy-start | bytes 1540
  7.2 43.0 %all-gather.5.cloned.1.call-start = ((), (), s32[]{:S(2)}) async-start(), calls=%async_computation.6 | async-start | bytes 2949120 | tf_op jit(solution)/shard_map/all_gather | solution.py:359
  9.1 53.7 %copy-start = (bf16[512,128]{1,0:T(8,128)(2,1)S(1)}, bf16[512,128]{1,0:T(8,128)(2,1)}, u32[]{:S(2)}) copy-start(bf16[512,128]{1,0:T(8,128)(2,1)} %get-tuple-element.64.own_ref) | copy-start | bytes 393220
  9.1 17.9 %all-to-all-start = ((bf16[16,32,128]{2,1,0:T(8,128)(2,1)}), bf16[16,32,128]{2,1,0:T(8,128)(2,1)S(1)}, u32[]{:S(2)}, u32[]{:S(2)}) async-start(bf16[16,32,128]{2,1,0:T(8,128)(2,1)} %bitcast.5), calls=%async_computation | async-start | bytes 262144 | tf_op jit(solution)/shard_map/all_to_all | solution.py:358
  17.7 11.9 %collective-permute-start.1 = (bf16[512,128]{1,0:T(8,128)(2,1)}, bf16[512,128]{1,0:T(8,128)(2,1)S(1)}, u32[]{:S(2)}, u32[]{:S(2)}) collective-permute-start(bf16[512,128]{1,0:T(8,128)(2,1)} %get-tuple-element.64.own_ref), channel_id=1, source_target_pairs={{0,64},{8,72},{16,80},{24,88},{32,96},{40,104},{48,112},{56,120},{... | collective-permute-start | bytes 393224 | tf_op jit(solution)/shard_map/ppermute | solution.py:366
  22.5 7.2 %collective-permute-start = (bf16[512,128]{1,0:T(8,128)(2,1)}, bf16[512,128]{1,0:T(8,128)(2,1)S(1)}, u32[]{:S(2)}, u32[]{:S(2)}) collective-permute-start(bf16[512,128]{1,0:T(8,128)(2,1)} %get-tuple-element.64.own_ref), channel_id=1, source_target_pairs={{0,8},{8,0},{16,24},{24,16},{32,40},{40,32},{48,56},{56,48},{64,72... | collective-permute-start | bytes 393224 | tf_op jit(solution)/shard_map/ppermute | solution.py:366
  27.0 0.7 copy-start.6
  29.7 25.6 %all-to-all-start.1 = ((bf16[4,2,32,128]{3,2,1,0:T(8,128)(2,1)}), bf16[4,2,32,128]{3,2,1,0:T(8,128)(2,1)S(1)}, u32[]{:S(2)}, u32[]{:S(2)}) async-start(bf16[4,2,32,128]{3,2,1,0:T(8,128)(2,1)} %pick.1), calls=%async_computation.1 | async-start | bytes 131072 | tf_op jit(solution)/shard_map/all_to_all | solution.py:379
  42.1 14.8 %collective-permute-start.3 = (bf16[512,128]{1,0:T(8,128)(2,1)}, bf16[512,128]{1,0:T(8,128)(2,1)S(1)}, u32[]{:S(2)}, u32[]{:S(2)}) collective-permute-start(bf16[512,128]{1,0:T(8,128)(2,1)} %get-tuple-element.64.own_ref), channel_id=1, source_target_pairs={{0,32},{8,40},{16,48},{24,56},{32,0},{40,8},{48,16},{56,24},{64,96... | collective-permute-start | bytes 393224 | tf_op jit(solution)/shard_map/ppermute | solution.py:381
  45.3 11.6 %collective-permute-start.2 = (bf16[512,128]{1,0:T(8,128)(2,1)}, bf16[512,128]{1,0:T(8,128)(2,1)S(1)}, u32[]{:S(2)}, u32[]{:S(2)}) collective-permute-start(bf16[512,128]{1,0:T(8,128)(2,1)} %get-tuple-element.64.own_ref), channel_id=1, source_target_pairs={{0,16},{8,24},{16,0},{24,8},{32,48},{40,56},{48,32},{56,40},{64,80... | collective-permute-start | bytes 393224 | tf_op jit(solution)/shard_map/ppermute | solution.py:381
  52.8 20.0 %copy-start.2 = (bf16[256,128]{1,0:T(8,128)(2,1)S(1)}, bf16[256,128]{1,0:T(8,128)(2,1)}, u32[]{:S(2)}) copy-start(bf16[256,128]{1,0:T(8,128)(2,1)} %get-tuple-element.79.gatt_ref) | copy-start | bytes 196612
  52.8 20.0 %copy-start.3 = (bf16[128,256]{1,0:T(8,128)(2,1)S(1)}, bf16[128,256]{1,0:T(8,128)(2,1)}, u32[]{:S(2)}) copy-start(bf16[128,256]{1,0:T(8,128)(2,1)} %get-tuple-element.76.gattt_ref) | copy-start | bytes 196612
  52.8 20.0 %copy-start.8 = (bf16[8,256,128]{2,1,0:T(8,128)(2,1)S(1)}, bf16[8,256,128]{2,1,0:T(8,128)(2,1)}, u32[]{:S(2)}) copy-start(bf16[8,256,128]{2,1,0:T(8,128)(2,1)} %get-tuple-element.78.gout_ref) | copy-start | bytes 1572868
  56.9 15.9 %all-to-all-start.2 = ((bf16[16,2,32,128]{3,2,1,0:T(8,128)(2,1)}), bf16[16,2,32,128]{3,2,1,0:T(8,128)(2,1)S(1)}, u32[]{:S(2)}, u32[]{:S(2)}) async-start(bf16[16,2,32,128]{3,2,1,0:T(8,128)(2,1)} %spread.1), calls=%async_computation.2 | async-start | bytes 524288 | tf_op jit(solution)/shard_map/all_to_all | solution.py:417
  62.8 10.0 %collective-permute-start.4 = (bf16[512,128]{1,0:T(8,128)(2,1)S(1)}, bf16[512,128]{1,0:T(8,128)(2,1)S(1)}, u32[]{:S(2)}, u32[]{:S(2)}) collective-permute-start(bf16[512,128]{1,0:T(8,128)(2,1)S(1)} %copy-done), channel_id=1, source_target_pairs={{8,16},{16,8},{24,32},{32,24},{40,48},{48,40},{56,64},{64,56},{72,... | collective-permute-start | bytes 393224 | tf_op jit(solution)/shard_map/ppermute | solution.py:418
  77.2 20.0 %all-to-all-start.3 = ((bf16[16,128,128]{2,1,0:T(8,128)(2,1)}), bf16[16,128,128]{2,1,0:T(8,128)(2,1)S(1)}, u32[]{:S(2)}, u32[]{:S(2)}) async-start(bf16[16,128,128]{2,1,0:T(8,128)(2,1)} %get-tuple-element.80), calls=%async_computation.3 | async-start | bytes 1048576 | tf_op jit(solution)/shard_map/all_to_all | solution.py:461
  84.6 48.4 %copy-start.4 = (bf16[8,128,128]{2,1,0:T(8,128)(2,1)S(1)}, bf16[8,128,128]{2,1,0:T(8,128)(2,1)}, u32[]{:S(2)}) copy-start(bf16[8,128,128]{2,1,0:T(8,128)(2,1)} %get-tuple-element.94.w_ref) | copy-start | bytes 786436
  84.6 39.7 %all-gather.7.cloned.1.call-start = ((), (), s32[]{:S(2)}) async-start(), calls=%async_computation.7 | async-start | bytes 1179648 | tf_op jit(solution)/shard_map/all_gather | solution.py:462
  87.7 9.6 %collective-permute-start.5 = (bf16[256,256]{1,0:T(8,128)(2,1)S(1)}, bf16[256,256]{1,0:T(8,128)(2,1)S(1)}, u32[]{:S(2)}, u32[]{:S(2)}) collective-permute-start(bf16[256,256]{1,0:T(8,128)(2,1)S(1)} %get-tuple-element.86), channel_id=1, source_target_pairs={{8,16},{16,8},{24,32},{32,24},{40,48},{48,40},{56,64},{64,56},{72,... | collective-permute-start | bytes 393224 | tf_op jit(solution)/shard_map/ppermute | solution.py:483
  88.3 9.5 %collective-permute-start.6 = (bf16[256,256]{1,0:T(8,128)(2,1)S(1)}, bf16[256,256]{1,0:T(8,128)(2,1)S(1)}, u32[]{:S(2)}, u32[]{:S(2)}) collective-permute-start(bf16[256,256]{1,0:T(8,128)(2,1)S(1)} %get-tuple-element.87), channel_id=1, source_target_pairs={{0,8},{8,0},{16,24},{24,16},{32,40},{40,32},{48,56},{56,48},{64,72... | collective-permute-start | bytes 393224 | tf_op jit(solution)/shard_map/ppermute | solution.py:483
  98.5 25.9 %all-to-all-start.4 = ((bf16[4,128,128]{2,1,0:T(8,128)(2,1)}), bf16[4,128,128]{2,1,0:T(8,128)(2,1)S(1)}, u32[]{:S(2)}, u32[]{:S(2)}) async-start(bf16[4,128,128]{2,1,0:T(8,128)(2,1)} %broadcast_in_dim.10), calls=%async_computation.4 | async-start | bytes 262144 | tf_op jit(solution)/shard_map/all_to_all | solution.py:487
  108.7 15.7 %collective-permute-start.7 = (bf16[256,256]{1,0:T(8,128)(2,1)S(1)}, bf16[256,256]{1,0:T(8,128)(2,1)S(1)}, u32[]{:S(2)}, u32[]{:S(2)}) collective-permute-start(bf16[256,256]{1,0:T(8,128)(2,1)S(1)} %get-tuple-element.89), channel_id=1, source_target_pairs={{0,64},{8,72},{16,80},{24,88},{32,96},{40,104},{48,112},{56,120},{... | collective-permute-start | bytes 393224 | tf_op jit(solution)/shard_map/ppermute | solution.py:490
  115.1 9.3 %collective-permute-start.8 = (bf16[256,256]{1,0:T(8,128)(2,1)S(1)}, bf16[256,256]{1,0:T(8,128)(2,1)S(1)}, u32[]{:S(2)}, u32[]{:S(2)}) collective-permute-start(bf16[256,256]{1,0:T(8,128)(2,1)S(1)} %get-tuple-element.91), channel_id=1, source_target_pairs={{0,16},{8,24},{16,0},{24,8},{32,48},{40,56},{48,32},{56,40},{64,80... | collective-permute-start | bytes 393224 | tf_op jit(solution)/shard_map/ppermute | solution.py:490
  125.3 16.2 %all-to-all-start.5 = ((bf16[16,128,128]{2,1,0:T(8,128)(2,1)}), bf16[16,128,128]{2,1,0:T(8,128)(2,1)S(1)}, u32[]{:S(2)}, u32[]{:S(2)}) async-start(bf16[16,128,128]{2,1,0:T(8,128)(2,1)} %broadcast_in_dim.11), calls=%async_computation.5 | async-start | bytes 1048576 | tf_op jit(solution)/shard_map/all_to_all | solution.py:495
  129.2 8.9 %collective-permute-start.9 = (bf16[256,256]{1,0:T(8,128)(2,1)S(1)}, bf16[256,256]{1,0:T(8,128)(2,1)S(1)}, u32[]{:S(2)}, u32[]{:S(2)}) collective-permute-start(bf16[256,256]{1,0:T(8,128)(2,1)S(1)} %get-tuple-element.98), channel_id=1, source_target_pairs={{0,32},{8,40},{16,48},{24,56},{32,0},{40,8},{48,16},{56,24},{64,96... | collective-permute-start | bytes 393224 | tf_op jit(solution)/shard_map/ppermute | solution.py:490
  133.1 1.2 copy-start.1
Sparse Core Ops, SparseCore 0:
  10.7 37.0 all-gather.4
  87.6 27.6 all-gather.6

commit v12 on v11

--- a/solution.py
+++ b/solution.py
@@ -362,7 +362,7 @@
     routes.append([(i, j) for i, j in enumerate(other) if 0 <= j < devices])
     routes += [[(i, i ^ (1 << k)) for i in range(devices)] for k in range(1, ROUNDS)]
     received = [None] * len(routes)
-    for n in (4, 0):
+    for n in (3, 0):
         received[n] = lax.ppermute(joined, CTX, routes[n])
     picked = pl.pallas_call(
         pick_kernel,
@@ -373,11 +373,11 @@
         compiler_params=limit(1),
         name="pick",
     )(global_ids, slices)
-    picked, joined_late, received[0], received[4] = lax.optimization_barrier(
-        (picked, joined, received[0], received[4])
+    picked, joined_late, received[0], received[3] = lax.optimization_barrier(
+        (picked, joined, received[0], received[3])
     )
     column = lax.all_to_all(picked, "hi", 0, 0)
-    for n in (3, 2):
+    for n in (4, 2):
         received[n] = lax.ppermute(joined_late, CTX, routes[n])
     portion_b, gatt, gatt_t, weight_cols = pl.pallas_call(
         cotangent_kernel,
@@ -411,8 +411,8 @@
         compiler_params=limit(1),
         name="spread",
     )(global_ids, column)
-    chosen, joined_late, received[2], received[3] = lax.optimization_barrier(
-        (chosen, joined, received[2], received[3])
+    chosen, joined_late, received[2], received[4] = lax.optimization_barrier(
+        (chosen, joined, received[2], received[4])
     )
     globals_all = lax.all_to_all(chosen, "lo", 0, 0)
     received[1] = lax.ppermute(joined_late, CTX, routes[1])
@@ -477,20 +477,20 @@
 
     whole = jax.ShapeDtypeStruct((2 * width, length), F32)
     terms = [None] * len(routes)
-    terms[0], terms[1], terms[4], gquery = backward((1, 2, 5), "backward", gglob)
+    terms[0], terms[1], terms[3], gquery = backward((1, 2, 4), "backward", gglob)
     returned = [None] * len(routes)
     for n in (1, 0):
         returned[n] = lax.ppermute(terms[n], CTX, routes[n])
-    shares, terms[4], gquery = lax.optimization_barrier((shares, terms[4], gquery))
+    shares, terms[3], gquery = lax.optimization_barrier((shares, terms[3], gquery))
     share = jnp.sum(shares.astype(F32), axis=0).astype(BF16)
     share, returned[1], returned[0] = lax.optimization_barrier((share, returned[1], returned[0]))
     column = lax.all_to_all(jnp.broadcast_to(share[None], (his,) + share.shape), "hi", 0, 0)
-    terms[2], terms[3], gown, gquery = backward((3, 4, 0), "backward_rest", gquery)
-    for n in (4, 2, 3):
+    terms[2], terms[4], gown, gquery = backward((3, 5, 0), "backward_rest", gquery)
+    for n in (3, 2, 4):
         returned[n] = lax.ppermute(terms[n], CTX, routes[n])
     share = jnp.sum(column.astype(F32), axis=0).astype(BF16)
-    share, returned[4], returned[2], attended_all = lax.optimization_barrier(
-        (share, returned[4], returned[2], attended_all)
+    share, returned[3], returned[2], attended_all = lax.optimization_barrier(
+        (share, returned[3], returned[2], attended_all)
     )
     totals = lax.all_to_all(jnp.broadcast_to(share[None], (los,) + share.shape), "lo", 0, 0)
 

time: 151 us -> 155 us (1.026); the launches traced: 150 us -> 152 us
  waiting for transfers between devices: 28.1 us -> 30.7 us
    ppermute x5, waiting for transfers between devices: 3.48 us -> 9.22 us  [local(): returned[n] = lax.ppermute(terms[n], CTX, routes[n])]
    all_to_all x1, waiting for transfers between devices: 3.35 us -> 0.01 us  [local(): lax.all_to_all(jnp.broadcast_to(share[None], (los,) + share.shape), 'lo',...]
  transfers between devices with their start and end apart: 18 -> 18, of which waited for: 9 -> 7; matrix products, arithmetic and copies ran while one was open for 1% -> 1% of each run, Pallas kernels for 8% -> 8%
where the time goes in v12:
time: 155 us; the launch traced here: 152 us
  starting transfers between devices  82.7 us (53%)
  waiting for transfers between devices  30.7 us (20%)
  Pallas kernels  20.5 us (13%)
  between operations  14.4 us (9%)
  local copies, waits for them, and re-layouts  3.48 us (2%)
    ppermute x5, starting transfers between devices, local(): returned[n] = lax.ppermute(terms[n], CTX, routes[n])  17.1 us
    all_to_all x1, starting transfers between devices, local(): column = lax.all_to_all(picked, 'hi', 0, 0)  12.4 us
    all_to_all x1, starting transfers between devices, local(): lax.all_to_all(jnp.broadcast_to(share[None], (his,) + share.shape), 'hi',...  10.7 us
    ppermute x5, waiting for transfers between devices, local(): returned[n] = lax.ppermute(terms[n], CTX, routes[n])  9.22 us
    ppermute x2, starting transfers between devices, local(): received[n] = lax.ppermute(joined_late, CTX, routes[n])  8.84 us
    all_to_all x1, starting transfers between devices, local(): slices = lax.all_to_all(joined.reshape(los, step, width), 'lo', 0, 0)  8.61 us
    all_to_all x1, starting transfers between devices, local(): shares = lax.all_to_all(sums, 'lo', 0, 0)  7.42 us
    all_to_all x1, waiting for transfers between devices, local(): globals_all = lax.all_to_all(chosen, 'lo', 0, 0)  7.4 us
  transfers between devices with their start and end apart: 18, of which 7 were waited for; matrix products, arithmetic and copies ran while one was open for 1% of the time, Pallas kernels for 8%

profile of v12, /device:TPU:24, one launch (start us, length us, event | category | flops | bytes accessed | tf_op | source)
XLA Modules:
  0.0 151.9 jit_solution(10580944004638205713)
XLA Ops:
  7.2 0.0 copy-start.7
  7.2 0.0 all-gather.5.cloned.1.call-start
  7.2 1.8 %pack.1 = (bf16[512,128]{1,0:T(8,128)(2,1)}, bf16[10,128,128]{2,1,0:T(8,128)(2,1)}) custom-call(bf16[256,128]{1,0:T(8,128)(2,1)} %qk_ref.1, bf16[256,128]{1,0:T(8,128)(2,1)} %val_ref.1, bf16[256,128]{1,0:T(8,128)(2,1)} %gout_ref.1, bf16[128,1024]{1,0:T(8,128)(2,1)} %w_hbm.1), custom_call_target="tpu_custom_call" | custom-call | tf_op jit(solution)/shard_map/pack/pallas_call | solution.py:347
  9.1 0.0 all-gather.5.cloned.1.call-update
  9.1 8.6 %all-to-all-start = ((bf16[16,32,128]{2,1,0:T(8,128)(2,1)}), bf16[16,32,128]{2,1,0:T(8,128)(2,1)S(1)}, u32[]{:S(2)}, u32[]{:S(2)}) async-start(bf16[16,32,128]{2,1,0:T(8,128)(2,1)} %bitcast.5), calls=%async_computation | async-start | bytes 262144 | tf_op jit(solution)/shard_map/all_to_all | solution.py:358
  17.7 3.8 %collective-permute-start.1 = (bf16[512,128]{1,0:T(8,128)(2,1)}, bf16[512,128]{1,0:T(8,128)(2,1)S(1)}, u32[]{:S(2)}, u32[]{:S(2)}) collective-permute-start(bf16[512,128]{1,0:T(8,128)(2,1)} %get-tuple-element.64.own_ref), channel_id=1, source_target_pairs={{0,32},{8,40},{16,48},{24,56},{32,0},{40,8},{48,16},{56,24},{64,96... | collective-permute-start | bytes 393224 | tf_op jit(solution)/shard_map/ppermute | solution.py:366
  21.6 3.4 %collective-permute-start = (bf16[512,128]{1,0:T(8,128)(2,1)}, bf16[512,128]{1,0:T(8,128)(2,1)S(1)}, u32[]{:S(2)}, u32[]{:S(2)}) collective-permute-start(bf16[512,128]{1,0:T(8,128)(2,1)} %get-tuple-element.64.own_ref), channel_id=1, source_target_pairs={{0,8},{8,0},{16,24},{24,16},{32,40},{40,32},{48,56},{56,48},{64,72... | collective-permute-start | bytes 393224 | tf_op jit(solution)/shard_map/ppermute | solution.py:366
  24.9 2.1 %all-to-all-done.slices_ref = bf16[16,32,128]{2,1,0:T(8,128)(2,1)S(1)} async-done(((bf16[16,32,128]{2,1,0:T(8,128)(2,1)}), bf16[16,32,128]{2,1,0:T(8,128)(2,1)S(1)}, u32[]{:S(2)}, u32[]{:S(2)}) %all-to-all-start) | async-done | bytes 131104 | tf_op jit(solution)/shard_map/all_to_all | solution.py:358
  27.0 0.7 copy-done.6
  27.6 1.2 pick.1
  28.9 12.4 %all-to-all-start.1 = ((bf16[4,2,32,128]{3,2,1,0:T(8,128)(2,1)}), bf16[4,2,32,128]{3,2,1,0:T(8,128)(2,1)S(1)}, u32[]{:S(2)}, u32[]{:S(2)}) async-start(bf16[4,2,32,128]{3,2,1,0:T(8,128)(2,1)} %pick.1), calls=%async_computation.1 | async-start | bytes 131072 | tf_op jit(solution)/shard_map/all_to_all | solution.py:379
  41.3 4.0 %collective-permute-start.3 = (bf16[512,128]{1,0:T(8,128)(2,1)}, bf16[512,128]{1,0:T(8,128)(2,1)S(1)}, u32[]{:S(2)}, u32[]{:S(2)}) collective-permute-start(bf16[512,128]{1,0:T(8,128)(2,1)} %get-tuple-element.64.own_ref), channel_id=1, source_target_pairs={{0,64},{8,72},{16,80},{24,88},{32,96},{40,104},{48,112},{56,120},{... | collective-permute-start | bytes 393224 | tf_op jit(solution)/shard_map/ppermute | solution.py:381
  45.3 4.9 %collective-permute-start.2 = (bf16[512,128]{1,0:T(8,128)(2,1)}, bf16[512,128]{1,0:T(8,128)(2,1)S(1)}, u32[]{:S(2)}, u32[]{:S(2)}) collective-permute-start(bf16[512,128]{1,0:T(8,128)(2,1)} %get-tuple-element.64.own_ref), channel_id=1, source_target_pairs={{0,16},{8,24},{16,0},{24,8},{32,48},{40,56},{48,32},{56,40},{64,80... | collective-permute-start | bytes 393224 | tf_op jit(solution)/shard_map/ppermute | solution.py:381
  50.2 0.0 all-gather.5.cloned.1.call-done
  50.2 2.6 %cotangent.1 = (bf16[8,256,128]{2,1,0:T(8,128)(2,1)}, bf16[256,128]{1,0:T(8,128)(2,1)}, bf16[128,256]{1,0:T(8,128)(2,1)}, bf16[8,128,128]{2,1,0:T(8,128)(2,1)}) custom-call(s32[1]{0:T(128)} %bitcast.2.head_ref, bf16[8,10,128,128]{3,2,1,0:T(8,128)(2,1)} %bitcast.7, bf16[128,1024]{1,0:T(8,128)(2,1)} %w_hbm.1), custom_call_target="tpu_custom_call" | custom-call | flops 600000000 | bytes 4000000 | tf_op jit(solution)/shard_map/cotangent/pallas_call | solution.py:382
  52.8 0.0 copy-start.2
  52.8 0.0 copy-start.3
  52.8 0.0 copy-start.8
  52.8 2.2 %all-to-all-done.1.slices_ref = bf16[4,2,32,128]{3,2,1,0:T(8,128)(2,1)S(1)} async-done(((bf16[4,2,32,128]{3,2,1,0:T(8,128)(2,1)}), bf16[4,2,32,128]{3,2,1,0:T(8,128)(2,1)S(1)}, u32[]{:S(2)}, u32[]{:S(2)}) %all-to-all-start.1) | async-done | bytes 65568 | tf_op jit(solution)/shard_map/all_to_all | solution.py:379
  55.0 1.6 %spread.1 = bf16[16,2,32,128]{3,2,1,0:T(8,128)(2,1)} custom-call(s32[2]{0:T(128)S(1)} %copy-done.7, bf16[4,2,32,128]{3,2,1,0:T(8,128)(2,1)S(1)} %all-to-all-done.1.slices_ref), custom_call_target="tpu_custom_call" | custom-call | tf_op jit(solution)/shard_map/spread/pallas_call | solution.py:405
  56.6 5.7 %all-to-all-start.2 = ((bf16[16,2,32,128]{3,2,1,0:T(8,128)(2,1)}), bf16[16,2,32,128]{3,2,1,0:T(8,128)(2,1)S(1)}, u32[]{:S(2)}, u32[]{:S(2)}) async-start(bf16[16,2,32,128]{3,2,1,0:T(8,128)(2,1)} %spread.1), calls=%async_computation.2 | async-start | bytes 524288 | tf_op jit(solution)/shard_map/all_to_all | solution.py:417
  62.4 0.7 collective-permute-start.4
  63.1 1.9 %near.1 = (f32[256,128]{1,0:T(8,128)S(1)}, f32[256,128]{1,0:T(8,128)S(1)}, bf16[128,256]{1,0:T(8,128)(2,1)S(1)}) custom-call(s32[1]{0:T(128)} %bitcast.pos_ref, s32[4,32]{1,0:T(4,128)S(1)} %copy-done.5, bf16[512,128]{1,0:T(8,128)(2,1)S(1)} %copy-done, bf16[512,128]{1,0:T(8,128)(2,1)S(1)} %collective-permute-done.p0.refs_0_, ...), custom_call_target="tpu_custom_call" | custom-call | flops 1000000000 | bytes 1000000 | tf_op jit(solution)/shard_map/near/pallas_call | solution.py:422
  64.9 7.4 %all-to-all-done.2.glob_ref = bf16[16,2,32,128]{3,2,1,0:T(8,128)(2,1)S(1)} async-done(((bf16[16,2,32,128]{3,2,1,0:T(8,128)(2,1)}), bf16[16,2,32,128]{3,2,1,0:T(8,128)(2,1)S(1)}, u32[]{:S(2)}, u32[]{:S(2)}) %all-to-all-start.2) | async-done | bytes 262176 | tf_op jit(solution)/shard_map/all_to_all | solution.py:417
  72.4 4.4 %forward.1 = (f32[256,128]{1,0:T(8,128)}, bf16[16,128,128]{2,1,0:T(8,128)(2,1)}, f32[256,128]{1,0:T(8,128)S(1)}, f32[256,128]{1,0:T(8,128)S(1)}) custom-call(s32[1]{0:T(128)} %bitcast.pos_ref, s32[4,32]{1,0:T(4,128)S(1)} %copy-done.5, bf16[512,128]{1,0:T(8,128)(2,1)S(1)} %copy-done, bf16[512,128]{1,0:T(8,128)(2,1)S(1)} %collective-permute-done.4.p1.refs_1_, ...), custom_call_target="tpu_custom_call" | custom-call | flops 3000000000 | bytes 4000000 | tf_op jit(solution)/shard_map/forward/pallas_call | solution.py:437
  76.8 7.4 %all-to-all-start.3 = ((bf16[16,128,128]{2,1,0:T(8,128)(2,1)}), bf16[16,128,128]{2,1,0:T(8,128)(2,1)S(1)}, u32[]{:S(2)}, u32[]{:S(2)}) async-start(bf16[16,128,128]{2,1,0:T(8,128)(2,1)} %get-tuple-element.80), calls=%async_computation.3 | async-start | bytes 1048576 | tf_op jit(solution)/shard_map/all_to_all | solution.py:461
  84.2 0.0 all-gather.7.cloned.1.call-start
  84.2 0.7 all-gather.7.cloned.1.call-update
  85.0 2.3 %backward.1 = (bf16[256,256]{1,0:T(8,128)(2,1)S(1)}, bf16[256,256]{1,0:T(8,128)(2,1)S(1)}, bf16[256,256]{1,0:T(8,128)(2,1)S(1)}, f32[256,128]{1,0:T(8,128)S(1)}) custom-call(s32[1]{0:T(128)} %bitcast.pos_ref, s32[4,32]{1,0:T(4,128)S(1)} %copy-done.5, bf16[512,128]{1,0:T(8,128)(2,1)S(1)} %copy-done, f32[256,128]{1,0:T(8,128)S(1)} %get-tuple-element.81.stats_ref, ...), custom_call_target="tpu_custom_call" | custom-call | flops 1000000 | bytes 10000 | tf_op jit(solution)/shard_map/backward/pallas_call | solution.py:466
  87.2 0.7 collective-permute-start.5
  87.9 6.5 %collective-permute-start.6 = (bf16[256,256]{1,0:T(8,128)(2,1)S(1)}, bf16[256,256]{1,0:T(8,128)(2,1)S(1)}, u32[]{:S(2)}, u32[]{:S(2)}) collective-permute-start(bf16[256,256]{1,0:T(8,128)(2,1)S(1)} %get-tuple-element.87), channel_id=1, source_target_pairs={{0,8},{8,0},{16,24},{24,16},{32,40},{40,32},{48,56},{56,48},{64,72... | collective-permute-start | bytes 393224 | tf_op jit(solution)/shard_map/ppermute | solution.py:483
  94.4 2.0 %all-to-all-done.3 = bf16[16,128,128]{2,1,0:T(8,128)(2,1)S(1)} async-done(((bf16[16,128,128]{2,1,0:T(8,128)(2,1)}), bf16[16,128,128]{2,1,0:T(8,128)(2,1)S(1)}, u32[]{:S(2)}, u32[]{:S(2)}) %all-to-all-start.3) | async-done | bytes 524320 | tf_op jit(solution)/shard_map/all_to_all | solution.py:461
  96.5 0.1 reduce_sum.24
  96.6 0.8 collective-permute-done.6.b0
  97.4 0.7 broadcast_in_dim.10
  98.0 10.7 %all-to-all-start.4 = ((bf16[4,128,128]{2,1,0:T(8,128)(2,1)}), bf16[4,128,128]{2,1,0:T(8,128)(2,1)S(1)}, u32[]{:S(2)}, u32[]{:S(2)}) async-start(bf16[4,128,128]{2,1,0:T(8,128)(2,1)} %broadcast_in_dim.10), calls=%async_computation.4 | async-start | bytes 262144 | tf_op jit(solution)/shard_map/all_to_all | solution.py:487
  108.7 2.3 %collective-permute-start.7 = (bf16[256,256]{1,0:T(8,128)(2,1)S(1)}, bf16[256,256]{1,0:T(8,128)(2,1)S(1)}, u32[]{:S(2)}, u32[]{:S(2)}) collective-permute-start(bf16[256,256]{1,0:T(8,128)(2,1)S(1)} %get-tuple-element.89), channel_id=1, source_target_pairs={{0,32},{8,40},{16,48},{24,56},{32,0},{40,8},{48,16},{56,24},{64,96... | collective-permute-start | bytes 393224 | tf_op jit(solution)/shard_map/ppermute | solution.py:490
  111.0 2.3 %backward_rest.1 = (bf16[256,256]{1,0:T(8,128)(2,1)S(1)}, bf16[256,256]{1,0:T(8,128)(2,1)S(1)}, f32[256,256]{1,0:T(8,128)S(1)}, f32[256,128]{1,0:T(8,128)S(1)}) custom-call(s32[1]{0:T(128)} %bitcast.pos_ref, s32[4,32]{1,0:T(4,128)S(1)} %copy-done.5, bf16[512,128]{1,0:T(8,128)(2,1)S(1)} %copy-done, f32[256,128]{1,0:T(8,128)S(1)} %get-tuple-element.81.stats_ref, ...), custom_call_target="tpu_custom_call" | custom-call | flops 1000000 | bytes 10000 | tf_op jit(solution)/shard_map/backward_rest/pallas_call | solution.py:466
  113.3 2.8 %collective-permute-start.8 = (bf16[256,256]{1,0:T(8,128)(2,1)S(1)}, bf16[256,256]{1,0:T(8,128)(2,1)S(1)}, u32[]{:S(2)}, u32[]{:S(2)}) collective-permute-start(bf16[256,256]{1,0:T(8,128)(2,1)S(1)} %get-tuple-element.91), channel_id=1, source_target_pairs={{0,16},{8,24},{16,0},{24,8},{32,48},{40,56},{48,32},{56,40},{64,80... | collective-permute-start | bytes 393224 | tf_op jit(solution)/shard_map/ppermute | solution.py:490
  116.1 7.1 %all-to-all-done.4 = bf16[4,128,128]{2,1,0:T(8,128)(2,1)S(1)} async-done(((bf16[4,128,128]{2,1,0:T(8,128)(2,1)}), bf16[4,128,128]{2,1,0:T(8,128)(2,1)S(1)}, u32[]{:S(2)}, u32[]{:S(2)}) %all-to-all-start.4) | async-done | bytes 131104 | tf_op jit(solution)/shard_map/all_to_all | solution.py:487
  123.2 0.0 all-gather.7.cloned.1.call-done
  123.3 0.9 broadcast_in_dim.11
  124.2 4.0 %all-to-all-start.5 = ((bf16[16,128,128]{2,1,0:T(8,128)(2,1)}), bf16[16,128,128]{2,1,0:T(8,128)(2,1)S(1)}, u32[]{:S(2)}, u32[]{:S(2)}) async-start(bf16[16,128,128]{2,1,0:T(8,128)(2,1)} %broadcast_in_dim.11), calls=%async_computation.5 | async-start | bytes 1048576 | tf_op jit(solution)/shard_map/all_to_all | solution.py:495
  128.2 4.7 %collective-permute-start.9 = (bf16[256,256]{1,0:T(8,128)(2,1)S(1)}, bf16[256,256]{1,0:T(8,128)(2,1)S(1)}, u32[]{:S(2)}, u32[]{:S(2)}) collective-permute-start(bf16[256,256]{1,0:T(8,128)(2,1)S(1)} %get-tuple-element.99), channel_id=1, source_target_pairs={{0,64},{8,72},{16,80},{24,88},{32,96},{40,104},{48,112},{56,120},{... | collective-permute-start | bytes 393224 | tf_op jit(solution)/shard_map/ppermute | solution.py:490
  132.9 1.2 copy-done.1
  134.1 0.9 project.1
  135.1 8.4 %collective-permute-done.9.b4 = bf16[256,256]{1,0:T(8,128)(2,1)S(1)} collective-permute-done((bf16[256,256]{1,0:T(8,128)(2,1)S(1)}, bf16[256,256]{1,0:T(8,128)(2,1)S(1)}, u32[]{:S(2)}, u32[]{:S(2)}) %collective-permute-start.9) | collective-permute-done | bytes 131104 | tf_op jit(solution)/shard_map/ppermute | solution.py:490
  143.5 1.6 %finish.1 = (bf16[256,128]{1,0:T(8,128)(2,1)}, bf16[256,128]{1,0:T(8,128)(2,1)}, f32[128,1024]{1,0:T(8,128)}) custom-call(s32[1]{0:T(128)} %bitcast.pos_ref, s32[2]{0:T(128)S(1)} %copy-done.7, bf16[256,256]{1,0:T(8,128)(2,1)S(1)} %collective-permute-done.6.b0, bf16[256,256]{1,0:T(8,128)(2,1)S(1)} %collective-permute-done.5.b1, ...), custom_call_target="tpu_custom_call" | custom-call | flops 2000000 | bytes 2500000 | tf_op jit(solution)/shard_map/finish/pallas_call | solution.py:508
  (22 shorter events, 0.1 us)
Async XLA Ops:
  7.2 47.9 %copy-start.7 = (s32[2]{0:T(128)S(1)}, s32[2]{0:T(128)}, u32[]{:S(2)}) copy-start(s32[2]{0:T(128)} %ids_ref.5) | copy-start | bytes 28
  7.2 55.9 %copy-start.5 = (s32[4,32]{1,0:T(4,128)S(1)}, s32[4,32]{1,0:T(4,128)}, u32[]{:S(2)}) copy-start(s32[4,32]{1,0:T(4,128)} %pair_ref.7) | copy-start | bytes 1540
  7.2 43.0 %all-gather.5.cloned.1.call-start = ((), (), s32[]{:S(2)}) async-start(), calls=%async_computation.6 | async-start | bytes 2949120 | tf_op jit(solution)/shard_map/all_gather | solution.py:359
  9.1 53.3 %copy-start = (bf16[512,128]{1,0:T(8,128)(2,1)S(1)}, bf16[512,128]{1,0:T(8,128)(2,1)}, u32[]{:S(2)}) copy-start(bf16[512,128]{1,0:T(8,128)(2,1)} %get-tuple-element.64.own_ref) | copy-start | bytes 393220
  9.1 17.9 %all-to-all-start = ((bf16[16,32,128]{2,1,0:T(8,128)(2,1)}), bf16[16,32,128]{2,1,0:T(8,128)(2,1)S(1)}, u32[]{:S(2)}, u32[]{:S(2)}) async-start(bf16[16,32,128]{2,1,0:T(8,128)(2,1)} %bitcast.5), calls=%async_computation | async-start | bytes 262144 | tf_op jit(solution)/shard_map/all_to_all | solution.py:358
  17.7 11.2 %collective-permute-start.1 = (bf16[512,128]{1,0:T(8,128)(2,1)}, bf16[512,128]{1,0:T(8,128)(2,1)S(1)}, u32[]{:S(2)}, u32[]{:S(2)}) collective-permute-start(bf16[512,128]{1,0:T(8,128)(2,1)} %get-tuple-element.64.own_ref), channel_id=1, source_target_pairs={{0,32},{8,40},{16,48},{24,56},{32,0},{40,8},{48,16},{56,24},{64,96... | collective-permute-start | bytes 393224 | tf_op jit(solution)/shard_map/ppermute | solution.py:366
  21.6 7.3 %collective-permute-start = (bf16[512,128]{1,0:T(8,128)(2,1)}, bf16[512,128]{1,0:T(8,128)(2,1)S(1)}, u32[]{:S(2)}, u32[]{:S(2)}) collective-permute-start(bf16[512,128]{1,0:T(8,128)(2,1)} %get-tuple-element.64.own_ref), channel_id=1, source_target_pairs={{0,8},{8,0},{16,24},{24,16},{32,40},{40,32},{48,56},{56,48},{64,72... | collective-permute-start | bytes 393224 | tf_op jit(solution)/shard_map/ppermute | solution.py:366
  27.0 0.7 copy-start.6
  28.9 26.1 %all-to-all-start.1 = ((bf16[4,2,32,128]{3,2,1,0:T(8,128)(2,1)}), bf16[4,2,32,128]{3,2,1,0:T(8,128)(2,1)S(1)}, u32[]{:S(2)}, u32[]{:S(2)}) async-start(bf16[4,2,32,128]{3,2,1,0:T(8,128)(2,1)} %pick.1), calls=%async_computation.1 | async-start | bytes 131072 | tf_op jit(solution)/shard_map/all_to_all | solution.py:379
  41.3 15.3 %collective-permute-start.3 = (bf16[512,128]{1,0:T(8,128)(2,1)}, bf16[512,128]{1,0:T(8,128)(2,1)S(1)}, u32[]{:S(2)}, u32[]{:S(2)}) collective-permute-start(bf16[512,128]{1,0:T(8,128)(2,1)} %get-tuple-element.64.own_ref), channel_id=1, source_target_pairs={{0,64},{8,72},{16,80},{24,88},{32,96},{40,104},{48,112},{56,120},{... | collective-permute-start | bytes 393224 | tf_op jit(solution)/shard_map/ppermute | solution.py:381
  45.3 11.3 %collective-permute-start.2 = (bf16[512,128]{1,0:T(8,128)(2,1)}, bf16[512,128]{1,0:T(8,128)(2,1)S(1)}, u32[]{:S(2)}, u32[]{:S(2)}) collective-permute-start(bf16[512,128]{1,0:T(8,128)(2,1)} %get-tuple-element.64.own_ref), channel_id=1, source_target_pairs={{0,16},{8,24},{16,0},{24,8},{32,48},{40,56},{48,32},{56,40},{64,80... | collective-permute-start | bytes 393224 | tf_op jit(solution)/shard_map/ppermute | solution.py:381
  52.8 19.6 %copy-start.2 = (bf16[256,128]{1,0:T(8,128)(2,1)S(1)}, bf16[256,128]{1,0:T(8,128)(2,1)}, u32[]{:S(2)}) copy-start(bf16[256,128]{1,0:T(8,128)(2,1)} %get-tuple-element.79.gatt_ref) | copy-start | bytes 196612
  52.8 19.6 %copy-start.3 = (bf16[128,256]{1,0:T(8,128)(2,1)S(1)}, bf16[128,256]{1,0:T(8,128)(2,1)}, u32[]{:S(2)}) copy-start(bf16[128,256]{1,0:T(8,128)(2,1)} %get-tuple-element.76.gattt_ref) | copy-start | bytes 196612
  52.8 19.5 %copy-start.8 = (bf16[8,256,128]{2,1,0:T(8,128)(2,1)S(1)}, bf16[8,256,128]{2,1,0:T(8,128)(2,1)}, u32[]{:S(2)}) copy-start(bf16[8,256,128]{2,1,0:T(8,128)(2,1)} %get-tuple-element.78.gout_ref) | copy-start | bytes 1572868
  56.6 15.7 %all-to-all-start.2 = ((bf16[16,2,32,128]{3,2,1,0:T(8,128)(2,1)}), bf16[16,2,32,128]{3,2,1,0:T(8,128)(2,1)S(1)}, u32[]{:S(2)}, u32[]{:S(2)}) async-start(bf16[16,2,32,128]{3,2,1,0:T(8,128)(2,1)} %spread.1), calls=%async_computation.2 | async-start | bytes 524288 | tf_op jit(solution)/shard_map/all_to_all | solution.py:417
  62.4 10.0 %collective-permute-start.4 = (bf16[512,128]{1,0:T(8,128)(2,1)S(1)}, bf16[512,128]{1,0:T(8,128)(2,1)S(1)}, u32[]{:S(2)}, u32[]{:S(2)}) collective-permute-start(bf16[512,128]{1,0:T(8,128)(2,1)S(1)} %copy-done), channel_id=1, source_target_pairs={{8,16},{16,8},{24,32},{32,24},{40,48},{48,40},{56,64},{64,56},{72,... | collective-permute-start | bytes 393224 | tf_op jit(solution)/shard_map/ppermute | solution.py:418
  76.8 19.7 %all-to-all-start.3 = ((bf16[16,128,128]{2,1,0:T(8,128)(2,1)}), bf16[16,128,128]{2,1,0:T(8,128)(2,1)S(1)}, u32[]{:S(2)}, u32[]{:S(2)}) async-start(bf16[16,128,128]{2,1,0:T(8,128)(2,1)} %get-tuple-element.80), calls=%async_computation.3 | async-start | bytes 1048576 | tf_op jit(solution)/shard_map/all_to_all | solution.py:461
  84.2 48.7 %copy-start.4 = (bf16[8,128,128]{2,1,0:T(8,128)(2,1)S(1)}, bf16[8,128,128]{2,1,0:T(8,128)(2,1)}, u32[]{:S(2)}) copy-start(bf16[8,128,128]{2,1,0:T(8,128)(2,1)} %get-tuple-element.94.w_ref) | copy-start | bytes 786436
  84.2 39.0 %all-gather.7.cloned.1.call-start = ((), (), s32[]{:S(2)}) async-start(), calls=%async_computation.7 | async-start | bytes 1179648 | tf_op jit(solution)/shard_map/all_gather | solution.py:462
  87.2 9.3 %collective-permute-start.5 = (bf16[256,256]{1,0:T(8,128)(2,1)S(1)}, bf16[256,256]{1,0:T(8,128)(2,1)S(1)}, u32[]{:S(2)}, u32[]{:S(2)}) collective-permute-start(bf16[256,256]{1,0:T(8,128)(2,1)S(1)} %get-tuple-element.86), channel_id=1, source_target_pairs={{8,16},{16,8},{24,32},{32,24},{40,48},{48,40},{56,64},{64,56},{72,... | collective-permute-start | bytes 393224 | tf_op jit(solution)/shard_map/ppermute | solution.py:483
  87.9 9.5 %collective-permute-start.6 = (bf16[256,256]{1,0:T(8,128)(2,1)S(1)}, bf16[256,256]{1,0:T(8,128)(2,1)S(1)}, u32[]{:S(2)}, u32[]{:S(2)}) collective-permute-start(bf16[256,256]{1,0:T(8,128)(2,1)S(1)} %get-tuple-element.87), channel_id=1, source_target_pairs={{0,8},{8,0},{16,24},{24,16},{32,40},{40,32},{48,56},{56,48},{64,72... | collective-permute-start | bytes 393224 | tf_op jit(solution)/shard_map/ppermute | solution.py:483
  98.0 25.1 %all-to-all-start.4 = ((bf16[4,128,128]{2,1,0:T(8,128)(2,1)}), bf16[4,128,128]{2,1,0:T(8,128)(2,1)S(1)}, u32[]{:S(2)}, u32[]{:S(2)}) async-start(bf16[4,128,128]{2,1,0:T(8,128)(2,1)} %broadcast_in_dim.10), calls=%async_computation.4 | async-start | bytes 262144 | tf_op jit(solution)/shard_map/all_to_all | solution.py:487
  108.7 14.5 %collective-permute-start.7 = (bf16[256,256]{1,0:T(8,128)(2,1)S(1)}, bf16[256,256]{1,0:T(8,128)(2,1)S(1)}, u32[]{:S(2)}, u32[]{:S(2)}) collective-permute-start(bf16[256,256]{1,0:T(8,128)(2,1)S(1)} %get-tuple-element.89), channel_id=1, source_target_pairs={{0,32},{8,40},{16,48},{24,56},{32,0},{40,8},{48,16},{56,24},{64,96... | collective-permute-start | bytes 393224 | tf_op jit(solution)/shard_map/ppermute | solution.py:490
  113.3 9.9 %collective-permute-start.8 = (bf16[256,256]{1,0:T(8,128)(2,1)S(1)}, bf16[256,256]{1,0:T(8,128)(2,1)S(1)}, u32[]{:S(2)}, u32[]{:S(2)}) collective-permute-start(bf16[256,256]{1,0:T(8,128)(2,1)S(1)} %get-tuple-element.91), channel_id=1, source_target_pairs={{0,16},{8,24},{16,0},{24,8},{32,48},{40,56},{48,32},{56,40},{64,80... | collective-permute-start | bytes 393224 | tf_op jit(solution)/shard_map/ppermute | solution.py:490
  124.2 19.3 %all-to-all-start.5 = ((bf16[16,128,128]{2,1,0:T(8,128)(2,1)}), bf16[16,128,128]{2,1,0:T(8,128)(2,1)S(1)}, u32[]{:S(2)}, u32[]{:S(2)}) async-start(bf16[16,128,128]{2,1,0:T(8,128)(2,1)} %broadcast_in_dim.11), calls=%async_computation.5 | async-start | bytes 1048576 | tf_op jit(solution)/shard_map/all_to_all | solution.py:495
  128.2 15.3 %collective-permute-start.9 = (bf16[256,256]{1,0:T(8,128)(2,1)S(1)}, bf16[256,256]{1,0:T(8,128)(2,1)S(1)}, u32[]{:S(2)}, u32[]{:S(2)}) collective-permute-start(bf16[256,256]{1,0:T(8,128)(2,1)S(1)} %get-tuple-element.99), channel_id=1, source_target_pairs={{0,64},{8,72},{16,80},{24,88},{32,96},{40,104},{48,112},{56,120},{... | collective-permute-start | bytes 393224 | tf_op jit(solution)/shard_map/ppermute | solution.py:490
  132.9 1.2 copy-start.1
Sparse Core Ops, SparseCore 0:
  10.7 37.0 all-gather.4
  87.2 27.1 all-gather.6

commit v13 on v11

--- a/solution.py
+++ b/solution.py
@@ -486,11 +486,11 @@
     share, returned[1], returned[0] = lax.optimization_barrier((share, returned[1], returned[0]))
     column = lax.all_to_all(jnp.broadcast_to(share[None], (his,) + share.shape), "hi", 0, 0)
     terms[2], terms[3], gown, gquery = backward((3, 4, 0), "backward_rest", gquery)
-    for n in (4, 2, 3):
+    for n in (4, 3, 2):
         returned[n] = lax.ppermute(terms[n], CTX, routes[n])
     share = jnp.sum(column.astype(F32), axis=0).astype(BF16)
-    share, returned[4], returned[2], attended_all = lax.optimization_barrier(
-        (share, returned[4], returned[2], attended_all)
+    share, returned[4], returned[3], attended_all = lax.optimization_barrier(
+        (share, returned[4], returned[3], attended_all)
     )
     totals = lax.all_to_all(jnp.broadcast_to(share[None], (los,) + share.shape), "lo", 0, 0)
 

time: 151 us -> 153 us (1.013); the launches traced: 150 us -> 150 us
  starting transfers between devices: 83.4 us -> 85.7 us
  waiting for transfers between devices: 28.1 us -> 26.1 us
    ppermute x5, starting transfers between devices: 18 us -> 20 us  [local(): returned[n] = lax.ppermute(terms[n], CTX, routes[n])]
where the time goes in v13:
time: 153 us; the launch traced here: 150 us
  starting transfers between devices  85.7 us (56%)
  waiting for transfers between devices  26.1 us (17%)
  Pallas kernels  20.5 us (13%)
  between operations  14.4 us (9%)
  local copies, waits for them, and re-layouts  3.48 us (2%)
    ppermute x5, starting transfers between devices, local(): returned[n] = lax.ppermute(terms[n], CTX, routes[n])  20 us
    all_to_all x1, starting transfers between devices, local(): column = lax.all_to_all(picked, 'hi', 0, 0)  12.4 us
    all_to_all x1, starting transfers between devices, local(): lax.all_to_all(jnp.broadcast_to(share[None], (his,) + share.shape), 'hi',...  10.3 us
    all_to_all x1, starting transfers between devices, local(): slices = lax.all_to_all(joined.reshape(los, step, width), 'lo', 0, 0)  8.61 us
    ppermute x2, starting transfers between devices, local(): received[n] = lax.ppermute(joined, CTX, routes[n])  8.1 us
    ppermute x2, starting transfers between devices, local(): received[n] = lax.ppermute(joined_late, CTX, routes[n])  8.09 us
    all_to_all x1, starting transfers between devices, local(): shares = lax.all_to_all(sums, 'lo', 0, 0)  7.42 us
    all_to_all x1, waiting for transfers between devices, local(): globals_all = lax.all_to_all(chosen, 'lo', 0, 0)  7.4 us
  transfers between devices with their start and end apart: 18, of which 9 were waited for; matrix products, arithmetic and copies ran while one was open for 1% of the time, Pallas kernels for 8%

profile of v13, /device:TPU:24, one launch (start us, length us, event | category | flops | bytes accessed | tf_op | source)
XLA Modules:
  0.0 150.2 jit_solution(12740658883778595982)
XLA Ops:
  7.2 0.0 all-gather.5.cloned.1.call-start
  7.2 1.8 %pack.1 = (bf16[512,128]{1,0:T(8,128)(2,1)}, bf16[10,128,128]{2,1,0:T(8,128)(2,1)}) custom-call(bf16[256,128]{1,0:T(8,128)(2,1)} %qk_ref.1, bf16[256,128]{1,0:T(8,128)(2,1)} %val_ref.1, bf16[256,128]{1,0:T(8,128)(2,1)} %gout_ref.1, bf16[128,1024]{1,0:T(8,128)(2,1)} %w_hbm.1), custom_call_target="tpu_custom_call" | custom-call | tf_op jit(solution)/shard_map/pack/pallas_call | solution.py:347
  9.1 0.0 all-gather.5.cloned.1.call-update
  9.1 8.6 %all-to-all-start = ((bf16[16,32,128]{2,1,0:T(8,128)(2,1)}), bf16[16,32,128]{2,1,0:T(8,128)(2,1)S(1)}, u32[]{:S(2)}, u32[]{:S(2)}) async-start(bf16[16,32,128]{2,1,0:T(8,128)(2,1)} %bitcast.5), calls=%async_computation | async-start | bytes 262144 | tf_op jit(solution)/shard_map/all_to_all | solution.py:358
  17.7 4.7 %collective-permute-start.1 = (bf16[512,128]{1,0:T(8,128)(2,1)}, bf16[512,128]{1,0:T(8,128)(2,1)S(1)}, u32[]{:S(2)}, u32[]{:S(2)}) collective-permute-start(bf16[512,128]{1,0:T(8,128)(2,1)} %get-tuple-element.64.own_ref), channel_id=1, source_target_pairs={{0,64},{8,72},{16,80},{24,88},{32,96},{40,104},{48,112},{56,120},{... | collective-permute-start | bytes 393224 | tf_op jit(solution)/shard_map/ppermute | solution.py:366
  22.5 3.4 %collective-permute-start = (bf16[512,128]{1,0:T(8,128)(2,1)}, bf16[512,128]{1,0:T(8,128)(2,1)S(1)}, u32[]{:S(2)}, u32[]{:S(2)}) collective-permute-start(bf16[512,128]{1,0:T(8,128)(2,1)} %get-tuple-element.64.own_ref), channel_id=1, source_target_pairs={{0,8},{8,0},{16,24},{24,16},{32,40},{40,32},{48,56},{56,48},{64,72... | collective-permute-start | bytes 393224 | tf_op jit(solution)/shard_map/ppermute | solution.py:366
  25.8 1.2 all-to-all-done.slices_ref
  27.0 0.7 copy-done.6
  27.6 1.2 pick.1
  28.9 0.8 collective-permute-done.1.p4.refs_2_
  29.7 12.4 %all-to-all-start.1 = ((bf16[4,2,32,128]{3,2,1,0:T(8,128)(2,1)}), bf16[4,2,32,128]{3,2,1,0:T(8,128)(2,1)S(1)}, u32[]{:S(2)}, u32[]{:S(2)}) async-start(bf16[4,2,32,128]{3,2,1,0:T(8,128)(2,1)} %pick.1), calls=%async_computation.1 | async-start | bytes 131072 | tf_op jit(solution)/shard_map/all_to_all | solution.py:379
  42.1 3.2 %collective-permute-start.3 = (bf16[512,128]{1,0:T(8,128)(2,1)}, bf16[512,128]{1,0:T(8,128)(2,1)S(1)}, u32[]{:S(2)}, u32[]{:S(2)}) collective-permute-start(bf16[512,128]{1,0:T(8,128)(2,1)} %get-tuple-element.64.own_ref), channel_id=1, source_target_pairs={{0,32},{8,40},{16,48},{24,56},{32,0},{40,8},{48,16},{56,24},{64,96... | collective-permute-start | bytes 393224 | tf_op jit(solution)/shard_map/ppermute | solution.py:381
  45.3 4.9 %collective-permute-start.2 = (bf16[512,128]{1,0:T(8,128)(2,1)}, bf16[512,128]{1,0:T(8,128)(2,1)S(1)}, u32[]{:S(2)}, u32[]{:S(2)}) collective-permute-start(bf16[512,128]{1,0:T(8,128)(2,1)} %get-tuple-element.64.own_ref), channel_id=1, source_target_pairs={{0,16},{8,24},{16,0},{24,8},{32,48},{40,56},{48,32},{56,40},{64,80... | collective-permute-start | bytes 393224 | tf_op jit(solution)/shard_map/ppermute | solution.py:381
  50.2 0.0 all-gather.5.cloned.1.call-done
  50.2 2.6 %cotangent.1 = (bf16[8,256,128]{2,1,0:T(8,128)(2,1)}, bf16[256,128]{1,0:T(8,128)(2,1)}, bf16[128,256]{1,0:T(8,128)(2,1)}, bf16[8,128,128]{2,1,0:T(8,128)(2,1)}) custom-call(s32[1]{0:T(128)} %bitcast.2.head_ref, bf16[8,10,128,128]{3,2,1,0:T(8,128)(2,1)} %bitcast.7, bf16[128,1024]{1,0:T(8,128)(2,1)} %w_hbm.1), custom_call_target="tpu_custom_call" | custom-call | flops 600000000 | bytes 4000000 | tf_op jit(solution)/shard_map/cotangent/pallas_call | solution.py:382
  52.8 0.0 copy-start.3
  52.8 0.0 copy-start.8
  52.8 2.5 %all-to-all-done.1.slices_ref = bf16[4,2,32,128]{3,2,1,0:T(8,128)(2,1)S(1)} async-done(((bf16[4,2,32,128]{3,2,1,0:T(8,128)(2,1)}), bf16[4,2,32,128]{3,2,1,0:T(8,128)(2,1)S(1)}, u32[]{:S(2)}, u32[]{:S(2)}) %all-to-all-start.1) | async-done | bytes 65568 | tf_op jit(solution)/shard_map/all_to_all | solution.py:379
  55.3 1.6 %spread.1 = bf16[16,2,32,128]{3,2,1,0:T(8,128)(2,1)} custom-call(s32[2]{0:T(128)S(1)} %copy-done.7, bf16[4,2,32,128]{3,2,1,0:T(8,128)(2,1)S(1)} %all-to-all-done.1.slices_ref), custom_call_target="tpu_custom_call" | custom-call | tf_op jit(solution)/shard_map/spread/pallas_call | solution.py:405
  56.9 5.9 %all-to-all-start.2 = ((bf16[16,2,32,128]{3,2,1,0:T(8,128)(2,1)}), bf16[16,2,32,128]{3,2,1,0:T(8,128)(2,1)S(1)}, u32[]{:S(2)}, u32[]{:S(2)}) async-start(bf16[16,2,32,128]{3,2,1,0:T(8,128)(2,1)} %spread.1), calls=%async_computation.2 | async-start | bytes 524288 | tf_op jit(solution)/shard_map/all_to_all | solution.py:417
  62.8 0.7 collective-permute-start.4
  63.5 1.9 %near.1 = (f32[256,128]{1,0:T(8,128)S(1)}, f32[256,128]{1,0:T(8,128)S(1)}, bf16[128,256]{1,0:T(8,128)(2,1)S(1)}) custom-call(s32[1]{0:T(128)} %bitcast.pos_ref, s32[4,32]{1,0:T(4,128)S(1)} %copy-done.5, bf16[512,128]{1,0:T(8,128)(2,1)S(1)} %copy-done, bf16[512,128]{1,0:T(8,128)(2,1)S(1)} %collective-permute-done.p0.refs_0_, ...), custom_call_target="tpu_custom_call" | custom-call | flops 1000000000 | bytes 1000000 | tf_op jit(solution)/shard_map/near/pallas_call | solution.py:422
  65.4 7.4 %all-to-all-done.2.glob_ref = bf16[16,2,32,128]{3,2,1,0:T(8,128)(2,1)S(1)} async-done(((bf16[16,2,32,128]{3,2,1,0:T(8,128)(2,1)}), bf16[16,2,32,128]{3,2,1,0:T(8,128)(2,1)S(1)}, u32[]{:S(2)}, u32[]{:S(2)}) %all-to-all-start.2) | async-done | bytes 262176 | tf_op jit(solution)/shard_map/all_to_all | solution.py:417
  72.8 4.4 %forward.1 = (f32[256,128]{1,0:T(8,128)}, bf16[16,128,128]{2,1,0:T(8,128)(2,1)}, f32[256,128]{1,0:T(8,128)S(1)}, f32[256,128]{1,0:T(8,128)S(1)}) custom-call(s32[1]{0:T(128)} %bitcast.pos_ref, s32[4,32]{1,0:T(4,128)S(1)} %copy-done.5, bf16[512,128]{1,0:T(8,128)(2,1)S(1)} %copy-done, bf16[512,128]{1,0:T(8,128)(2,1)S(1)} %collective-permute-done.4.p1.refs_1_, ...), custom_call_target="tpu_custom_call" | custom-call | flops 3000000000 | bytes 4000000 | tf_op jit(solution)/shard_map/forward/pallas_call | solution.py:437
  77.2 7.4 %all-to-all-start.3 = ((bf16[16,128,128]{2,1,0:T(8,128)(2,1)}), bf16[16,128,128]{2,1,0:T(8,128)(2,1)S(1)}, u32[]{:S(2)}, u32[]{:S(2)}) async-start(bf16[16,128,128]{2,1,0:T(8,128)(2,1)} %get-tuple-element.80), calls=%async_computation.3 | async-start | bytes 1048576 | tf_op jit(solution)/shard_map/all_to_all | solution.py:461
  84.6 0.0 all-gather.7.cloned.1.call-start
  84.7 0.7 all-gather.7.cloned.1.call-update
  85.4 2.3 %backward.1 = (bf16[256,256]{1,0:T(8,128)(2,1)S(1)}, bf16[256,256]{1,0:T(8,128)(2,1)S(1)}, bf16[256,256]{1,0:T(8,128)(2,1)S(1)}, f32[256,128]{1,0:T(8,128)S(1)}) custom-call(s32[1]{0:T(128)} %bitcast.pos_ref, s32[4,32]{1,0:T(4,128)S(1)} %copy-done.5, bf16[512,128]{1,0:T(8,128)(2,1)S(1)} %copy-done, f32[256,128]{1,0:T(8,128)S(1)} %get-tuple-element.81.stats_ref, ...), custom_call_target="tpu_custom_call" | custom-call | flops 1000000 | bytes 10000 | tf_op jit(solution)/shard_map/backward/pallas_call | solution.py:466
  87.7 0.7 collective-permute-start.5
  88.3 6.5 %collective-permute-start.6 = (bf16[256,256]{1,0:T(8,128)(2,1)S(1)}, bf16[256,256]{1,0:T(8,128)(2,1)S(1)}, u32[]{:S(2)}, u32[]{:S(2)}) collective-permute-start(bf16[256,256]{1,0:T(8,128)(2,1)S(1)} %get-tuple-element.87), channel_id=1, source_target_pairs={{0,8},{8,0},{16,24},{24,16},{32,40},{40,32},{48,56},{56,48},{64,72... | collective-permute-start | bytes 393224 | tf_op jit(solution)/shard_map/ppermute | solution.py:483
  94.9 2.3 %all-to-all-done.3 = bf16[16,128,128]{2,1,0:T(8,128)(2,1)S(1)} async-done(((bf16[16,128,128]{2,1,0:T(8,128)(2,1)}), bf16[16,128,128]{2,1,0:T(8,128)(2,1)S(1)}, u32[]{:S(2)}, u32[]{:S(2)}) %all-to-all-start.3) | async-done | bytes 524320 | tf_op jit(solution)/shard_map/all_to_all | solution.py:461
  97.2 0.1 reduce_sum.24
  97.3 0.5 collective-permute-done.6.b0
  97.8 0.7 broadcast_in_dim.10
  98.5 10.3 %all-to-all-start.4 = ((bf16[4,128,128]{2,1,0:T(8,128)(2,1)}), bf16[4,128,128]{2,1,0:T(8,128)(2,1)S(1)}, u32[]{:S(2)}, u32[]{:S(2)}) async-start(bf16[4,128,128]{2,1,0:T(8,128)(2,1)} %broadcast_in_dim.10), calls=%async_computation.4 | async-start | bytes 262144 | tf_op jit(solution)/shard_map/all_to_all | solution.py:487
  108.7 4.1 %collective-permute-start.7 = (bf16[256,256]{1,0:T(8,128)(2,1)S(1)}, bf16[256,256]{1,0:T(8,128)(2,1)S(1)}, u32[]{:S(2)}, u32[]{:S(2)}) collective-permute-start(bf16[256,256]{1,0:T(8,128)(2,1)S(1)} %get-tuple-element.89), channel_id=1, source_target_pairs={{0,64},{8,72},{16,80},{24,88},{32,96},{40,104},{48,112},{56,120},{... | collective-permute-start | bytes 393224 | tf_op jit(solution)/shard_map/ppermute | solution.py:490
  112.9 2.3 %backward_rest.1 = (bf16[256,256]{1,0:T(8,128)(2,1)S(1)}, bf16[256,256]{1,0:T(8,128)(2,1)S(1)}, f32[256,256]{1,0:T(8,128)S(1)}, f32[256,128]{1,0:T(8,128)S(1)}) custom-call(s32[1]{0:T(128)} %bitcast.pos_ref, s32[4,32]{1,0:T(4,128)S(1)} %copy-done.5, bf16[512,128]{1,0:T(8,128)(2,1)S(1)} %copy-done, f32[256,128]{1,0:T(8,128)S(1)} %get-tuple-element.81.stats_ref, ...), custom_call_target="tpu_custom_call" | custom-call | flops 1000000 | bytes 10000 | tf_op jit(solution)/shard_map/backward_rest/pallas_call | solution.py:466
  115.1 3.4 %collective-permute-start.8 = (bf16[256,256]{1,0:T(8,128)(2,1)S(1)}, bf16[256,256]{1,0:T(8,128)(2,1)S(1)}, u32[]{:S(2)}, u32[]{:S(2)}) collective-permute-start(bf16[256,256]{1,0:T(8,128)(2,1)S(1)} %get-tuple-element.91), channel_id=1, source_target_pairs={{0,32},{8,40},{16,48},{24,56},{32,0},{40,8},{48,16},{56,24},{64,96... | collective-permute-start | bytes 393224 | tf_op jit(solution)/shard_map/ppermute | solution.py:490
  118.5 5.9 %all-to-all-done.4 = bf16[4,128,128]{2,1,0:T(8,128)(2,1)S(1)} async-done(((bf16[4,128,128]{2,1,0:T(8,128)(2,1)}), bf16[4,128,128]{2,1,0:T(8,128)(2,1)S(1)}, u32[]{:S(2)}, u32[]{:S(2)}) %all-to-all-start.4) | async-done | bytes 131104 | tf_op jit(solution)/shard_map/all_to_all | solution.py:487
  124.4 0.0 all-gather.7.cloned.1.call-done
  124.5 0.9 broadcast_in_dim.11
  125.4 4.1 %all-to-all-start.5 = ((bf16[16,128,128]{2,1,0:T(8,128)(2,1)}), bf16[16,128,128]{2,1,0:T(8,128)(2,1)S(1)}, u32[]{:S(2)}, u32[]{:S(2)}) async-start(bf16[16,128,128]{2,1,0:T(8,128)(2,1)} %broadcast_in_dim.11), calls=%async_computation.5 | async-start | bytes 1048576 | tf_op jit(solution)/shard_map/all_to_all | solution.py:495
  129.5 5.3 %collective-permute-start.9 = (bf16[256,256]{1,0:T(8,128)(2,1)S(1)}, bf16[256,256]{1,0:T(8,128)(2,1)S(1)}, u32[]{:S(2)}, u32[]{:S(2)}) collective-permute-start(bf16[256,256]{1,0:T(8,128)(2,1)S(1)} %get-tuple-element.97), channel_id=1, source_target_pairs={{0,16},{8,24},{16,0},{24,8},{32,48},{40,56},{48,32},{56,40},{64,80... | collective-permute-start | bytes 393224 | tf_op jit(solution)/shard_map/ppermute | solution.py:490
  134.9 1.2 copy-done.1
  136.1 0.9 project.1
  137.0 1.6 %collective-permute-done.9.b2 = bf16[256,256]{1,0:T(8,128)(2,1)S(1)} collective-permute-done((bf16[256,256]{1,0:T(8,128)(2,1)S(1)}, bf16[256,256]{1,0:T(8,128)(2,1)S(1)}, u32[]{:S(2)}, u32[]{:S(2)}) %collective-permute-start.9) | collective-permute-done | bytes 131104 | tf_op jit(solution)/shard_map/ppermute | solution.py:490
  138.6 3.2 %all-to-all-done.5.total_ref = bf16[16,128,128]{2,1,0:T(8,128)(2,1)S(1)} async-done(((bf16[16,128,128]{2,1,0:T(8,128)(2,1)}), bf16[16,128,128]{2,1,0:T(8,128)(2,1)S(1)}, u32[]{:S(2)}, u32[]{:S(2)}) %all-to-all-start.5) | async-done | bytes 524320 | tf_op jit(solution)/shard_map/all_to_all | solution.py:495
  141.8 1.6 %finish.1 = (bf16[256,128]{1,0:T(8,128)(2,1)}, bf16[256,128]{1,0:T(8,128)(2,1)}, f32[128,1024]{1,0:T(8,128)}) custom-call(s32[1]{0:T(128)} %bitcast.pos_ref, s32[2]{0:T(128)S(1)} %copy-done.7, bf16[256,256]{1,0:T(8,128)(2,1)S(1)} %collective-permute-done.6.b0, bf16[256,256]{1,0:T(8,128)(2,1)S(1)} %collective-permute-done.5.b1, ...), custom_call_target="tpu_custom_call" | custom-call | flops 2000000 | bytes 2500000 | tf_op jit(solution)/shard_map/finish/pallas_call | solution.py:508
  (22 shorter events, 0.1 us)
Async XLA Ops:
  7.2 48.1 %copy-start.7 = (s32[2]{0:T(128)S(1)}, s32[2]{0:T(128)}, u32[]{:S(2)}) copy-start(s32[2]{0:T(128)} %ids_ref.5) | copy-start | bytes 28
  7.2 56.3 %copy-start.5 = (s32[4,32]{1,0:T(4,128)S(1)}, s32[4,32]{1,0:T(4,128)}, u32[]{:S(2)}) copy-start(s32[4,32]{1,0:T(4,128)} %pair_ref.7) | copy-start | bytes 1540
  7.2 43.0 %all-gather.5.cloned.1.call-start = ((), (), s32[]{:S(2)}) async-start(), calls=%async_computation.6 | async-start | bytes 2949120 | tf_op jit(solution)/shard_map/all_gather | solution.py:359
  9.1 53.7 %copy-start = (bf16[512,128]{1,0:T(8,128)(2,1)S(1)}, bf16[512,128]{1,0:T(8,128)(2,1)}, u32[]{:S(2)}) copy-start(bf16[512,128]{1,0:T(8,128)(2,1)} %get-tuple-element.64.own_ref) | copy-start | bytes 393220
  9.1 17.9 %all-to-all-start = ((bf16[16,32,128]{2,1,0:T(8,128)(2,1)}), bf16[16,32,128]{2,1,0:T(8,128)(2,1)S(1)}, u32[]{:S(2)}, u32[]{:S(2)}) async-start(bf16[16,32,128]{2,1,0:T(8,128)(2,1)} %bitcast.5), calls=%async_computation | async-start | bytes 262144 | tf_op jit(solution)/shard_map/all_to_all | solution.py:358
  17.7 11.9 %collective-permute-start.1 = (bf16[512,128]{1,0:T(8,128)(2,1)}, bf16[512,128]{1,0:T(8,128)(2,1)S(1)}, u32[]{:S(2)}, u32[]{:S(2)}) collective-permute-start(bf16[512,128]{1,0:T(8,128)(2,1)} %get-tuple-element.64.own_ref), channel_id=1, source_target_pairs={{0,64},{8,72},{16,80},{24,88},{32,96},{40,104},{48,112},{56,120},{... | collective-permute-start | bytes 393224 | tf_op jit(solution)/shard_map/ppermute | solution.py:366
  22.5 7.2 %collective-permute-start = (bf16[512,128]{1,0:T(8,128)(2,1)}, bf16[512,128]{1,0:T(8,128)(2,1)S(1)}, u32[]{:S(2)}, u32[]{:S(2)}) collective-permute-start(bf16[512,128]{1,0:T(8,128)(2,1)} %get-tuple-element.64.own_ref), channel_id=1, source_target_pairs={{0,8},{8,0},{16,24},{24,16},{32,40},{40,32},{48,56},{56,48},{64,72... | collective-permute-start | bytes 393224 | tf_op jit(solution)/shard_map/ppermute | solution.py:366
  27.0 0.7 copy-start.6
  29.7 25.6 %all-to-all-start.1 = ((bf16[4,2,32,128]{3,2,1,0:T(8,128)(2,1)}), bf16[4,2,32,128]{3,2,1,0:T(8,128)(2,1)S(1)}, u32[]{:S(2)}, u32[]{:S(2)}) async-start(bf16[4,2,32,128]{3,2,1,0:T(8,128)(2,1)} %pick.1), calls=%async_computation.1 | async-start | bytes 131072 | tf_op jit(solution)/shard_map/all_to_all | solution.py:379
  42.1 14.8 %collective-permute-start.3 = (bf16[512,128]{1,0:T(8,128)(2,1)}, bf16[512,128]{1,0:T(8,128)(2,1)S(1)}, u32[]{:S(2)}, u32[]{:S(2)}) collective-permute-start(bf16[512,128]{1,0:T(8,128)(2,1)} %get-tuple-element.64.own_ref), channel_id=1, source_target_pairs={{0,32},{8,40},{16,48},{24,56},{32,0},{40,8},{48,16},{56,24},{64,96... | collective-permute-start | bytes 393224 | tf_op jit(solution)/shard_map/ppermute | solution.py:381
  45.3 11.6 %collective-permute-start.2 = (bf16[512,128]{1,0:T(8,128)(2,1)}, bf16[512,128]{1,0:T(8,128)(2,1)S(1)}, u32[]{:S(2)}, u32[]{:S(2)}) collective-permute-start(bf16[512,128]{1,0:T(8,128)(2,1)} %get-tuple-element.64.own_ref), channel_id=1, source_target_pairs={{0,16},{8,24},{16,0},{24,8},{32,48},{40,56},{48,32},{56,40},{64,80... | collective-permute-start | bytes 393224 | tf_op jit(solution)/shard_map/ppermute | solution.py:381
  52.8 20.0 %copy-start.2 = (bf16[256,128]{1,0:T(8,128)(2,1)S(1)}, bf16[256,128]{1,0:T(8,128)(2,1)}, u32[]{:S(2)}) copy-start(bf16[256,128]{1,0:T(8,128)(2,1)} %get-tuple-element.79.gatt_ref) | copy-start | bytes 196612
  52.8 20.0 %copy-start.3 = (bf16[128,256]{1,0:T(8,128)(2,1)S(1)}, bf16[128,256]{1,0:T(8,128)(2,1)}, u32[]{:S(2)}) copy-start(bf16[128,256]{1,0:T(8,128)(2,1)} %get-tuple-element.76.gattt_ref) | copy-start | bytes 196612
  52.8 20.0 %copy-start.8 = (bf16[8,256,128]{2,1,0:T(8,128)(2,1)S(1)}, bf16[8,256,128]{2,1,0:T(8,128)(2,1)}, u32[]{:S(2)}) copy-start(bf16[8,256,128]{2,1,0:T(8,128)(2,1)} %get-tuple-element.78.gout_ref) | copy-start | bytes 1572868
  56.9 15.9 %all-to-all-start.2 = ((bf16[16,2,32,128]{3,2,1,0:T(8,128)(2,1)}), bf16[16,2,32,128]{3,2,1,0:T(8,128)(2,1)S(1)}, u32[]{:S(2)}, u32[]{:S(2)}) async-start(bf16[16,2,32,128]{3,2,1,0:T(8,128)(2,1)} %spread.1), calls=%async_computation.2 | async-start | bytes 524288 | tf_op jit(solution)/shard_map/all_to_all | solution.py:417
  62.8 10.0 %collective-permute-start.4 = (bf16[512,128]{1,0:T(8,128)(2,1)S(1)}, bf16[512,128]{1,0:T(8,128)(2,1)S(1)}, u32[]{:S(2)}, u32[]{:S(2)}) collective-permute-start(bf16[512,128]{1,0:T(8,128)(2,1)S(1)} %copy-done), channel_id=1, source_target_pairs={{8,16},{16,8},{24,32},{32,24},{40,48},{48,40},{56,64},{64,56},{72,... | collective-permute-start | bytes 393224 | tf_op jit(solution)/shard_map/ppermute | solution.py:418
  77.2 20.0 %all-to-all-start.3 = ((bf16[16,128,128]{2,1,0:T(8,128)(2,1)}), bf16[16,128,128]{2,1,0:T(8,128)(2,1)S(1)}, u32[]{:S(2)}, u32[]{:S(2)}) async-start(bf16[16,128,128]{2,1,0:T(8,128)(2,1)} %get-tuple-element.80), calls=%async_computation.3 | async-start | bytes 1048576 | tf_op jit(solution)/shard_map/all_to_all | solution.py:461
  84.6 50.2 %copy-start.4 = (bf16[8,128,128]{2,1,0:T(8,128)(2,1)S(1)}, bf16[8,128,128]{2,1,0:T(8,128)(2,1)}, u32[]{:S(2)}) copy-start(bf16[8,128,128]{2,1,0:T(8,128)(2,1)} %get-tuple-element.94.w_ref) | copy-start | bytes 786436
  84.6 39.8 %all-gather.7.cloned.1.call-start = ((), (), s32[]{:S(2)}) async-start(), calls=%async_computation.7 | async-start | bytes 1179648 | tf_op jit(solution)/shard_map/all_gather | solution.py:462
  87.7 9.6 %collective-permute-start.5 = (bf16[256,256]{1,0:T(8,128)(2,1)S(1)}, bf16[256,256]{1,0:T(8,128)(2,1)S(1)}, u32[]{:S(2)}, u32[]{:S(2)}) collective-permute-start(bf16[256,256]{1,0:T(8,128)(2,1)S(1)} %get-tuple-element.86), channel_id=1, source_target_pairs={{8,16},{16,8},{24,32},{32,24},{40,48},{48,40},{56,64},{64,56},{72,... | collective-permute-start | bytes 393224 | tf_op jit(solution)/shard_map/ppermute | solution.py:483
  88.3 9.5 %collective-permute-start.6 = (bf16[256,256]{1,0:T(8,128)(2,1)S(1)}, bf16[256,256]{1,0:T(8,128)(2,1)S(1)}, u32[]{:S(2)}, u32[]{:S(2)}) collective-permute-start(bf16[256,256]{1,0:T(8,128)(2,1)S(1)} %get-tuple-element.87), channel_id=1, source_target_pairs={{0,8},{8,0},{16,24},{24,16},{32,40},{40,32},{48,56},{56,48},{64,72... | collective-permute-start | bytes 393224 | tf_op jit(solution)/shard_map/ppermute | solution.py:483
  98.5 25.9 %all-to-all-start.4 = ((bf16[4,128,128]{2,1,0:T(8,128)(2,1)}), bf16[4,128,128]{2,1,0:T(8,128)(2,1)S(1)}, u32[]{:S(2)}, u32[]{:S(2)}) async-start(bf16[4,128,128]{2,1,0:T(8,128)(2,1)} %broadcast_in_dim.10), calls=%async_computation.4 | async-start | bytes 262144 | tf_op jit(solution)/shard_map/all_to_all | solution.py:487
  108.7 15.7 %collective-permute-start.7 = (bf16[256,256]{1,0:T(8,128)(2,1)S(1)}, bf16[256,256]{1,0:T(8,128)(2,1)S(1)}, u32[]{:S(2)}, u32[]{:S(2)}) collective-permute-start(bf16[256,256]{1,0:T(8,128)(2,1)S(1)} %get-tuple-element.89), channel_id=1, source_target_pairs={{0,64},{8,72},{16,80},{24,88},{32,96},{40,104},{48,112},{56,120},{... | collective-permute-start | bytes 393224 | tf_op jit(solution)/shard_map/ppermute | solution.py:490
  115.1 9.3 %collective-permute-start.8 = (bf16[256,256]{1,0:T(8,128)(2,1)S(1)}, bf16[256,256]{1,0:T(8,128)(2,1)S(1)}, u32[]{:S(2)}, u32[]{:S(2)}) collective-permute-start(bf16[256,256]{1,0:T(8,128)(2,1)S(1)} %get-tuple-element.91), channel_id=1, source_target_pairs={{0,32},{8,40},{16,48},{24,56},{32,0},{40,8},{48,16},{56,24},{64,96... | collective-permute-start | bytes 393224 | tf_op jit(solution)/shard_map/ppermute | solution.py:490
  125.4 16.4 %all-to-all-start.5 = ((bf16[16,128,128]{2,1,0:T(8,128)(2,1)}), bf16[16,128,128]{2,1,0:T(8,128)(2,1)S(1)}, u32[]{:S(2)}, u32[]{:S(2)}) async-start(bf16[16,128,128]{2,1,0:T(8,128)(2,1)} %broadcast_in_dim.11), calls=%async_computation.5 | async-start | bytes 1048576 | tf_op jit(solution)/shard_map/all_to_all | solution.py:495
  129.5 9.1 %collective-permute-start.9 = (bf16[256,256]{1,0:T(8,128)(2,1)S(1)}, bf16[256,256]{1,0:T(8,128)(2,1)S(1)}, u32[]{:S(2)}, u32[]{:S(2)}) collective-permute-start(bf16[256,256]{1,0:T(8,128)(2,1)S(1)} %get-tuple-element.97), channel_id=1, source_target_pairs={{0,16},{8,24},{16,0},{24,8},{32,48},{40,56},{48,32},{56,40},{64,80... | collective-permute-start | bytes 393224 | tf_op jit(solution)/shard_map/ppermute | solution.py:490
  134.9 1.2 copy-start.1
Sparse Core Ops, SparseCore 0:
  10.7 37.0 all-gather.4
  87.6 27.6 all-gather.6
